TPU v7x, 32 devices: a whole 2x2x4 slice. The times are simulated.
32 devices in a mesh: dp: 16 (over z, y, x), mp: 2 (over core).
Axes of the slice: x: 2, y: 2, z: 4, core: 2. Of those that a mesh axis runs over, the one named last changes fastest.
Arguments:
- patches: bfloat16 [32, 28, 14, 768], P('dp', 'mp'), may hold values from -6 to 6
- norm1_gain: bfloat16 [768], P(('dp', 'mp')), may hold values from 0.099609375 to 1.8984375
- norm1_bias: bfloat16 [768], P(('dp', 'mp')), may hold values from -1.75 to 1.75
- qkv_weight: bfloat16 [768, 2304], P(('dp', 'mp')), may hold values from -0.21875 to 0.21875
- qv_bias: bfloat16 [2, 768], P(None, ('dp', 'mp')), may hold values from -1.75 to 1.75
- rel_pos_h: bfloat16 [27, 64], replicated, may hold values from -0.75 to 0.75
- rel_pos_w: bfloat16 [27, 64], replicated, may hold values from -0.75 to 0.75
- proj_weight: bfloat16 [768, 768], P(('dp', 'mp')), may hold values from -0.875 to 0.875
- proj_bias: bfloat16 [768], P(('dp', 'mp')), may hold values from -1.75 to 1.75
- norm2_gain: bfloat16 [768], P(('dp', 'mp')), may hold values from 0.099609375 to 1.8984375
- norm2_bias: bfloat16 [768], P(('dp', 'mp')), may hold values from -1.75 to 1.75
- fc1_weight: bfloat16 [768, 3072], P('dp', 'mp'), may hold values from -0.21875 to 0.21875
- fc1_bias: bfloat16 [3072], P('mp'), may hold values from -1.75 to 1.75
- fc2_weight: bfloat16 [3072, 768], P('mp', 'dp'), may hold values from -0.109375 to 0.109375
- fc2_bias: bfloat16 [768], P(('dp', 'mp')), may hold values from -1.75 to 1.75
- heights: int32 [32], P('dp'), may hold values from 15 to 28, as said below
- widths: int32 [32], P('dp'), may hold values from 8 to 14, as said below
- out_grad: bfloat16 [32, 28, 14, 768], P('dp', 'mp'), may hold values from -8 to 8
Outputs:
- block_out: bfloat16 [32, 28, 14, 768], P('dp', 'mp')
- patches_grad: float32 [32, 28, 14, 768], P('dp', 'mp')
- norm1_gain_grad: float32 [768], P(('dp', 'mp'))
- norm1_bias_grad: float32 [768], P(('dp', 'mp'))
- qkv_weight_grad: float32 [768, 2304], P(('dp', 'mp'))
- qv_bias_grad: float32 [2, 768], P(None, ('dp', 'mp'))
- rel_pos_h_grad: float32 [27, 64], replicated
- rel_pos_w_grad: float32 [27, 64], replicated
- proj_weight_grad: float32 [768, 768], P(('dp', 'mp'))
- proj_bias_grad: float32 [768], P(('dp', 'mp'))
- norm2_gain_grad: float32 [768], P(('dp', 'mp'))
- norm2_bias_grad: float32 [768], P(('dp', 'mp'))
- fc1_weight_grad: float32 [768, 3072], P('dp', 'mp')
- fc1_bias_grad: float32 [3072], P('mp')
- fc2_weight_grad: float32 [3072, 768], P('mp', 'dp')
- fc2_bias_grad: float32 [768], P(('dp', 'mp'))
Inputs may be any that keep to these rules, and one draw needn't show every extreme that they name: `heights`: some image has the full height and some the least one. `widths`: some image has the full width and some the least one.
All inputs are finite; a program needn't handle non-finite values.
Results may differ from a plain program's by a relative error of at most 0.012.
The roundings to bfloat16 on the way count: a program that leaves them out, or rounds other values in their place, can miss the bound.
Values may be sent and summed in bfloat16 or wider, within the bound.
No kernel may reach another device: no remote copies, remote signals or barrier semaphores. Data moves between devices by JAX's collectives and lax.ppermute only.
A program may use at most 128 MiB of HBM per device.

v0:
```python
from functools import partial

import jax
import jax.numpy as jnp
from jax import lax
from jax.sharding import PartitionSpec as P

HEADS = 12
HDIM = 64


EPSILON = 1e-06
MASKED_SCORE = -1e30
HIGHEST = lax.Precision.HIGHEST


def rounders():

    def value_plain(v):
        return lax.optimization_barrier(v.astype(jnp.bfloat16)).astype(jnp.float32)

    round_value = jax.custom_vjp(value_plain)

    def value_keep(v):
        return (value_plain(v), None)

    def value_pass(kept, grad):
        return (grad,)

    round_value.defvjp(value_keep, value_pass)

    def grad_plain(v):
        return v

    round_grad = jax.custom_vjp(grad_plain)

    def grad_keep(v):
        return (v, None)

    def grad_round(kept, grad):
        return (value_plain(grad),)

    round_grad.defvjp(grad_keep, grad_round)
    return (round_value, round_grad)


def table_rows(rel_table, window):
    offsets = jnp.arange(window)
    rel_index = offsets[:, None] - offsets[None, :] + window - 1
    one_hot = (rel_index[:, :, None] == jnp.arange(2 * window - 1)[None, None, :]).astype(
        jnp.float32
    )
    return jnp.einsum("ykj,jc->ykc", one_hot, rel_table, precision=HIGHEST)


def layer_norm(values, gain_vec, shift_vec):
    row_mean = jnp.mean(values, axis=-1, keepdims=True)
    centered = values - row_mean
    variance = jnp.mean(centered * centered, axis=-1, keepdims=True)
    return centered * lax.rsqrt(variance + EPSILON) * gain_vec + shift_vec


def gelu_exact(inner_val):
    return jax.nn.gelu(inner_val, approximate=False)


def attend(
    tokens_win,
    norm1_gain,
    norm1_bias,
    qkv_weight,
    qv_bias,
    rel_pos_h,
    rel_pos_w,
    proj_weight,
    proj_bias,
    key_mask,
):
    round_value, round_grad = rounders()
    win_count, win_tokens, model_width = tokens_win.shape
    window = (rel_pos_h.shape[0] + 1) // 2
    normed = round_value(layer_norm(tokens_win, norm1_gain, norm1_bias))
    projected = jnp.einsum("bnd,de->bne", normed, qkv_weight)
    queries = projected[..., :model_width] + qv_bias[0]
    key_rows = projected[..., model_width : 2 * model_width]
    value_rows = projected[..., 2 * model_width :] + qv_bias[1]

    def split_heads(inner_val):
        return round_grad(round_value(inner_val)).reshape(win_count, win_tokens, HEADS, HDIM)

    queries, key_rows, value_rows = (
        split_heads(queries),
        split_heads(key_rows),
        split_heads(value_rows),
    )
    score_scale = HDIM ** (-0.5)
    scores = jnp.einsum("bqhc,bkhc->bhqk", queries, key_rows) * score_scale
    query_grid = queries.reshape(win_count, window, window, HEADS, HDIM)
    along_h = round_grad(jnp.einsum("byxhc,ykc->bhyxk", query_grid, table_rows(rel_pos_h, window)))
    along_w = round_grad(jnp.einsum("byxhc,xkc->bhyxk", query_grid, table_rows(rel_pos_w, window)))
    key_place = jnp.arange(win_tokens)[None, :]
    side_place = jnp.arange(window)[:, None]
    spread_h = (key_place // window == side_place).astype(jnp.float32)
    spread_w = (key_place % window == side_place).astype(jnp.float32)
    offsets_h = jnp.einsum(
        "bhnk,km->bhnm",
        along_h.reshape(win_count, HEADS, win_tokens, window),
        spread_h,
        precision=HIGHEST,
    )
    offsets_w = jnp.einsum(
        "bhnk,km->bhnm",
        along_w.reshape(win_count, HEADS, win_tokens, window),
        spread_w,
        precision=HIGHEST,
    )
    scores = round_grad(scores + offsets_h + offsets_w)
    scores = jnp.where(key_mask[:, None, None, :], scores, MASKED_SCORE)
    row_max = jnp.max(scores, axis=-1, keepdims=True)
    exp_terms = jnp.exp(scores - row_max)
    soft_weights = exp_terms / jnp.sum(exp_terms, axis=-1, keepdims=True)
    attended = jnp.einsum("bhqk,bkhc->bqhc", round_value(soft_weights), value_rows)
    attended = round_grad(round_value(attended.reshape(win_count, win_tokens, model_width)))
    branch = round_grad(jnp.einsum("bnd,de->bne", attended, proj_weight) + proj_bias)
    return tokens_win + branch


def local(
    patches,
    norm1_gain,
    norm1_bias,
    qkv_weight,
    qv_bias,
    rel_pos_h,
    rel_pos_w,
    proj_weight,
    proj_bias,
    norm2_gain,
    norm2_bias,
    fc1_weight,
    fc1_bias,
    fc2_weight,
    fc2_bias,
    heights,
    widths,
    out_grad,
):
    image_count, canvas_rows, window, model_width = patches.shape
    row_index = lax.axis_index("mp") * canvas_rows + jnp.arange(canvas_rows)
    col_index = jnp.arange(window)
    valid = (row_index[None, :, None] < heights[:, None, None]) & (
        col_index[None, None, :] < widths[:, None, None]
    )
    key_mask = valid.reshape(-1, window * window)
    row_mask = valid.reshape(-1, 1)
    tokens_win = patches.reshape(-1, window * window, model_width).astype(jnp.float32)
    shared = (
        norm1_gain,
        norm1_bias,
        qkv_weight,
        qv_bias,
        proj_weight,
        proj_bias,
        norm2_gain,
        norm2_bias,
        fc2_bias,
    )
    fetched = (
        lax.all_gather(shared[0], ("dp", "mp"), axis=0, tiled=True),
        lax.all_gather(shared[1], ("dp", "mp"), axis=0, tiled=True),
        lax.all_gather(shared[2], ("dp", "mp"), axis=0, tiled=True),
        lax.all_gather(shared[3], ("dp", "mp"), axis=1, tiled=True),
        lax.all_gather(shared[4], ("dp", "mp"), axis=0, tiled=True),
        lax.all_gather(shared[5], ("dp", "mp"), axis=0, tiled=True),
        lax.all_gather(shared[6], ("dp", "mp"), axis=0, tiled=True),
        lax.all_gather(shared[7], ("dp", "mp"), axis=0, tiled=True),
        lax.all_gather(shared[8], ("dp", "mp"), axis=0, tiled=True),
    )
    hidden_weights = (
        lax.all_gather(fc1_weight, "dp", axis=0, tiled=True),
        lax.all_gather(fc2_weight, "dp", axis=1, tiled=True),
    )
    attend_here = partial(attend, key_mask=key_mask)

    def attend_inputs(params_in):
        return (
            tokens_win,
            params_in[0].astype(jnp.float32),
            params_in[1].astype(jnp.float32),
            params_in[2].astype(jnp.float32),
            params_in[3].astype(jnp.float32),
            rel_pos_h.astype(jnp.float32),
            rel_pos_w.astype(jnp.float32),
            params_in[4].astype(jnp.float32),
            params_in[5].astype(jnp.float32),
        )

    resid_win = attend_here(*attend_inputs(fetched))
    resid = resid_win.reshape(-1, model_width)
    gain_two = fetched[6].astype(jnp.float32)
    shift_two = fetched[7].astype(jnp.float32)
    out_bias = fetched[8].astype(jnp.float32)
    normed = layer_norm(resid, gain_two, shift_two).astype(jnp.bfloat16)
    gathered = lax.all_gather(normed, "mp", axis=0, tiled=True)
    weight_in, weight_out = hidden_weights
    pre_act = jnp.dot(gathered, weight_in, preferred_element_type=jnp.float32) + fc1_bias.astype(
        jnp.float32
    )
    active = gelu_exact(pre_act).astype(jnp.bfloat16)
    token_count = resid.shape[0]
    branch_out = (
        lax.psum_scatter(
            jnp.dot(
                lax.slice_in_dim(active, 0, token_count * lax.axis_size("mp"), axis=0),
                weight_out,
                preferred_element_type=jnp.float32,
            ).astype(jnp.bfloat16),
            "mp",
            scatter_dimension=0,
            tiled=True,
        ).astype(jnp.float32)
        + out_bias
    )
    block_out = (
        jnp.where(row_mask, resid + branch_out, 0.0).reshape(patches.shape).astype(jnp.bfloat16)
    )
    grad_out = jnp.where(row_mask, out_grad.reshape(-1, model_width).astype(jnp.float32), 0.0)
    grad_gathered = lax.all_gather(grad_out.astype(jnp.bfloat16), "mp", axis=0, tiled=True)
    weight_in_back, weight_out_back = (
        lax.all_gather(fc1_weight, "dp", axis=0, tiled=True),
        lax.all_gather(fc2_weight, "dp", axis=1, tiled=True),
    )
    fc2_part = jnp.einsum("nf,nd->fd", active, grad_gathered, preferred_element_type=jnp.float32)
    back_active = jnp.einsum(
        "nd,fd->nf", grad_gathered, weight_out_back, preferred_element_type=jnp.float32
    )
    unused_val, gelu_pull = jax.vjp(gelu_exact, pre_act)
    back_pre = gelu_pull(back_active)[0].astype(jnp.bfloat16)
    fc1_part = jnp.einsum("nd,nf->df", gathered, back_pre, preferred_element_type=jnp.float32)
    fc1_bias_part = jnp.sum(back_pre.astype(jnp.float32), axis=0)
    back_normed = lax.psum_scatter(
        jnp.einsum(
            "nf,df->nd",
            lax.slice_in_dim(back_pre, 0, token_count * lax.axis_size("mp"), axis=0),
            weight_in_back,
            preferred_element_type=jnp.float32,
        ),
        "mp",
        scatter_dimension=0,
        tiled=True,
    )
    unused_norm, norm_pull = jax.vjp(layer_norm, resid, gain_two, shift_two)
    back_resid, gain_two_grad, shift_two_grad = norm_pull(back_normed)
    back_resid = (back_resid + grad_out).reshape(resid_win.shape)
    out_bias_grad = jnp.sum(grad_out, axis=0)
    refetched = (
        lax.all_gather(shared[0], ("dp", "mp"), axis=0, tiled=True),
        lax.all_gather(shared[1], ("dp", "mp"), axis=0, tiled=True),
        lax.all_gather(shared[2], ("dp", "mp"), axis=0, tiled=True),
        lax.all_gather(shared[3], ("dp", "mp"), axis=1, tiled=True),
        lax.all_gather(shared[4], ("dp", "mp"), axis=0, tiled=True),
        lax.all_gather(shared[5], ("dp", "mp"), axis=0, tiled=True),
        lax.all_gather(shared[6], ("dp", "mp"), axis=0, tiled=True),
        lax.all_gather(shared[7], ("dp", "mp"), axis=0, tiled=True),
        lax.all_gather(shared[8], ("dp", "mp"), axis=0, tiled=True),
    )
    unused_attend, again_pull = jax.vjp(attend_here, *attend_inputs(refetched))
    attend_grads = again_pull(back_resid)
    patches_grad = attend_grads[0].reshape(patches.shape)
    summed = (
        lax.psum_scatter(attend_grads[1], ("dp", "mp"), scatter_dimension=0, tiled=True),
        lax.psum_scatter(attend_grads[2], ("dp", "mp"), scatter_dimension=0, tiled=True),
        lax.psum_scatter(attend_grads[3], ("dp", "mp"), scatter_dimension=0, tiled=True),
        lax.psum_scatter(attend_grads[4], ("dp", "mp"), scatter_dimension=1, tiled=True),
        lax.psum_scatter(attend_grads[7], ("dp", "mp"), scatter_dimension=0, tiled=True),
        lax.psum_scatter(attend_grads[8], ("dp", "mp"), scatter_dimension=0, tiled=True),
        lax.psum_scatter(gain_two_grad, ("dp", "mp"), scatter_dimension=0, tiled=True),
        lax.psum_scatter(shift_two_grad, ("dp", "mp"), scatter_dimension=0, tiled=True),
        lax.psum_scatter(out_bias_grad, ("dp", "mp"), scatter_dimension=0, tiled=True),
    )
    rel_summed = lax.psum((attend_grads[5], attend_grads[6]), ("dp", "mp"))
    hidden_summed = (
        lax.psum_scatter(fc1_part, "dp", scatter_dimension=0, tiled=True),
        lax.psum_scatter(fc2_part, "dp", scatter_dimension=1, tiled=True),
    )
    fc1_bias_grad = lax.psum(fc1_bias_part, "dp")
    return (
        block_out,
        patches_grad,
        summed[0],
        summed[1],
        summed[2],
        summed[3],
        rel_summed[0],
        rel_summed[1],
        summed[4],
        summed[5],
        summed[6],
        summed[7],
        hidden_summed[0],
        fc1_bias_grad,
        hidden_summed[1],
        summed[8],
    )


def solution(mesh):
    return jax.shard_map(
        local,
        mesh=mesh,
        in_specs=(
            P("dp", "mp", None, None),
            P(("dp", "mp")),
            P(("dp", "mp")),
            P(("dp", "mp"), None),
            P(None, ("dp", "mp")),
            P(),
            P(),
            P(("dp", "mp"), None),
            P(("dp", "mp")),
            P(("dp", "mp")),
            P(("dp", "mp")),
            P("dp", "mp"),
            P("mp"),
            P("mp", "dp"),
            P(("dp", "mp")),
            P("dp"),
            P("dp"),
            P("dp", "mp", None, None),
        ),
        out_specs=(
            P("dp", "mp", None, None),
            P("dp", "mp", None, None),
            P(("dp", "mp")),
            P(("dp", "mp")),
            P(("dp", "mp"), None),
            P(None, ("dp", "mp")),
            P(),
            P(),
            P(("dp", "mp"), None),
            P(("dp", "mp")),
            P(("dp", "mp")),
            P(("dp", "mp")),
            P("dp", "mp"),
            P("mp"),
            P("mp", "dp"),
            P(("dp", "mp")),
        ),
        check_vma=False,
    )
```

profile of v0, /device:TPU:0, one launch (start us, length us, event | category | flops | bytes accessed | tf_op | source)
XLA Modules:
  0.0 852.6 jit_solution(7126670218056089443)
XLA Ops:
  19.6 42.4 %all-reduce.19 = (bf16[768]{0:T(1024)(128)(2,1)S(1)}, bf16[768]{0:T(1024)(128)(2,1)S(1)}, bf16[768]{0:T(1024)(128)(2,1)S(1)}, bf16[768]{0:T(1024)(128)(2,1)S(1)}...) all-reduce(bf16[768]{0:T(1024)(128)(2,1)S(1)} %dynamic-update-slice, ...), channel_id=1, replica_groups=mesh['dp'=16,'mp'=2] {'dp','mp'}, use_global_device_ids=true, to_apply=%add.6 | all-reduce | flops 4608 | bytes 18432
  63.4 40.8 %all-gather = bf16[32,24,2]{1,2,0:T(2,128)(2,1)S(1)} all-gather(bf16[1,24,2]{1,2,0:T(2,128)(2,1)S(1)} %bitcast.172), channel_id=1, replica_groups=mesh['dp'=16,'mp'=2] {'dp','mp'}, dimensions={0}, use_global_device_ids=true | all-gather | bytes 3168 | tf_op jit(solution)/shard_map/all_gather | solution.py:172
  113.4 4.9 convolution_bitcast_fusion.2
  121.9 4.7 copy.197
  130.0 4.9 convolution_bitcast_fusion.1
  168.0 25.9 %all-gather.14.cloned.1.call-done = bf16[768,1536]{1,0:T(8,128)(2,1)} async-done(((bf16[48,1536]{1,0:T(8,128)(2,1)}), bf16[768,1536]{1,0:T(8,128)(2,1)}) %all-gather.14.cloned.1.call-update) | async-done | bytes 2359312 | tf_op jit(solution)/shard_map/all_gather | solution.py:180
  193.8 10.1 %all-gather.12.cloned.1.call-done = bf16[784,768]{1,0:T(8,128)(2,1)} async-done(((bf16[392,768]{1,0:T(8,128)(2,1)}), bf16[784,768]{1,0:T(8,128)(2,1)}) %all-gather.12.cloned.1.call-update) | async-done | bytes 1204240 | tf_op jit(solution)/shard_map/all_gather | solution.py:204
  203.9 6.3 fusion.71
  210.2 6.2 all-gather.18.cloned.1.call-done
  216.3 66.1 %all-gather.16.cloned.1.call-done = bf16[1536,768]{0,1:T(8,128)(2,1)} async-done(((bf16[1536,48]{0,1:T(8,128)(2,1)}), bf16[1536,768]{0,1:T(8,128)(2,1)}) %all-gather.16.cloned.1.call-update) | async-done | bytes 2359312 | tf_op jit(solution)/shard_map/all_gather | solution.py:181
  282.5 17.7 %convert_reduce_fusion.1 = (f32[1536]{0:T(1024)}, bf16[784,1536]{1,0:T(8,128)(2,1)S(1)}, f32[784,1536]{1,0:T(8,128)}) fusion(f32[784,1536]{1,0:T(8,128)} %fusion.71, f32[1536]{0:T(1024)S(1)} %convert_element_type.210, bf16[784,768]{1,0:T(8,128)(2,1)} %all-gather.18.cloned.1.call-done, bf16[1536,768]{0,1:T(8,128)(2,1)} %all-gather.16.cloned.1.call-done), kind=kOutput, calls=%fused_computation.13 | convolution fusion | flops 1940003328 | bytes 15618048 | tf_op jit(solution)/shard_map/nd,fd->nf/dot_general | solution.py:234
  305.3 5.2 multiply_convert_fusion
  316.9 10.0 %reduce-scatter.8.cloned.1.call-done = bf16[392,768]{1,0:T(8,128)(2,1)} async-done(((bf16[784,768]{1,0:T(8,128)(2,1)}), bf16[392,768]{1,0:T(8,128)(2,1)}) %reduce-scatter.8.cloned.1.call-update) | async-done | bytes 602128 | tf_op jit(solution)/shard_map/reduce_scatter | solution.py:212
  337.1 5.9 fusion.73
  344.8 5.6 fusion.74
  361.7 4.8 multiply_reduce_fusion
  377.7 5.3 copy.166
  404.8 7.0 convolution_bitcast_fusion
  413.6 43.1 %psum.23 = f32[1536]{0:T(1024)} all-reduce(f32[1536]{0:T(1024)S(1)} %copy-done.53), channel_id=1, replica_groups=mesh['dp'=16,'mp'=2] {'dp'}, use_global_device_ids=true, to_apply=%region_34.35 | all-reduce | flops 1536 | bytes 12288 | tf_op jit(solution)/shard_map/psum | solution.py:286
  456.7 4.9 copy.178
  477.5 39.1 %all-reduce.18 = (f32[768]{0:T(1024)S(1)}, f32[768]{0:T(1024)S(1)}, f32[2,768]{1,0:T(2,128)S(1)}, f32[27,64]{1,0:T(8,128)}, f32[27,64]{1,0:T(8,128)}, /*index=5*...) all-reduce(f32[768]{0:T(1024)S(1)} %get-tuple-element.80, ...), channel_id=4, replica_groups=mesh['dp'=16,'mp'=2] {'dp','mp'}, use_global_device_ids=true, to_apply=%region_16.17.clone | all-reduce | flops 9600 | bytes 76800
  525.7 52.9 %reduce-scatter.16.cloned.1.call-done = f32[48,1536]{1,0:T(8,128)} async-done(((f32[768,1536]{1,0:T(8,128)}), f32[48,1536]{1,0:T(8,128)}) %reduce-scatter.16.cloned.1.call-update) | async-done | bytes 294928 | tf_op jit(solution)/shard_map/reduce_scatter | solution.py:283
  578.6 142.7 %reduce-scatter.18.cloned.1.call-done = f32[1536,48]{0,1:T(8,128)} async-done(((f32[1536,768]{0,1:T(8,128)}), f32[1536,48]{0,1:T(8,128)}) %reduce-scatter.18.cloned.1.call-update) | async-done | bytes 294928 | tf_op jit(solution)/shard_map/reduce_scatter | solution.py:284
  721.2 124.3 %reduce-scatter.12.cloned.1.call-done = f32[24,2304]{1,0:T(8,128)} async-done(((f32[768,2304]{1,0:T(8,128)}), f32[24,2304]{1,0:T(8,128)}) %reduce-scatter.12.cloned.1.call-update) | async-done | bytes 221200 | tf_op jit(solution)/shard_map/reduce_scatter | solution.py:273
  (298 shorter events, 156.6 us)
Async XLA Ops:
  7.2 97.4 %copy-start = (bf16[27,64]{1,0:T(8,128)(2,1)S(1)}, bf16[27,64]{1,0:T(8,128)(2,1)}, u32[]{:S(2)}) copy-start(bf16[27,64]{1,0:T(8,128)(2,1)} %param.23) | copy-start | bytes 10372
  7.2 54.8 %copy-start.24 = (bf16[2,14,14,768]{3,0,2,1:T(2,128)(2,1)S(1)}, bf16[2,14,14,768]{3,0,2,1:T(2,128)(2,1)}, u32[]{:S(2)}) copy-start(bf16[2,14,14,768]{3,0,2,1:T(2,128)(2,1)} %param.18) | copy-start | bytes 1806340
  7.2 98.7 %all-gather.8.cloned.1.call-start = ((), (), s32[]{:S(2)}) async-start(), calls=%async_computation.6 | async-start | bytes 3649536 | tf_op jit(solution)/shard_map/all_gather | solution.py:171
  7.9 151.3 %all-gather.10.cloned.1.call-start = ((), (), s32[]{:S(2)}) async-start(), calls=%async_computation.7 | async-start | bytes 1216512 | tf_op jit(solution)/shard_map/all_gather | solution.py:173
  8.7 185.1 %all-gather.14.cloned.1.call-start = ((), (), s32[]{:S(2)}) async-start(), calls=%async_computation.9 | async-start | bytes 2506752 | tf_op jit(solution)/shard_map/all_gather | solution.py:180
  9.4 194.5 %all-gather.12.cloned.1.call-start = ((), (), s32[]{:S(2)}) async-start(), calls=%async_computation.8 | async-start | bytes 1806336 | tf_op jit(solution)/shard_map/all_gather | solution.py:204
  11.1 52.3 %copy-start.59 = (bf16[2,24]{1,0:T(2,128)(2,1)S(1)}, bf16[2,24]{1,0:T(2,128)(2,1)}, u32[]{:S(2)}) copy-start(bf16[2,24]{1,0:T(2,128)(2,1)} %param.22) | copy-start | bytes 292
  13.2 91.6 %copy-start.64 = (bf16[27,64]{1,0:T(8,128)(2,1)S(1)}, bf16[27,64]{1,0:T(8,128)(2,1)}, u32[]{:S(2)}) copy-start(bf16[27,64]{1,0:T(8,128)(2,1)} %param.24) | copy-start | bytes 10372
  13.2 91.8 %copy-start.60 = (s32[2]{0:T(128)S(1)}, s32[2]{0:T(128)}, u32[]{:S(2)}) copy-start(s32[2]{0:T(128)} %param.34) | copy-start | bytes 28
  13.2 91.8 %copy-start.61 = (s32[2]{0:T(128)S(1)}, s32[2]{0:T(128)}, u32[]{:S(2)}) copy-start(s32[2]{0:T(128)} %param.33) | copy-start | bytes 28
  13.5 96.1 %copy-start.42 = (s32[14,14]{1,0:T(8,128)}, s32[14,14]{1,0:T(8,128)S(1)}, u32[]{:S(2)}) copy-start(s32[14,14]{1,0:T(8,128)S(1)} %subtract_add_fusion) | copy-start | bytes 2356
  62.0 47.6 %copy-start.44 = (f32[768]{0:T(1024)}, f32[768]{0:T(1024)S(1)}, u32[]{:S(2)}) copy-start(f32[768]{0:T(1024)S(1)} %convert_element_type.196) | copy-start | bytes 9220
  62.4 96.9 %copy-start.3 = (f32[2,196,768]{2,0,1:T(2,128)}, f32[2,196,768]{2,0,1:T(2,128)S(1)}, u32[]{:S(2)}) copy-start(f32[2,196,768]{2,0,1:T(2,128)S(1)} %convert.9) | copy-start | bytes 3612676
  63.4 46.1 %copy-start.22 = (bf16[2,196,768]{2,1,0:T(8,128)(2,1)}, bf16[2,196,768]{2,1,0:T(8,128)(2,1)S(1)}, u32[]{:S(2)}) copy-start(bf16[2,196,768]{2,1,0:T(8,128)(2,1)S(1)} %add_convert_fusion.1) | copy-start | bytes 1806340
  163.4 53.0 %all-gather.18.cloned.1.call-start = ((), (), s32[]{:S(2)}) async-start(), calls=%async_computation.12 | async-start | bytes 1806336 | tf_op jit(solution)/shard_map/all_gather | solution.py:228
  167.3 115.2 %all-gather.16.cloned.1.call-start = ((), (), s32[]{:S(2)}) async-start(), calls=%async_computation.10 | async-start | bytes 2506752 | tf_op jit(solution)/shard_map/all_gather | solution.py:181
  167.9 147.2 %reduce-scatter.10.cloned.1.call-start = ((), (), s32[]{:S(2)}) async-start(), calls=%async_computation.13 | async-start | bytes 3612672 | tf_op jit(solution)/shard_map/reduce_scatter | solution.py:241
  305.2 21.7 %reduce-scatter.8.cloned.1.call-start = ((), (), s32[]{:S(2)}) async-start(), calls=%async_computation.11 | async-start | bytes 1806336 | tf_op jit(solution)/shard_map/reduce_scatter | solution.py:212
  315.0 210.6 %reduce-scatter.14.cloned.1.call-start = ((), (), s32[]{:S(2)}) async-start(), calls=%async_computation.15 | async-start | bytes 2433024 | tf_op jit(solution)/shard_map/reduce_scatter | solution.py:275
  335.9 242.7 %reduce-scatter.16.cloned.1.call-start = ((), (), s32[]{:S(2)}) async-start(), calls=%async_computation.16 | async-start | bytes 5013504 | tf_op jit(solution)/shard_map/reduce_scatter | solution.py:283
  343.1 378.1 %reduce-scatter.18.cloned.1.call-start = ((), (), s32[]{:S(2)}) async-start(), calls=%async_computation.17 | async-start | bytes 5013504 | tf_op jit(solution)/shard_map/reduce_scatter | solution.py:284
  350.4 495.1 %reduce-scatter.12.cloned.1.call-start = ((), (), s32[]{:S(2)}) async-start(), calls=%async_computation.14 | async-start | bytes 7299072 | tf_op jit(solution)/shard_map/reduce_scatter | solution.py:273
  411.8 49.8 %copy-start.7 = (bf16[2,12,14,14,14]{3,2,0,4,1:T(8,128)(2,1)S(1)}, bf16[2,12,14,14,14]{3,2,0,4,1:T(8,128)(2,1)}, u32[]{:S(2)}) copy-start(bf16[2,12,14,14,14]{3,2,0,4,1:T(8,128)(2,1)} %convert_element_type.236) | copy-start | bytes 395140
  520.1 325.4 %copy-start.1 = (bf16[27,64]{1,0:T(8,128)(2,1)S(1)}, bf16[27,64]{1,0:T(8,128)(2,1)}, u32[]{:S(2)}) copy-start(bf16[27,64]{1,0:T(8,128)(2,1)} %param.23) | copy-start | bytes 10372
  (55 other events, 265.4 us)
Sparse Core Ops, SparseCore 0:
  10.9 63.1 all-gather.7
  77.0 52.7 all-gather.9
  132.6 61.2 all-gather.13
  195.8 8.0 all-gather.11
  205.9 10.4 all-gather.17
  219.0 63.4 all-gather.15
  305.3 8.7 reduce-scatter.9
  317.1 9.8 reduce-scatter.7
  336.0 100.2 reduce-scatter.13
  441.9 136.6 reduce-scatter.15
  585.1 136.0 reduce-scatter.17
  727.3 118.1 reduce-scatter.11
where the time goes:
time: 858 us; the launch traced here: 853 us
  waiting for transfers between devices  441 us (51%)
  blocking collectives  165 us (19%)
  matrix products  105 us (12%)
  local copies, waits for them, and re-layouts  88.4 us (10%)
  other arithmetic  36.8 us (4%)
  between operations  15.5 us (2%)
    reduce_scatter x1, waiting for transfers between devices, local(): lax.psum_scatter(fc2_part, 'dp', scatter_dimension=1, tiled=True)  143 us
    reduce_scatter x1, waiting for transfers between devices, local(): lax.psum_scatter(attend_grads[3], ('dp', 'mp'), scatter_dimension=0, tile...  124 us
    unnamed x2, blocking collectives  81.4 us
    all_gather x1, waiting for transfers between devices, local(): lax.all_gather(fc2_weight, 'dp', axis=1, tiled=True)  66.1 us
    reduce_scatter x1, waiting for transfers between devices, local(): lax.psum_scatter(fc1_part, 'dp', scatter_dimension=0, tiled=True)  52.9 us
    psum x1, blocking collectives, local(): fc1_bias_grad = lax.psum(fc1_bias_part, 'dp')  43.1 us
    all_gather x1, blocking collectives, local(): lax.all_gather(shared[3], ('dp', 'mp'), axis=1, tiled=True)  40.8 us
    all_gather x1, waiting for transfers between devices, local(): lax.all_gather(fc1_weight, 'dp', axis=0, tiled=True)  25.9 us
  transfers between devices with their start and end apart: 12, of which 8 were waited for; matrix products, arithmetic and copies ran while one was open for 22% of the time, Pallas kernels for 0%

commit v1 on v0

v1 whole, which is shorter than its diff:
```python
from functools import partial

import jax
import jax.numpy as jnp
import numpy as np
from jax import lax
from jax.experimental import pallas as pl
from jax.experimental.pallas import tpu as pltpu
from jax.sharding import PartitionSpec as P

HEADS = 12
HDIM = 64
LANES = 128
PAIRS = HEADS // 2
WIN = 14
SIDE = 16
TOK = WIN * SIDE
KEYS = 256
PIECES = 16
EPSILON = 1e-06
MASKED_SCORE = -1e30
MASK_LANE = 60
FFN_CHUNKS = 3
BACK_CHUNKS = 1
F32 = jnp.float32
BF16 = jnp.bfloat16
SMEM = pl.BlockSpec(memory_space=pltpu.SMEM)
HBM = pl.BlockSpec(memory_space=pl.ANY)
WHOLE = pl.BlockSpec(memory_space=pltpu.VMEM)
VMEM_BYTES = 52 * 2**20


def params():
    return pltpu.CompilerParams(vmem_limit_bytes=VMEM_BYTES)


def shape(dims, dtype):
    return jax.ShapeDtypeStruct(dims, dtype)


def dot(a, b):
    return jnp.dot(a, b, preferred_element_type=F32)


def dot_nt(a, b):
    return lax.dot_general(a, b, (((1,), (1,)), ((), ())), preferred_element_type=F32)


def dot_tn(a, b):
    return lax.dot_general(a, b, (((0,), (0,)), ((), ())), preferred_element_type=F32)


def lanes(rows):
    return lax.broadcasted_iota(jnp.int32, (rows, LANES), 1)


def moments(values):
    centered = values - jnp.mean(values, axis=-1, keepdims=True)
    inverse = lax.rsqrt(jnp.mean(centered * centered, axis=-1, keepdims=True) + EPSILON)
    return centered * inverse, inverse


def norm_back(grad, xhat, inverse, gain):
    scaled = grad * gain
    first = jnp.mean(scaled, axis=-1, keepdims=True)
    second = jnp.mean(scaled * xhat, axis=-1, keepdims=True)
    return inverse * (scaled - first - xhat * second)


def pieces_in(meta, at, refs, rows, cols, dest, sems, first):
    copies = []
    for ref in refs:
        for part in range(ref.shape[0] // rows):
            place = pl.multiple_of(meta[at + len(copies)] * rows, rows)
            copy = pltpu.make_async_copy(
                ref.at[pl.ds(part * rows, rows), cols],
                dest.at[pl.ds(place, rows), :],
                sems.at[first + len(copies)],
            )
            copy.start()
            copies.append(copy)
    return copies


def row_valid(meta, core, window, rows, width):
    place = lax.broadcasted_iota(jnp.int32, (rows, width), 0)
    row, col = place // SIDE, place % SIDE
    inside = (row < WIN) & (col < WIN)
    return inside & (core * WIN + row < meta[33 + window]) & (col < meta[35 + window])


def relative(turned):
    out = []
    for row in range(WIN):
        slab = turned[row * SIDE : (row + 1) * SIDE]
        down = pltpu.roll(slab, row, 1) if row else slab
        across = pltpu.roll(slab, 0, 1, stride=1, stride_axis=0)
        out.append(jnp.where(lanes(SIDE) % 64 < 32, down, across))
    return jnp.concatenate(out, axis=0)


def attend_kernel(count, meta, tok, table, spread, *refs):
    own0, own1 = refs[:count], refs[count : 2 * count]
    other0, other1 = refs[2 * count : 3 * count], refs[3 * count : 4 * count]
    (n1, q_out, k_out, v_out, p_out, att, x1, n2, vecs, w_out) = refs[4 * count : 4 * count + 10]
    weights, small, aug, sems, out_sem = refs[4 * count + 10 :]
    width = weights.shape[1]
    rows = width // PIECES
    core = meta[32]
    copies = []
    for refs_here, at, which, extra in (
        (own0, 0, 2 * core, True),
        (own1, 16, 2 * core + 1, False),
        (other0, 0, 2 - 2 * core, False),
        (other1, 16, 3 - 2 * core, False),
    ):
        copies += pieces_in(
            meta, at, refs_here, rows, pl.ds(0, width), weights.at[which], sems, len(copies)
        )
        if extra:
            copies += pieces_in(
                meta, at, refs_here, rows, pl.ds(width, LANES), small, sems, len(copies)
            )
    for window in range(2):
        keys = lanes(KEYS)
        valid = row_valid(meta, core, window, KEYS, LANES)
        aug[window] = jnp.where(
            (keys == MASK_LANE) & ~valid, MASKED_SCORE, spread[...].astype(F32)
        ).astype(BF16)
        k_out[window, TOK:] = jnp.zeros((KEYS - TOK, width), BF16)
        v_out[window, TOK:] = jnp.zeros((KEYS - TOK, width), BF16)
    tokens = tok[...].reshape(2 * TOK, width).astype(F32)
    xhat, _ = moments(tokens)
    for copy in copies:
        copy.wait()
    out_copy = pltpu.make_async_copy(weights, w_out, out_sem)
    out_copy.start()
    vecs[...] = small[...].astype(F32).T[:8]
    normed = (xhat * vecs[0:1] + vecs[1:2]).astype(BF16)
    n1[...] = normed.reshape(2, TOK, width)
    for mat, dest in enumerate((q_out, k_out, v_out)):
        for start in range(0, width, 256):
            cols = pl.ds(start, 256)
            made = dot(normed, weights[mat, :, cols])
            if mat != 1:
                made = made + vecs[2 + mat // 2 : 3 + mat // 2, cols]
            made = made.astype(BF16)
            dest[0, :TOK, cols] = made[:TOK]
            dest[1, :TOK, cols] = made[TOK:]

    def heads_of(step, _):
        window, pair = step // PAIRS, step % PAIRS
        cols = pl.ds(pl.multiple_of(pair * LANES, LANES), LANES)
        q2, k2, v2 = q_out[window, :, cols], k_out[window, :, cols], v_out[window, :, cols]
        turned = dot(q2, table[...])
        place = lanes(TOK)
        keys_aug = jnp.concatenate([k2, aug[window]], axis=1)
        parts = []
        for half in range(2):
            rel = relative(turned[:, half * LANES : (half + 1) * LANES])
            high = rel.astype(BF16).astype(F32)
            rel = jnp.where(place < 64, high, rel - high)
            rel = jnp.where(place == MASK_LANE, 1.0, rel).astype(BF16)
            mine = jnp.where(place // 64 == half, q2.astype(F32) * HDIM**-0.5, 0.0).astype(BF16)
            scores = dot_nt(jnp.concatenate([mine, rel], axis=1), keys_aug)
            terms = jnp.exp(scores - jnp.max(scores, axis=-1, keepdims=True))
            soft = terms * (1.0 / jnp.sum(terms, axis=-1, keepdims=True))
            soft = soft.astype(BF16)
            p_out[window, 2 * pair + half] = soft
            parts.append(dot(soft, v2))
        att[window, :, cols] = jnp.where(place < 64, parts[0], parts[1]).astype(BF16)
        return 0

    lax.fori_loop(0, 2 * PAIRS, heads_of, 0)
    attended = att[...].reshape(2 * TOK, width)
    tokens = tok[...].reshape(2 * TOK, width).astype(F32)
    resid = tokens + (dot(attended, weights[3]) + vecs[4:5])
    x1[...] = resid.reshape(2, TOK, width)
    xhat2, _ = moments(resid)
    n2[...] = (xhat2 * vecs[5:6] + vecs[6:7]).astype(BF16).reshape(2, TOK, width)
    out_copy.wait()


def attend(meta, tok, table, spread, own0, own1, other0, other1):
    count, width = len(own0), tok.shape[-1]
    rows = (2, TOK, width)
    keys = (2, KEYS, width)
    return pl.pallas_call(
        partial(attend_kernel, count),
        out_shape=[
            shape(rows, BF16),
            shape(rows, BF16),
            shape(keys, BF16),
            shape(keys, BF16),
            shape((2, HEADS, TOK, KEYS), BF16),
            shape(rows, BF16),
            shape(rows, F32),
            shape(rows, BF16),
            shape((8, width), F32),
            shape((4, width, width), BF16),
        ],
        in_specs=[SMEM, WHOLE, WHOLE, WHOLE] + [HBM] * (4 * count),
        out_specs=[WHOLE] * 9 + [HBM],
        scratch_shapes=[
            pltpu.VMEM((4, width, width), BF16),
            pltpu.VMEM((width, LANES), BF16),
            pltpu.VMEM((2, KEYS, LANES), BF16),
            pltpu.SemaphoreType.DMA((5 * PIECES,)),
            pltpu.SemaphoreType.DMA,
        ],
        compiler_params=params(),
        cost_estimate=pl.CostEstimate(
            flops=6_000_000_000, bytes_accessed=20_000_000, transcendentals=1_500_000
        ),
        name="attend",
    )(meta, tok, table, spread, *own0, *own1, *other0, *other1)


def hidden_kernel(count, first, last, meta, n2a, n2b, dma, dmb, bias, *refs):
    refs = list(refs)
    in0, in1 = refs[:count], refs[count : 2 * count]
    refs = refs[2 * count :]
    if not first:
        out_in, back_in = refs[:2]
        refs = refs[2:]
    g0_keep, g0_send, g1_keep, g1_send, bias_grad = refs[:5]
    refs = refs[5:]
    if last:
        out_own, out_far, back_own, back_far = refs[:4]
        refs = refs[4:]
    else:
        out_acc, back_acc = refs[:2]
        refs = refs[2:]
    w0, w1, n2s, dms, acts, backs, g0, g1, sems, out_sems = refs
    width, cols_here = w0.shape
    rows = width // PIECES
    copies = pieces_in(meta, 0, in0, rows, pl.ds(0, cols_here), w0, sems, 0)
    copies += pieces_in(meta, 16, in1, rows, pl.ds(0, cols_here), w1, sems, PIECES)
    n2s[: 2 * TOK] = n2a[...].reshape(2 * TOK, width)
    n2s[2 * TOK :] = n2b[...].reshape(2 * TOK, width)
    dms[: 2 * TOK] = dma[...].reshape(2 * TOK, width)
    dms[2 * TOK :] = dmb[...].reshape(2 * TOK, width)
    for copy in copies:
        copy.wait()
    outs = []
    for start in range(0, cols_here, 256):
        cols = pl.ds(start, 256)
        inner = dot(n2s[...], w0[:, cols]) + bias[:, cols]
        back = dot(dms[...], w1[:, cols])
        cdf = 0.5 + 0.5 * lax.erf(inner * 0.7071067811865476)
        density = jnp.exp(inner * inner * -0.5) * 0.3989422804014327
        acts[:, cols] = (inner * cdf).astype(BF16)
        back_pre = (back * (cdf + inner * density)).astype(BF16)
        backs[:, cols] = back_pre
        bias_grad[:, cols] = jnp.sum(back_pre.astype(F32), axis=0, keepdims=True)
        g0[:, cols] = dot_tn(n2s[...], back_pre).astype(BF16)
        g1[:, cols] = dot_tn(dms[...], acts[:, cols]).astype(BF16)
        for which, (made, keep, send) in enumerate(((g0, g0_keep, g0_send), (g1, g1_keep, g1_send))):
            for piece in range(PIECES):
                dest = keep if piece < PIECES // 2 else send
                place = pl.multiple_of(meta[16 * which + piece] * rows, rows)
                at = (piece % (PIECES // 2)) * rows
                copy = pltpu.make_async_copy(
                    made.at[pl.ds(place, rows), cols],
                    dest.at[pl.ds(at, rows), cols],
                    out_sems.at[len(outs)],
                )
                copy.start()
                outs.append(copy)
    made_out = dot_nt(acts[...], w1[...])
    made_back = dot_nt(backs[...], w0[...])
    if not first:
        made_out = made_out + out_in[...]
        made_back = made_back + back_in[...]
    if last:
        out_own[...] = made_out[: 2 * TOK]
        out_far[...] = made_out[2 * TOK :].astype(BF16)
        back_own[...] = made_back[: 2 * TOK]
        back_far[...] = made_back[2 * TOK :].astype(BF16)
    else:
        out_acc[...] = made_out
        back_acc[...] = made_back
    for copy in outs:
        copy.wait()


def hidden(meta, n2a, n2b, dma, dmb, bias, in0, in1, carried, last):
    count, width, cols_here = len(in0), n2a.shape[-1], bias.shape[-1]
    first = carried is None
    half = (width // 2, cols_here)
    out_shape = [shape(half, BF16)] * 4 + [shape((1, cols_here), F32)]
    if last:
        one = (2 * TOK, width)
        out_shape += [shape(one, F32), shape(one, BF16), shape(one, F32), shape(one, BF16)]
    else:
        out_shape += [shape((4 * TOK, width), F32)] * 2
    carried = () if first else carried
    return pl.pallas_call(
        partial(hidden_kernel, count, first, last),
        out_shape=out_shape,
        in_specs=[SMEM] + [WHOLE] * 5 + [HBM] * (2 * count) + [WHOLE] * len(carried),
        out_specs=[HBM] * 4 + [WHOLE] * (len(out_shape) - 4),
        scratch_shapes=[
            pltpu.VMEM((width, cols_here), BF16),
            pltpu.VMEM((width, cols_here), BF16),
            pltpu.VMEM((4 * TOK, width), BF16),
            pltpu.VMEM((4 * TOK, width), BF16),
            pltpu.VMEM((4 * TOK, cols_here), BF16),
            pltpu.VMEM((4 * TOK, cols_here), BF16),
            pltpu.VMEM((width, cols_here), BF16),
            pltpu.VMEM((width, cols_here), BF16),
            pltpu.SemaphoreType.DMA((2 * PIECES,)),
            pltpu.SemaphoreType.DMA((2 * PIECES * (cols_here // 256),)),
        ],
        compiler_params=params(),
        cost_estimate=pl.CostEstimate(
            flops=12 * 4 * TOK * width * cols_here,
            bytes_accessed=20_000_000,
            transcendentals=8 * TOK * cols_here,
        ),
        name="hidden",
    )(meta, n2a, n2b, dma, dmb, bias, *in0, *in1, *carried)


def middle_kernel(meta, out_own, out_far, back_own, back_far, x1, dm, vecs, block, dx1, da, sums):
    width = x1.shape[-1]
    core = meta[32]
    total = [jnp.zeros((1, width), F32) for _ in range(4)]
    for window in range(2):
        rows = pl.ds(window * TOK, TOK)
        resid = x1[window]
        valid = row_valid(meta, core, window, TOK, width)
        branch = out_own[rows] + out_far[rows].astype(F32) + vecs[7:8]
        block[window] = jnp.where(valid, resid + branch, 0.0).astype(BF16)
        grad = back_own[rows] + back_far[rows].astype(F32)
        xhat, inverse = moments(resid)
        out_grad = dm[window].astype(F32)
        dresid = out_grad + norm_back(grad, xhat, inverse, vecs[5:6])
        dx1[window] = dresid
        rounded = dresid.astype(BF16)
        da[window] = rounded
        for slot, value in enumerate((rounded.astype(F32), grad * xhat, grad, out_grad)):
            total[slot] = total[slot] + jnp.sum(value, axis=0, keepdims=True)
    sums[...] = jnp.concatenate([jnp.zeros((4, width), F32)] + total, axis=0)


def middle(meta, out_own, out_far, back_own, back_far, x1, dm, vecs):
    rows = x1.shape
    return pl.pallas_call(
        middle_kernel,
        out_shape=[
            shape(rows, BF16),
            shape(rows, F32),
            shape(rows, BF16),
            shape((8, rows[-1]), F32),
        ],
        in_specs=[SMEM] + [WHOLE] * 7,
        out_specs=[WHOLE] * 4,
        compiler_params=params(),
        cost_estimate=pl.CostEstimate(
            flops=20_000_000, bytes_accessed=9_000_000, transcendentals=0
        ),
        name="middle",
    )(meta, out_own, out_far, back_own, back_far, x1, dm, vecs)


def unrelative(grads):
    out = []
    for row in range(WIN):
        slab = grads[row * SIDE : (row + 1) * SIDE]
        down = pltpu.roll(slab, row, 1) if row else slab
        across = pltpu.roll(slab, 0, 1, stride=1, stride_axis=0)
        out.append(jnp.where(lanes(SIDE) < 32, down, across))
    return jnp.concatenate(out, axis=0)


def attend_back_kernel(
    first, last, meta, q, k, v, p, wqkv, wproj, da, da_cols, att, n1, tok, dx1, vecs, gather, table, *refs
):
    refs = list(refs)
    if not first:
        dn1_in = refs.pop(0)
    mine0, mine1, theirs0, theirs1, bias_sums, table_grad, result = refs[:7]
    refs = refs[7:]
    if last:
        norm_sums = refs.pop(0)
    dat, dqkv, grads, sems = refs
    core = meta[32]
    width, cols_here = da.shape[-1], q.shape[-1]
    pairs, rows = cols_here // LANES, width // PIECES
    dat[...] = (
        dot_nt(da[...].reshape(2 * TOK, width), wproj[0]).astype(BF16).reshape(2, TOK, cols_here)
    )
    table_grad[...] = jnp.zeros_like(table_grad)
    outs = []

    def send(mat, made):
        grads[mat] = made.astype(BF16)
        own, far = (mine0, theirs0) if mat % 2 == 0 else (mine1, theirs1)
        for piece in range(PIECES):
            place = pl.multiple_of(meta[16 * (mat % 2) + piece] * rows, rows)
            source = grads.at[mat, pl.ds(place, rows), :]
            to, sem = pl.ds(piece * rows, rows), sems.at[len(outs)]
            copies = [pltpu.make_async_copy(source, ref.at[to, :], sem) for ref in (own, far)]
            pl.when(core == mat // 2)(copies[0].start)
            pl.when(core != mat // 2)(copies[1].start)
            outs.append(copies[0])

    send(3, dot_tn(att[...].reshape(2 * TOK, width), da_cols[...].reshape(2 * TOK, cols_here)))

    def heads_of(step, _):
        window, pair = step // pairs, step % pairs
        cols = pl.ds(pl.multiple_of(pair * LANES, LANES), LANES)
        q2, k2, v2 = q[window, :, cols], k[window, :, cols], v[window, :, cols]
        dat2 = dat[window, :, cols]
        place = lanes(TOK)
        q8 = (q2.astype(F32) * HDIM**-0.5).astype(BF16)
        k8 = (k2.astype(F32) * HDIM**-0.5).astype(BF16)
        dqs, dks, dvs, dts = [], [], [], []
        for half in range(2):
            soft = p[window, 2 * pair + half]
            soft32 = soft.astype(F32)
            mine = jnp.where(place // 64 == half, dat2.astype(F32), 0.0).astype(BF16)
            weighted = soft32 * dot_nt(mine, v2)
            ds = (weighted - soft32 * jnp.sum(weighted, axis=-1, keepdims=True)).astype(BF16)
            turned = dot(ds, gather[...]).astype(BF16).astype(F32)
            turned = unrelative(turned).astype(BF16)
            dqs.append(dot(ds, k8) + dot(turned, table[half]))
            dks.append(dot_tn(ds, q8))
            dvs.append(dot_tn(soft, dat2))
            dts.append(dot_tn(turned, q2))
        key_place = lanes(TOK)
        dqkv[0, window, :, cols] = jnp.where(place < 64, dqs[0], dqs[1]).astype(BF16)
        dqkv[1, window, :, cols] = jnp.where(key_place < 64, dks[0][:TOK], dks[1][:TOK]).astype(BF16)
        dqkv[2, window, :, cols] = jnp.where(key_place < 64, dvs[0][:TOK], dvs[1][:TOK]).astype(BF16)
        table_grad[...] += jnp.where(lanes(LANES) < 64, dts[0], dts[1])
        return 0

    lax.fori_loop(0, 2 * pairs, heads_of, 0)
    normed = n1[...].reshape(2 * TOK, width)
    dn1 = jnp.zeros((2 * TOK, width), F32) if first else dn1_in[...].reshape(2 * TOK, width)
    for mat in range(3):
        change = dqkv[mat].reshape(2 * TOK, cols_here)
        send(mat, dot_tn(normed, change))
        dn1 = dn1 + dot_nt(change, wqkv[mat])
        if mat != 1:
            bias_sums[mat // 2 : mat // 2 + 1] = jnp.sum(change.astype(F32), axis=0, keepdims=True)
    if last:
        xhat, inverse = moments(tok[...].reshape(2 * TOK, width).astype(F32))
        norm_sums[0:1] = jnp.sum(dn1 * xhat, axis=0, keepdims=True)
        norm_sums[1:2] = jnp.sum(dn1, axis=0, keepdims=True)
        back = norm_back(dn1, xhat, inverse, vecs[0:1])
        result[...] = dx1[...] + back.reshape(2, TOK, width)
    else:
        result[...] = dn1.reshape(2, TOK, width)
    for copy in outs:
        copy.wait()


def attend_back(chunk, chunks, meta, q, k, v, p, weights, da, att, n1, tok, dx1, vecs, gather, table, dn1):
    width = q.shape[-1]
    cols_here, heads_here = width // chunks, HEADS // chunks
    first, last = chunk == 0, chunk == chunks - 1
    part = lambda rows: pl.BlockSpec((2, rows, cols_here), lambda i: (0, 0, chunk))
    out_shape = [shape((width, cols_here), BF16)] * 4 + [
        shape((2, cols_here), F32),
        shape((LANES, LANES), F32),
        shape((2, TOK, width), F32),
    ]
    if last:
        out_shape.append(shape((2, width), F32))
    extra = () if first else (dn1,)
    return pl.pallas_call(
        partial(attend_back_kernel, first, last),
        out_shape=out_shape,
        grid=(1,),
        in_specs=[
            SMEM,
            part(TOK),
            part(KEYS),
            part(KEYS),
            pl.BlockSpec((2, heads_here, TOK, KEYS), lambda i: (0, chunk, 0, 0)),
            pl.BlockSpec((3, width, cols_here), lambda i: (0, 0, chunk)),
            pl.BlockSpec((1, cols_here, width), lambda i: (3, chunk, 0)),
            WHOLE,
            part(TOK),
        ]
        + [WHOLE] * (7 + len(extra)),
        out_specs=[HBM] * 4 + [WHOLE] * (len(out_shape) - 4),
        scratch_shapes=[
            pltpu.VMEM((2, TOK, cols_here), BF16),
            pltpu.VMEM((3, 2, TOK, cols_here), BF16),
            pltpu.VMEM((4, width, cols_here), BF16),
            pltpu.SemaphoreType.DMA((4 * PIECES,)),
        ],
        compiler_params=params(),
        cost_estimate=pl.CostEstimate(
            flops=12_000_000_000 // chunks, bytes_accessed=24_000_000 // chunks, transcendentals=0
        ),
        name="attend_back",
    )(meta, q, k, v, p, weights, weights, da, da, att, n1, tok, dx1, vecs, gather, table, *extra)


def grid_of(count):
    return (4, 2, 2) if count == 16 else None


def turn(values, dims, axis, by):
    pairs = []
    for chip in range(dims[0] * dims[1] * dims[2]):
        place = list(np.unravel_index(chip, dims))
        place[axis] = (place[axis] + by) % dims[axis]
        pairs.append((chip, int(np.ravel_multi_index(place, dims))))
    return lax.ppermute(values, "dp", pairs)


def other_core(values):
    return lax.ppermute(values, "mp", [(0, 1), (1, 0)])


def place_order(dims, first, second):
    here = lax.axis_index("dp")
    z, y, x = here // (dims[1] * dims[2]), here // dims[2] % dims[1], here % dims[2]
    found = []
    for outer in range(2):
        for inner in range(2):
            at = [z, y, x]
            at[first] = (at[first] + inner) % 2
            at[second] = (at[second] + outer) % 2
            for step in range(dims[0]):
                found.append(((z - step) % dims[0] * dims[1] + at[1]) * dims[2] + at[2])
    return jnp.stack(found).astype(jnp.int32)


def gather_rows(block, dims, first, second):
    near = jnp.concatenate(
        [block] + [turn(block, dims, 0, step) for step in range(1, dims[0])], axis=0
    )
    beside = turn(near, dims, first, 1)
    return [near, beside, turn(near, dims, second, 1), turn(beside, dims, second, 1)]


def add(a, b):
    return a.astype(F32) + b.astype(F32)


def scatter_rows(keep, far, dims, first, second):
    half = keep.shape[0] // 2
    came = turn(far, dims, second, 1)
    beside = turn(add(keep[half:], came[half:]).astype(BF16), dims, first, 1)
    near = add(keep[:half], came[:half]) + beside.astype(F32)
    rows = half // dims[0]
    total = near[:rows]
    for step in range(1, dims[0]):
        part = near[step * rows : (step + 1) * rows].astype(BF16)
        total = total + turn(part, dims, 0, dims[0] - step).astype(F32)
    return total


def add_all(values, dims):
    values = values + other_core(values)
    if dims is None:
        return lax.psum(values, "dp")
    values = values + turn(values, dims, 2, 1)
    values = values + turn(values, dims, 1, 1)
    return values + sum(turn(values, dims, 0, step) for step in range(1, dims[0]))


def constants():
    key = np.arange(KEYS)
    row, col = key // SIDE, key % SIDE
    inside = (row < WIN) & (col < WIN)
    spread = np.zeros((KEYS, LANES), np.float32)
    gather = np.zeros((KEYS, LANES), np.float32)
    for place in key[inside]:
        for base in (0, 64):
            spread[place, base + WIN - 1 + row[place]] = 1.0
            spread[place, base + 32 + WIN - 1 + col[place]] = 1.0
        gather[place, WIN - 1 - row[place]] = 1.0
        gather[place, 32 + WIN - 1 - col[place]] = 1.0
    return spread, gather


def tables(rel_pos_h, rel_pos_w):
    count = rel_pos_h.shape[0]
    gap = jnp.zeros((32 - count, HDIM), BF16)
    turned = jnp.concatenate([rel_pos_h[::-1], gap, rel_pos_w[::-1], gap], axis=0)
    turned = jnp.concatenate([turned, turned], axis=0).T
    none = jnp.zeros_like(turned)
    forward = jnp.concatenate(
        [jnp.concatenate([turned, none], axis=0), jnp.concatenate([none, turned], axis=0)], axis=1
    )
    straight = jnp.concatenate([rel_pos_h, gap, rel_pos_w, gap], axis=0)
    straight = jnp.concatenate([straight, jnp.zeros_like(straight)], axis=0)
    none = jnp.zeros_like(straight)
    backward = jnp.stack(
        [
            jnp.concatenate([straight, none], axis=1),
            jnp.concatenate([none, straight], axis=1),
        ]
    )
    return forward, backward


def padded(values):
    images, rows, _, width = values.shape
    values = jnp.pad(values, ((0, 0), (0, 0), (0, SIDE - WIN), (0, 0)))
    return values.reshape(images, rows * SIDE, width)


def unpadded(values):
    images, _, width = values.shape
    return values.reshape(images, WIN, SIDE, width)[:, :, :WIN]


def local(
    patches,
    norm1_gain,
    norm1_bias,
    qkv_weight,
    qv_bias,
    rel_pos_h,
    rel_pos_w,
    proj_weight,
    proj_bias,
    norm2_gain,
    norm2_bias,
    fc1_weight,
    fc1_bias,
    fc2_weight,
    fc2_bias,
    heights,
    widths,
    out_grad,
):
    width = patches.shape[-1]
    dims = grid_of(lax.axis_size("dp"))
    core = lax.axis_index("mp")
    is_first = core == 0
    if dims is None:
        order = jnp.tile(jnp.arange(PIECES, dtype=jnp.int32), 2)
    else:
        order = jnp.concatenate([place_order(dims, 2, 1), place_order(dims, 1, 2)])
    meta = jnp.concatenate(
        [order, core.astype(jnp.int32)[None], heights, widths, jnp.zeros((27,), jnp.int32)]
    )

    vectors = (norm1_gain, norm1_bias, qv_bias[0], qv_bias[1], proj_bias, norm2_gain, norm2_bias, fc2_bias)
    small = jnp.pad(jnp.stack(vectors, axis=1), ((0, 0), (0, LANES - len(vectors))))
    qk = jnp.concatenate([qkv_weight[:, :width], small, qkv_weight[:, width : 2 * width]], axis=1)
    vp = jnp.concatenate([qkv_weight[:, 2 * width :], small, proj_weight], axis=1)
    if dims is None:
        qk = lax.all_gather(qk, ("dp", "mp"), axis=0, tiled=True)
        vp = lax.all_gather(vp, ("dp", "mp"), axis=0, tiled=True)
        own = jnp.where(is_first, qk, vp)
        far = jnp.where(is_first, vp, qk)
        own0, own1 = [own[:, : width + LANES]], [own[:, width + LANES :]]
        far0, far1 = [far[:, : width + LANES]], [far[:, width + LANES :]]
        hidden_in = [
            (
                [lax.all_gather(fc1_weight, "dp", axis=0, tiled=True)],
                [lax.all_gather(fc2_weight.T, "dp", axis=0, tiled=True)],
            )
        ]
    else:
        near = jnp.where(is_first, qk, vp)
        came = other_core(jnp.where(is_first, vp, qk))
        block = jnp.concatenate(
            [jnp.where(is_first, near, came), jnp.where(is_first, came, near)], axis=0
        )
        own0 = gather_rows(block[:, : width + LANES], dims, 2, 1)
        own1 = gather_rows(block[:, width + LANES :], dims, 1, 2)
        far0 = [other_core(part) for part in own0]
        far1 = [other_core(part) for part in own1]
        hidden_in = []
        part = fc1_weight.shape[1] // FFN_CHUNKS
        for chunk in range(FFN_CHUNKS):
            cols = slice(chunk * part, (chunk + 1) * part)
            hidden_in.append(
                (
                    gather_rows(fc1_weight[:, cols], dims, 2, 1),
                    gather_rows(fc2_weight.T[:, cols], dims, 1, 2),
                )
            )

    tok = padded(patches)
    row_index = core * WIN + jnp.arange(WIN)
    valid = (row_index[None, :, None] < heights[:, None, None]) & (
        jnp.arange(WIN)[None, None, :] < widths[:, None, None]
    )
    dm = padded(jnp.where(valid[..., None], out_grad, jnp.zeros_like(out_grad)))
    dm_far = other_core(dm)
    spread, gather = constants()
    table, table_back = tables(rel_pos_h, rel_pos_w)

    n1, q, k, v, p, att, x1, n2, vecs, weights = attend(
        meta, tok, table, jnp.asarray(spread, BF16), own0, own1, far0, far1
    )
    n2_far = other_core(n2)

    carried = None
    hidden_grads, bias_grads = [], []
    part = fc1_weight.shape[1] // len(hidden_in)
    for chunk, (in0, in1) in enumerate(hidden_in):
        bias = fc1_bias[None, chunk * part : (chunk + 1) * part].astype(F32)
        last = chunk == len(hidden_in) - 1
        made = hidden(meta, n2, n2_far, dm, dm_far, bias, in0, in1, carried, last)
        bias_grads.append(made[4])
        carried = made[5:]
        if dims is None:
            hidden_grads.append(
                [
                    lax.psum_scatter(
                        jnp.concatenate(pair, axis=0).astype(F32), "dp", scatter_dimension=0, tiled=True
                    )
                    for pair in (made[0:2], made[2:4])
                ]
            )
        else:
            hidden_grads.append(
                (
                    scatter_rows(made[0], made[1], dims, 2, 1),
                    scatter_rows(made[2], made[3], dims, 1, 2),
                )
            )
    out_own, out_far, back_own, back_far = carried
    block_out, dx1, da, sums2 = middle(
        meta, out_own, other_core(out_far), back_own, other_core(back_far), x1, dm, vecs
    )

    dn1 = None
    bias_sums, table_grad, attend_grads = [], 0.0, []
    for chunk in range(BACK_CHUNKS):
        made = attend_back(
            chunk,
            BACK_CHUNKS,
            meta,
            q,
            k,
            v,
            p,
            weights,
            da,
            att,
            n1,
            tok,
            dx1,
            vecs,
            jnp.asarray(gather, BF16),
            table_back,
            dn1,
        )
        bias_sums.append(made[4])
        table_grad = table_grad + made[5]
        dn1 = made[6]
        if chunk == BACK_CHUNKS - 1:
            sums1 = made[7]
        halves = []
        for mine, theirs, axes in ((made[0], made[2], (2, 1)), (made[1], made[3], (1, 2))):
            if dims is None:
                whole = lax.psum_scatter(
                    add(mine, other_core(theirs)), "dp", scatter_dimension=0, tiled=True
                )
            else:
                came = other_core(theirs)
                half = width // 2
                whole = scatter_rows(
                    add(mine[:half], came[:half]).astype(BF16),
                    add(mine[half:], came[half:]).astype(BF16),
                    dims,
                    *axes,
                )
            halves.append(whole)
        whole = jnp.stack(halves)
        rows = whole.shape[1] // 2
        near = jnp.where(is_first, whole[:, :rows], whole[:, rows:])
        came = other_core(jnp.where(is_first, whole[:, rows:], whole[:, :rows]))
        attend_grads.append((jnp.where(is_first, near, came), jnp.where(is_first, came, near)))
    qk_grad = [jnp.concatenate([g[0][i] for g in attend_grads], axis=1) for i in range(2)]
    vp_grad = [jnp.concatenate([g[1][i] for g in attend_grads], axis=1) for i in range(2)]
    qkv_grad = jnp.concatenate([qk_grad[0], qk_grad[1], vp_grad[0]], axis=1)

    qv_sums = jnp.concatenate(bias_sums, axis=1)
    rel_sums = table_grad[:64, :HDIM] + table_grad[:64, HDIM:]
    fc1_sums = jnp.concatenate(bias_grads, axis=1)
    fc1_sums = jnp.concatenate(
        [jnp.where(is_first, fc1_sums, 0.0), jnp.where(is_first, 0.0, fc1_sums)], axis=1
    )
    flat = jnp.concatenate(
        [
            jnp.concatenate([sums1, qv_sums, sums2[4:]], axis=0).reshape(-1, LANES),
            rel_sums.reshape(-1, LANES),
            fc1_sums.reshape(-1, LANES),
        ],
        axis=0,
    )
    flat = add_all(flat, dims)
    at = 8 * width // LANES
    vec_sums = flat[:at].reshape(8, width)
    rel = flat[at : at + 32].reshape(64, HDIM)
    fc1_bias_grad = lax.dynamic_index_in_dim(flat[at + 32 :].reshape(2, -1), core, 0, keepdims=False)
    share = norm1_gain.shape[0]
    device = lax.axis_index("dp") * 2 + core
    mine = lax.dynamic_slice_in_dim(vec_sums, device * share, share, axis=1)
    rels = rel_pos_h.shape[0]
    return (
        unpadded(block_out),
        unpadded(dn1),
        mine[0],
        mine[1],
        qkv_grad,
        mine[2:4],
        rel[:rels],
        rel[32 : 32 + rels],
        vp_grad[1],
        mine[4],
        mine[5],
        mine[6],
        jnp.concatenate([g[0] for g in hidden_grads], axis=1),
        fc1_bias_grad,
        jnp.concatenate([g[1] for g in hidden_grads], axis=1).T,
        mine[7],
    )


def solution(mesh):
    return jax.shard_map(
        local,
        mesh=mesh,
        in_specs=(
            P("dp", "mp", None, None),
            P(("dp", "mp")),
            P(("dp", "mp")),
            P(("dp", "mp"), None),
            P(None, ("dp", "mp")),
            P(),
            P(),
            P(("dp", "mp"), None),
            P(("dp", "mp")),
            P(("dp", "mp")),
            P(("dp", "mp")),
            P("dp", "mp"),
            P("mp"),
            P("mp", "dp"),
            P(("dp", "mp")),
            P("dp"),
            P("dp"),
            P("dp", "mp", None, None),
        ),
        out_specs=(
            P("dp", "mp", None, None),
            P("dp", "mp", None, None),
            P(("dp", "mp")),
            P(("dp", "mp")),
            P(("dp", "mp"), None),
            P(None, ("dp", "mp")),
            P(),
            P(),
            P(("dp", "mp"), None),
            P(("dp", "mp")),
            P(("dp", "mp")),
            P(("dp", "mp")),
            P("dp", "mp"),
            P("mp"),
            P("mp", "dp"),
            P(("dp", "mp")),
        ),
        check_vma=False,
    )
```

time: 858 us -> 353 us (0.41)
  waiting for transfers between devices: 441 us -> 85.6 us
  blocking collectives: 165 us -> 0 us
  starting transfers between devices: 0.65 us -> 125 us
  matrix products: 105 us -> 0 us
  Pallas kernels: 0 us -> 98.5 us
  local copies, waits for them, and re-layouts: 88.4 us -> 22.9 us
  other arithmetic: 36.8 us -> 13.4 us
  between operations: 15.5 us -> 2.19 us
    reduce_scatter x6 -> x0, waiting for transfers between devices: 330 us -> none  [the longest x1 143 us: local(): lax.psum_scatter(fc2_part, 'dp', scatter_dimension=1, tiled=True)]
    ppermute x0 -> x110, starting transfers between devices: none -> 125 us  [the longest x93 123 us: turn(): return lax.ppermute(values, 'dp', pairs)]
    all_gather x6 -> x0, waiting for transfers between devices: 108 us -> none  [the longest x1 66.1 us: local(): lax.all_gather(fc2_weight, 'dp', axis=1, tiled=True)]
    dot_general x32 -> x0, matrix products: 105 us -> none  [the longest x1 17.7 us: local(): jnp.einsum('nd,fd->nf', grad_gathered, weight_out_back, preferred_element...]
    pallas_call x0 -> x6, Pallas kernels: none -> 98.5 us  [the longest x3 43 us: hidden(): pl.pallas_call(partial(hidden_kernel, count, first, last), out_shape=out_...]
    ppermute x0 -> x110, waiting for transfers between devices: none -> 85.6 us  [the longest x93 82.8 us: turn(): return lax.ppermute(values, 'dp', pairs)]
    unnamed x2 -> x0, blocking collectives: 81.4 us -> none
    psum x1 -> x0, blocking collectives: 43.1 us -> none  [local(): fc1_bias_grad = lax.psum(fc1_bias_part, 'dp')]
  transfers between devices with their start and end apart: 12 -> 110, of which waited for: 8 -> 38; matrix products, arithmetic and copies ran while one was open for 22% -> 9% of each run, Pallas kernels for 0% -> 28%
where the time goes in v1:
time: 353 us; the launch traced here: 348 us
  starting transfers between devices  125 us (35%)
  Pallas kernels  98.5 us (28%)
  waiting for transfers between devices  85.6 us (24%)
  local copies, waits for them, and re-layouts  22.9 us (6%)
  other arithmetic  13.4 us (4%)
    ppermute x93, starting transfers between devices, turn(): return lax.ppermute(values, 'dp', pairs)  123 us
    ppermute x93, waiting for transfers between devices, turn(): return lax.ppermute(values, 'dp', pairs)  82.8 us
    pallas_call x3, Pallas kernels, hidden(): pl.pallas_call(partial(hidden_kernel, count, first, last), out_shape=out_...  43 us
    pallas_call x1, Pallas kernels, attend_back(): pl.pallas_call(partial(attend_back_kernel, first, last), out_shape=out_sh...  28.1 us
    pallas_call x1, Pallas kernels, attend(): pl.pallas_call(partial(attend_kernel, count), out_shape=[shape(rows, BF16...  22 us
    unnamed x128, local copies, waits for them, and re-layouts  9.91 us
  transfers between devices with their start and end apart: 110, of which 38 were waited for; matrix products, arithmetic and copies ran while one was open for 9% of the time, Pallas kernels for 28%

profile of v1, /device:TPU:0, one launch (start us, length us, event | category | flops | bytes accessed | tf_op | source)
XLA Modules:
  0.0 347.6 jit_solution(3510452715403258474)
XLA Ops:
  14.6 3.5 %collective-permute-start.8 = (bf16[48,768]{1,0:T(8,128)(2,1)S(1)}, bf16[48,768]{1,0:T(8,128)(2,1)S(1)}, u32[]{:S(2)}, u32[]{:S(2)}) collective-permute-start(bf16[48,768]{1,0:T(8,128)(2,1)S(1)} %pad_maximum_fusion.13), channel_id=1, source_target_pairs={{0,16},{2,18},{4,20},{6,22},{8,24},{10,26},{12,28},{14,30},{16,0},... | collective-permute-start | bytes 221192 | tf_op jit(solution)/shard_map/ppermute | solution.py:514
  24.4 5.7 %collective-permute-start.3 = (bf16[48,896]{1,0:T(8,128)(2,1)S(1)}, bf16[48,896]{1,0:T(8,128)(2,1)S(1)}, u32[]{:S(2)}, u32[]{:S(2)}) collective-permute-start(bf16[48,896]{1,0:T(8,128)(2,1)S(1)} %fusion.23), channel_id=1, source_target_pairs={{0,24},{2,26},{4,28},{6,30},{8,0},{10,2},{12,4},{14,6},{16,8},{18,... | collective-permute-start | bytes 258056 | tf_op jit(solution)/shard_map/ppermute | solution.py:514
  35.8 3.7 %collective-permute-start.42 = (bf16[48,512]{1,0:T(8,128)(2,1)S(1)}, bf16[48,512]{1,0:T(8,128)(2,1)S(1)}, u32[]{:S(2)}, u32[]{:S(2)}) collective-permute-start(bf16[48,512]{1,0:T(8,128)(2,1)S(1)} %get-tuple-element.159), channel_id=1, source_target_pairs={{0,16},{2,18},{4,20},{6,22},{8,24},{10,26},{12,28},{14,30},{16,0},... | collective-permute-start | bytes 147464 | tf_op jit(solution)/shard_map/ppermute | solution.py:514
  46.1 5.4 %collective-permute-done.23 = bf16[48,512]{1,0:T(8,128)(2,1)S(1)} collective-permute-done((bf16[48,512]{1,0:T(8,128)(2,1)S(1)}, bf16[48,512]{1,0:T(8,128)(2,1)S(1)}, u32[]{:S(2)}, u32[]{:S(2)}) %collective-permute-start.23) | collective-permute-done | bytes 49184 | tf_op jit(solution)/shard_map/ppermute | solution.py:514
  54.2 5.6 %collective-permute-done.4.refs_1_ = bf16[192,896]{1,0:T(8,128)(2,1)} collective-permute-done((bf16[192,896]{1,0:T(8,128)(2,1)S(1)}, bf16[192,896]{1,0:T(8,128)(2,1)}, u32[]{:S(2)}, u32[]{:S(2)}) %collective-permute-start.4) | collective-permute-done | bytes 344096 | tf_op jit(solution)/shard_map/ppermute | solution.py:514
  79.2 22.0 %attend.1 = (bf16[2,224,768]{2,1,0:T(8,128)(2,1)}, bf16[2,224,768]{2,1,0:T(8,128)(2,1)}, bf16[2,256,768]{2,1,0:T(8,128)(2,1)}, bf16[2,256,768]{2,1,0:T(8,128)(2,...) custom-call(s32[64]{0:T(128)S(1)} %concatenate.96.meta, ...), custom_call_target="tpu_custom_call" | custom-call | flops 6000000000 | bytes 20000000 | tf_op jit(solution)/shard_map/attend/pallas_call | solution.py:188
  110.1 3.9 %collective-permute-done.56.refs_5_ = bf16[192,512]{1,0:T(8,128)(2,1)S(1)} collective-permute-done((bf16[192,512]{1,0:T(8,128)(2,1)S(1)}, bf16[192,512]{1,0:T(8,128)(2,1)S(1)}, u32[]{:S(2)}, u32[]{:S(2)}) %collective-permute-start.56) | collective-permute-done | bytes 196640 | tf_op jit(solution)/shard_map/ppermute | solution.py:514
  116.6 3.5 %collective-permute-done.38.refs_1_ = bf16[192,512]{1,0:T(8,128)(2,1)S(1)} collective-permute-done((bf16[192,512]{1,0:T(8,128)(2,1)S(1)}, bf16[192,512]{1,0:T(8,128)(2,1)S(1)}, u32[]{:S(2)}, u32[]{:S(2)}) %collective-permute-start.38) | collective-permute-done | bytes 196640 | tf_op jit(solution)/shard_map/ppermute | solution.py:514
  133.2 13.1 %hidden.3 = (bf16[384,512]{1,0:T(8,128)(2,1)S(1)}, bf16[384,512]{1,0:T(8,128)(2,1)}, bf16[384,512]{1,0:T(8,128)(2,1)}, bf16[384,512]{1,0:T(8,128)(2,1)}, f32[1,5...) custom-call(s32[64]{0:T(128)S(1)} %concatenate.96.meta, bf16[2,224,768]{2,1,0:T(8,128)(2,1)} %get-tuple-element.61.n2a, ...), custom_call_target="tpu_custom_call" | custom-call | flops 4227858432 | bytes 20000000 | tf_op jit(solution)/shard_map/hidden/pallas_call | solution.py:298
  151.7 15.2 %hidden.4 = (bf16[384,512]{1,0:T(8,128)(2,1)S(1)}, bf16[384,512]{1,0:T(8,128)(2,1)}, bf16[384,512]{1,0:T(8,128)(2,1)}, bf16[384,512]{1,0:T(8,128)(2,1)}, f32[1,5...) custom-call(s32[64]{0:T(128)S(1)} %concatenate.96.meta, bf16[2,224,768]{2,1,0:T(8,128)(2,1)} %get-tuple-element.61.n2a, ...), custom_call_target="tpu_custom_call" | custom-call | flops 4227858432 | bytes 20000000 | tf_op jit(solution)/shard_map/hidden/pallas_call | solution.py:298
  167.8 14.7 %hidden.5 = (bf16[384,512]{1,0:T(8,128)(2,1)S(1)}, bf16[384,512]{1,0:T(8,128)(2,1)}, bf16[384,512]{1,0:T(8,128)(2,1)}, bf16[384,512]{1,0:T(8,128)(2,1)}, f32[1,5...) custom-call(s32[64]{0:T(128)S(1)} %concatenate.96.meta, ...), custom_call_target="tpu_custom_call" | custom-call | flops 4227858432 | bytes 20000000 | tf_op jit(solution)/shard_map/hidden/pallas_call | solution.py:298
  190.6 5.2 %collective-permute-done.80 = bf16[384,512]{1,0:T(8,128)(2,1)S(1)} collective-permute-done((bf16[384,512]{1,0:T(8,128)(2,1)S(1)}, bf16[384,512]{1,0:T(8,128)(2,1)S(1)}, u32[]{:S(2)}, u32[]{:S(2)}) %collective-permute-start.80) | collective-permute-done | bytes 393248 | tf_op jit(solution)/shard_map/ppermute | solution.py:514
  197.4 6.9 %collective-permute-done.85 = bf16[384,512]{1,0:T(8,128)(2,1)S(1)} collective-permute-done((bf16[384,512]{1,0:T(8,128)(2,1)S(1)}, bf16[384,512]{1,0:T(8,128)(2,1)S(1)}, u32[]{:S(2)}, u32[]{:S(2)}) %collective-permute-start.85) | collective-permute-done | bytes 393248 | tf_op jit(solution)/shard_map/ppermute | solution.py:514
  205.8 6.9 %collective-permute-done.90 = bf16[384,512]{1,0:T(8,128)(2,1)S(1)} collective-permute-done((bf16[384,512]{1,0:T(8,128)(2,1)}, bf16[384,512]{1,0:T(8,128)(2,1)S(1)}, u32[]{:S(2)}, u32[]{:S(2)}) %collective-permute-start.90) | collective-permute-done | bytes 393248 | tf_op jit(solution)/shard_map/ppermute | solution.py:514
  228.4 3.3 collective-permute-start.102
  234.3 3.3 collective-permute-start.107
  239.6 4.4 %collective-permute-start.82 = (bf16[48,512]{1,0:T(8,128)(2,1)S(1)}, bf16[48,512]{1,0:T(8,128)(2,1)S(1)}, u32[]{:S(2)}, u32[]{:S(2)}) collective-permute-start(bf16[48,512]{1,0:T(8,128)(2,1)S(1)} %get-tuple-element.145), channel_id=1, source_target_pairs={{0,24},{2,26},{4,28},{6,30},{8,0},{10,2},{12,4},{14,6},{16,8},{18,... | collective-permute-start | bytes 147464 | tf_op jit(solution)/shard_map/ppermute | solution.py:514
  245.7 4.1 %collective-permute-start.87 = (bf16[48,512]{1,0:T(8,128)(2,1)}, bf16[48,512]{1,0:T(8,128)(2,1)}, u32[]{:S(2)}, u32[]{:S(2)}) collective-permute-start(bf16[48,512]{1,0:T(8,128)(2,1)} %get-tuple-element.148), channel_id=1, source_target_pairs={{0,24},{2,26},{4,28},{6,30},{8,0},{10,2},{12,4},{14,6},{16,8},{18,... | collective-permute-start | bytes 147464 | tf_op jit(solution)/shard_map/ppermute | solution.py:514
  251.5 3.8 %collective-permute-start.92 = (bf16[48,512]{1,0:T(8,128)(2,1)}, bf16[48,512]{1,0:T(8,128)(2,1)}, u32[]{:S(2)}, u32[]{:S(2)}) collective-permute-start(bf16[48,512]{1,0:T(8,128)(2,1)} %get-tuple-element.151), channel_id=1, source_target_pairs={{0,24},{2,26},{4,28},{6,30},{8,0},{10,2},{12,4},{14,6},{16,8},{18,... | collective-permute-start | bytes 147464 | tf_op jit(solution)/shard_map/ppermute | solution.py:514
  256.2 5.4 %middle.1 = (bf16[2,224,768]{2,1,0:T(8,128)(2,1)S(1)}, f32[2,224,768]{2,1,0:T(8,128)}, bf16[2,224,768]{2,1,0:T(8,128)(2,1)S(1)}, f32[8,768]{1,0:T(8,128)S(1)}) custom-call(s32[64]{0:T(128)S(1)} %concatenate.96.meta, f32[448,768]{1,0:T(8,128)} %get-tuple-element.66.out_own, bf16[448,768]{1,0:T(8,128)(2,1)} %copy-done.7, ...), custom_call_target="tpu_custom_call" | custom-call | flops 20000000 | bytes 9000000 | tf_op jit(solution)/shard_map/middle/pallas_call | solution.py:349
  261.7 28.1 %attend_back.1 = (bf16[768,768]{1,0:T(8,128)(2,1)}, bf16[768,768]{1,0:T(8,128)(2,1)}, bf16[768,768]{1,0:T(8,128)(2,1)}, bf16[768,768]{1,0:T(8,128)(2,1)}, f32[2,...) custom-call(s32[64]{0:T(128)S(1)} %concatenate.96.meta, ...), custom_call_target="tpu_custom_call" | custom-call | flops 12000000000 | bytes 24000000 | tf_op jit(solution)/shard_map/attend_back/pallas_call | solution.py:473
  295.3 3.5 %collective-permute-done.94 = bf16[48,512]{1,0:T(8,128)(2,1)S(1)} collective-permute-done((bf16[48,512]{1,0:T(8,128)(2,1)S(1)}, bf16[48,512]{1,0:T(8,128)(2,1)S(1)}, u32[]{:S(2)}, u32[]{:S(2)}) %collective-permute-start.94) | collective-permute-done | bytes 49184 | tf_op jit(solution)/shard_map/ppermute | solution.py:514
  313.6 10.8 %collective-permute-done.68 = bf16[384,768]{1,0:T(8,128)(2,1)S(1)} collective-permute-done((bf16[384,768]{1,0:T(8,128)(2,1)}, bf16[384,768]{1,0:T(8,128)(2,1)S(1)}, u32[]{:S(2)}, u32[]{:S(2)}) %collective-permute-start.68) | collective-permute-done | bytes 589856 | tf_op jit(solution)/shard_map/ppermute | solution.py:514
  328.0 4.0 %collective-permute-done.69 = bf16[192,768]{1,0:T(8,128)(2,1)S(1)} collective-permute-done((bf16[192,768]{1,0:T(8,128)(2,1)}, bf16[192,768]{1,0:T(8,128)(2,1)S(1)}, u32[]{:S(2)}, u32[]{:S(2)}) %collective-permute-start.69) | collective-permute-done | bytes 294944 | tf_op jit(solution)/shard_map/ppermute | solution.py:514
  (432 shorter events, 159.2 us)
Async XLA Ops:
  72.1 29.0 %collective-permute-start.24 = (bf16[48,512]{1,0:T(8,128)(2,1)S(1)}, bf16[48,512]{1,0:T(8,128)(2,1)S(1)}, u32[]{:S(2)}, u32[]{:S(2)}) collective-permute-start(bf16[48,512]{1,0:T(8,128)(2,1)S(1)} %get-tuple-element.162), channel_id=1, source_target_pairs={{0,16},{2,18},{4,20},{6,22},{8,24},{10,26},{12,28},{14,30},{16,0},... | collective-permute-start | bytes 147464 | tf_op jit(solution)/shard_map/ppermute | solution.py:514
  72.9 28.4 %collective-permute-start.25 = (bf16[48,512]{1,0:T(8,128)(2,1)S(1)}, bf16[48,512]{1,0:T(8,128)(2,1)S(1)}, u32[]{:S(2)}, u32[]{:S(2)}) collective-permute-start(bf16[48,512]{1,0:T(8,128)(2,1)S(1)} %get-tuple-element.162), channel_id=1, source_target_pairs={{0,24},{2,26},{4,28},{6,30},{8,0},{10,2},{12,4},{14,6},{16,8},{18,... | collective-permute-start | bytes 147464 | tf_op jit(solution)/shard_map/ppermute | solution.py:514
  75.0 27.9 %collective-permute-start.29 = (bf16[48,512]{1,0:T(8,128)(2,1)S(1)}, bf16[48,512]{1,0:T(8,128)(2,1)S(1)}, u32[]{:S(2)}, u32[]{:S(2)}) collective-permute-start(bf16[48,512]{1,0:T(8,128)(2,1)S(1)} %get-tuple-element.160), channel_id=1, source_target_pairs={{0,8},{2,10},{4,12},{6,14},{8,16},{10,18},{12,20},{14,22},{16,24},... | collective-permute-start | bytes 147464 | tf_op jit(solution)/shard_map/ppermute | solution.py:514
  75.0 29.3 %collective-permute-start.30 = (bf16[48,512]{1,0:T(8,128)(2,1)S(1)}, bf16[48,512]{1,0:T(8,128)(2,1)S(1)}, u32[]{:S(2)}, u32[]{:S(2)}) collective-permute-start(bf16[48,512]{1,0:T(8,128)(2,1)S(1)} %get-tuple-element.160), channel_id=1, source_target_pairs={{0,16},{2,18},{4,20},{6,22},{8,24},{10,26},{12,28},{14,30},{16,0},... | collective-permute-start | bytes 147464 | tf_op jit(solution)/shard_map/ppermute | solution.py:514
  77.1 27.7 %collective-permute-start.31 = (bf16[48,512]{1,0:T(8,128)(2,1)S(1)}, bf16[48,512]{1,0:T(8,128)(2,1)S(1)}, u32[]{:S(2)}, u32[]{:S(2)}) collective-permute-start(bf16[48,512]{1,0:T(8,128)(2,1)S(1)} %get-tuple-element.160), channel_id=1, source_target_pairs={{0,24},{2,26},{4,28},{6,30},{8,0},{10,2},{12,4},{14,6},{16,8},{18,... | collective-permute-start | bytes 147464 | tf_op jit(solution)/shard_map/ppermute | solution.py:514
  101.2 30.6 %collective-permute-start.22 = (bf16[2,224,768]{2,1,0:T(8,128)(2,1)S(1)}, bf16[2,224,768]{2,1,0:T(8,128)(2,1)S(1)}, u32[]{:S(2)}, u32[]{:S(2)}) collective-permute-start(bf16[2,224,768]{2,1,0:T(8,128)(2,1)S(1)} %bitcast.73), channel_id=1, source_target_pairs={{0,1},{1,0},{2,3},{3,2},{4,5},{5,4},{6,7},{7,6},{8,9},{9,8},{10,11... | collective-permute-start | bytes 2064392 | tf_op jit(solution)/shard_map/ppermute | solution.py:518
  104.9 27.5 %collective-permute-start.21 = (bf16[2,224,768]{2,1,0:T(8,128)(2,1)}, bf16[2,224,768]{2,1,0:T(8,128)(2,1)S(1)}, u32[]{:S(2)}, u32[]{:S(2)}) collective-permute-start(bf16[2,224,768]{2,1,0:T(8,128)(2,1)} %get-tuple-element.61.n2a), channel_id=1, source_target_pairs={{0,1},{1,0},{2,3},{3,2},{4,5},{5,4},{6,7},{7,6},{8,9},{9,8},{10,11... | collective-permute-start | bytes 2064392 | tf_op jit(solution)/shard_map/ppermute | solution.py:518
  126.6 19.7 %collective-permute-start.45 = (bf16[192,512]{1,0:T(8,128)(2,1)S(1)}, bf16[192,512]{1,0:T(8,128)(2,1)S(1)}, u32[]{:S(2)}, u32[]{:S(2)}) collective-permute-start(bf16[192,512]{1,0:T(8,128)(2,1)S(1)} %pad_maximum_fusion.7.refs_4_), channel_id=1, source_target_pairs={{0,2},{2,0},{4,6},{6,4},{8,10},{10,8},{12,14},{14,12},{16,18},{18,... | collective-permute-start | bytes 589832 | tf_op jit(solution)/shard_map/ppermute | solution.py:514
  128.8 19.0 %collective-permute-start.26 = (bf16[192,512]{1,0:T(8,128)(2,1)S(1)}, bf16[192,512]{1,0:T(8,128)(2,1)S(1)}, u32[]{:S(2)}, u32[]{:S(2)}) collective-permute-start(bf16[192,512]{1,0:T(8,128)(2,1)S(1)} %pad_maximum_fusion.4.refs_0_), channel_id=1, source_target_pairs={{0,2},{2,0},{4,6},{6,4},{8,10},{10,8},{12,14},{14,12},{16,18},{18,... | collective-permute-start | bytes 589832 | tf_op jit(solution)/shard_map/ppermute | solution.py:514
  146.3 20.5 %collective-permute-start.27 = (bf16[192,512]{1,0:T(8,128)(2,1)S(1)}, bf16[192,512]{1,0:T(8,128)(2,1)S(1)}, u32[]{:S(2)}, u32[]{:S(2)}) collective-permute-start(bf16[192,512]{1,0:T(8,128)(2,1)S(1)} %pad_maximum_fusion.4.refs_0_), channel_id=1, source_target_pairs={{0,4},{2,6},{4,0},{6,2},{8,12},{10,14},{12,8},{14,10},{16,20},{18,... | collective-permute-start | bytes 589832 | tf_op jit(solution)/shard_map/ppermute | solution.py:514
  147.9 19.9 %collective-permute-start.33 = (bf16[192,512]{1,0:T(8,128)(2,1)S(1)}, bf16[192,512]{1,0:T(8,128)(2,1)S(1)}, u32[]{:S(2)}, u32[]{:S(2)}) collective-permute-start(bf16[192,512]{1,0:T(8,128)(2,1)S(1)} %pad_maximum_fusion.5.refs_4_), channel_id=1, source_target_pairs={{0,2},{2,0},{4,6},{6,4},{8,10},{10,8},{12,14},{14,12},{16,18},{18,... | collective-permute-start | bytes 589832 | tf_op jit(solution)/shard_map/ppermute | solution.py:514
  150.5 35.4 %collective-permute-start.95 = (bf16[384,512]{1,0:T(8,128)(2,1)}, bf16[384,512]{1,0:T(8,128)(2,1)S(1)}, u32[]{:S(2)}, u32[]{:S(2)}) collective-permute-start(bf16[384,512]{1,0:T(8,128)(2,1)} %get-tuple-element.101), channel_id=1, source_target_pairs={{0,2},{2,0},{4,6},{6,4},{8,10},{10,8},{12,14},{14,12},{16,18},{18,... | collective-permute-start | bytes 1179656 | tf_op jit(solution)/shard_map/ppermute | solution.py:514
  166.9 20.6 %collective-permute-start.100 = (bf16[384,512]{1,0:T(8,128)(2,1)}, bf16[384,512]{1,0:T(8,128)(2,1)S(1)}, u32[]{:S(2)}, u32[]{:S(2)}) collective-permute-start(bf16[384,512]{1,0:T(8,128)(2,1)} %get-tuple-element.103), channel_id=1, source_target_pairs={{0,2},{2,0},{4,6},{6,4},{8,10},{10,8},{12,14},{14,12},{16,18},{18,... | collective-permute-start | bytes 1179656 | tf_op jit(solution)/shard_map/ppermute | solution.py:514
  185.3 19.0 %collective-permute-start.85 = (bf16[384,512]{1,0:T(8,128)(2,1)S(1)}, bf16[384,512]{1,0:T(8,128)(2,1)S(1)}, u32[]{:S(2)}, u32[]{:S(2)}) collective-permute-start(bf16[384,512]{1,0:T(8,128)(2,1)S(1)} %copy-done.54), channel_id=1, source_target_pairs={{0,4},{2,6},{4,0},{6,2},{8,12},{10,14},{12,8},{14,10},{16,20},{18,... | collective-permute-start | bytes 1179656 | tf_op jit(solution)/shard_map/ppermute | solution.py:514
  185.9 26.8 %collective-permute-start.90 = (bf16[384,512]{1,0:T(8,128)(2,1)}, bf16[384,512]{1,0:T(8,128)(2,1)S(1)}, u32[]{:S(2)}, u32[]{:S(2)}) collective-permute-start(bf16[384,512]{1,0:T(8,128)(2,1)} %get-tuple-element.99), channel_id=1, source_target_pairs={{0,4},{2,6},{4,0},{6,2},{8,12},{10,14},{12,8},{14,10},{16,20},{18,... | collective-permute-start | bytes 1179656 | tf_op jit(solution)/shard_map/ppermute | solution.py:514
  187.5 64.0 %collective-permute-start.59 = (bf16[448,768]{1,0:T(8,128)(2,1)}, bf16[448,768]{1,0:T(8,128)(2,1)S(1)}, u32[]{:S(2)}, u32[]{:S(2)}) collective-permute-start(bf16[448,768]{1,0:T(8,128)(2,1)} %get-tuple-element.67), channel_id=1, source_target_pairs={{0,1},{1,0},{2,3},{3,2},{4,5},{5,4},{6,7},{7,6},{8,9},{9,8},{10,11... | collective-permute-start | bytes 2064392 | tf_op jit(solution)/shard_map/ppermute | solution.py:518
  190.6 64.8 %collective-permute-start.60 = (bf16[448,768]{1,0:T(8,128)(2,1)S(1)}, bf16[448,768]{1,0:T(8,128)(2,1)S(1)}, u32[]{:S(2)}, u32[]{:S(2)}) collective-permute-start(bf16[448,768]{1,0:T(8,128)(2,1)S(1)} %copy-done.50), channel_id=1, source_target_pairs={{0,1},{1,0},{2,3},{3,2},{4,5},{5,4},{6,7},{7,6},{8,9},{9,8},{10,11... | collective-permute-start | bytes 2064392 | tf_op jit(solution)/shard_map/ppermute | solution.py:518
  195.9 19.3 %collective-permute-start.96 = (bf16[192,512]{1,0:T(8,128)(2,1)S(1)}, bf16[192,512]{1,0:T(8,128)(2,1)S(1)}, u32[]{:S(2)}, u32[]{:S(2)}) collective-permute-start(bf16[192,512]{1,0:T(8,128)(2,1)S(1)} %add_convert_fusion.8), channel_id=1, source_target_pairs={{0,4},{2,6},{4,0},{6,2},{8,12},{10,14},{12,8},{14,10},{16,20},{18,... | collective-permute-start | bytes 589832 | tf_op jit(solution)/shard_map/ppermute | solution.py:514
  245.7 44.3 %collective-permute-start.87 = (bf16[48,512]{1,0:T(8,128)(2,1)}, bf16[48,512]{1,0:T(8,128)(2,1)}, u32[]{:S(2)}, u32[]{:S(2)}) collective-permute-start(bf16[48,512]{1,0:T(8,128)(2,1)} %get-tuple-element.148), channel_id=1, source_target_pairs={{0,24},{2,26},{4,28},{6,30},{8,0},{10,2},{12,4},{14,6},{16,8},{18,... | collective-permute-start | bytes 147464 | tf_op jit(solution)/shard_map/ppermute | solution.py:514
  249.9 40.5 %collective-permute-start.88 = (bf16[48,512]{1,0:T(8,128)(2,1)}, bf16[48,512]{1,0:T(8,128)(2,1)}, u32[]{:S(2)}, u32[]{:S(2)}) collective-permute-start(bf16[48,512]{1,0:T(8,128)(2,1)} %get-tuple-element.150), channel_id=1, source_target_pairs={{0,16},{2,18},{4,20},{6,22},{8,24},{10,26},{12,28},{14,30},{16,0},... | collective-permute-start | bytes 147464 | tf_op jit(solution)/shard_map/ppermute | solution.py:514
  250.8 39.9 %collective-permute-start.89 = (bf16[48,512]{1,0:T(8,128)(2,1)}, bf16[48,512]{1,0:T(8,128)(2,1)}, u32[]{:S(2)}, u32[]{:S(2)}) collective-permute-start(bf16[48,512]{1,0:T(8,128)(2,1)} %get-tuple-element.149), channel_id=1, source_target_pairs={{0,8},{2,10},{4,12},{6,14},{8,16},{10,18},{12,20},{14,22},{16,24},... | collective-permute-start | bytes 147464 | tf_op jit(solution)/shard_map/ppermute | solution.py:514
  251.5 42.5 %collective-permute-start.92 = (bf16[48,512]{1,0:T(8,128)(2,1)}, bf16[48,512]{1,0:T(8,128)(2,1)}, u32[]{:S(2)}, u32[]{:S(2)}) collective-permute-start(bf16[48,512]{1,0:T(8,128)(2,1)} %get-tuple-element.151), channel_id=1, source_target_pairs={{0,24},{2,26},{4,28},{6,30},{8,0},{10,2},{12,4},{14,6},{16,8},{18,... | collective-permute-start | bytes 147464 | tf_op jit(solution)/shard_map/ppermute | solution.py:514
  289.7 20.1 %collective-permute-start.67 = (bf16[768,768]{1,0:T(8,128)(2,1)}, bf16[768,768]{1,0:T(8,128)(2,1)S(1)}, u32[]{:S(2)}, u32[]{:S(2)}) collective-permute-start(bf16[768,768]{1,0:T(8,128)(2,1)} %get-tuple-element.91), channel_id=1, source_target_pairs={{0,1},{1,0},{2,3},{3,2},{4,5},{5,4},{6,7},{7,6},{8,9},{9,8},{10,11... | collective-permute-start | bytes 3538952 | tf_op jit(solution)/shard_map/ppermute | solution.py:518
  290.4 21.1 %collective-permute-start.73 = (bf16[768,768]{1,0:T(8,128)(2,1)}, bf16[768,768]{1,0:T(8,128)(2,1)S(1)}, u32[]{:S(2)}, u32[]{:S(2)}) collective-permute-start(bf16[768,768]{1,0:T(8,128)(2,1)} %get-tuple-element.93), channel_id=1, source_target_pairs={{0,1},{1,0},{2,3},{3,2},{4,5},{5,4},{6,7},{7,6},{8,9},{9,8},{10,11... | collective-permute-start | bytes 3538952 | tf_op jit(solution)/shard_map/ppermute | solution.py:518
  (146 other events, 1486.4 us)

commit v2 on v1

--- a/solution.py
+++ b/solution.py
@@ -20,8 +20,8 @@
 EPSILON = 1e-06
 MASKED_SCORE = -1e30
 MASK_LANE = 60
-FFN_CHUNKS = 3
-BACK_CHUNKS = 1
+FFN_CHUNKS = 2
+BACK_PARTS = ((0, 4), (4, 2))
 F32 = jnp.float32
 BF16 = jnp.bfloat16
 SMEM = pl.BlockSpec(memory_space=pltpu.SMEM)
@@ -86,7 +86,7 @@
     place = lax.broadcasted_iota(jnp.int32, (rows, width), 0)
     row, col = place // SIDE, place % SIDE
     inside = (row < WIN) & (col < WIN)
-    return inside & (core * WIN + row < meta[33 + window]) & (col < meta[35 + window])
+    return inside & (core * WIN + row < meta[65 + window]) & (col < meta[67 + window])
 
 
 def relative(turned):
@@ -100,26 +100,20 @@
 
 
 def attend_kernel(count, meta, tok, table, spread, *refs):
-    own0, own1 = refs[:count], refs[count : 2 * count]
-    other0, other1 = refs[2 * count : 3 * count], refs[3 * count : 4 * count]
-    (n1, q_out, k_out, v_out, p_out, att, x1, n2, vecs, w_out) = refs[4 * count : 4 * count + 10]
-    weights, small, aug, sems, out_sem = refs[4 * count + 10 :]
+    own, other = refs[:count], refs[count : 2 * count]
+    n1, q_out, k_out, v_out, p_out, att, vecs, w_out = refs[2 * count : 2 * count + 8]
+    weights, small, aug, sems, out_sem = refs[2 * count + 8 :]
     width = weights.shape[1]
     rows = width // PIECES
-    core = meta[32]
+    core = meta[64]
     copies = []
-    for refs_here, at, which, extra in (
-        (own0, 0, 2 * core, True),
-        (own1, 16, 2 * core + 1, False),
-        (other0, 0, 2 - 2 * core, False),
-        (other1, 16, 3 - 2 * core, False),
-    ):
-        copies += pieces_in(
-            meta, at, refs_here, rows, pl.ds(0, width), weights.at[which], sems, len(copies)
-        )
+    for refs_here, at, half, extra in ((own, 0, core, True), (other, 16, 1 - core, False)):
+        places = [(0, width, weights.at[2 * half]), (width + LANES, width, weights.at[2 * half + 1])]
         if extra:
+            places.append((width, LANES, small))
+        for start, size, dest in places:
             copies += pieces_in(
-                meta, at, refs_here, rows, pl.ds(width, LANES), small, sems, len(copies)
+                meta, at, refs_here, rows, pl.ds(start, size), dest, sems, len(copies)
             )
     for window in range(2):
         keys = lanes(KEYS)
@@ -172,17 +166,11 @@
         return 0
 
     lax.fori_loop(0, 2 * PAIRS, heads_of, 0)
-    attended = att[...].reshape(2 * TOK, width)
-    tokens = tok[...].reshape(2 * TOK, width).astype(F32)
-    resid = tokens + (dot(attended, weights[3]) + vecs[4:5])
-    x1[...] = resid.reshape(2, TOK, width)
-    xhat2, _ = moments(resid)
-    n2[...] = (xhat2 * vecs[5:6] + vecs[6:7]).astype(BF16).reshape(2, TOK, width)
     out_copy.wait()
 
 
-def attend(meta, tok, table, spread, own0, own1, other0, other1):
-    count, width = len(own0), tok.shape[-1]
+def attend(meta, tok, table, spread, own, other):
+    count, width = len(own), tok.shape[-1]
     rows = (2, TOK, width)
     keys = (2, KEYS, width)
     return pl.pallas_call(
@@ -194,13 +182,11 @@
             shape(keys, BF16),
             shape((2, HEADS, TOK, KEYS), BF16),
             shape(rows, BF16),
-            shape(rows, F32),
-            shape(rows, BF16),
             shape((8, width), F32),
             shape((4, width, width), BF16),
         ],
-        in_specs=[SMEM, WHOLE, WHOLE, WHOLE] + [HBM] * (4 * count),
-        out_specs=[WHOLE] * 9 + [HBM],
+        in_specs=[SMEM, WHOLE, WHOLE, WHOLE] + [HBM] * (2 * count),
+        out_specs=[WHOLE] * 7 + [HBM],
         scratch_shapes=[
             pltpu.VMEM((4, width, width), BF16),
             pltpu.VMEM((width, LANES), BF16),
@@ -210,21 +196,50 @@
         ],
         compiler_params=params(),
         cost_estimate=pl.CostEstimate(
-            flops=6_000_000_000, bytes_accessed=20_000_000, transcendentals=1_500_000
+            flops=6_000_000_000, bytes_accessed=60_000_000, transcendentals=1_500_000
         ),
         name="attend",
-    )(meta, tok, table, spread, *own0, *own1, *other0, *other1)
-
-
-def hidden_kernel(count, first, last, meta, n2a, n2b, dma, dmb, bias, *refs):
+    )(meta, tok, table, spread, *own, *other)
+
+
+def join_kernel(tok, att, weights, vecs, x1, n2):
+    width = tok.shape[-1]
+    for window in range(2):
+        resid = tok[window].astype(F32) + (dot(att[window], weights[0]) + vecs[4:5])
+        x1[window] = resid
+        xhat, _ = moments(resid)
+        n2[window] = (xhat * vecs[5:6] + vecs[6:7]).astype(BF16)
+
+
+def join(tok, att, weights, vecs):
+    width = tok.shape[-1]
+    return pl.pallas_call(
+        join_kernel,
+        out_shape=[shape(tok.shape, F32), shape(tok.shape, BF16)],
+        grid=(1,),
+        in_specs=[
+            WHOLE,
+            WHOLE,
+            pl.BlockSpec((1, width, width), lambda i: (3, 0, 0)),
+            WHOLE,
+        ],
+        out_specs=[WHOLE] * 2,
+        compiler_params=params(),
+        cost_estimate=pl.CostEstimate(
+            flops=600_000_000, bytes_accessed=9_000_000, transcendentals=0
+        ),
+        name="join",
+    )(tok, att, weights, vecs)
+
+
+def hidden_kernel(count, starts, first, last, meta, n2a, n2b, dma, dmb, bias, *refs):
     refs = list(refs)
-    in0, in1 = refs[:count], refs[count : 2 * count]
-    refs = refs[2 * count :]
+    ins, refs = refs[:count], refs[count:]
     if not first:
         out_in, back_in = refs[:2]
         refs = refs[2:]
-    g0_keep, g0_send, g1_keep, g1_send, bias_grad = refs[:5]
-    refs = refs[5:]
+    keep, send, bias_grad = refs[:3]
+    refs = refs[3:]
     if last:
         out_own, out_far, back_own, back_far = refs[:4]
         refs = refs[4:]
@@ -234,8 +249,9 @@
     w0, w1, n2s, dms, acts, backs, g0, g1, sems, out_sems = refs
     width, cols_here = w0.shape
     rows = width // PIECES
-    copies = pieces_in(meta, 0, in0, rows, pl.ds(0, cols_here), w0, sems, 0)
-    copies += pieces_in(meta, 16, in1, rows, pl.ds(0, cols_here), w1, sems, PIECES)
+    copies = []
+    for start, dest in zip(starts, (w0, w1)):
+        copies += pieces_in(meta, 0, ins, rows, pl.ds(start, cols_here), dest, sems, len(copies))
     n2s[: 2 * TOK] = n2a[...].reshape(2 * TOK, width)
     n2s[2 * TOK :] = n2b[...].reshape(2 * TOK, width)
     dms[: 2 * TOK] = dma[...].reshape(2 * TOK, width)
@@ -255,14 +271,14 @@
         bias_grad[:, cols] = jnp.sum(back_pre.astype(F32), axis=0, keepdims=True)
         g0[:, cols] = dot_tn(n2s[...], back_pre).astype(BF16)
         g1[:, cols] = dot_tn(dms[...], acts[:, cols]).astype(BF16)
-        for which, (made, keep, send) in enumerate(((g0, g0_keep, g0_send), (g1, g1_keep, g1_send))):
+        for which, made in enumerate((g0, g1)):
             for piece in range(PIECES):
                 dest = keep if piece < PIECES // 2 else send
-                place = pl.multiple_of(meta[16 * which + piece] * rows, rows)
+                place = pl.multiple_of(meta[32 + piece] * rows, rows)
                 at = (piece % (PIECES // 2)) * rows
                 copy = pltpu.make_async_copy(
                     made.at[pl.ds(place, rows), cols],
-                    dest.at[pl.ds(at, rows), cols],
+                    dest.at[pl.ds(at, rows), pl.ds(which * cols_here + start, 256)],
                     out_sems.at[len(outs)],
                 )
                 copy.start()
@@ -284,11 +300,10 @@
         copy.wait()
 
 
-def hidden(meta, n2a, n2b, dma, dmb, bias, in0, in1, carried, last):
-    count, width, cols_here = len(in0), n2a.shape[-1], bias.shape[-1]
+def hidden(meta, n2a, n2b, dma, dmb, bias, ins, starts, carried, last):
+    count, width, cols_here = len(ins), n2a.shape[-1], bias.shape[-1]
     first = carried is None
-    half = (width // 2, cols_here)
-    out_shape = [shape(half, BF16)] * 4 + [shape((1, cols_here), F32)]
+    out_shape = [shape((width // 2, 2 * cols_here), BF16)] * 2 + [shape((1, cols_here), F32)]
     if last:
         one = (2 * TOK, width)
         out_shape += [shape(one, F32), shape(one, BF16), shape(one, F32), shape(one, BF16)]
@@ -296,10 +311,10 @@
         out_shape += [shape((4 * TOK, width), F32)] * 2
     carried = () if first else carried
     return pl.pallas_call(
-        partial(hidden_kernel, count, first, last),
+        partial(hidden_kernel, count, starts, first, last),
         out_shape=out_shape,
-        in_specs=[SMEM] + [WHOLE] * 5 + [HBM] * (2 * count) + [WHOLE] * len(carried),
-        out_specs=[HBM] * 4 + [WHOLE] * (len(out_shape) - 4),
+        in_specs=[SMEM] + [WHOLE] * 5 + [HBM] * count + [WHOLE] * len(carried),
+        out_specs=[HBM] * 2 + [WHOLE] * (len(out_shape) - 2),
         scratch_shapes=[
             pltpu.VMEM((width, cols_here), BF16),
             pltpu.VMEM((width, cols_here), BF16),
@@ -319,12 +334,12 @@
             transcendentals=8 * TOK * cols_here,
         ),
         name="hidden",
-    )(meta, n2a, n2b, dma, dmb, bias, *in0, *in1, *carried)
+    )(meta, n2a, n2b, dma, dmb, bias, *ins, *carried)
 
 
 def middle_kernel(meta, out_own, out_far, back_own, back_far, x1, dm, vecs, block, dx1, da, sums):
     width = x1.shape[-1]
-    core = meta[32]
+    core = meta[64]
     total = [jnp.zeros((1, width), F32) for _ in range(4)]
     for window in range(2):
         rows = pl.ds(window * TOK, TOK)
@@ -380,12 +395,12 @@
     refs = list(refs)
     if not first:
         dn1_in = refs.pop(0)
-    mine0, mine1, theirs0, theirs1, bias_sums, table_grad, result = refs[:7]
-    refs = refs[7:]
+    mine, theirs, bias_sums, table_grad, result = refs[:5]
+    refs = refs[5:]
     if last:
         norm_sums = refs.pop(0)
     dat, dqkv, grads, sems = refs
-    core = meta[32]
+    core = meta[64]
     width, cols_here = da.shape[-1], q.shape[-1]
     pairs, rows = cols_here // LANES, width // PIECES
     dat[...] = (
@@ -396,14 +411,16 @@
 
     def send(mat, made):
         grads[mat] = made.astype(BF16)
-        own, far = (mine0, theirs0) if mat % 2 == 0 else (mine1, theirs1)
+        is_own = core == mat // 2
+        at = jnp.where(is_own, 32, 48)
         for piece in range(PIECES):
-            place = pl.multiple_of(meta[16 * (mat % 2) + piece] * rows, rows)
+            place = pl.multiple_of(meta[at + piece] * rows, rows)
             source = grads.at[mat, pl.ds(place, rows), :]
-            to, sem = pl.ds(piece * rows, rows), sems.at[len(outs)]
-            copies = [pltpu.make_async_copy(source, ref.at[to, :], sem) for ref in (own, far)]
-            pl.when(core == mat // 2)(copies[0].start)
-            pl.when(core != mat // 2)(copies[1].start)
+            to = pl.ds(piece * rows, rows), pl.ds(mat % 2 * cols_here, cols_here)
+            sem = sems.at[len(outs)]
+            copies = [pltpu.make_async_copy(source, ref.at[to], sem) for ref in (mine, theirs)]
+            pl.when(is_own)(copies[0].start)
+            pl.when(~is_own)(copies[1].start)
             outs.append(copies[0])
 
     send(3, dot_tn(att[...].reshape(2 * TOK, width), da_cols[...].reshape(2 * TOK, cols_here)))
@@ -457,12 +474,12 @@
         copy.wait()
 
 
-def attend_back(chunk, chunks, meta, q, k, v, p, weights, da, att, n1, tok, dx1, vecs, gather, table, dn1):
+def attend_back(start, count, meta, q, k, v, p, weights, da, att, n1, tok, dx1, vecs, gather, table, dn1):
     width = q.shape[-1]
-    cols_here, heads_here = width // chunks, HEADS // chunks
-    first, last = chunk == 0, chunk == chunks - 1
+    cols_here, heads_here = count * LANES, 2 * count
+    first, last, chunk = start == 0, start + count == PAIRS, start // count
     part = lambda rows: pl.BlockSpec((2, rows, cols_here), lambda i: (0, 0, chunk))
-    out_shape = [shape((width, cols_here), BF16)] * 4 + [
+    out_shape = [shape((width, 2 * cols_here), BF16)] * 2 + [
         shape((2, cols_here), F32),
         shape((LANES, LANES), F32),
         shape((2, TOK, width), F32),
@@ -486,7 +503,7 @@
             part(TOK),
         ]
         + [WHOLE] * (7 + len(extra)),
-        out_specs=[HBM] * 4 + [WHOLE] * (len(out_shape) - 4),
+        out_specs=[HBM] * 2 + [WHOLE] * (len(out_shape) - 2),
         scratch_shapes=[
             pltpu.VMEM((2, TOK, cols_here), BF16),
             pltpu.VMEM((3, 2, TOK, cols_here), BF16),
@@ -495,7 +512,7 @@
         ],
         compiler_params=params(),
         cost_estimate=pl.CostEstimate(
-            flops=12_000_000_000 // chunks, bytes_accessed=24_000_000 // chunks, transcendentals=0
+            flops=2_000_000_000 * count, bytes_accessed=10_000_000 * count, transcendentals=0
         ),
         name="attend_back",
     )(meta, q, k, v, p, weights, weights, da, da, att, n1, tok, dx1, vecs, gather, table, *extra)
@@ -505,65 +522,81 @@
     return (4, 2, 2) if count == 16 else None
 
 
-def turn(values, dims, axis, by):
+def turn(values, dims, moves):
     pairs = []
     for chip in range(dims[0] * dims[1] * dims[2]):
-        place = list(np.unravel_index(chip, dims))
-        place[axis] = (place[axis] + by) % dims[axis]
-        pairs.append((chip, int(np.ravel_multi_index(place, dims))))
-    return lax.ppermute(values, "dp", pairs)
+        for core, (axis, by) in enumerate(moves):
+            place = list(np.unravel_index(chip, dims))
+            place[axis] = (place[axis] + by) % dims[axis]
+            pairs.append((2 * chip + core, 2 * int(np.ravel_multi_index(place, dims)) + core))
+    return lax.ppermute(values, ("dp", "mp"), pairs)
+
+
+ALONG_X, ALONG_Y = ((2, 1),) * 2, ((1, 1),) * 2
+FIRST, SECOND = ((2, 1), (1, 1)), ((1, 1), (2, 1))
+
+
+def along_z(values, dims):
+    return [turn(values, dims, ((0, step),) * 2) for step in range(1, dims[0])]
 
 
 def other_core(values):
     return lax.ppermute(values, "mp", [(0, 1), (1, 0)])
 
 
-def place_order(dims, first, second):
+def after(values, *others):
+    return lax.optimization_barrier((values, *others))[0]
+
+
+def place_orders(dims, core):
     here = lax.axis_index("dp")
     z, y, x = here // (dims[1] * dims[2]), here // dims[2] % dims[1], here % dims[2]
-    found = []
-    for outer in range(2):
-        for inner in range(2):
-            at = [z, y, x]
-            at[first] = (at[first] + inner) % 2
-            at[second] = (at[second] + outer) % 2
-            for step in range(dims[0]):
-                found.append(((z - step) % dims[0] * dims[1] + at[1]) * dims[2] + at[2])
-    return jnp.stack(found).astype(jnp.int32)
-
-
-def gather_rows(block, dims, first, second):
-    near = jnp.concatenate(
-        [block] + [turn(block, dims, 0, step) for step in range(1, dims[0])], axis=0
-    )
-    beside = turn(near, dims, first, 1)
-    return [near, beside, turn(near, dims, second, 1), turn(beside, dims, second, 1)]
+
+    def chip(step, inner, outer):
+        by_x = jnp.where(core == 0, inner, outer)
+        by_y = jnp.where(core == 0, outer, inner)
+        return ((z - step) % dims[0] * dims[1] + (y + by_y) % 2) * dims[2] + (x + by_x) % 2
+
+    square = [(inner, outer) for outer in range(2) for inner in range(2)]
+    gather = [chip(0, *at) for at in square]
+    gather += [chip(step, *at) for at in square for step in range(1, dims[0])]
+    scatter = [chip(step, *at) for at in square for step in range(dims[0])]
+    return [jnp.stack(found).astype(jnp.int32) for found in (gather, scatter)]
 
 
 def add(a, b):
     return a.astype(F32) + b.astype(F32)
 
 
-def scatter_rows(keep, far, dims, first, second):
-    half = keep.shape[0] // 2
-    came = turn(far, dims, second, 1)
-    beside = turn(add(keep[half:], came[half:]).astype(BF16), dims, first, 1)
-    near = add(keep[:half], came[:half]) + beside.astype(F32)
-    rows = half // dims[0]
-    total = near[:rows]
-    for step in range(1, dims[0]):
-        part = near[step * rows : (step + 1) * rows].astype(BF16)
-        total = total + turn(part, dims, 0, dims[0] - step).astype(F32)
-    return total
-
-
-def add_all(values, dims):
-    values = values + other_core(values)
-    if dims is None:
-        return lax.psum(values, "dp")
-    values = values + turn(values, dims, 2, 1)
-    values = values + turn(values, dims, 1, 1)
-    return values + sum(turn(values, dims, 0, step) for step in range(1, dims[0]))
+class Scatter:
+    def __init__(self, keep, far, dims):
+        self.keep, self.dims = keep, dims
+        self.came = turn(far, dims, SECOND)
+
+    def second(self, *others):
+        half = self.keep.shape[0] // 2
+        came = after(self.came, *others)
+        send = add(self.keep[half:], came[half:]).astype(BF16)
+        self.near = add(self.keep[:half], came[:half])
+        self.came = turn(send, self.dims, FIRST)
+        return send
+
+    def third(self, *others):
+        near = self.near + after(self.came, *others).astype(F32)
+        rows = near.shape[0] // self.dims[0]
+        self.near = near[:rows]
+        sends = [near[at * rows : (at + 1) * rows].astype(BF16) for at in range(1, self.dims[0])]
+        self.came = [
+            turn(part, self.dims, ((0, self.dims[0] - step),) * 2)
+            for step, part in enumerate(sends, 1)
+        ]
+        return sends[0]
+
+    def last(self, *others):
+        total = self.near
+        for part in self.came:
+            total = total + after(part, *others).astype(F32)
+        return total
 
 
 def constants():
@@ -638,12 +671,14 @@
     core = lax.axis_index("mp")
     is_first = core == 0
     if dims is None:
-        order = jnp.tile(jnp.arange(PIECES, dtype=jnp.int32), 2)
+        orders = [jnp.tile(jnp.arange(PIECES, dtype=jnp.int32), 4)]
     else:
-        order = jnp.concatenate([place_order(dims, 2, 1), place_order(dims, 1, 2)])
+        own, far = place_orders(dims, core), place_orders(dims, 1 - core)
+        orders = [own[0], far[0], own[1], far[1]]
     meta = jnp.concatenate(
-        [order, core.astype(jnp.int32)[None], heights, widths, jnp.zeros((27,), jnp.int32)]
-    )
+        orders + [core.astype(jnp.int32)[None], heights, widths, jnp.zeros((11,), jnp.int32)]
+    )
+    hidden_count = fc1_weight.shape[1]
 
     vectors = (norm1_gain, norm1_bias, qv_bias[0], qv_bias[1], proj_bias, norm2_gain, norm2_bias, fc2_bias)
     small = jnp.pad(jnp.stack(vectors, axis=1), ((0, 0), (0, LANES - len(vectors))))
@@ -652,36 +687,41 @@
     if dims is None:
         qk = lax.all_gather(qk, ("dp", "mp"), axis=0, tiled=True)
         vp = lax.all_gather(vp, ("dp", "mp"), axis=0, tiled=True)
-        own = jnp.where(is_first, qk, vp)
-        far = jnp.where(is_first, vp, qk)
-        own0, own1 = [own[:, : width + LANES]], [own[:, width + LANES :]]
-        far0, far1 = [far[:, : width + LANES]], [far[:, width + LANES :]]
+        attend_own = [jnp.where(is_first, qk, vp)]
+        attend_far = [jnp.where(is_first, vp, qk)]
         hidden_in = [
-            (
-                [lax.all_gather(fc1_weight, "dp", axis=0, tiled=True)],
-                [lax.all_gather(fc2_weight.T, "dp", axis=0, tiled=True)],
+            jnp.concatenate(
+                [
+                    lax.all_gather(fc1_weight, "dp", axis=0, tiled=True),
+                    lax.all_gather(fc2_weight.T, "dp", axis=0, tiled=True),
+                ],
+                axis=1,
             )
         ]
     else:
+        came = other_core(jnp.where(is_first, vp, qk))
+        hidden_block = jnp.concatenate([fc1_weight, fc2_weight.T], axis=1)
+        hidden_beside = turn(hidden_block, dims, FIRST)
         near = jnp.where(is_first, qk, vp)
-        came = other_core(jnp.where(is_first, vp, qk))
         block = jnp.concatenate(
             [jnp.where(is_first, near, came), jnp.where(is_first, came, near)], axis=0
         )
-        own0 = gather_rows(block[:, : width + LANES], dims, 2, 1)
-        own1 = gather_rows(block[:, width + LANES :], dims, 1, 2)
-        far0 = [other_core(part) for part in own0]
-        far1 = [other_core(part) for part in own1]
-        hidden_in = []
-        part = fc1_weight.shape[1] // FFN_CHUNKS
-        for chunk in range(FFN_CHUNKS):
-            cols = slice(chunk * part, (chunk + 1) * part)
-            hidden_in.append(
-                (
-                    gather_rows(fc1_weight[:, cols], dims, 2, 1),
-                    gather_rows(fc2_weight.T[:, cols], dims, 1, 2),
-                )
-            )
+        attend_z = along_z(block, dims)
+        beside = turn(block, dims, FIRST)
+        both = jnp.concatenate([block, beside], axis=0)
+        over = turn(both, dims, SECOND)
+        both = jnp.concatenate([hidden_block, after(hidden_beside, both)], axis=0)
+        hidden_over = turn(both, dims, SECOND)
+        attend_z = jnp.concatenate([after(attend_z[0], both)] + attend_z[1:], axis=0)
+        z_beside = turn(attend_z, dims, FIRST)
+        hidden_z = along_z(after(hidden_block, attend_z), dims)
+        both = jnp.concatenate([attend_z, z_beside], axis=0)
+        z_over = turn(both, dims, SECOND)
+        attend_own = [block, beside, over, attend_z, z_beside, z_over]
+        attend_far = [other_core(part) for part in attend_own]
+        hidden_z = jnp.concatenate([after(hidden_z[0], both)] + hidden_z[1:], axis=0)
+        hidden_z_beside = turn(hidden_z, dims, FIRST)
+        hidden_z_over = turn(hidden_z, dims, SECOND)
 
     tok = padded(patches)
     row_index = core * WIN + jnp.arange(WIN)
@@ -693,47 +733,52 @@
     spread, gather = constants()
     table, table_back = tables(rel_pos_h, rel_pos_w)
 
-    n1, q, k, v, p, att, x1, n2, vecs, weights = attend(
-        meta, tok, table, jnp.asarray(spread, BF16), own0, own1, far0, far1
-    )
+    if dims is not None:
+        tok = after(tok, hidden_z)
+    n1, q, k, v, p, att, vecs, weights = attend(
+        meta, tok, table, jnp.asarray(spread, BF16), attend_own, attend_far
+    )
+    if dims is not None:
+        hidden_z_both = turn(after(hidden_z_beside, att), dims, SECOND)
+        hidden_in = [
+            hidden_block, hidden_beside, hidden_over, hidden_z, hidden_z_beside, hidden_z_over, hidden_z_both,
+        ]
+    x1, n2 = join(tok, att, weights, vecs)
     n2_far = other_core(n2)
 
     carried = None
-    hidden_grads, bias_grads = [], []
-    part = fc1_weight.shape[1] // len(hidden_in)
-    for chunk, (in0, in1) in enumerate(hidden_in):
+    hidden_sums, bias_grads = [], []
+    part = hidden_count // FFN_CHUNKS
+    for chunk in range(FFN_CHUNKS):
         bias = fc1_bias[None, chunk * part : (chunk + 1) * part].astype(F32)
-        last = chunk == len(hidden_in) - 1
-        made = hidden(meta, n2, n2_far, dm, dm_far, bias, in0, in1, carried, last)
-        bias_grads.append(made[4])
-        carried = made[5:]
+        last = chunk == FFN_CHUNKS - 1
+        starts = (chunk * part, hidden_count + chunk * part)
+        made = hidden(meta, n2, n2_far, dm, dm_far, bias, hidden_in, starts, carried, last)
+        bias_grads.append(made[2])
+        carried = made[3:]
         if dims is None:
-            hidden_grads.append(
-                [
-                    lax.psum_scatter(
-                        jnp.concatenate(pair, axis=0).astype(F32), "dp", scatter_dimension=0, tiled=True
-                    )
-                    for pair in (made[0:2], made[2:4])
-                ]
+            hidden_sums.append(
+                lax.psum_scatter(
+                    jnp.concatenate(made[:2], axis=0).astype(F32), "dp", scatter_dimension=0, tiled=True
+                )
             )
         else:
-            hidden_grads.append(
-                (
-                    scatter_rows(made[0], made[1], dims, 2, 1),
-                    scatter_rows(made[2], made[3], dims, 1, 2),
-                )
-            )
+            if chunk:
+                sent = hidden_sums[-1].second(made[2])
+                made = [made[0], after(made[1], sent)]
+            hidden_sums.append(Scatter(made[0], made[1], dims))
     out_own, out_far, back_own, back_far = carried
+    back_far = other_core(back_far)
     block_out, dx1, da, sums2 = middle(
-        meta, out_own, other_core(out_far), back_own, other_core(back_far), x1, dm, vecs
+        meta, out_own, other_core(out_far), back_own, back_far, x1, dm, vecs
     )
 
     dn1 = None
-    bias_sums, table_grad, attend_grads = [], 0.0, []
-    for chunk in range(BACK_CHUNKS):
+    bias_sums, table_grad, attend_sums = [], 0.0, []
+    for start, count in BACK_PARTS:
         made = attend_back(
-            chunk,
-            BACK_CHUNKS,
+            start,
+            count,
             meta,
             q,
             k,
@@ -750,35 +795,24 @@
             table_back,
             dn1,
         )
-        bias_sums.append(made[4])
-        table_grad = table_grad + made[5]
-        dn1 = made[6]
-        if chunk == BACK_CHUNKS - 1:
-            sums1 = made[7]
-        halves = []
-        for mine, theirs, axes in ((made[0], made[2], (2, 1)), (made[1], made[3], (1, 2))):
-            if dims is None:
-                whole = lax.psum_scatter(
-                    add(mine, other_core(theirs)), "dp", scatter_dimension=0, tiled=True
-                )
-            else:
-                came = other_core(theirs)
-                half = width // 2
-                whole = scatter_rows(
-                    add(mine[:half], came[:half]).astype(BF16),
-                    add(mine[half:], came[half:]).astype(BF16),
-                    dims,
-                    *axes,
-                )
-            halves.append(whole)
-        whole = jnp.stack(halves)
-        rows = whole.shape[1] // 2
-        near = jnp.where(is_first, whole[:, :rows], whole[:, rows:])
-        came = other_core(jnp.where(is_first, whole[:, rows:], whole[:, :rows]))
-        attend_grads.append((jnp.where(is_first, near, came), jnp.where(is_first, came, near)))
-    qk_grad = [jnp.concatenate([g[0][i] for g in attend_grads], axis=1) for i in range(2)]
-    vp_grad = [jnp.concatenate([g[1][i] for g in attend_grads], axis=1) for i in range(2)]
-    qkv_grad = jnp.concatenate([qk_grad[0], qk_grad[1], vp_grad[0]], axis=1)
+        bias_sums.append(made[2])
+        table_grad = table_grad + made[3]
+        dn1 = made[4]
+        mine, theirs = made[0], made[1]
+        came = other_core(theirs)
+        if dims is None:
+            attend_sums.append(
+                lax.psum_scatter(add(mine, came), "dp", scatter_dimension=0, tiled=True)
+            )
+            continue
+        half = width // 2
+        if start == 0:
+            sent = hidden_sums[0].third(dn1)
+            sent = hidden_sums[1].second(sent)
+            both = add(mine, after(came, sent)).astype(BF16)
+            attend_sums.append(Scatter(both[:half], both[half:], dims))
+            da = after(da, both)
+    sums1 = made[5]
 
     qv_sums = jnp.concatenate(bias_sums, axis=1)
     rel_sums = table_grad[:64, :HDIM] + table_grad[:64, HDIM:]
@@ -794,7 +828,49 @@
         ],
         axis=0,
     )
-    flat = add_all(flat, dims)
+    if dims is None:
+        flat = lax.psum(flat + other_core(flat), "dp")
+    else:
+        flat_came = other_core(flat)
+        sent = hidden_sums[1].third(dn1)
+        sent = attend_sums[0].second(sent)
+        both = add(mine, after(came, sent)).astype(BF16)
+        attend_sums.append(Scatter(both[:half], both[half:], dims))
+        flat = flat + after(flat_came, both)
+        flat_came = turn(flat, dims, SECOND)
+        sent = attend_sums[0].third(flat)
+        flat = flat + after(flat_came, sent)
+        flat_came = turn(flat, dims, FIRST)
+        sent = attend_sums[1].second(flat)
+        flat = flat + after(flat_came, sent)
+        flat_came = along_z(flat, dims)
+        hidden_sums = [found.last(sent) for found in hidden_sums]
+        sent = attend_sums[1].third(flat, *hidden_sums)
+        attend_sums[0] = attend_sums[0].last(sent)
+        flat = flat + sum(flat_came)
+        attend_sums[1] = attend_sums[1].last(flat, attend_sums[0])
+
+    whole = jnp.concatenate(attend_sums, axis=1)
+    rows = whole.shape[0] // 2
+    near = jnp.where(is_first, whole[:rows], whole[rows:])
+    came = other_core(jnp.where(is_first, whole[rows:], whole[:rows]))
+    halves = [[], []]
+    at = 0
+    for _, count in BACK_PARTS:
+        for half in range(2):
+            halves[half].append(slice(at, at + count * LANES))
+            at += count * LANES
+    qk, vp = jnp.where(is_first, near, came), jnp.where(is_first, came, near)
+    q_grad, k_grad, v_grad, proj_grad = (
+        jnp.concatenate([found[:, cols] for cols in half], axis=1)
+        for found in (qk, vp)
+        for half in halves
+    )
+    qkv_grad = jnp.concatenate([q_grad, k_grad, v_grad], axis=1)
+    cols = hidden_sums[0].shape[1] // 2
+    fc1_grad = jnp.concatenate([found[:, :cols] for found in hidden_sums], axis=1)
+    fc2_grad = jnp.concatenate([found[:, cols:] for found in hidden_sums], axis=1).T
+
     at = 8 * width // LANES
     vec_sums = flat[:at].reshape(8, width)
     rel = flat[at : at + 32].reshape(64, HDIM)
@@ -812,13 +888,13 @@
         mine[2:4],
         rel[:rels],
         rel[32 : 32 + rels],
-        vp_grad[1],
+        proj_grad,
         mine[4],
         mine[5],
         mine[6],
-        jnp.concatenate([g[0] for g in hidden_grads], axis=1),
+        fc1_grad,
         fc1_bias_grad,
-        jnp.concatenate([g[1] for g in hidden_grads], axis=1).T,
+        fc2_grad,
         mine[7],
     )
 

time: 353 us -> 283 us (0.80)
  starting transfers between devices: 125 us -> 60.2 us
  Pallas kernels: 98.5 us -> 91.7 us
  other arithmetic: 13.4 us -> 18.4 us
    ppermute x93 -> x40, starting transfers between devices: 123 us -> 56.2 us  [turn(): return lax.ppermute(values, ('dp', 'mp'), pairs)]
    pallas_call x3, Pallas kernels: 43 us -> 34.1 us  [the longest x2 30.6 us: hidden(): pl.pallas_call(partial(hidden_kernel, count, starts, first, last), out_sh...]
    pallas_call x1 -> x2, Pallas kernels: 28.1 us -> 33.6 us  [attend_back(): pl.pallas_call(partial(attend_back_kernel, first, last), out_shape=out_sh...]
    ppermute x93 -> x40, waiting for transfers between devices: 82.8 us -> 81.3 us  [turn(): return lax.ppermute(values, ('dp', 'mp'), pairs)]
    unnamed x128 -> x88, local copies, waits for them, and re-layouts: 9.91 us -> 11.1 us
  transfers between devices with their start and end apart: 110 -> 55, of which waited for: 38 -> 26; matrix products, arithmetic and copies ran while one was open for 9% -> 10% of each run, Pallas kernels for 28% -> 28%
where the time goes in v2:
time: 283 us; the launch traced here: 279 us
  Pallas kernels  91.7 us (32%)
  waiting for transfers between devices  85.9 us (30%)
  starting transfers between devices  60.2 us (21%)
  local copies, waits for them, and re-layouts  21.2 us (7%)
  other arithmetic  18.4 us (7%)
    ppermute x40, waiting for transfers between devices, turn(): return lax.ppermute(values, ('dp', 'mp'), pairs)  81.3 us
    ppermute x40, starting transfers between devices, turn(): return lax.ppermute(values, ('dp', 'mp'), pairs)  56.2 us
    pallas_call x2, Pallas kernels, attend_back(): pl.pallas_call(partial(attend_back_kernel, first, last), out_shape=out_sh...  33.6 us
    pallas_call x2, Pallas kernels, hidden(): pl.pallas_call(partial(hidden_kernel, count, starts, first, last), out_sh...  30.6 us
    pallas_call x1, Pallas kernels, attend(): pl.pallas_call(partial(attend_kernel, count), out_shape=[shape(rows, BF16...  18.5 us
    unnamed x88, local copies, waits for them, and re-layouts  11.1 us
  transfers between devices with their start and end apart: 55, of which 26 were waited for; matrix products, arithmetic and copies ran while one was open for 10% of the time, Pallas kernels for 28%

profile of v2, /device:TPU:0, one launch (start us, length us, event | category | flops | bytes accessed | tf_op | source)
XLA Modules:
  0.0 279.4 jit_solution(3347728605212761956)
XLA Ops:
  6.2 2.9 %collective-permute-start.3 = (bf16[48,1664]{1,0:T(8,128)(2,1)S(1)}, bf16[48,1664]{1,0:T(8,128)(2,1)S(1)}, u32[]{:S(2)}, u32[]{:S(2)}) collective-permute-start(bf16[48,1664]{1,0:T(8,128)(2,1)S(1)} %pad_maximum_fusion.4.refs_0_), channel_id=1, source_target_pairs={{0,2},{1,5},{2,0},{3,7},{4,6},{5,1},{6,4},{7,3},{8,10},{9,13},{10,... | collective-permute-start | bytes 479240 | tf_op jit(solution)/shard_map/ppermute | solution.py:532
  19.1 5.0 %collective-permute-done.4 = bf16[48,1664]{1,0:T(8,128)(2,1)S(1)} collective-permute-done((bf16[48,1664]{1,0:T(8,128)(2,1)S(1)}, bf16[48,1664]{1,0:T(8,128)(2,1)S(1)}, u32[]{:S(2)}, u32[]{:S(2)}) %collective-permute-start.4) | collective-permute-done | bytes 159776 | tf_op jit(solution)/shard_map/ppermute | solution.py:532
  27.0 7.2 %collective-permute-done.7.refs_4_ = bf16[144,1664]{1,0:T(8,128)(2,1)S(1)} collective-permute-done((bf16[144,1664]{1,0:T(8,128)(2,1)S(1)}, bf16[144,1664]{1,0:T(8,128)(2,1)S(1)}, u32[]{:S(2)}, u32[]{:S(2)}) %collective-permute-start.7) | collective-permute-done | bytes 479264 | tf_op jit(solution)/shard_map/ppermute | solution.py:532
  38.5 3.3 %collective-permute-start.6 = (bf16[48,3072]{1,0:T(8,128)(2,1)S(1)}, bf16[48,3072]{1,0:T(8,128)(2,1)S(1)}, u32[]{:S(2)}, u32[]{:S(2)}) collective-permute-start(bf16[48,3072]{1,0:T(8,128)(2,1)S(1)} %pad_maximum_fusion.2.refs_0_), channel_id=1, source_target_pairs={{0,8},{1,9},{2,10},{3,11},{4,12},{5,13},{6,14},{7,15},{8,16},{9,17... | collective-permute-start | bytes 884744 | tf_op jit(solution)/shard_map/ppermute | solution.py:532
  43.6 4.7 %collective-permute-done.6 = bf16[48,3072]{1,0:T(8,128)(2,1)S(1)} collective-permute-done((bf16[48,3072]{1,0:T(8,128)(2,1)S(1)}, bf16[48,3072]{1,0:T(8,128)(2,1)S(1)}, u32[]{:S(2)}, u32[]{:S(2)}) %collective-permute-start.6) | collective-permute-done | bytes 294944 | tf_op jit(solution)/shard_map/ppermute | solution.py:532
  50.0 11.1 %collective-permute-done.8 = bf16[48,3072]{1,0:T(8,128)(2,1)S(1)} collective-permute-done((bf16[48,3072]{1,0:T(8,128)(2,1)S(1)}, bf16[48,3072]{1,0:T(8,128)(2,1)S(1)}, u32[]{:S(2)}, u32[]{:S(2)}) %collective-permute-start.8) | collective-permute-done | bytes 294944 | tf_op jit(solution)/shard_map/ppermute | solution.py:532
  64.7 4.0 %collective-permute-done.9 = bf16[48,3072]{1,0:T(8,128)(2,1)S(1)} collective-permute-done((bf16[48,3072]{1,0:T(8,128)(2,1)S(1)}, bf16[48,3072]{1,0:T(8,128)(2,1)S(1)}, u32[]{:S(2)}, u32[]{:S(2)}) %collective-permute-start.9) | collective-permute-done | bytes 294944 | tf_op jit(solution)/shard_map/ppermute | solution.py:532
  74.4 18.5 %attend.1 = (bf16[2,224,768]{2,1,0:T(8,128)(2,1)}, bf16[2,224,768]{2,1,0:T(8,128)(2,1)}, bf16[2,256,768]{2,1,0:T(8,128)(2,1)}, bf16[2,256,768]{2,1,0:T(8,128)(2,...) custom-call(s32[80]{0:T(128)S(1)} %concatenate.101.meta, ...), custom_call_target="tpu_custom_call" | custom-call | flops 6000000000 | bytes 60000000 | tf_op jit(solution)/shard_map/attend/pallas_call | solution.py:176
  96.5 3.5 %join.1 = (f32[2,224,768]{2,1,0:T(8,128)}, bf16[2,224,768]{2,1,0:T(8,128)(2,1)S(1)}) custom-call(bf16[2,224,768]{2,1,0:T(8,128)(2,1)S(1)} %bitcast.65, bf16[2,224,768]{2,1,0:T(8,128)(2,1)} %get-tuple-element.91.att, bf16[4,768,768]{2,1,0:T(8,128)(2,1)} %get-tuple-element.92.weights.wqkv.wproj, f32[8,768]{1,0:T(8,128)S(1)} %get-tuple-element.93.vecs), custom_call_target="tpu_custom_call" | custom-call | flops 600000000 | bytes 9000000 | tf_op jit(solution)/shard_map/join/pallas_call | solution.py:216
  100.7 11.9 %collective-permute-done.20.refs_2_ = bf16[96,3072]{1,0:T(8,128)(2,1)S(1)} collective-permute-done((bf16[96,3072]{1,0:T(8,128)(2,1)}, bf16[96,3072]{1,0:T(8,128)(2,1)S(1)}, u32[]{:S(2)}, u32[]{:S(2)}) %collective-permute-start.20) | collective-permute-done | bytes 589856 | tf_op jit(solution)/shard_map/ppermute | solution.py:532
  112.5 14.7 %hidden.2 = (bf16[384,1536]{1,0:T(8,128)(2,1)}, bf16[384,1536]{1,0:T(8,128)(2,1)}, f32[1,768]{1,0:T(1,128)S(1)}, f32[896,768]{1,0:T(8,128)}, f32[896,768]{1,0:T(8,128)}) custom-call(s32[80]{0:T(128)S(1)} %concatenate.101.meta, bf16[2,224,768]{2,1,0:T(8,128)(2,1)S(1)} %get-tuple-element.94.n2a, bf16[2,224,768]{2,1,0:T(8,128)(2,1)} %collective-permute-done.18.n2b, ...), custom_call_target="tpu_custom_call" | custom-call | flops 6341787648 | bytes 20000000 | tf_op jit(solution)/shard_map/hidden/pallas_call | solution.py:313
  129.0 16.0 %hidden.3 = (bf16[384,1536]{1,0:T(8,128)(2,1)}, bf16[384,1536]{1,0:T(8,128)(2,1)}, f32[1,768]{1,0:T(1,128)S(1)}, f32[448,768]{1,0:T(8,128)}, bf16[448,768]{1,0:T...) custom-call(s32[80]{0:T(128)S(1)} %concatenate.101.meta, bf16[2,224,768]{2,1,0:T(8,128)(2,1)} %copy-done.3, ...), custom_call_target="tpu_custom_call" | custom-call | flops 6341787648 | bytes 20000000 | tf_op jit(solution)/shard_map/hidden/pallas_call | solution.py:313
  149.2 5.5 %middle.1 = (bf16[2,224,768]{2,1,0:T(8,128)(2,1)S(1)}, f32[2,224,768]{2,1,0:T(8,128)}, bf16[2,224,768]{2,1,0:T(8,128)(2,1)S(1)}, f32[8,768]{1,0:T(8,128)S(1)}) custom-call(s32[80]{0:T(128)S(1)} %concatenate.101.meta, f32[448,768]{1,0:T(8,128)} %get-tuple-element.98.out_own, bf16[448,768]{1,0:T(8,128)(2,1)} %copy-done.14, ...), custom_call_target="tpu_custom_call" | custom-call | flops 20000000 | bytes 9000000 | tf_op jit(solution)/shard_map/middle/pallas_call | solution.py:364
  156.6 20.2 %attend_back.2 = (bf16[768,1024]{1,0:T(8,128)(2,1)}, bf16[768,1024]{1,0:T(8,128)(2,1)}, f32[2,512]{1,0:T(2,128)S(1)}, f32[128,128]{1,0:T(8,128)S(1)}, f32[2,224,768]{2,1,0:T(8,128)}) custom-call(s32[80]{0:T(128)S(1)} %concatenate.101.meta, bf16[2,224,768]{2,1,0:T(8,128)(2,1)S(1)} %copy-done.1, bf16[2,256,768]{2,1,0:T(8,128)(2,1)} %get-tuple-element.105.k, ...), custom_call_target="tpu_custom_call" | custom-call | flops 8000000000 | bytes 40000000 | tf_op jit(solution)/shard_map/attend_back/pallas_call | solution.py:490
  183.6 4.3 %collective-permute-start.43 = (bf16[48,1536]{1,0:T(8,128)(2,1)}, bf16[48,1536]{1,0:T(8,128)(2,1)}, u32[]{:S(2)}, u32[]{:S(2)}) collective-permute-start(bf16[48,1536]{1,0:T(8,128)(2,1)} %get-tuple-element.169), channel_id=1, source_target_pairs={{0,24},{1,25},{2,26},{3,27},{4,28},{5,29},{6,30},{7,31},{8,0},{9,1... | collective-permute-start | bytes 442376 | tf_op jit(solution)/shard_map/ppermute | solution.py:532
  187.9 5.3 %collective-permute-done.28 = bf16[384,1536]{1,0:T(8,128)(2,1)S(1)} collective-permute-done((bf16[384,1536]{1,0:T(8,128)(2,1)S(1)}, bf16[384,1536]{1,0:T(8,128)(2,1)S(1)}, u32[]{:S(2)}, u32[]{:S(2)}) %collective-permute-start.28) | collective-permute-done | bytes 1179680 | tf_op jit(solution)/shard_map/ppermute | solution.py:532
  196.8 13.4 %attend_back.3 = (bf16[768,512]{1,0:T(8,128)(2,1)}, bf16[768,512]{1,0:T(8,128)(2,1)}, f32[2,256]{1,0:T(2,128)S(1)}, f32[128,128]{1,0:T(8,128)S(1)}, f32[2,224,768]{2,1,0:T(8,128)}, /*index=5*/f32[2,768]{1,0:T(2,128)S(1)}) custom-call(s32[80]{0:T(128)S(1)} %concatenate.101.meta, bf16[2,224,768]{2,1,0:T(8,128)(2,1)S(1)} %copy-done.1, ...), custom_call_target="tpu_custom_call" | custom-call | flops 4000000000 | bytes 20000000 | tf_op jit(solution)/shard_map/attend_back/pallas_call | solution.py:490
  215.6 7.8 %collective-permute-done.32 = bf16[384,1024]{1,0:T(8,128)(2,1)} collective-permute-done((bf16[384,1024]{1,0:T(8,128)(2,1)}, bf16[384,1024]{1,0:T(8,128)(2,1)}, u32[]{:S(2)}, u32[]{:S(2)}) %collective-permute-start.32) | collective-permute-done | bytes 786464 | tf_op jit(solution)/shard_map/ppermute | solution.py:532
  223.4 4.3 %collective-permute-start.46 = (bf16[48,1536]{1,0:T(8,128)(2,1)S(1)}, bf16[48,1536]{1,0:T(8,128)(2,1)S(1)}, u32[]{:S(2)}, u32[]{:S(2)}) collective-permute-start(bf16[48,1536]{1,0:T(8,128)(2,1)S(1)} %get-tuple-element.166), channel_id=1, source_target_pairs={{0,24},{1,25},{2,26},{3,27},{4,28},{5,29},{6,30},{7,31},{8,0},{9,1... | collective-permute-start | bytes 442376 | tf_op jit(solution)/shard_map/ppermute | solution.py:532
  232.6 4.1 %collective-permute-done.35 = bf16[192,1024]{1,0:T(8,128)(2,1)S(1)} collective-permute-done((bf16[192,1024]{1,0:T(8,128)(2,1)S(1)}, bf16[192,1024]{1,0:T(8,128)(2,1)S(1)}, u32[]{:S(2)}, u32[]{:S(2)}) %collective-permute-start.35) | collective-permute-done | bytes 393248 | tf_op jit(solution)/shard_map/ppermute | solution.py:532
  239.2 5.4 %collective-permute-done.37 = bf16[384,512]{1,0:T(8,128)(2,1)S(1)} collective-permute-done((bf16[384,512]{1,0:T(8,128)(2,1)S(1)}, bf16[384,512]{1,0:T(8,128)(2,1)S(1)}, u32[]{:S(2)}, u32[]{:S(2)}) %collective-permute-start.37) | collective-permute-done | bytes 393248 | tf_op jit(solution)/shard_map/ppermute | solution.py:532
  245.2 4.7 %collective-permute-start.42 = (bf16[192,512]{1,0:T(8,128)(2,1)S(1)}, bf16[192,512]{1,0:T(8,128)(2,1)S(1)}, u32[]{:S(2)}, u32[]{:S(2)}) collective-permute-start(bf16[192,512]{1,0:T(8,128)(2,1)S(1)} %add_convert_fusion.5), channel_id=1, source_target_pairs={{0,2},{1,5},{2,0},{3,7},{4,6},{5,1},{6,4},{7,3},{8,10},{9,13},{10,... | collective-permute-start | bytes 589832 | tf_op jit(solution)/shard_map/ppermute | solution.py:532
  266.3 3.6 %collective-permute-start.51 = (bf16[48,512]{1,0:T(8,128)(2,1)S(1)}, bf16[48,512]{1,0:T(8,128)(2,1)S(1)}, u32[]{:S(2)}, u32[]{:S(2)}) collective-permute-start(bf16[48,512]{1,0:T(8,128)(2,1)S(1)} %get-tuple-element.183), channel_id=1, source_target_pairs={{0,24},{1,25},{2,26},{3,27},{4,28},{5,29},{6,30},{7,31},{8,0},{9,1... | collective-permute-start | bytes 147464 | tf_op jit(solution)/shard_map/ppermute | solution.py:532
  271.7 3.7 %collective-permute-done.52 = bf16[48,512]{1,0:T(8,128)(2,1)S(1)} collective-permute-done((bf16[48,512]{1,0:T(8,128)(2,1)S(1)}, bf16[48,512]{1,0:T(8,128)(2,1)S(1)}, u32[]{:S(2)}, u32[]{:S(2)}) %collective-permute-start.52) | collective-permute-done | bytes 49184 | tf_op jit(solution)/shard_map/ppermute | solution.py:532
  (268 shorter events, 92.4 us)
Async XLA Ops:
  11.3 12.8 %collective-permute-start.4 = (bf16[48,1664]{1,0:T(8,128)(2,1)S(1)}, bf16[48,1664]{1,0:T(8,128)(2,1)S(1)}, u32[]{:S(2)}, u32[]{:S(2)}) collective-permute-start(bf16[48,1664]{1,0:T(8,128)(2,1)S(1)} %pad_maximum_fusion.4.refs_0_), channel_id=1, source_target_pairs={{0,16},{1,17},{2,18},{3,19},{4,20},{5,21},{6,22},{7,23},{8,24},{9,... | collective-permute-start | bytes 479240 | tf_op jit(solution)/shard_map/ppermute | solution.py:532
  35.1 28.3 %collective-permute-start.11 = (bf16[288,1664]{1,0:T(8,128)(2,1)}, bf16[288,1664]{1,0:T(8,128)(2,1)}, u32[]{:S(2)}, u32[]{:S(2)}) collective-permute-start(bf16[288,1664]{1,0:T(8,128)(2,1)} %constant_dynamic-update-slice_fusion.3), channel_id=1, source_target_pairs={{0,4},{1,3},{2,6},{3,1},{4,0},{5,7},{6,2},{7,5},{8,12},{9,11},{10,... | collective-permute-start | bytes 2875400 | tf_op jit(solution)/shard_map/ppermute | solution.py:532
  41.8 22.3 %collective-permute-start.12 = (bf16[48,1664]{1,0:T(8,128)(2,1)S(1)}, bf16[48,1664]{1,0:T(8,128)(2,1)S(1)}, u32[]{:S(2)}, u32[]{:S(2)}) collective-permute-start(bf16[48,1664]{1,0:T(8,128)(2,1)S(1)} %pad_maximum_fusion.4.refs_0_), channel_id=1, source_target_pairs={{0,1},{1,0},{2,3},{3,2},{4,5},{5,4},{6,7},{7,6},{8,9},{9,8},{10,11... | collective-permute-start | bytes 479240 | tf_op jit(solution)/shard_map/ppermute | solution.py:544
  41.9 27.6 %collective-permute-start.10 = (bf16[96,1664]{1,0:T(8,128)(2,1)S(1)}, bf16[96,1664]{1,0:T(8,128)(2,1)S(1)}, u32[]{:S(2)}, u32[]{:S(2)}) collective-permute-start(bf16[96,1664]{1,0:T(8,128)(2,1)S(1)} %copy-done.23), channel_id=1, source_target_pairs={{0,4},{1,3},{2,6},{3,1},{4,0},{5,7},{6,2},{7,5},{8,12},{9,11},{10,... | collective-permute-start | bytes 958472 | tf_op jit(solution)/shard_map/ppermute | solution.py:532
  42.4 27.5 %collective-permute-start.13 = (bf16[48,1664]{1,0:T(8,128)(2,1)S(1)}, bf16[48,1664]{1,0:T(8,128)(2,1)S(1)}, u32[]{:S(2)}, u32[]{:S(2)}) collective-permute-start(bf16[48,1664]{1,0:T(8,128)(2,1)S(1)} %collective-permute-done.3.refs_1_), channel_id=1, source_target_pairs={{0,1},{1,0},{2,3},{3,2},{4,5},{5,4},{6,7},{7,6},{8,9},{9,8},{10,11... | collective-permute-start | bytes 479240 | tf_op jit(solution)/shard_map/ppermute | solution.py:544
  48.2 12.9 %collective-permute-start.8 = (bf16[48,3072]{1,0:T(8,128)(2,1)S(1)}, bf16[48,3072]{1,0:T(8,128)(2,1)S(1)}, u32[]{:S(2)}, u32[]{:S(2)}) collective-permute-start(bf16[48,3072]{1,0:T(8,128)(2,1)S(1)} %pad_maximum_fusion.2.refs_0_), channel_id=1, source_target_pairs={{0,16},{1,17},{2,18},{3,19},{4,20},{5,21},{6,22},{7,23},{8,24},{9,... | collective-permute-start | bytes 884744 | tf_op jit(solution)/shard_map/ppermute | solution.py:532
  70.0 22.9 %collective-permute-start.21 = (bf16[144,3072]{1,0:T(8,128)(2,1)}, bf16[144,3072]{1,0:T(8,128)(2,1)}, u32[]{:S(2)}, u32[]{:S(2)}) collective-permute-start(bf16[144,3072]{1,0:T(8,128)(2,1)} %constant_dynamic-update-slice_fusion.7.refs_3_), channel_id=1, source_target_pairs={{0,2},{1,5},{2,0},{3,7},{4,6},{5,1},{6,4},{7,3},{8,10},{9,13},{10,... | collective-permute-start | bytes 2654216 | tf_op jit(solution)/shard_map/ppermute | solution.py:532
  71.3 41.3 %collective-permute-start.22 = (bf16[144,3072]{1,0:T(8,128)(2,1)}, bf16[144,3072]{1,0:T(8,128)(2,1)}, u32[]{:S(2)}, u32[]{:S(2)}) collective-permute-start(bf16[144,3072]{1,0:T(8,128)(2,1)} %constant_dynamic-update-slice_fusion.7.refs_3_), channel_id=1, source_target_pairs={{0,4},{1,3},{2,6},{3,1},{4,0},{5,7},{6,2},{7,5},{8,12},{9,11},{10,... | collective-permute-start | bytes 2654216 | tf_op jit(solution)/shard_map/ppermute | solution.py:532
  92.9 19.6 %collective-permute-start.23 = (bf16[144,3072]{1,0:T(8,128)(2,1)}, bf16[144,3072]{1,0:T(8,128)(2,1)}, u32[]{:S(2)}, u32[]{:S(2)}) collective-permute-start(bf16[144,3072]{1,0:T(8,128)(2,1)} %collective-permute-done.21.refs_4_), channel_id=1, source_target_pairs={{0,4},{1,3},{2,6},{3,1},{4,0},{5,7},{6,2},{7,5},{8,12},{9,11},{10,... | collective-permute-start | bytes 2654216 | tf_op jit(solution)/shard_map/ppermute | solution.py:532
  100.0 12.6 %collective-permute-start.18 = (bf16[2,224,768]{2,1,0:T(8,128)(2,1)S(1)}, bf16[2,224,768]{2,1,0:T(8,128)(2,1)}, u32[]{:S(2)}, u32[]{:S(2)}) collective-permute-start(bf16[2,224,768]{2,1,0:T(8,128)(2,1)S(1)} %get-tuple-element.94.n2a), channel_id=1, source_target_pairs={{0,1},{1,0},{2,3},{3,2},{4,5},{5,4},{6,7},{7,6},{8,9},{9,8},{10,11... | collective-permute-start | bytes 2064392 | tf_op jit(solution)/shard_map/ppermute | solution.py:544
  100.0 12.6 %collective-permute-start.20 = (bf16[96,3072]{1,0:T(8,128)(2,1)}, bf16[96,3072]{1,0:T(8,128)(2,1)S(1)}, u32[]{:S(2)}, u32[]{:S(2)}) collective-permute-start(bf16[96,3072]{1,0:T(8,128)(2,1)} %pad_maximum_fusion), channel_id=1, source_target_pairs={{0,4},{1,3},{2,6},{3,1},{4,0},{5,7},{6,2},{7,5},{8,12},{9,11},{10,... | collective-permute-start | bytes 1769480 | tf_op jit(solution)/shard_map/ppermute | solution.py:532
  127.2 27.5 %collective-permute-start.27 = (bf16[384,1536]{1,0:T(8,128)(2,1)}, bf16[384,1536]{1,0:T(8,128)(2,1)}, u32[]{:S(2)}, u32[]{:S(2)}) collective-permute-start(bf16[384,1536]{1,0:T(8,128)(2,1)} %get-tuple-element.116), channel_id=1, source_target_pairs={{0,4},{1,3},{2,6},{3,1},{4,0},{5,7},{6,2},{7,5},{8,12},{9,11},{10,... | collective-permute-start | bytes 3538952 | tf_op jit(solution)/shard_map/ppermute | solution.py:532
  156.1 24.3 %collective-permute-start.29 = (bf16[192,1536]{1,0:T(8,128)(2,1)S(1)}, bf16[192,1536]{1,0:T(8,128)(2,1)S(1)}, u32[]{:S(2)}, u32[]{:S(2)}) collective-permute-start(bf16[192,1536]{1,0:T(8,128)(2,1)S(1)} %add_convert_fusion.3), channel_id=1, source_target_pairs={{0,2},{1,5},{2,0},{3,7},{4,6},{5,1},{6,4},{7,3},{8,10},{9,13},{10,... | collective-permute-start | bytes 1769480 | tf_op jit(solution)/shard_map/ppermute | solution.py:532
  176.8 19.2 %collective-permute-start.26 = (bf16[768,1024]{1,0:T(8,128)(2,1)}, bf16[768,1024]{1,0:T(8,128)(2,1)S(1)}, u32[]{:S(2)}, u32[]{:S(2)}) collective-permute-start(bf16[768,1024]{1,0:T(8,128)(2,1)} %get-tuple-element.112), channel_id=1, source_target_pairs={{0,1},{1,0},{2,3},{3,2},{4,5},{5,4},{6,7},{7,6},{8,9},{9,8},{10,11... | collective-permute-start | bytes 4718600 | tf_op jit(solution)/shard_map/ppermute | solution.py:544
  176.9 16.3 %collective-permute-start.28 = (bf16[384,1536]{1,0:T(8,128)(2,1)S(1)}, bf16[384,1536]{1,0:T(8,128)(2,1)S(1)}, u32[]{:S(2)}, u32[]{:S(2)}) collective-permute-start(bf16[384,1536]{1,0:T(8,128)(2,1)S(1)} %copy-done.32), channel_id=1, source_target_pairs={{0,4},{1,3},{2,6},{3,1},{4,0},{5,7},{6,2},{7,5},{8,12},{9,11},{10,... | collective-permute-start | bytes 3538952 | tf_op jit(solution)/shard_map/ppermute | solution.py:532
  183.6 69.0 %collective-permute-start.43 = (bf16[48,1536]{1,0:T(8,128)(2,1)}, bf16[48,1536]{1,0:T(8,128)(2,1)}, u32[]{:S(2)}, u32[]{:S(2)}) collective-permute-start(bf16[48,1536]{1,0:T(8,128)(2,1)} %get-tuple-element.169), channel_id=1, source_target_pairs={{0,24},{1,25},{2,26},{3,27},{4,28},{5,29},{6,30},{7,31},{8,0},{9,1... | collective-permute-start | bytes 442376 | tf_op jit(solution)/shard_map/ppermute | solution.py:532
  187.9 64.8 %collective-permute-start.44 = (bf16[48,1536]{1,0:T(8,128)(2,1)}, bf16[48,1536]{1,0:T(8,128)(2,1)}, u32[]{:S(2)}, u32[]{:S(2)}) collective-permute-start(bf16[48,1536]{1,0:T(8,128)(2,1)} %get-tuple-element.167), channel_id=1, source_target_pairs={{0,16},{1,17},{2,18},{3,19},{4,20},{5,21},{6,22},{7,23},{8,24},{9,... | collective-permute-start | bytes 442376 | tf_op jit(solution)/shard_map/ppermute | solution.py:532
  194.3 19.4 %collective-permute-start.33 = (bf16[192,1536]{1,0:T(8,128)(2,1)}, bf16[192,1536]{1,0:T(8,128)(2,1)}, u32[]{:S(2)}, u32[]{:S(2)}) collective-permute-start(bf16[192,1536]{1,0:T(8,128)(2,1)} %add_convert_fusion.2), channel_id=1, source_target_pairs={{0,2},{1,5},{2,0},{3,7},{4,6},{5,1},{6,4},{7,3},{8,10},{9,13},{10,... | collective-permute-start | bytes 1769480 | tf_op jit(solution)/shard_map/ppermute | solution.py:532
  211.1 12.3 %collective-permute-start.32 = (bf16[384,1024]{1,0:T(8,128)(2,1)}, bf16[384,1024]{1,0:T(8,128)(2,1)}, u32[]{:S(2)}, u32[]{:S(2)}) collective-permute-start(bf16[384,1024]{1,0:T(8,128)(2,1)} %slice.314), channel_id=1, source_target_pairs={{0,4},{1,3},{2,6},{3,1},{4,0},{5,7},{6,2},{7,5},{8,12},{9,11},{10,... | collective-permute-start | bytes 2359304 | tf_op jit(solution)/shard_map/ppermute | solution.py:532
  211.4 17.4 %collective-permute-start.31 = (bf16[768,512]{1,0:T(8,128)(2,1)}, bf16[768,512]{1,0:T(8,128)(2,1)}, u32[]{:S(2)}, u32[]{:S(2)}) collective-permute-start(bf16[768,512]{1,0:T(8,128)(2,1)} %get-tuple-element.134), channel_id=1, source_target_pairs={{0,1},{1,0},{2,3},{3,2},{4,5},{5,4},{6,7},{7,6},{8,9},{9,8},{10,11... | collective-permute-start | bytes 2359304 | tf_op jit(solution)/shard_map/ppermute | solution.py:544
  213.7 16.8 %collective-permute-start.30 = (f32[104,128]{1,0:T(8,128)S(1)}, f32[104,128]{1,0:T(8,128)S(1)}, u32[]{:S(2)}, u32[]{:S(2)}) collective-permute-start(f32[104,128]{1,0:T(8,128)S(1)} %pad_maximum_fusion.10), channel_id=1, source_target_pairs={{0,1},{1,0},{2,3},{3,2},{4,5},{5,4},{6,7},{7,6},{8,9},{9,8},{10,11... | collective-permute-start | bytes 159752 | tf_op jit(solution)/shard_map/ppermute | solution.py:544
  223.4 21.2 %collective-permute-start.46 = (bf16[48,1536]{1,0:T(8,128)(2,1)S(1)}, bf16[48,1536]{1,0:T(8,128)(2,1)S(1)}, u32[]{:S(2)}, u32[]{:S(2)}) collective-permute-start(bf16[48,1536]{1,0:T(8,128)(2,1)S(1)} %get-tuple-element.166), channel_id=1, source_target_pairs={{0,24},{1,25},{2,26},{3,27},{4,28},{5,29},{6,30},{7,31},{8,0},{9,1... | collective-permute-start | bytes 442376 | tf_op jit(solution)/shard_map/ppermute | solution.py:532
  245.2 21.0 %collective-permute-start.42 = (bf16[192,512]{1,0:T(8,128)(2,1)S(1)}, bf16[192,512]{1,0:T(8,128)(2,1)S(1)}, u32[]{:S(2)}, u32[]{:S(2)}) collective-permute-start(bf16[192,512]{1,0:T(8,128)(2,1)S(1)} %add_convert_fusion.5), channel_id=1, source_target_pairs={{0,2},{1,5},{2,0},{3,7},{4,6},{5,1},{6,4},{7,3},{8,10},{9,13},{10,... | collective-permute-start | bytes 589832 | tf_op jit(solution)/shard_map/ppermute | solution.py:532
  252.6 17.3 %collective-permute-start.41 = (bf16[48,1024]{1,0:T(8,128)(2,1)S(1)}, bf16[48,1024]{1,0:T(8,128)(2,1)S(1)}, u32[]{:S(2)}, u32[]{:S(2)}) collective-permute-start(bf16[48,1024]{1,0:T(8,128)(2,1)S(1)} %get-tuple-element.174), channel_id=1, source_target_pairs={{0,24},{1,25},{2,26},{3,27},{4,28},{5,29},{6,30},{7,31},{8,0},{9,1... | collective-permute-start | bytes 294920 | tf_op jit(solution)/shard_map/ppermute | solution.py:532
  (67 other events, 486.7 us)

commit v3 on v2

v3 whole, which is shorter than its diff:
```python
from functools import partial

import jax
import jax.numpy as jnp
import numpy as np
from jax import lax
from jax.experimental import pallas as pl
from jax.experimental.pallas import tpu as pltpu
from jax.sharding import PartitionSpec as P

HEADS = 12
HDIM = 64
LANES = 128
PAIRS = HEADS // 2
WIN = 14
SIDE = 16
TOK = WIN * SIDE
KEYS = 256
PIECES = 16
EPSILON = 1e-06
MASKED_SCORE = -1e30
MASK_LANE = 60
CHUNK = 512
BACK_PARTS = ((0, 2), (2, 2), (4, 2))
F32 = jnp.float32
BF16 = jnp.bfloat16
SMEM = pl.BlockSpec(memory_space=pltpu.SMEM)
HBM = pl.BlockSpec(memory_space=pl.ANY)
WHOLE = pl.BlockSpec(memory_space=pltpu.VMEM)
VMEM_BYTES = 52 * 2**20


def params():
    return pltpu.CompilerParams(vmem_limit_bytes=VMEM_BYTES)


def shape(dims, dtype):
    return jax.ShapeDtypeStruct(dims, dtype)


def dot(a, b):
    return jnp.dot(a, b, preferred_element_type=F32)


def dot_nt(a, b):
    return lax.dot_general(a, b, (((1,), (1,)), ((), ())), preferred_element_type=F32)


def dot_tn(a, b):
    return lax.dot_general(a, b, (((0,), (0,)), ((), ())), preferred_element_type=F32)


def lanes(rows):
    return lax.broadcasted_iota(jnp.int32, (rows, LANES), 1)


def moments(values):
    centered = values - jnp.mean(values, axis=-1, keepdims=True)
    inverse = lax.rsqrt(jnp.mean(centered * centered, axis=-1, keepdims=True) + EPSILON)
    return centered * inverse, inverse


def norm_back(grad, xhat, inverse, gain):
    scaled = grad * gain
    first = jnp.mean(scaled, axis=-1, keepdims=True)
    second = jnp.mean(scaled * xhat, axis=-1, keepdims=True)
    return inverse * (scaled - first - xhat * second)


def begin(source, dest, sem):
    copy = pltpu.make_async_copy(source, dest, sem)
    copy.start()
    return copy


def finish(copies):
    for copy in copies:
        copy.wait()


def pieces_in(meta, at, ins, start, dest, sems, first):
    rows, cols = dest.shape[0] // PIECES, dest.shape[1]
    copies = []
    for ref, base in ins:
        for part in range(ref.shape[0] // rows):
            place = pl.multiple_of(meta[at + len(copies)] * rows, rows)
            source = ref.at[pl.ds(part * rows, rows), pl.ds(base + start, cols)]
            copies.append(begin(source, dest.at[pl.ds(place, rows), :], sems.at[first + len(copies)]))
    return copies


def row_valid(meta, core, window, rows, width):
    place = lax.broadcasted_iota(jnp.int32, (rows, width), 0)
    row, col = place // SIDE, place % SIDE
    inside = (row < WIN) & (col < WIN)
    return inside & (core * WIN + row < meta[65 + window]) & (col < meta[67 + window])


def relative(turned):
    out = []
    for row in range(WIN):
        slab = turned[row * SIDE : (row + 1) * SIDE]
        down = pltpu.roll(slab, row, 1) if row else slab
        across = pltpu.roll(slab, 0, 1, stride=1, stride_axis=0)
        out.append(jnp.where(lanes(SIDE) % 64 < 32, down, across))
    return jnp.concatenate(out, axis=0)


def attend_kernel(count, total, meta, tok, table, spread, *refs):
    own, other = refs[:count], refs[count:total]
    vecs, n1, q, k, v, p, att, w_out = refs[total : total + 8]
    toks, weights, small, aug, n1s, qs, ks, vs, ps, atts, sems, out_sems = refs[total + 8 :]
    width = weights.shape[1]
    core = meta[64]
    tok_copy = begin(tok, toks, sems.at[5 * PIECES])
    own, other = ([(ref, 0) for ref in found] for found in (own, other))
    copies = pieces_in(meta, 0, own, width, small, sems, 0)
    for found, at, half in ((own, 0, core), (other, 16, 1 - core)):
        for start, mat in ((0, 2 * half), (width + LANES, 2 * half + 1)):
            copies += pieces_in(meta, at, found, start, weights.at[mat], sems, len(copies))
    for window in range(2):
        valid = row_valid(meta, core, window, KEYS, LANES)
        aug[window] = jnp.where(
            (lanes(KEYS) == MASK_LANE) & ~valid, MASKED_SCORE, spread[...].astype(F32)
        ).astype(BF16)
        ks[window, TOK:] = jnp.zeros((KEYS - TOK, width), BF16)
        vs[window, TOK:] = jnp.zeros((KEYS - TOK, width), BF16)
    tok_copy.wait()
    xhat, _ = moments(toks[...].reshape(2 * TOK, width).astype(F32))
    finish(copies)
    outs = [begin(weights, w_out, out_sems.at[0])]
    vecs[...] = small[...].astype(F32).T[:8]
    normed = (xhat * vecs[0:1] + vecs[1:2]).astype(BF16)
    n1s[...] = normed.reshape(2, TOK, width)
    outs.append(begin(n1s, n1, out_sems.at[1]))
    for mat, (made_in, dest) in enumerate(((qs, q), (ks, k), (vs, v))):
        for start in range(0, width, 256):
            cols = pl.ds(start, 256)
            made = dot(normed, weights[mat, :, cols])
            if mat != 1:
                made = made + vecs[2 + mat // 2 : 3 + mat // 2, cols]
            made = made.astype(BF16)
            made_in[0, :TOK, cols] = made[:TOK]
            made_in[1, :TOK, cols] = made[TOK:]
        outs.append(begin(made_in, dest, out_sems.at[2 + mat]))

    place = lanes(TOK)
    for step in range(2 * PAIRS):
        window, pair = step // PAIRS, step % PAIRS
        cols = pl.ds(pair * LANES, LANES)
        q2, k2, v2 = qs[window, :, cols], ks[window, :, cols], vs[window, :, cols]
        turned = dot(q2, table[...])
        keys_aug = jnp.concatenate([k2, aug[window]], axis=1)
        parts = []
        for half in range(2):
            rel = relative(turned[:, half * LANES : (half + 1) * LANES])
            high = rel.astype(BF16).astype(F32)
            rel = jnp.where(place < 64, high, rel - high)
            rel = jnp.where(place == MASK_LANE, 1.0, rel).astype(BF16)
            mine = jnp.where(place // 64 == half, q2.astype(F32) * HDIM**-0.5, 0.0).astype(BF16)
            scores = dot_nt(jnp.concatenate([mine, rel], axis=1), keys_aug)
            terms = jnp.exp(scores - jnp.max(scores, axis=-1, keepdims=True))
            soft = terms * (1.0 / jnp.sum(terms, axis=-1, keepdims=True))
            soft = soft.astype(BF16)
            ps[window, 2 * pair + half] = soft
            parts.append(dot(soft, v2))
        atts[window, :, cols] = jnp.where(place < 64, parts[0], parts[1]).astype(BF16)
        heads = pl.ds(2 * pair, 2)
        outs.append(begin(ps.at[window, heads], p.at[window, heads], out_sems.at[len(outs)]))
    outs.append(begin(atts, att, out_sems.at[len(outs)]))
    finish(outs)


def attend(meta, tok, table, spread, own, other):
    count, total, width = len(own), len(own) + len(other), tok.shape[-1]
    rows, keys, heads = (2, TOK, width), (2, KEYS, width), (2, HEADS, TOK, KEYS)
    mats = (4, width, width)
    outs = (rows, rows, keys, keys, heads, rows, mats)
    return pl.pallas_call(
        partial(attend_kernel, count, total),
        out_shape=[shape((8, width), F32)] + [shape(dims, BF16) for dims in outs],
        in_specs=[SMEM, HBM, WHOLE, WHOLE] + [HBM] * total,
        out_specs=[WHOLE] + [HBM] * len(outs),
        scratch_shapes=[
            pltpu.VMEM(dims, BF16)
            for dims in (rows, mats, (width, LANES), (2, KEYS, LANES), rows, rows, keys, keys, heads, rows)
        ]
        + [
            pltpu.SemaphoreType.DMA((5 * PIECES + 1,)),
            pltpu.SemaphoreType.DMA((6 + 2 * PAIRS,)),
        ],
        compiler_params=params(),
        cost_estimate=pl.CostEstimate(
            flops=20_000_000_000, bytes_accessed=40_000_000, transcendentals=1_500_000
        ),
        name="attend",
    )(meta, tok, table, spread, *own, *other)


def join_kernel(tok, att, weights, vecs, x1, n2):
    for window in range(2):
        resid = tok[window].astype(F32) + (dot(att[window], weights[0]) + vecs[4:5])
        x1[window] = resid
        xhat, _ = moments(resid)
        n2[window] = (xhat * vecs[5:6] + vecs[6:7]).astype(BF16)


def join(tok, att, weights, vecs):
    width = tok.shape[-1]
    return pl.pallas_call(
        join_kernel,
        out_shape=[shape(tok.shape, F32), shape(tok.shape, BF16)],
        grid=(1,),
        in_specs=[
            WHOLE,
            WHOLE,
            pl.BlockSpec((1, width, width), lambda i: (3, 0, 0)),
            WHOLE,
        ],
        out_specs=[WHOLE] * 2,
        compiler_params=params(),
        cost_estimate=pl.CostEstimate(
            flops=600_000_000, bytes_accessed=9_000_000, transcendentals=0
        ),
        name="join",
    )(tok, att, weights, vecs)


def pieces_out(meta, made, cols, keep, send, sems, first):
    rows = made.shape[0] // PIECES
    copies = []
    for piece in range(PIECES):
        dest = keep if piece < PIECES // 2 else send
        place = pl.multiple_of(meta[32 + piece] * rows, rows)
        at = pl.ds(piece % (PIECES // 2) * rows, rows)
        source = made.at[pl.ds(place, rows), cols]
        copies.append(begin(source, dest.at[at, cols], sems.at[first + len(copies)]))
    return copies


def hidden_fwd_kernel(bases, meta, n2a, n2b, dm_turned, bias, *refs):
    count = len(bases)
    ins, (keep, send) = list(zip(refs[:count], bases)), refs[count : count + 2]
    w0, n2s, dms, grad, sems, out_sems = refs[count + 2 :]
    width, hidden = w0.shape
    starts = range(0, hidden, CHUNK)
    at = PIECES * len(starts)
    n2_copies = [
        begin(n2a, n2s.at[: 2 * TOK], sems.at[at]),
        begin(n2b, n2s.at[2 * TOK :], sems.at[at + 1]),
    ]
    copies = [
        pieces_in(meta, 0, ins, start, w0.at[:, pl.ds(start, CHUNK)], sems, PIECES * step)
        for step, start in enumerate(starts)
    ]
    dm_copy = begin(dm_turned, dms, sems.at[at + 2])
    finish(n2_copies)
    outs = []
    for step, start in enumerate(starts):
        cols = pl.ds(start, CHUNK)
        finish(copies[step])
        inner = dot(n2s[...], w0[:, cols]) + bias[:, cols]
        act = (inner * (0.5 + 0.5 * lax.erf(inner * 0.7071067811865476))).astype(BF16)
        if step == 0:
            dm_copy.wait()
        grad[:, cols] = dot(dms[...], act).astype(BF16)
        outs += pieces_out(meta, grad, cols, keep, send, out_sems, len(outs))
    finish(outs)


def hidden_fwd(meta, n2a, n2b, dm_turned, bias, ins):
    refs, bases = zip(*ins)
    width, hidden = n2a.shape[-1], bias.shape[-1]
    steps = hidden // CHUNK
    return pl.pallas_call(
        partial(hidden_fwd_kernel, bases),
        out_shape=[shape((width // 2, hidden), BF16)] * 2,
        in_specs=[SMEM] + [HBM] * 3 + [WHOLE] + [HBM] * len(refs),
        out_specs=[HBM] * 2,
        scratch_shapes=[
            pltpu.VMEM((width, hidden), BF16),
            pltpu.VMEM((4 * TOK, width), BF16),
            pltpu.VMEM((width, 4 * TOK), BF16),
            pltpu.VMEM((width, hidden), BF16),
            pltpu.SemaphoreType.DMA((PIECES * steps + 3,)),
            pltpu.SemaphoreType.DMA((PIECES * steps,)),
        ],
        compiler_params=params(),
        cost_estimate=pl.CostEstimate(
            flops=12 * 4 * TOK * width * hidden,
            bytes_accessed=12_000_000,
            transcendentals=4 * TOK * hidden,
        ),
        name="hidden_fwd",
    )(meta, n2a, n2b, dm_turned, bias, *refs)


def hidden_back_kernel(bases0, bases1, meta, n2a, n2b, dma, dmb, bias, *refs):
    count = len(bases0)
    ins0, ins1 = list(zip(refs[:count], bases0)), list(zip(refs[count : 2 * count], bases1))
    refs = refs[2 * count :]
    bias_grad, keep, send, back_own, back_far, out_own, out_far = refs[:7]
    w0, w1, n2s, n2t, dms, acts, backs, grad, big, small, sems, out_sems = refs[7:]
    width, hidden = w0.shape
    starts = range(0, hidden, CHUNK)
    halves = (pl.ds(0, 2 * TOK), pl.ds(2 * TOK, 2 * TOK))
    at = 2 * PIECES * len(starts)
    n2_copies = [
        begin(ref, n2s.at[half], sems.at[at + i]) for i, (ref, half) in enumerate(zip((n2a, n2b), halves))
    ]
    copies = []
    for step, start in enumerate(starts):
        cols = pl.ds(start, CHUNK)
        copies.append(pieces_in(meta, 0, ins0, start, w0.at[:, cols], sems, 2 * PIECES * step))
        if step == 0:
            dm_copies = [
                begin(ref, dms.at[half], sems.at[at + 2 + i])
                for i, (ref, half) in enumerate(zip((dma, dmb), halves))
            ]
        copies.append(pieces_in(meta, 0, ins1, start, w1.at[:, cols], sems, 2 * PIECES * step + PIECES))
    finish(n2_copies)
    n2t[...] = n2s[...].T
    outs = []
    for step, start in enumerate(starts):
        cols = pl.ds(start, CHUNK)
        finish(copies[2 * step])
        inner = dot(n2s[...], w0[:, cols]) + bias[:, cols]
        if step == 0:
            finish(dm_copies)
        finish(copies[2 * step + 1])
        back = dot(dms[...], w1[:, cols])
        cdf = 0.5 + 0.5 * lax.erf(inner * 0.7071067811865476)
        density = jnp.exp(inner * inner * -0.5) * 0.3989422804014327
        acts[:, cols] = (inner * cdf).astype(BF16)
        back_pre = (back * (cdf + inner * density)).astype(BF16)
        backs[:, cols] = back_pre
        bias_grad[:, cols] = jnp.sum(back_pre.astype(F32), axis=0, keepdims=True)
        grad[:, cols] = dot(n2t[...], back_pre).astype(BF16)
        outs += pieces_out(meta, grad, cols, keep, send, out_sems, len(outs))
    for which, (left, right, own, far) in enumerate(
        ((backs, w0, back_own, back_far), (acts, w1, out_own, out_far))
    ):
        small[which] = dot_nt(left[halves[1]], right[...]).astype(BF16)
        outs.append(begin(small.at[which], far, out_sems.at[len(outs)]))
        big[which] = dot_nt(left[halves[0]], right[...])
        outs.append(begin(big.at[which], own, out_sems.at[len(outs)]))
    finish(outs)


def hidden_back(meta, n2a, n2b, dma, dmb, bias, ins0, ins1):
    (refs0, bases0), (refs1, bases1) = zip(*ins0), zip(*ins1)
    width, hidden = n2a.shape[-1], bias.shape[-1]
    steps = hidden // CHUNK
    one = (2 * TOK, width)
    tall = pltpu.VMEM((4 * TOK, width), BF16)
    wide = pltpu.VMEM((width, hidden), BF16)
    return pl.pallas_call(
        partial(hidden_back_kernel, bases0, bases1),
        out_shape=[shape((1, hidden), F32)]
        + [shape((width // 2, hidden), BF16)] * 2
        + [shape(one, F32), shape(one, BF16)] * 2,
        in_specs=[SMEM] + [HBM] * 4 + [WHOLE] + [HBM] * (2 * len(refs0)),
        out_specs=[WHOLE] + [HBM] * 6,
        scratch_shapes=[
            wide,
            wide,
            tall,
            pltpu.VMEM((width, 4 * TOK), BF16),
            tall,
            pltpu.VMEM((4 * TOK, hidden), BF16),
            pltpu.VMEM((4 * TOK, hidden), BF16),
            wide,
            pltpu.VMEM((2,) + one, F32),
            pltpu.VMEM((2,) + one, BF16),
            pltpu.SemaphoreType.DMA((2 * PIECES * steps + 4,)),
            pltpu.SemaphoreType.DMA((PIECES * steps + 4,)),
        ],
        compiler_params=params(),
        cost_estimate=pl.CostEstimate(
            flops=24 * 4 * TOK * width * hidden,
            bytes_accessed=20_000_000,
            transcendentals=8 * TOK * hidden,
        ),
        name="hidden_back",
    )(meta, n2a, n2b, dma, dmb, bias, *refs0, *refs1)


def unrelative(grads):
    out = []
    for row in range(WIN):
        slab = grads[row * SIDE : (row + 1) * SIDE]
        down = pltpu.roll(slab, row, 1) if row else slab
        across = pltpu.roll(slab, 0, 1, stride=1, stride_axis=0)
        out.append(jnp.where(lanes(SIDE) < 32, down, across))
    return jnp.concatenate(out, axis=0)


def attend_back_kernel(start, count, meta, vecs, gather, table, q, k, v, p, weights, att, n1, *refs):
    first, last = start == 0, start + count == PAIRS
    parts = start // count
    if first:
        back_own, back_far, x1, dm = refs[:4]
        norm_sums, bias_sums, table_grad, mine, theirs, dqkv_out, dx1, da = refs[4:12]
        refs = refs[12:]
        owns, fars, x1s, dms, dx1s = refs[-5:]
        refs = refs[:-5]
    else:
        da, refs = refs[0], refs[1:]
        if last:
            tok, dx1, *changes = refs[: 2 + parts]
            norm_sums, bias_sums, table_grad, mine, theirs, result = refs[2 + parts : 8 + parts]
            refs = refs[8 + parts :]
            wqkv, toks, dx1s, results, *changed = refs[-4 - parts :]
            refs = refs[: -4 - parts]
        else:
            bias_sums, table_grad, mine, theirs, dqkv_out = refs[:5]
            refs = refs[5:]
    das, wproj, atts, n1s, qs, ks, vs, ps, dat, dqkv, grads, turned_in, sems, out_sems = refs
    core = meta[64]
    width, cols_here = das.shape[-1], qs.shape[-1]
    rows = width // PIECES
    columns = pl.ds(start * LANES, cols_here)
    tokens = (2 * TOK, width)
    early = []
    if first:
        early = [(back_own, owns), (back_far, fars), (x1, x1s), (dm, dms)]
    else:
        early = [(da, das)]
    early = [begin(ref, dest, sems.at[at]) for at, (ref, dest) in enumerate(early)]
    wait_proj = begin(weights.at[3, columns, :], wproj, sems.at[4])
    wait_att = begin(att, atts, sems.at[5])
    wait_v = begin(v.at[:, :, columns], vs, sems.at[6])
    wait_p = []
    for window in range(2):
        for pair in range(count):
            heads = pl.ds(2 * (start + pair), 2)
            wait_p.append(
                begin(p.at[window, heads], ps.at[window, pl.ds(2 * pair, 2)], sems.at[10 + len(wait_p)])
            )
        if window == 0:
            wait_qk = [
                begin(ref.at[:, :, columns], dest, sems.at[7 + at])
                for at, (ref, dest) in enumerate(((q, qs), (k, ks)))
            ]
    wait_n1 = begin(n1, n1s, sems.at[9])
    if last:
        at = 10 + 2 * count
        ends = [begin(tok, toks, sems.at[at]), begin(dx1, dx1s, sems.at[at + 1])]
        ends += [begin(weights.at[mat], wqkv.at[mat], sems.at[at + 2 + mat]) for mat in range(3)]
        for part in range(parts):
            ends.append(begin(changes[part], changed[part], sems.at[at + 5 + part]))
    outs = []
    finish(early)
    if first:
        total = [jnp.zeros((1, width), F32) for _ in range(4)]
        for window in range(2):
            here = pl.ds(window * TOK, TOK)
            grad = owns[here] + fars[here].astype(F32)
            xhat, inverse = moments(x1s[window])
            out_grad = dms[window].astype(F32)
            dresid = out_grad + norm_back(grad, xhat, inverse, vecs[5:6])
            dx1s[window] = dresid
            rounded = dresid.astype(BF16)
            das[window] = rounded
            for slot, value in enumerate((rounded.astype(F32), grad * xhat, grad, out_grad)):
                total[slot] = total[slot] + jnp.sum(value, axis=0, keepdims=True)
        norm_sums[...] = jnp.concatenate(total, axis=0)
        outs.append(begin(dx1s, dx1, out_sems.at[4 * PIECES]))
        outs.append(begin(das, da, out_sems.at[4 * PIECES + 1]))
    wait_proj.wait()
    dat[...] = dot_nt(das[...].reshape(tokens), wproj[...]).astype(BF16).reshape(2, TOK, cols_here)

    def send(mat, made):
        grads[mat] = made.astype(BF16)
        is_own = core == mat // 2
        at = jnp.where(is_own, 32, 48)
        for piece in range(PIECES):
            place = pl.multiple_of(meta[at + piece] * rows, rows)
            source = grads.at[mat, pl.ds(place, rows), :]
            to = pl.ds(piece * rows, rows), pl.ds(mat % 2 * cols_here, cols_here)
            sem = out_sems.at[mat * PIECES + piece]
            copies = [pltpu.make_async_copy(source, ref.at[to], sem) for ref in (mine, theirs)]
            pl.when(is_own)(copies[0].start)
            pl.when(~is_own)(copies[1].start)
            outs.append(copies[0])

    wait_att.wait()
    turned_in[...] = atts[...].reshape(tokens).T
    send(3, dot(turned_in[...], das[:, :, columns].reshape(2 * TOK, cols_here)))
    finish(wait_qk + [wait_v])
    place = lanes(TOK)
    table_sum = jnp.zeros((LANES, LANES), F32)
    for step in range(2 * count):
        window, pair = step // count, step % count
        cols = pl.ds(pair * LANES, LANES)
        q2, k2, v2, dat2 = (ref[window, :, cols] for ref in (qs, ks, vs, dat))
        q8 = (q2.astype(F32) * HDIM**-0.5).astype(BF16)
        k8 = (k2.astype(F32) * HDIM**-0.5).astype(BF16)
        wait_p[step].wait()
        dqs, dks, dvs, dts = [], [], [], []
        for half in range(2):
            soft = ps[window, 2 * pair + half]
            soft32 = soft.astype(F32)
            own_lanes = jnp.where(place // 64 == half, dat2.astype(F32), 0.0).astype(BF16)
            weighted = soft32 * dot_nt(own_lanes, v2)
            ds = (weighted - soft32 * jnp.sum(weighted, axis=-1, keepdims=True)).astype(BF16)
            turned = dot(ds, gather[...]).astype(BF16).astype(F32)
            turned = unrelative(turned).astype(BF16)
            dqs.append(dot(ds, k8) + dot(turned, table[half]))
            dks.append(dot_tn(ds, q8))
            dvs.append(dot_tn(soft, dat2))
            dts.append(dot_tn(turned, q2))
        dqkv[0, window, :, cols] = jnp.where(place < 64, dqs[0], dqs[1]).astype(BF16)
        dqkv[1, window, :, cols] = jnp.where(place < 64, dks[0][:TOK], dks[1][:TOK]).astype(BF16)
        dqkv[2, window, :, cols] = jnp.where(place < 64, dvs[0][:TOK], dvs[1][:TOK]).astype(BF16)
        table_sum = table_sum + jnp.where(lanes(LANES) < 64, dts[0], dts[1])
    table_grad[...] = table_sum
    if not last:
        outs.append(begin(dqkv, dqkv_out, out_sems.at[4 * PIECES + 2]))
    wait_n1.wait()
    turned_in[...] = n1s[...].reshape(tokens).T
    for mat in range(3):
        change = dqkv[mat].reshape(2 * TOK, cols_here)
        send(mat, dot(turned_in[...], change))
        if mat != 1:
            bias_sums[mat // 2 : mat // 2 + 1] = jnp.sum(change.astype(F32), axis=0, keepdims=True)
    if last:
        finish(ends)
        total = [jnp.zeros((1, width), F32) for _ in range(2)]
        for window in range(2):
            grad = jnp.zeros((TOK, width), F32)
            for part, change in enumerate([*changed, dqkv]):
                here = pl.ds(part * cols_here, cols_here)
                for mat in range(3):
                    grad = grad + dot_nt(change[mat, window], wqkv[mat, :, here])
            xhat, inverse = moments(toks[window].astype(F32))
            results[window] = dx1s[window] + norm_back(grad, xhat, inverse, vecs[0:1])
            outs.append(begin(results.at[window], result.at[window], out_sems.at[4 * PIECES + window]))
            for slot, value in enumerate((grad * xhat, grad)):
                total[slot] = total[slot] + jnp.sum(value, axis=0, keepdims=True)
        norm_sums[...] = jnp.concatenate(total, axis=0)
    finish(outs)


def attend_back(start, count, meta, vecs, gather, table, q, k, v, p, weights, att, n1, ins):
    width, cols_here = q.shape[-1], count * LANES
    first, last, parts = start == 0, start + count == PAIRS, start // count
    rows, keys = (2, TOK, width), (2, KEYS, cols_here)
    part, flat = (2, TOK, cols_here), (2 * TOK, width)
    heads = (2, 2 * count, TOK, KEYS)
    small = [shape((2, cols_here), F32), shape((LANES, LANES), F32)]
    large = [shape((width, 2 * cols_here), BF16)] * 2
    large.append(shape(rows, F32) if last else shape((3,) + part, BF16))
    if last:
        small = [shape((2, width), F32)] + small
    if first:
        small = [shape((4, width), F32)] + small
        large += [shape(rows, F32), shape(rows, BF16)]
    scratch = [rows, (cols_here, width), rows, rows, part, keys, keys, heads, part, (3,) + part]
    scratch += [(4, width, cols_here), (width, 2 * TOK)]
    scratch = [pltpu.VMEM(dims, BF16) for dims in scratch]
    scratch += [pltpu.SemaphoreType.DMA((15 + 2 * count + parts,)), pltpu.SemaphoreType.DMA((4 * PIECES + 3,))]
    if first:
        scratch += [
            pltpu.VMEM(flat, F32),
            pltpu.VMEM(flat, BF16),
            pltpu.VMEM(rows, F32),
            pltpu.VMEM(rows, BF16),
            pltpu.VMEM(rows, F32),
        ]
    if last:
        scratch += [
            pltpu.VMEM((3, width, width), BF16),
            pltpu.VMEM(rows, BF16),
            pltpu.VMEM(rows, F32),
            pltpu.VMEM(rows, F32),
        ] + [pltpu.VMEM((3,) + part, BF16)] * parts
    return pl.pallas_call(
        partial(attend_back_kernel, start, count),
        out_shape=small + large,
        in_specs=[SMEM] + [WHOLE] * 3 + [HBM] * (7 + len(ins)),
        out_specs=[WHOLE] * len(small) + [HBM] * len(large),
        scratch_shapes=scratch,
        compiler_params=params(),
        cost_estimate=pl.CostEstimate(
            flops=8_000_000_000 * count, bytes_accessed=10_000_000 * count, transcendentals=0
        ),
        name="attend_back",
    )(meta, vecs, gather, table, q, k, v, p, weights, att, n1, *ins)


def grid_of(count):
    return (4, 2, 2) if count == 16 else None


def turn(values, dims, moves):
    pairs = []
    for chip in range(dims[0] * dims[1] * dims[2]):
        for core, (axis, by) in enumerate(moves):
            place = list(np.unravel_index(chip, dims))
            place[axis] = (place[axis] + by) % dims[axis]
            pairs.append((2 * chip + core, 2 * int(np.ravel_multi_index(place, dims)) + core))
    return lax.ppermute(values, ("dp", "mp"), pairs)


ALONG_X, ALONG_Y = ((2, 1),) * 2, ((1, 1),) * 2
FIRST, SECOND = ((2, 1), (1, 1)), ((1, 1), (2, 1))


def along_z(values, dims):
    return [turn(values, dims, ((0, step),) * 2) for step in range(1, dims[0])]


def swap_z(values, dims, by):
    chips = dims[1] * dims[2]
    pairs = [(chip, (chip // chips ^ by) * chips + chip % chips) for chip in range(dims[0] * chips)]
    return lax.ppermute(values, "dp", pairs)


def other_core(values):
    return lax.ppermute(values, "mp", [(0, 1), (1, 0)])


def after(values, *others):
    return lax.optimization_barrier((values, *others))[0]


class Flow:
    def __init__(self, *came):
        self.came = list(came)


def meet(flows, *values):
    sizes = [len(flow.came) for flow in flows]
    found = list(lax.optimization_barrier((*(part for flow in flows for part in flow.came), *values)))
    for flow, size in zip(flows, sizes):
        flow.came, found = found[:size], found[size:]
    return found


def place_orders(dims, core):
    here = lax.axis_index("dp")
    z, y, x = here // (dims[1] * dims[2]), here // dims[2] % dims[1], here % dims[2]

    def chip(step, inner, outer):
        by_x = jnp.where(core == 0, inner, outer)
        by_y = jnp.where(core == 0, outer, inner)
        return ((z - step) % dims[0] * dims[1] + (y + by_y) % 2) * dims[2] + (x + by_x) % 2

    square = [(inner, outer) for outer in range(2) for inner in range(2)]
    gather = [chip(0, *at) for at in square]
    gather += [chip(step, *at) for at in square for step in range(1, dims[0])]
    scatter = [chip(step, *at) for at in square for step in range(dims[0])]
    return [jnp.stack(found).astype(jnp.int32) for found in (gather, scatter)]


def add(a, b):
    return a.astype(F32) + b.astype(F32)


class Scatter(Flow):
    def __init__(self, keep, far, dims):
        super().__init__(turn(far, dims, SECOND))
        self.keep, self.dims = keep, dims

    def second(self):
        half = self.keep.shape[0] // 2
        send = add(self.keep[half:], self.came[0][half:]).astype(BF16)
        self.near = add(self.keep[:half], self.came[0][:half])
        self.came = [turn(send, self.dims, FIRST)]

    def third(self):
        near = self.near + self.came[0].astype(F32)
        rows = near.shape[0] // self.dims[0]
        self.near = near[:rows]
        self.came = [
            turn(near[step * rows : (step + 1) * rows].astype(BF16), self.dims, ((0, self.dims[0] - step),) * 2)
            for step in range(1, self.dims[0])
        ]

    def last(self):
        return sum((part.astype(F32) for part in self.came), self.near)


def constants():
    key = np.arange(KEYS)
    row, col = key // SIDE, key % SIDE
    inside = (row < WIN) & (col < WIN)
    spread = np.zeros((KEYS, LANES), np.float32)
    gather = np.zeros((KEYS, LANES), np.float32)
    for place in key[inside]:
        for base in (0, 64):
            spread[place, base + WIN - 1 + row[place]] = 1.0
            spread[place, base + 32 + WIN - 1 + col[place]] = 1.0
        gather[place, WIN - 1 - row[place]] = 1.0
        gather[place, 32 + WIN - 1 - col[place]] = 1.0
    return spread, gather


def tables(rel_pos_h, rel_pos_w):
    count = rel_pos_h.shape[0]
    gap = jnp.zeros((32 - count, HDIM), BF16)
    turned = jnp.concatenate([rel_pos_h[::-1], gap, rel_pos_w[::-1], gap], axis=0)
    turned = jnp.concatenate([turned, turned], axis=0).T
    none = jnp.zeros_like(turned)
    forward = jnp.concatenate(
        [jnp.concatenate([turned, none], axis=0), jnp.concatenate([none, turned], axis=0)], axis=1
    )
    straight = jnp.concatenate([rel_pos_h, gap, rel_pos_w, gap], axis=0)
    straight = jnp.concatenate([straight, jnp.zeros_like(straight)], axis=0)
    none = jnp.zeros_like(straight)
    backward = jnp.stack(
        [
            jnp.concatenate([straight, none], axis=1),
            jnp.concatenate([none, straight], axis=1),
        ]
    )
    return forward, backward


def padded(values):
    images, rows, _, width = values.shape
    values = jnp.pad(values, ((0, 0), (0, 0), (0, SIDE - WIN), (0, 0)))
    return values.reshape(images, rows * SIDE, width)


def unpadded(values):
    images, _, width = values.shape
    return values.reshape(images, WIN, SIDE, width)[:, :, :WIN]


def local(
    patches,
    norm1_gain,
    norm1_bias,
    qkv_weight,
    qv_bias,
    rel_pos_h,
    rel_pos_w,
    proj_weight,
    proj_bias,
    norm2_gain,
    norm2_bias,
    fc1_weight,
    fc1_bias,
    fc2_weight,
    fc2_bias,
    heights,
    widths,
    out_grad,
):
    width = patches.shape[-1]
    dims = grid_of(lax.axis_size("dp"))
    core = lax.axis_index("mp")
    is_first = core == 0
    if dims is None:
        orders = [jnp.tile(jnp.arange(PIECES, dtype=jnp.int32), 4)]
    else:
        own, far = place_orders(dims, core), place_orders(dims, 1 - core)
        orders = [own[0], far[0], own[1], far[1]]
    meta = jnp.concatenate(
        orders + [core.astype(jnp.int32)[None], heights, widths, jnp.zeros((11,), jnp.int32)]
    )

    tok = padded(patches)
    row_index = core * WIN + jnp.arange(WIN)
    valid = (row_index[None, :, None] < heights[:, None, None]) & (
        jnp.arange(WIN)[None, None, :] < widths[:, None, None]
    )
    dm = padded(jnp.where(valid[..., None], out_grad, jnp.zeros_like(out_grad)))
    dm_far = other_core(dm)

    vectors = (norm1_gain, norm1_bias, qv_bias[0], qv_bias[1], proj_bias, norm2_gain, norm2_bias, fc2_bias)
    small = jnp.pad(jnp.stack(vectors, axis=1), ((0, 0), (0, LANES - len(vectors))))
    qk = jnp.concatenate([qkv_weight[:, :width], small, qkv_weight[:, width : 2 * width]], axis=1)
    vp = jnp.concatenate([qkv_weight[:, 2 * width :], small, proj_weight], axis=1)
    if dims is None:
        qk = lax.all_gather(qk, ("dp", "mp"), axis=0, tiled=True)
        vp = lax.all_gather(vp, ("dp", "mp"), axis=0, tiled=True)
        attend_own = [jnp.where(is_first, qk, vp)]
        attend_far = [jnp.where(is_first, vp, qk)]
        hidden_in = tuple(
            ((lax.all_gather(part, "dp", axis=0, tiled=True), 0),) for part in (fc1_weight, fc2_weight.T)
        )
    else:
        fc1, fc2 = fc1_weight, fc2_weight.T
        came = other_core(jnp.where(is_first, vp, qk))
        near = jnp.where(is_first, qk, vp)
        block = jnp.concatenate(
            [jnp.where(is_first, near, came), jnp.where(is_first, came, near)], axis=0
        )
        attend_size, hidden_size = block.shape[1], fc1.shape[1]
        own = jnp.concatenate([block, fc1, fc2], axis=1)
        attend_z, beside = Flow(*along_z(block, dims)), Flow(turn(own, dims, FIRST))
        dm_flow = Flow(dm_far)
        fc1, fc2 = meet([attend_z, beside, dm_flow], fc1, fc2)
        dm_far = dm_flow.came[0]

        own = jnp.concatenate([own, *beside.came], axis=0)
        over = Flow(turn(own, dims, SECOND))
        attend_z = jnp.concatenate(attend_z.came, axis=0)
        z_beside, fc1_z = Flow(turn(attend_z, dims, FIRST)), Flow(*along_z(fc1, dims))
        (fc2,) = meet([over, z_beside, fc1_z], fc2)

        over = over.came[0]
        attend_z = jnp.concatenate([attend_z, *z_beside.came], axis=0)
        fc1_z = jnp.concatenate(fc1_z.came, axis=0)
        z_over, fc1_beside = Flow(turn(attend_z, dims, SECOND)), Flow(turn(fc1_z, dims, FIRST))
        fc2_z = Flow(*along_z(fc2, dims))
        own_attend = jnp.concatenate([own[:, :attend_size], over[:, :attend_size]], axis=0)
        own_attend, attend_z = meet([z_over, fc1_beside, fc2_z], own_attend, attend_z)

        z_over = z_over.came[0]
        far = Flow(*(other_core(part) for part in (own_attend, attend_z, z_over)))
        fc1_z = jnp.concatenate([fc1_z, *fc1_beside.came], axis=0)
        fc1_over = Flow(turn(fc1_z, dims, SECOND))
        fc2_z = jnp.concatenate(fc2_z.came, axis=0)
        fc2_beside = Flow(turn(fc2_z, dims, FIRST))
        tok, fc1_z, fc2_z = meet([far], tok, fc1_z, fc2_z)
        attend_own, attend_far = [own, over, attend_z, z_over], far.came

    dm_flat, dm_far = dm.reshape(-1, width), dm_far.reshape(-1, width)
    dm_turned = jnp.concatenate([dm_flat, dm_far], axis=0).T
    spread, gather = constants()
    table, table_back = tables(rel_pos_h, rel_pos_w)

    vecs, n1, q, k, v, p, att, weights = attend(
        meta, tok, table, jnp.asarray(spread, BF16), attend_own, attend_far
    )
    if dims is not None:
        (att,) = meet([fc1_over, fc2_beside], att)
        fc2_z = jnp.concatenate([fc2_z, *fc2_beside.came], axis=0)
        fc2_over = Flow(turn(fc2_z, dims, SECOND))
        att = after(att, fc2_z)
    x1, n2 = join(tok, att, weights, vecs)
    n2_far = other_core(n2).reshape(-1, width)
    n2 = n2.reshape(-1, width)
    bias = fc1_bias[None].astype(F32)
    if dims is not None:
        places = (attend_size, attend_size), (attend_size + hidden_size,) * 2
        hidden_in = [tuple(zip((own, over, fc1_z, *fc1_over.came), (*places[0], 0, 0)))]
    fc2_part = hidden_fwd(meta, n2, n2_far, dm_turned, bias, hidden_in[0])
    if dims is not None:
        fc2_part = meet([fc2_over], *fc2_part)
        hidden_in.append(tuple(zip((own, over, fc2_z, *fc2_over.came), (*places[1], 0, 0))))
        fc2_sum = Scatter(*fc2_part, dims)
    fc1_bias_part, *fc1_part, back_own, back_far, out_own, out_far = hidden_back(
        meta, n2, n2_far, dm_flat, dm_far, bias, *hidden_in
    )
    back_far = other_core(back_far)
    if dims is not None:
        fc1_part = meet([fc2_sum], *fc1_part)
        fc2_sum.second()
        fc1_sum = Scatter(*fc1_part, dims)
    out_far = other_core(out_far)

    shared = (meta, vecs, jnp.asarray(gather, BF16), table_back, q, k, v, p, weights, att, n1)
    bias_sums, table_grad, attend_sums, changes = [], 0.0, [], []
    ins = (back_own, back_far, x1, dm)
    half = width // 2
    for start, count in BACK_PARTS:
        made = attend_back(start, count, *shared, ins)
        if start == 0:
            sums2, *made, dx1, da = made
        if start + count == PAIRS:
            sums1, *made = made
        bias_sums.append(made[0])
        table_grad = table_grad + made[1]
        mine, theirs, change = made[2:]
        changes.append(change)
        if dims is None:
            attend_sums.append(
                lax.psum_scatter(add(mine, other_core(theirs)), "dp", scatter_dimension=0, tiled=True)
            )
        elif start + count < PAIRS:
            came = Flow(other_core(theirs))
            if start == 0:
                da, mine = meet([fc2_sum, fc1_sum], da, mine)
                fc2_sum.third()
                fc1_sum.second()
            else:
                da, mine = meet([fc2_sum, fc1_sum, *attend_sums], da, mine)
                fc2_sum = fc2_sum.last()
                fc1_sum.third()
                attend_sums[0].second()
            both = add(mine, came.came[0]).astype(BF16)
            attend_sums.append(Scatter(both[:half], both[half:], dims))
            da = after(da, both)
        ins = (da,) if start + 2 * count < PAIRS else (da, tok, dx1, *changes)
    result = change
    branch = add(out_own, out_far).reshape(x1.shape) + vecs[7]
    block_out = unpadded(x1 + branch)
    block_out = jnp.where(valid[..., None], block_out, 0.0).astype(BF16)

    qv_sums = jnp.concatenate(bias_sums, axis=1)
    rel_sums = table_grad[:64, :HDIM] + table_grad[:64, HDIM:]
    fc1_sums = jnp.concatenate(
        [jnp.where(is_first, fc1_bias_part, 0.0), jnp.where(is_first, 0.0, fc1_bias_part)], axis=1
    )
    flat = jnp.concatenate(
        [
            jnp.concatenate([sums1, qv_sums, sums2], axis=0).reshape(-1, LANES),
            rel_sums.reshape(-1, LANES),
            fc1_sums.reshape(-1, LANES),
        ],
        axis=0,
    )
    if dims is None:
        flat = lax.psum(flat + other_core(flat), "dp")
        fc1_sum, fc2_sum = (
            lax.psum_scatter(
                jnp.concatenate(parts, axis=0).astype(F32), "dp", scatter_dimension=0, tiled=True
            )
            for parts in (fc1_part, fc2_part)
        )
    else:
        mine, theirs, flat = meet([fc1_sum, *attend_sums], mine, theirs, flat)
        came, flat_came = Flow(other_core(theirs)), Flow(other_core(flat))
        attend_sums[1].second()
        fc1_sum = fc1_sum.last()
        mine, flat = meet([came, flat_came, attend_sums[1]], mine, flat)
        both = add(mine, came.came[0]).astype(BF16)
        attend_sums.append(Scatter(both[:half], both[half:], dims))
        flat = flat + flat_came.came[0]
        flat_came = Flow(turn(flat, dims, SECOND))
        attend_sums[0].third()
        (flat,) = meet([flat_came, attend_sums[0], attend_sums[2]], flat)
        flat = flat + flat_came.came[0]
        flat_came = Flow(turn(flat, dims, FIRST))
        attend_sums[2].second()
        attend_sums[1].third()
        attend_sums[0] = attend_sums[0].last()
        (flat,) = meet([flat_came, attend_sums[1], attend_sums[2]], flat)
        flat = flat + flat_came.came[0]
        flat_came = Flow(swap_z(flat, dims, 2))
        attend_sums[2].third()
        attend_sums[1] = attend_sums[1].last()
        (flat,) = meet([flat_came, attend_sums[2]], flat)
        flat = flat + flat_came.came[0]
        flat = flat + swap_z(flat, dims, 1)
        attend_sums[2] = attend_sums[2].last()

    whole = jnp.concatenate(attend_sums, axis=1)
    rows = whole.shape[0] // 2
    near = jnp.where(is_first, whole[:rows], whole[rows:])
    came = other_core(jnp.where(is_first, whole[rows:], whole[:rows]))
    halves = [[], []]
    at = 0
    for _, count in BACK_PARTS:
        for half in range(2):
            halves[half].append(slice(at, at + count * LANES))
            at += count * LANES
    qk, vp = jnp.where(is_first, near, came), jnp.where(is_first, came, near)
    q_grad, k_grad, v_grad, proj_grad = (
        jnp.concatenate([found[:, cols] for cols in half], axis=1)
        for found in (qk, vp)
        for half in halves
    )
    qkv_grad = jnp.concatenate([q_grad, k_grad, v_grad], axis=1)
    at = 8 * width // LANES
    vec_sums = flat[:at].reshape(8, width)
    rel = flat[at : at + 32].reshape(64, HDIM)
    fc1_bias_grad = lax.dynamic_index_in_dim(flat[at + 32 :].reshape(2, -1), core, 0, keepdims=False)
    share = norm1_gain.shape[0]
    device = lax.axis_index("dp") * 2 + core
    mine = lax.dynamic_slice_in_dim(vec_sums, device * share, share, axis=1)
    rels = rel_pos_h.shape[0]
    return (
        block_out,
        unpadded(result),
        mine[0],
        mine[1],
        qkv_grad,
        mine[2:4],
        rel[:rels],
        rel[32 : 32 + rels],
        proj_grad,
        mine[4],
        mine[5],
        mine[6],
        fc1_sum,
        fc1_bias_grad,
        fc2_sum.T,
        mine[7],
    )


def solution(mesh):
    return jax.shard_map(
        local,
        mesh=mesh,
        in_specs=(
            P("dp", "mp", None, None),
            P(("dp", "mp")),
            P(("dp", "mp")),
            P(("dp", "mp"), None),
            P(None, ("dp", "mp")),
            P(),
            P(),
            P(("dp", "mp"), None),
            P(("dp", "mp")),
            P(("dp", "mp")),
            P(("dp", "mp")),
            P("dp", "mp"),
            P("mp"),
            P("mp", "dp"),
            P(("dp", "mp")),
            P("dp"),
            P("dp"),
            P("dp", "mp", None, None),
        ),
        out_specs=(
            P("dp", "mp", None, None),
            P("dp", "mp", None, None),
            P(("dp", "mp")),
            P(("dp", "mp")),
            P(("dp", "mp"), None),
            P(None, ("dp", "mp")),
            P(),
            P(),
            P(("dp", "mp"), None),
            P(("dp", "mp")),
            P(("dp", "mp")),
            P(("dp", "mp")),
            P("dp", "mp"),
            P("mp"),
            P("mp", "dp"),
            P(("dp", "mp")),
        ),
        check_vma=False,
    )
```

time: 283 us -> 264 us (0.933)
  waiting for transfers between devices: 85.9 us -> 62.1 us
  starting transfers between devices: 60.2 us -> 69.2 us
  Pallas kernels: 91.7 us -> 84 us
  local copies, waits for them, and re-layouts: 21.2 us -> 26.5 us
    ppermute x40 -> x44, waiting for transfers between devices: 81.3 us -> 54.2 us  [turn(): return lax.ppermute(values, ('dp', 'mp'), pairs)]
    ppermute x40 -> x44, starting transfers between devices: 56.2 us -> 64.5 us  [turn(): return lax.ppermute(values, ('dp', 'mp'), pairs)]
    pallas_call x6, Pallas kernels: 88.2 us -> 80.5 us  [the longest x3 36.4 us: attend_back(): pl.pallas_call(partial(attend_back_kernel, start, count), out_shape=small...]
    ppermute x0 -> x2, waiting for transfers between devices: none -> 3.95 us  [swap_z(): return lax.ppermute(values, 'dp', pairs)]
    unnamed x88 -> x110, local copies, waits for them, and re-layouts: 11.1 us -> 14.6 us
    another operation x4 -> x5, other arithmetic: 5.07 us -> 1.64 us
  transfers between devices with their start and end apart: 55 -> 59, of which waited for: 26 -> 23; matrix products, arithmetic and copies ran while one was open for 10% -> 11% of each run, Pallas kernels for 28% -> 23%
where the time goes in v3:
time: 264 us; the launch traced here: 260 us
  Pallas kernels  84 us (32%)
  starting transfers between devices  69.2 us (26%)
  waiting for transfers between devices  62.1 us (24%)
  local copies, waits for them, and re-layouts  26.5 us (10%)
  other arithmetic  16.7 us (6%)
    ppermute x44, starting transfers between devices, turn(): return lax.ppermute(values, ('dp', 'mp'), pairs)  64.5 us
    ppermute x44, waiting for transfers between devices, turn(): return lax.ppermute(values, ('dp', 'mp'), pairs)  54.2 us
    pallas_call x3, Pallas kernels, attend_back(): pl.pallas_call(partial(attend_back_kernel, start, count), out_shape=small...  36.4 us
    pallas_call x1, Pallas kernels, hidden_back(): pl.pallas_call(partial(hidden_back_kernel, bases0, bases1), out_shape=[sh...  20.4 us
    unnamed x110, local copies, waits for them, and re-layouts  14.6 us
    pallas_call x1, Pallas kernels, attend(): pl.pallas_call(partial(attend_kernel, count, total), out_shape=[shape((8,...  14 us
    pallas_call x1, Pallas kernels, hidden_fwd(): pl.pallas_call(partial(hidden_fwd_kernel, bases), out_shape=[shape((width...  9.74 us
  transfers between devices with their start and end apart: 59, of which 23 were waited for; matrix products, arithmetic and copies ran while one was open for 11% of the time, Pallas kernels for 23%

profile of v3, /device:TPU:0, one launch (start us, length us, event | category | flops | bytes accessed | tf_op | source)
XLA Modules:
  0.0 260.4 jit_solution(2002616986596832298)
XLA Ops:
  12.2 2.6 collective-permute-start.2
  16.6 2.8 %collective-permute-done.1 = bf16[48,1664]{1,0:T(8,128)(2,1)S(1)} collective-permute-done((bf16[48,1664]{1,0:T(8,128)(2,1)S(1)}, bf16[48,1664]{1,0:T(8,128)(2,1)S(1)}, u32[]{:S(2)}, u32[]{:S(2)}) %collective-permute-start.1) | collective-permute-done | bytes 159776 | tf_op jit(solution)/shard_map/ppermute | solution.py:603
  19.4 6.2 %collective-permute-done.2 = bf16[48,1664]{1,0:T(8,128)(2,1)S(1)} collective-permute-done((bf16[48,1664]{1,0:T(8,128)(2,1)S(1)}, bf16[48,1664]{1,0:T(8,128)(2,1)S(1)}, u32[]{:S(2)}, u32[]{:S(2)}) %collective-permute-start.2) | collective-permute-done | bytes 159776 | tf_op jit(solution)/shard_map/ppermute | solution.py:603
  30.6 3.9 %collective-permute-start.8 = (bf16[48,1536]{1,0:T(8,128)(2,1)S(1)}, bf16[48,1536]{1,0:T(8,128)(2,1)S(1)}, u32[]{:S(2)}, u32[]{:S(2)}) collective-permute-start(bf16[48,1536]{1,0:T(8,128)(2,1)S(1)} %copy-done.21), channel_id=1, source_target_pairs={{0,8},{1,9},{2,10},{3,11},{4,12},{5,13},{6,14},{7,15},{8,16},{9,17... | collective-permute-start | bytes 442376 | tf_op jit(solution)/shard_map/ppermute | solution.py:603
  40.4 4.5 %collective-permute-done.9 = bf16[48,1536]{1,0:T(8,128)(2,1)S(1)} collective-permute-done((bf16[48,1536]{1,0:T(8,128)(2,1)S(1)}, bf16[48,1536]{1,0:T(8,128)(2,1)S(1)}, u32[]{:S(2)}, u32[]{:S(2)}) %collective-permute-start.9) | collective-permute-done | bytes 147488 | tf_op jit(solution)/shard_map/ppermute | solution.py:603
  50.2 4.0 %collective-permute-start.13 = (bf16[48,1536]{1,0:T(8,128)(2,1)S(1)}, bf16[48,1536]{1,0:T(8,128)(2,1)S(1)}, u32[]{:S(2)}, u32[]{:S(2)}) collective-permute-start(bf16[48,1536]{1,0:T(8,128)(2,1)S(1)} %bitcast.87), channel_id=1, source_target_pairs={{0,8},{1,9},{2,10},{3,11},{4,12},{5,13},{6,14},{7,15},{8,16},{9,17... | collective-permute-start | bytes 442376 | tf_op jit(solution)/shard_map/ppermute | solution.py:603
  60.1 5.0 %collective-permute-done.14 = bf16[48,1536]{1,0:T(8,128)(2,1)S(1)} collective-permute-done((bf16[48,1536]{1,0:T(8,128)(2,1)S(1)}, bf16[48,1536]{1,0:T(8,128)(2,1)S(1)}, u32[]{:S(2)}, u32[]{:S(2)}) %collective-permute-start.14) | collective-permute-done | bytes 147488 | tf_op jit(solution)/shard_map/ppermute | solution.py:603
  72.4 14.0 %attend.1 = (f32[8,768]{1,0:T(8,128)S(1)}, bf16[2,224,768]{2,1,0:T(8,128)(2,1)S(1)}, bf16[2,224,768]{2,1,0:T(8,128)(2,1)}, bf16[2,256,768]{2,1,0:T(8,128)(2,1)},...) custom-call(s32[80]{0:T(128)S(1)} %concatenate.99.meta, ...), custom_call_target="tpu_custom_call" | custom-call | flops 20000000000 | bytes 40000000 | tf_op jit(solution)/shard_map/attend/pallas_call | solution.py:179
  88.0 3.5 %join.1 = (f32[2,224,768]{2,1,0:T(8,128)}, bf16[2,224,768]{2,1,0:T(8,128)(2,1)S(1)}) custom-call(bf16[2,224,768]{2,1,0:T(8,128)(2,1)S(1)} %bitcast.71, bf16[2,224,768]{2,1,0:T(8,128)(2,1)} %get-tuple-element.160.att, bf16[4,768,768]{2,1,0:T(8,128)(2,1)} %get-tuple-element.161.weights, f32[8,768]{1,0:T(8,128)S(1)} %get-tuple-element.162.vecs), custom_call_target="tpu_custom_call" | custom-call | flops 600000000 | bytes 9000000 | tf_op jit(solution)/shard_map/join/pallas_call | solution.py:210
  96.2 9.7 %hidden_fwd.1 = (bf16[384,1536]{1,0:T(8,128)(2,1)}, bf16[384,1536]{1,0:T(8,128)(2,1)}) custom-call(s32[80]{0:T(128)S(1)} %concatenate.99.meta, bf16[448,768]{1,0:T(8,128)(2,1)S(1)} %bitcast.72, bf16[448,768]{1,0:T(8,128)(2,1)S(1)} %bitcast.74, bf16[768,896]{1,0:T(8,128)(2,1)} %copy.66.dm_turned, f32[1,1536]{1,0:T(1,128)S(1)} %reshape.150.bias, ...), custom_call_target="tpu_custom_call" | custom-call | flops 12683575296 | bytes 12000000 | tf_op jit(solution)/shard_map/hidden_fwd/pallas_call | solution.py:275
  108.9 20.4 %hidden_back.1 = (f32[1,1536]{1,0:T(1,128)S(1)}, bf16[384,1536]{1,0:T(8,128)(2,1)}, bf16[384,1536]{1,0:T(8,128)(2,1)}, f32[448,768]{1,0:T(8,128)}, bf16[448,768]...) custom-call(s32[80]{0:T(128)S(1)} %concatenate.99.meta, bf16[448,768]{1,0:T(8,128)(2,1)} %bitcast.73, ...), custom_call_target="tpu_custom_call" | custom-call | flops 25367150592 | bytes 20000000 | tf_op jit(solution)/shard_map/hidden_back/pallas_call | solution.py:357
  134.0 12.9 %attend_back.3 = (f32[4,768]{1,0:T(4,128)S(1)}, f32[2,256]{1,0:T(2,128)S(1)}, f32[128,128]{1,0:T(8,128)S(1)}, bf16[768,512]{1,0:T(8,128)(2,1)}, bf16[768,512]{1,...) custom-call(s32[80]{0:T(128)S(1)} %concatenate.99.meta, ...), custom_call_target="tpu_custom_call" | custom-call | flops 16000000000 | bytes 20000000 | tf_op jit(solution)/shard_map/attend_back/pallas_call | solution.py:578
  152.9 11.7 %collective-permute-done.25 = bf16[192,1536]{1,0:T(8,128)(2,1)S(1)} collective-permute-done((bf16[192,1536]{1,0:T(8,128)(2,1)S(1)}, bf16[192,1536]{1,0:T(8,128)(2,1)S(1)}, u32[]{:S(2)}, u32[]{:S(2)}) %collective-permute-start.25) | collective-permute-done | bytes 589856 | tf_op jit(solution)/shard_map/ppermute | solution.py:603
  164.5 5.3 %collective-permute-done.26 = bf16[384,1536]{1,0:T(8,128)(2,1)S(1)} collective-permute-done((bf16[384,1536]{1,0:T(8,128)(2,1)}, bf16[384,1536]{1,0:T(8,128)(2,1)S(1)}, u32[]{:S(2)}, u32[]{:S(2)}) %collective-permute-start.26) | collective-permute-done | bytes 1179680 | tf_op jit(solution)/shard_map/ppermute | solution.py:603
  170.1 4.3 %collective-permute-start.28 = (bf16[48,1536]{1,0:T(8,128)(2,1)S(1)}, bf16[48,1536]{1,0:T(8,128)(2,1)S(1)}, u32[]{:S(2)}, u32[]{:S(2)}) collective-permute-start(bf16[48,1536]{1,0:T(8,128)(2,1)S(1)} %get-tuple-element.265), channel_id=1, source_target_pairs={{0,24},{1,25},{2,26},{3,27},{4,28},{5,29},{6,30},{7,31},{8,0},{9,1... | collective-permute-start | bytes 442376 | tf_op jit(solution)/shard_map/ppermute | solution.py:603
  177.8 10.3 %attend_back.4 = (f32[2,256]{1,0:T(2,128)S(1)}, f32[128,128]{1,0:T(8,128)S(1)}, bf16[768,512]{1,0:T(8,128)(2,1)}, bf16[768,512]{1,0:T(8,128)(2,1)}, bf16[3,2,224,256]{3,2,1,0:T(8,128)(2,1)S(1)}) custom-call(s32[80]{0:T(128)S(1)} %concatenate.99.meta, f32[8,768]{1,0:T(8,128)S(1)} %get-tuple-element.162.vecs, bf16[256,128]{1,0:T(8,128)(2,1)S(1)} %copy-done.4, ...), custom_call_target="tpu_custom_call" | custom-call | flops 16000000000 | bytes 20000000 | tf_op jit(solution)/shard_map/attend_back/pallas_call | solution.py:578
  190.0 3.6 %collective-permute-start.35 = (bf16[48,1536]{1,0:T(8,128)(2,1)}, bf16[48,1536]{1,0:T(8,128)(2,1)}, u32[]{:S(2)}, u32[]{:S(2)}) collective-permute-start(bf16[48,1536]{1,0:T(8,128)(2,1)} %get-tuple-element.262), channel_id=1, source_target_pairs={{0,24},{1,25},{2,26},{3,27},{4,28},{5,29},{6,30},{7,31},{8,0},{9,1... | collective-permute-start | bytes 442376 | tf_op jit(solution)/shard_map/ppermute | solution.py:603
  199.0 13.2 %attend_back.5 = (f32[2,768]{1,0:T(2,128)S(1)}, f32[2,256]{1,0:T(2,128)S(1)}, f32[128,128]{1,0:T(8,128)S(1)}, bf16[768,512]{1,0:T(8,128)(2,1)}, bf16[768,512]{1,0:T(8,128)(2,1)}, /*index=5*/f32[2,224,768]{2,1,0:T(8,128)}) custom-call(s32[80]{0:T(128)S(1)} %concatenate.99.meta, f32[8,768]{1,0:T(8,128)S(1)} %get-tuple-element.162.vecs, ...), custom_call_target="tpu_custom_call" | custom-call | flops 16000000000 | bytes 20000000 | tf_op jit(solution)/shard_map/attend_back/pallas_call | solution.py:578
  212.3 3.3 %copy.70 = f32[2,14,14,768]{3,0,2,1:T(2,128)} copy(f32[2,14,14,768]{3,2,1,0:T(8,128)} %bitcast.82) | data formatting | bytes 2408448
  218.6 3.9 %collective-permute-start.44 = (bf16[48,512]{1,0:T(8,128)(2,1)S(1)}, bf16[48,512]{1,0:T(8,128)(2,1)S(1)}, u32[]{:S(2)}, u32[]{:S(2)}) collective-permute-start(bf16[48,512]{1,0:T(8,128)(2,1)S(1)} %get-tuple-element.278), channel_id=1, source_target_pairs={{0,24},{1,25},{2,26},{3,27},{4,28},{5,29},{6,30},{7,31},{8,0},{9,1... | collective-permute-start | bytes 147464 | tf_op jit(solution)/shard_map/ppermute | solution.py:603
  228.4 3.4 %collective-permute-start.49 = (bf16[48,512]{1,0:T(8,128)(2,1)S(1)}, bf16[48,512]{1,0:T(8,128)(2,1)S(1)}, u32[]{:S(2)}, u32[]{:S(2)}) collective-permute-start(bf16[48,512]{1,0:T(8,128)(2,1)S(1)} %get-tuple-element.275), channel_id=1, source_target_pairs={{0,24},{1,25},{2,26},{3,27},{4,28},{5,29},{6,30},{7,31},{8,0},{9,1... | collective-permute-start | bytes 147464 | tf_op jit(solution)/shard_map/ppermute | solution.py:603
  243.0 3.0 %collective-permute-start.54 = (bf16[48,512]{1,0:T(8,128)(2,1)S(1)}, bf16[48,512]{1,0:T(8,128)(2,1)S(1)}, u32[]{:S(2)}, u32[]{:S(2)}) collective-permute-start(bf16[48,512]{1,0:T(8,128)(2,1)S(1)} %get-tuple-element.272), channel_id=1, source_target_pairs={{0,24},{1,25},{2,26},{3,27},{4,28},{5,29},{6,30},{7,31},{8,0},{9,1... | collective-permute-start | bytes 147464 | tf_op jit(solution)/shard_map/ppermute | solution.py:603
  247.8 3.2 %collective-permute-done.55 = bf16[48,512]{1,0:T(8,128)(2,1)S(1)} collective-permute-done((bf16[48,512]{1,0:T(8,128)(2,1)S(1)}, bf16[48,512]{1,0:T(8,128)(2,1)S(1)}, u32[]{:S(2)}, u32[]{:S(2)}) %collective-permute-start.55) | collective-permute-done | bytes 49184 | tf_op jit(solution)/shard_map/ppermute | solution.py:603
  252.8 4.0 %collective-permute-done.57 = f32[104,128]{1,0:T(8,128)S(1)} collective-permute-done((f32[104,128]{1,0:T(8,128)S(1)}, f32[104,128]{1,0:T(8,128)S(1)}, u32[]{:S(2)}, u32[]{:S(2)}) %collective-permute-start.57) | collective-permute-done | bytes 53280 | tf_op jit(solution)/shard_map/ppermute | solution.py:617
  (309 shorter events, 100.0 us)
Async XLA Ops:
  7.1 19.3 %collective-permute-start.5 = (bf16[2,224,768]{2,1,0:T(8,128)(2,1)S(1)}, bf16[2,224,768]{2,1,0:T(8,128)(2,1)S(1)}, u32[]{:S(2)}, u32[]{:S(2)}) collective-permute-start(bf16[2,224,768]{2,1,0:T(8,128)(2,1)S(1)} %bitcast.77), channel_id=1, source_target_pairs={{0,1},{1,0},{2,3},{3,2},{4,5},{5,4},{6,7},{7,6},{8,9},{9,8},{10,11... | collective-permute-start | bytes 2064392 | tf_op jit(solution)/shard_map/ppermute | solution.py:621
  7.9 17.7 %collective-permute-start.4 = (bf16[48,4736]{1,0:T(8,128)(2,1)S(1)}, bf16[48,4736]{1,0:T(8,128)(2,1)S(1)}, u32[]{:S(2)}, u32[]{:S(2)}) collective-permute-start(bf16[48,4736]{1,0:T(8,128)(2,1)S(1)} %pad_maximum_fusion.3), channel_id=1, source_target_pairs={{0,2},{1,5},{2,0},{3,7},{4,6},{5,1},{6,4},{7,3},{8,10},{9,13},{10,... | collective-permute-start | bytes 1363976 | tf_op jit(solution)/shard_map/ppermute | solution.py:603
  12.2 13.5 %collective-permute-start.2 = (bf16[48,1664]{1,0:T(8,128)(2,1)S(1)}, bf16[48,1664]{1,0:T(8,128)(2,1)S(1)}, u32[]{:S(2)}, u32[]{:S(2)}) collective-permute-start(bf16[48,1664]{1,0:T(8,128)(2,1)S(1)} %pad_maximum_fusion.6), channel_id=1, source_target_pairs={{0,16},{1,17},{2,18},{3,19},{4,20},{5,21},{6,22},{7,23},{8,24},{9,... | collective-permute-start | bytes 479240 | tf_op jit(solution)/shard_map/ppermute | solution.py:603
  27.8 18.4 %collective-permute-start.6 = (bf16[96,4736]{1,0:T(8,128)(2,1)S(1)}, bf16[96,4736]{1,0:T(8,128)(2,1)S(1)}, u32[]{:S(2)}, u32[]{:S(2)}) collective-permute-start(bf16[96,4736]{1,0:T(8,128)(2,1)S(1)} %pad_maximum_fusion.refs_0_.refs_4_), channel_id=1, source_target_pairs={{0,4},{1,3},{2,6},{3,1},{4,0},{5,7},{6,2},{7,5},{8,12},{9,11},{10,... | collective-permute-start | bytes 2727944 | tf_op jit(solution)/shard_map/ppermute | solution.py:603
  28.4 16.6 %collective-permute-start.7 = (bf16[144,1664]{1,0:T(8,128)(2,1)S(1)}, bf16[144,1664]{1,0:T(8,128)(2,1)S(1)}, u32[]{:S(2)}, u32[]{:S(2)}) collective-permute-start(bf16[144,1664]{1,0:T(8,128)(2,1)S(1)} %pad_maximum_fusion.2), channel_id=1, source_target_pairs={{0,2},{1,5},{2,0},{3,7},{4,6},{5,1},{6,4},{7,3},{8,10},{9,13},{10,... | collective-permute-start | bytes 1437704 | tf_op jit(solution)/shard_map/ppermute | solution.py:603
  47.2 19.2 %collective-permute-start.11 = (bf16[288,1664]{1,0:T(8,128)(2,1)}, bf16[288,1664]{1,0:T(8,128)(2,1)}, u32[]{:S(2)}, u32[]{:S(2)}) collective-permute-start(bf16[288,1664]{1,0:T(8,128)(2,1)} %constant_dynamic-update-slice_fusion.refs_2_), channel_id=1, source_target_pairs={{0,4},{1,3},{2,6},{3,1},{4,0},{5,7},{6,2},{7,5},{8,12},{9,11},{10,... | collective-permute-start | bytes 2875400 | tf_op jit(solution)/shard_map/ppermute | solution.py:603
  67.1 19.4 %collective-permute-start.19 = (bf16[288,1536]{1,0:T(8,128)(2,1)S(1)}, bf16[288,1536]{1,0:T(8,128)(2,1)S(1)}, u32[]{:S(2)}, u32[]{:S(2)}) collective-permute-start(bf16[288,1536]{1,0:T(8,128)(2,1)S(1)} %constant_dynamic-update-slice_fusion.4.refs_2_), channel_id=1, source_target_pairs={{0,4},{1,3},{2,6},{3,1},{4,0},{5,7},{6,2},{7,5},{8,12},{9,11},{10,... | collective-permute-start | bytes 2654216 | tf_op jit(solution)/shard_map/ppermute | solution.py:603
  68.7 17.8 %collective-permute-start.20 = (bf16[144,1536]{1,0:T(8,128)(2,1)S(1)}, bf16[144,1536]{1,0:T(8,128)(2,1)S(1)}, u32[]{:S(2)}, u32[]{:S(2)}) collective-permute-start(bf16[144,1536]{1,0:T(8,128)(2,1)S(1)} %constant_dynamic-update-slice_fusion.8), channel_id=1, source_target_pairs={{0,2},{1,5},{2,0},{3,7},{4,6},{5,1},{6,4},{7,3},{8,10},{9,13},{10,... | collective-permute-start | bytes 1327112 | tf_op jit(solution)/shard_map/ppermute | solution.py:603
  94.7 13.3 %collective-permute-start.22 = (bf16[288,1536]{1,0:T(8,128)(2,1)}, bf16[288,1536]{1,0:T(8,128)(2,1)S(1)}, u32[]{:S(2)}, u32[]{:S(2)}) collective-permute-start(bf16[288,1536]{1,0:T(8,128)(2,1)} %copy-done.28), channel_id=1, source_target_pairs={{0,4},{1,3},{2,6},{3,1},{4,0},{5,7},{6,2},{7,5},{8,12},{9,11},{10,... | collective-permute-start | bytes 2654216 | tf_op jit(solution)/shard_map/ppermute | solution.py:603
  129.3 20.0 %collective-permute-start.23 = (bf16[448,768]{1,0:T(8,128)(2,1)S(1)}, bf16[448,768]{1,0:T(8,128)(2,1)S(1)}, u32[]{:S(2)}, u32[]{:S(2)}) collective-permute-start(bf16[448,768]{1,0:T(8,128)(2,1)S(1)} %get-tuple-element.172), channel_id=1, source_target_pairs={{0,1},{1,0},{2,3},{3,2},{4,5},{5,4},{6,7},{7,6},{8,9},{9,8},{10,11... | collective-permute-start | bytes 2064392 | tf_op jit(solution)/shard_map/ppermute | solution.py:621
  129.4 17.7 %collective-permute-start.24 = (bf16[384,1536]{1,0:T(8,128)(2,1)S(1)}, bf16[384,1536]{1,0:T(8,128)(2,1)S(1)}, u32[]{:S(2)}, u32[]{:S(2)}) collective-permute-start(bf16[384,1536]{1,0:T(8,128)(2,1)S(1)} %copy-done.38), channel_id=1, source_target_pairs={{0,4},{1,3},{2,6},{3,1},{4,0},{5,7},{6,2},{7,5},{8,12},{9,11},{10,... | collective-permute-start | bytes 3538952 | tf_op jit(solution)/shard_map/ppermute | solution.py:603
  146.9 29.9 %collective-permute-start.32 = (bf16[768,512]{1,0:T(8,128)(2,1)}, bf16[768,512]{1,0:T(8,128)(2,1)S(1)}, u32[]{:S(2)}, u32[]{:S(2)}) collective-permute-start(bf16[768,512]{1,0:T(8,128)(2,1)} %get-tuple-element.192), channel_id=1, source_target_pairs={{0,1},{1,0},{2,3},{3,2},{4,5},{5,4},{6,7},{7,6},{8,9},{9,8},{10,11... | collective-permute-start | bytes 2359304 | tf_op jit(solution)/shard_map/ppermute | solution.py:621
  147.1 22.7 %collective-permute-start.26 = (bf16[384,1536]{1,0:T(8,128)(2,1)}, bf16[384,1536]{1,0:T(8,128)(2,1)S(1)}, u32[]{:S(2)}, u32[]{:S(2)}) collective-permute-start(bf16[384,1536]{1,0:T(8,128)(2,1)} %get-tuple-element.183), channel_id=1, source_target_pairs={{0,4},{1,3},{2,6},{3,1},{4,0},{5,7},{6,2},{7,5},{8,12},{9,11},{10,... | collective-permute-start | bytes 3538952 | tf_op jit(solution)/shard_map/ppermute | solution.py:603
  148.2 16.3 %collective-permute-start.25 = (bf16[192,1536]{1,0:T(8,128)(2,1)S(1)}, bf16[192,1536]{1,0:T(8,128)(2,1)S(1)}, u32[]{:S(2)}, u32[]{:S(2)}) collective-permute-start(bf16[192,1536]{1,0:T(8,128)(2,1)S(1)} %add_convert_fusion.4), channel_id=1, source_target_pairs={{0,2},{1,5},{2,0},{3,7},{4,6},{5,1},{6,4},{7,3},{8,10},{9,13},{10,... | collective-permute-start | bytes 1769480 | tf_op jit(solution)/shard_map/ppermute | solution.py:603
  170.1 18.0 %collective-permute-start.28 = (bf16[48,1536]{1,0:T(8,128)(2,1)S(1)}, bf16[48,1536]{1,0:T(8,128)(2,1)S(1)}, u32[]{:S(2)}, u32[]{:S(2)}) collective-permute-start(bf16[48,1536]{1,0:T(8,128)(2,1)S(1)} %get-tuple-element.265), channel_id=1, source_target_pairs={{0,24},{1,25},{2,26},{3,27},{4,28},{5,29},{6,30},{7,31},{8,0},{9,1... | collective-permute-start | bytes 442376 | tf_op jit(solution)/shard_map/ppermute | solution.py:603
  174.4 13.8 %collective-permute-start.29 = (bf16[48,1536]{1,0:T(8,128)(2,1)S(1)}, bf16[48,1536]{1,0:T(8,128)(2,1)S(1)}, u32[]{:S(2)}, u32[]{:S(2)}) collective-permute-start(bf16[48,1536]{1,0:T(8,128)(2,1)S(1)} %get-tuple-element.264), channel_id=1, source_target_pairs={{0,16},{1,17},{2,18},{3,19},{4,20},{5,21},{6,22},{7,23},{8,24},{9,... | collective-permute-start | bytes 442376 | tf_op jit(solution)/shard_map/ppermute | solution.py:603
  174.8 13.4 %collective-permute-start.30 = (bf16[48,1536]{1,0:T(8,128)(2,1)S(1)}, bf16[48,1536]{1,0:T(8,128)(2,1)S(1)}, u32[]{:S(2)}, u32[]{:S(2)}) collective-permute-start(bf16[48,1536]{1,0:T(8,128)(2,1)S(1)} %get-tuple-element.263), channel_id=1, source_target_pairs={{0,8},{1,9},{2,10},{3,11},{4,12},{5,13},{6,14},{7,15},{8,16},{9,17... | collective-permute-start | bytes 442376 | tf_op jit(solution)/shard_map/ppermute | solution.py:603
  175.6 13.4 %collective-permute-start.31 = (bf16[192,1536]{1,0:T(8,128)(2,1)S(1)}, bf16[192,1536]{1,0:T(8,128)(2,1)S(1)}, u32[]{:S(2)}, u32[]{:S(2)}) collective-permute-start(bf16[192,1536]{1,0:T(8,128)(2,1)S(1)} %add_convert_fusion.3), channel_id=1, source_target_pairs={{0,2},{1,5},{2,0},{3,7},{4,6},{5,1},{6,4},{7,3},{8,10},{9,13},{10,... | collective-permute-start | bytes 1769480 | tf_op jit(solution)/shard_map/ppermute | solution.py:603
  190.0 25.7 %collective-permute-start.35 = (bf16[48,1536]{1,0:T(8,128)(2,1)}, bf16[48,1536]{1,0:T(8,128)(2,1)}, u32[]{:S(2)}, u32[]{:S(2)}) collective-permute-start(bf16[48,1536]{1,0:T(8,128)(2,1)} %get-tuple-element.262), channel_id=1, source_target_pairs={{0,24},{1,25},{2,26},{3,27},{4,28},{5,29},{6,30},{7,31},{8,0},{9,1... | collective-permute-start | bytes 442376 | tf_op jit(solution)/shard_map/ppermute | solution.py:603
  193.6 22.1 %collective-permute-start.36 = (bf16[48,1536]{1,0:T(8,128)(2,1)}, bf16[48,1536]{1,0:T(8,128)(2,1)}, u32[]{:S(2)}, u32[]{:S(2)}) collective-permute-start(bf16[48,1536]{1,0:T(8,128)(2,1)} %get-tuple-element.261), channel_id=1, source_target_pairs={{0,16},{1,17},{2,18},{3,19},{4,20},{5,21},{6,22},{7,23},{8,24},{9,... | collective-permute-start | bytes 442376 | tf_op jit(solution)/shard_map/ppermute | solution.py:603
  194.0 21.7 %collective-permute-start.37 = (bf16[48,1536]{1,0:T(8,128)(2,1)}, bf16[48,1536]{1,0:T(8,128)(2,1)}, u32[]{:S(2)}, u32[]{:S(2)}) collective-permute-start(bf16[48,1536]{1,0:T(8,128)(2,1)} %get-tuple-element.260), channel_id=1, source_target_pairs={{0,8},{1,9},{2,10},{3,11},{4,12},{5,13},{6,14},{7,15},{8,16},{9,17... | collective-permute-start | bytes 442376 | tf_op jit(solution)/shard_map/ppermute | solution.py:603
  195.2 20.5 %collective-permute-start.38 = (bf16[192,512]{1,0:T(8,128)(2,1)}, bf16[192,512]{1,0:T(8,128)(2,1)S(1)}, u32[]{:S(2)}, u32[]{:S(2)}) collective-permute-start(bf16[192,512]{1,0:T(8,128)(2,1)} %add_convert_fusion.7), channel_id=1, source_target_pairs={{0,2},{1,5},{2,0},{3,7},{4,6},{5,1},{6,4},{7,3},{8,10},{9,13},{10,... | collective-permute-start | bytes 589832 | tf_op jit(solution)/shard_map/ppermute | solution.py:603
  197.8 18.0 %collective-permute-start.39 = (bf16[384,512]{1,0:T(8,128)(2,1)}, bf16[384,512]{1,0:T(8,128)(2,1)}, u32[]{:S(2)}, u32[]{:S(2)}) collective-permute-start(bf16[384,512]{1,0:T(8,128)(2,1)} %slice.361), channel_id=1, source_target_pairs={{0,4},{1,3},{2,6},{3,1},{4,0},{5,7},{6,2},{7,5},{8,12},{9,11},{10,... | collective-permute-start | bytes 1179656 | tf_op jit(solution)/shard_map/ppermute | solution.py:603
  240.6 11.9 %collective-permute-start.53 = (f32[104,128]{1,0:T(8,128)S(1)}, f32[104,128]{1,0:T(8,128)S(1)}, u32[]{:S(2)}, u32[]{:S(2)}) collective-permute-start(f32[104,128]{1,0:T(8,128)S(1)} %add.887), channel_id=1, source_target_pairs={{0,16},{2,18},{4,20},{6,22},{8,24},{10,26},{12,28},{14,30},{16,0},... | collective-permute-start | bytes 159752 | tf_op jit(solution)/shard_map/ppermute | solution.py:617
  (79 other events, 604.8 us)

commit v4 on v3

--- a/solution.py
+++ b/solution.py
@@ -21,13 +21,14 @@
 MASKED_SCORE = -1e30
 MASK_LANE = 60
 CHUNK = 512
-BACK_PARTS = ((0, 2), (2, 2), (4, 2))
+BACK_PARTS = (4, 2)
 F32 = jnp.float32
 BF16 = jnp.bfloat16
 SMEM = pl.BlockSpec(memory_space=pltpu.SMEM)
 HBM = pl.BlockSpec(memory_space=pl.ANY)
 WHOLE = pl.BlockSpec(memory_space=pltpu.VMEM)
 VMEM_BYTES = 52 * 2**20
+COST = pl.CostEstimate(flops=1000, bytes_accessed=1000, transcendentals=0)
 
 
 def params():
@@ -106,18 +107,20 @@
     return jnp.concatenate(out, axis=0)
 
 
+def columns_of(mat, width, start=0, size=None):
+    return mat // 2, pl.ds(mat % 2 * (width + LANES) + start, width if size is None else size)
+
+
 def attend_kernel(count, total, meta, tok, table, spread, *refs):
     own, other = refs[:count], refs[count:total]
-    vecs, n1, q, k, v, p, att, w_out = refs[total : total + 8]
-    toks, weights, small, aug, n1s, qs, ks, vs, ps, atts, sems, out_sems = refs[total + 8 :]
-    width = weights.shape[1]
+    vecs, n1, q, k, v, p, att, w_out, x1, n2 = refs[total : total + 10]
+    toks, weights, aug, n1s, qs, ks, vs, ps, atts, x1s, n2s, sems, out_sems = refs[total + 10 :]
+    width = toks.shape[-1]
     core = meta[64]
-    tok_copy = begin(tok, toks, sems.at[5 * PIECES])
-    own, other = ([(ref, 0) for ref in found] for found in (own, other))
-    copies = pieces_in(meta, 0, own, width, small, sems, 0)
+    copies = [begin(tok, toks, sems.at[2 * PIECES])]
     for found, at, half in ((own, 0, core), (other, 16, 1 - core)):
-        for start, mat in ((0, 2 * half), (width + LANES, 2 * half + 1)):
-            copies += pieces_in(meta, at, found, start, weights.at[mat], sems, len(copies))
+        found = [(ref, 0) for ref in found]
+        copies += pieces_in(meta, at, found, 0, weights.at[half], sems, at)
     for window in range(2):
         valid = row_valid(meta, core, window, KEYS, LANES)
         aug[window] = jnp.where(
@@ -125,18 +128,20 @@
         ).astype(BF16)
         ks[window, TOK:] = jnp.zeros((KEYS - TOK, width), BF16)
         vs[window, TOK:] = jnp.zeros((KEYS - TOK, width), BF16)
-    tok_copy.wait()
-    xhat, _ = moments(toks[...].reshape(2 * TOK, width).astype(F32))
-    finish(copies)
+    copies[0].wait()
+    tokens = toks[...].reshape(2 * TOK, width).astype(F32)
+    xhat, _ = moments(tokens)
+    finish(copies[1:])
     outs = [begin(weights, w_out, out_sems.at[0])]
-    vecs[...] = small[...].astype(F32).T[:8]
+    vecs[...] = weights[0, :, width : width + LANES].astype(F32).T[:8]
     normed = (xhat * vecs[0:1] + vecs[1:2]).astype(BF16)
     n1s[...] = normed.reshape(2, TOK, width)
     outs.append(begin(n1s, n1, out_sems.at[1]))
     for mat, (made_in, dest) in enumerate(((qs, q), (ks, k), (vs, v))):
         for start in range(0, width, 256):
             cols = pl.ds(start, 256)
-            made = dot(normed, weights[mat, :, cols])
+            half, here = columns_of(mat, width, start, 256)
+            made = dot(normed, weights[half, :, here])
             if mat != 1:
                 made = made + vecs[2 + mat // 2 : 3 + mat // 2, cols]
             made = made.astype(BF16)
@@ -168,62 +173,40 @@
         heads = pl.ds(2 * pair, 2)
         outs.append(begin(ps.at[window, heads], p.at[window, heads], out_sems.at[len(outs)]))
     outs.append(begin(atts, att, out_sems.at[len(outs)]))
+    half, here = columns_of(3, width)
+    for window in range(2):
+        resid = toks[window].astype(F32) + (dot(atts[window], weights[half, :, here]) + vecs[4:5])
+        x1s[window] = resid
+        xhat, _ = moments(resid)
+        n2s[window] = (xhat * vecs[5:6] + vecs[6:7]).astype(BF16)
+        outs.append(begin(x1s.at[window], x1.at[window], out_sems.at[len(outs)]))
+        outs.append(begin(n2s.at[window], n2.at[window], out_sems.at[len(outs)]))
     finish(outs)
 
 
 def attend(meta, tok, table, spread, own, other):
     count, total, width = len(own), len(own) + len(other), tok.shape[-1]
     rows, keys, heads = (2, TOK, width), (2, KEYS, width), (2, HEADS, TOK, KEYS)
-    mats = (4, width, width)
-    outs = (rows, rows, keys, keys, heads, rows, mats)
+    halves = (2, width, 2 * width + LANES)
+    outs = [shape(dims, BF16) for dims in (rows, rows, keys, keys, heads, rows, halves)]
+    outs += [shape(rows, F32), shape(rows, BF16)]
+    scratch = (rows, halves, (2, KEYS, LANES), rows, rows, keys, keys, heads, rows)
     return pl.pallas_call(
         partial(attend_kernel, count, total),
-        out_shape=[shape((8, width), F32)] + [shape(dims, BF16) for dims in outs],
+        out_shape=[shape((8, width), F32)] + outs,
         in_specs=[SMEM, HBM, WHOLE, WHOLE] + [HBM] * total,
         out_specs=[WHOLE] + [HBM] * len(outs),
-        scratch_shapes=[
-            pltpu.VMEM(dims, BF16)
-            for dims in (rows, mats, (width, LANES), (2, KEYS, LANES), rows, rows, keys, keys, heads, rows)
-        ]
+        scratch_shapes=[pltpu.VMEM(dims, BF16) for dims in scratch]
         + [
-            pltpu.SemaphoreType.DMA((5 * PIECES + 1,)),
-            pltpu.SemaphoreType.DMA((6 + 2 * PAIRS,)),
+            pltpu.VMEM(rows, F32),
+            pltpu.VMEM(rows, BF16),
+            pltpu.SemaphoreType.DMA((2 * PIECES + 1,)),
+            pltpu.SemaphoreType.DMA((10 + 2 * PAIRS,)),
         ],
         compiler_params=params(),
-        cost_estimate=pl.CostEstimate(
-            flops=20_000_000_000, bytes_accessed=40_000_000, transcendentals=1_500_000
-        ),
+        cost_estimate=COST,
         name="attend",
     )(meta, tok, table, spread, *own, *other)
-
-
-def join_kernel(tok, att, weights, vecs, x1, n2):
-    for window in range(2):
-        resid = tok[window].astype(F32) + (dot(att[window], weights[0]) + vecs[4:5])
-        x1[window] = resid
-        xhat, _ = moments(resid)
-        n2[window] = (xhat * vecs[5:6] + vecs[6:7]).astype(BF16)
-
-
-def join(tok, att, weights, vecs):
-    width = tok.shape[-1]
-    return pl.pallas_call(
-        join_kernel,
-        out_shape=[shape(tok.shape, F32), shape(tok.shape, BF16)],
-        grid=(1,),
-        in_specs=[
-            WHOLE,
-            WHOLE,
-            pl.BlockSpec((1, width, width), lambda i: (3, 0, 0)),
-            WHOLE,
-        ],
-        out_specs=[WHOLE] * 2,
-        compiler_params=params(),
-        cost_estimate=pl.CostEstimate(
-            flops=600_000_000, bytes_accessed=9_000_000, transcendentals=0
-        ),
-        name="join",
-    )(tok, att, weights, vecs)
 
 
 def pieces_out(meta, made, cols, keep, send, sems, first):
@@ -238,61 +221,53 @@
     return copies
 
 
-def hidden_fwd_kernel(bases, meta, n2a, n2b, dm_turned, bias, *refs):
+def hidden_fwd_kernel(bases, meta, n2a, n2b, dma, dmb, bias, *refs):
     count = len(bases)
     ins, (keep, send) = list(zip(refs[:count], bases)), refs[count : count + 2]
     w0, n2s, dms, grad, sems, out_sems = refs[count + 2 :]
     width, hidden = w0.shape
-    starts = range(0, hidden, CHUNK)
-    at = PIECES * len(starts)
-    n2_copies = [
-        begin(n2a, n2s.at[: 2 * TOK], sems.at[at]),
-        begin(n2b, n2s.at[2 * TOK :], sems.at[at + 1]),
+    at = PIECES
+    copies = [begin(n2a, n2s.at[: 2 * TOK], sems.at[at]), begin(n2b, n2s.at[2 * TOK :], sems.at[at + 1])]
+    copies += pieces_in(meta, 0, ins, 0, w0, sems, 0)
+    dm_copies = [
+        begin(dma, dms.at[: 2 * TOK], sems.at[at + 2]),
+        begin(dmb, dms.at[2 * TOK :], sems.at[at + 3]),
     ]
-    copies = [
-        pieces_in(meta, 0, ins, start, w0.at[:, pl.ds(start, CHUNK)], sems, PIECES * step)
-        for step, start in enumerate(starts)
-    ]
-    dm_copy = begin(dm_turned, dms, sems.at[at + 2])
-    finish(n2_copies)
+    finish(copies)
     outs = []
-    for step, start in enumerate(starts):
+    for start in range(0, hidden, CHUNK):
         cols = pl.ds(start, CHUNK)
-        finish(copies[step])
         inner = dot(n2s[...], w0[:, cols]) + bias[:, cols]
         act = (inner * (0.5 + 0.5 * lax.erf(inner * 0.7071067811865476))).astype(BF16)
-        if step == 0:
-            dm_copy.wait()
-        grad[:, cols] = dot(dms[...], act).astype(BF16)
-        outs += pieces_out(meta, grad, cols, keep, send, out_sems, len(outs))
+        if start == 0:
+            finish(dm_copies)
+        grad[:, cols] = dot_tn(dms[...], act).astype(BF16)
+        if start + CHUNK == hidden - CHUNK:
+            outs += pieces_out(meta, grad, pl.ds(0, hidden - CHUNK), keep, send, out_sems, 0)
+    outs += pieces_out(meta, grad, pl.ds(hidden - CHUNK, CHUNK), keep, send, out_sems, PIECES)
     finish(outs)
 
 
-def hidden_fwd(meta, n2a, n2b, dm_turned, bias, ins):
+def hidden_fwd(meta, n2a, n2b, dma, dmb, bias, ins):
     refs, bases = zip(*ins)
     width, hidden = n2a.shape[-1], bias.shape[-1]
-    steps = hidden // CHUNK
     return pl.pallas_call(
         partial(hidden_fwd_kernel, bases),
         out_shape=[shape((width // 2, hidden), BF16)] * 2,
-        in_specs=[SMEM] + [HBM] * 3 + [WHOLE] + [HBM] * len(refs),
+        in_specs=[SMEM] + [HBM] * 4 + [WHOLE] + [HBM] * len(refs),
         out_specs=[HBM] * 2,
         scratch_shapes=[
             pltpu.VMEM((width, hidden), BF16),
             pltpu.VMEM((4 * TOK, width), BF16),
-            pltpu.VMEM((width, 4 * TOK), BF16),
+            pltpu.VMEM((4 * TOK, width), BF16),
             pltpu.VMEM((width, hidden), BF16),
-            pltpu.SemaphoreType.DMA((PIECES * steps + 3,)),
-            pltpu.SemaphoreType.DMA((PIECES * steps,)),
+            pltpu.SemaphoreType.DMA((PIECES + 4,)),
+            pltpu.SemaphoreType.DMA((2 * PIECES,)),
         ],
         compiler_params=params(),
-        cost_estimate=pl.CostEstimate(
-            flops=12 * 4 * TOK * width * hidden,
-            bytes_accessed=12_000_000,
-            transcendentals=4 * TOK * hidden,
-        ),
+        cost_estimate=COST,
         name="hidden_fwd",
-    )(meta, n2a, n2b, dm_turned, bias, *refs)
+    )(meta, n2a, n2b, dma, dmb, bias, *refs)
 
 
 def hidden_back_kernel(bases0, bases1, meta, n2a, n2b, dma, dmb, bias, *refs):
@@ -300,34 +275,22 @@
     ins0, ins1 = list(zip(refs[:count], bases0)), list(zip(refs[count : 2 * count], bases1))
     refs = refs[2 * count :]
     bias_grad, keep, send, back_own, back_far, out_own, out_far = refs[:7]
-    w0, w1, n2s, n2t, dms, acts, backs, grad, big, small, sems, out_sems = refs[7:]
+    w0, w1, n2s, dms, acts, backs, grad, big, small, sems, out_sems = refs[7:]
     width, hidden = w0.shape
-    starts = range(0, hidden, CHUNK)
     halves = (pl.ds(0, 2 * TOK), pl.ds(2 * TOK, 2 * TOK))
-    at = 2 * PIECES * len(starts)
-    n2_copies = [
-        begin(ref, n2s.at[half], sems.at[at + i]) for i, (ref, half) in enumerate(zip((n2a, n2b), halves))
-    ]
-    copies = []
-    for step, start in enumerate(starts):
+    at = 2 * PIECES
+    copies = [begin(ref, n2s.at[half], sems.at[at + i]) for i, (ref, half) in enumerate(zip((n2a, n2b), halves))]
+    copies += pieces_in(meta, 0, ins0, 0, w0, sems, 0)
+    at += 2
+    later = [begin(ref, dms.at[half], sems.at[at + i]) for i, (ref, half) in enumerate(zip((dma, dmb), halves))]
+    later += pieces_in(meta, 0, ins1, 0, w1, sems, PIECES)
+    finish(copies)
+    outs = []
+    for start in range(0, hidden, CHUNK):
         cols = pl.ds(start, CHUNK)
-        copies.append(pieces_in(meta, 0, ins0, start, w0.at[:, cols], sems, 2 * PIECES * step))
-        if step == 0:
-            dm_copies = [
-                begin(ref, dms.at[half], sems.at[at + 2 + i])
-                for i, (ref, half) in enumerate(zip((dma, dmb), halves))
-            ]
-        copies.append(pieces_in(meta, 0, ins1, start, w1.at[:, cols], sems, 2 * PIECES * step + PIECES))
-    finish(n2_copies)
-    n2t[...] = n2s[...].T
-    outs = []
-    for step, start in enumerate(starts):
-        cols = pl.ds(start, CHUNK)
-        finish(copies[2 * step])
         inner = dot(n2s[...], w0[:, cols]) + bias[:, cols]
-        if step == 0:
-            finish(dm_copies)
-        finish(copies[2 * step + 1])
+        if start == 0:
+            finish(later)
         back = dot(dms[...], w1[:, cols])
         cdf = 0.5 + 0.5 * lax.erf(inner * 0.7071067811865476)
         density = jnp.exp(inner * inner * -0.5) * 0.3989422804014327
@@ -335,8 +298,8 @@
         back_pre = (back * (cdf + inner * density)).astype(BF16)
         backs[:, cols] = back_pre
         bias_grad[:, cols] = jnp.sum(back_pre.astype(F32), axis=0, keepdims=True)
-        grad[:, cols] = dot(n2t[...], back_pre).astype(BF16)
-        outs += pieces_out(meta, grad, cols, keep, send, out_sems, len(outs))
+        grad[:, cols] = dot_tn(n2s[...], back_pre).astype(BF16)
+    outs = pieces_out(meta, grad, pl.ds(0, hidden), keep, send, out_sems, 0)
     for which, (left, right, own, far) in enumerate(
         ((backs, w0, back_own, back_far), (acts, w1, out_own, out_far))
     ):
@@ -350,7 +313,6 @@
 def hidden_back(meta, n2a, n2b, dma, dmb, bias, ins0, ins1):
     (refs0, bases0), (refs1, bases1) = zip(*ins0), zip(*ins1)
     width, hidden = n2a.shape[-1], bias.shape[-1]
-    steps = hidden // CHUNK
     one = (2 * TOK, width)
     tall = pltpu.VMEM((4 * TOK, width), BF16)
     wide = pltpu.VMEM((width, hidden), BF16)
@@ -365,22 +327,17 @@
             wide,
             wide,
             tall,
-            pltpu.VMEM((width, 4 * TOK), BF16),
             tall,
             pltpu.VMEM((4 * TOK, hidden), BF16),
             pltpu.VMEM((4 * TOK, hidden), BF16),
             wide,
             pltpu.VMEM((2,) + one, F32),
             pltpu.VMEM((2,) + one, BF16),
-            pltpu.SemaphoreType.DMA((2 * PIECES * steps + 4,)),
-            pltpu.SemaphoreType.DMA((PIECES * steps + 4,)),
+            pltpu.SemaphoreType.DMA((2 * PIECES + 4,)),
+            pltpu.SemaphoreType.DMA((PIECES + 4,)),
         ],
         compiler_params=params(),
-        cost_estimate=pl.CostEstimate(
-            flops=24 * 4 * TOK * width * hidden,
-            bytes_accessed=20_000_000,
-            transcendentals=8 * TOK * hidden,
-        ),
+        cost_estimate=COST,
         name="hidden_back",
     )(meta, n2a, n2b, dma, dmb, bias, *refs0, *refs1)
 
@@ -395,9 +352,9 @@
     return jnp.concatenate(out, axis=0)
 
 
-def attend_back_kernel(start, count, meta, vecs, gather, table, q, k, v, p, weights, att, n1, *refs):
+def attend_back_kernel(before, count, meta, vecs, gather, table, q, k, v, p, weights, att, n1, *refs):
+    start, parts = sum(before), len(before)
     first, last = start == 0, start + count == PAIRS
-    parts = start // count
     if first:
         back_own, back_far, x1, dm = refs[:4]
         norm_sums, bias_sums, table_grad, mine, theirs, dqkv_out, dx1, da = refs[4:12]
@@ -415,7 +372,7 @@
         else:
             bias_sums, table_grad, mine, theirs, dqkv_out = refs[:5]
             refs = refs[5:]
-    das, wproj, atts, n1s, qs, ks, vs, ps, dat, dqkv, grads, turned_in, sems, out_sems = refs
+    das, wproj, atts, n1s, qs, ks, vs, ps, dat, dqkv, grads, sems, out_sems = refs
     core = meta[64]
     width, cols_here = das.shape[-1], qs.shape[-1]
     rows = width // PIECES
@@ -427,7 +384,8 @@
     else:
         early = [(da, das)]
     early = [begin(ref, dest, sems.at[at]) for at, (ref, dest) in enumerate(early)]
-    wait_proj = begin(weights.at[3, columns, :], wproj, sems.at[4])
+    half, here = columns_of(3, width)
+    wait_proj = begin(weights.at[half, columns, here], wproj, sems.at[4])
     wait_att = begin(att, atts, sems.at[5])
     wait_v = begin(v.at[:, :, columns], vs, sems.at[6])
     wait_p = []
@@ -446,7 +404,9 @@
     if last:
         at = 10 + 2 * count
         ends = [begin(tok, toks, sems.at[at]), begin(dx1, dx1s, sems.at[at + 1])]
-        ends += [begin(weights.at[mat], wqkv.at[mat], sems.at[at + 2 + mat]) for mat in range(3)]
+        for mat in range(3):
+            half, here = columns_of(mat, width)
+            ends.append(begin(weights.at[half, :, here], wqkv.at[mat], sems.at[at + 2 + mat]))
         for part in range(parts):
             ends.append(begin(changes[part], changed[part], sems.at[at + 5 + part]))
     outs = []
@@ -465,28 +425,26 @@
             for slot, value in enumerate((rounded.astype(F32), grad * xhat, grad, out_grad)):
                 total[slot] = total[slot] + jnp.sum(value, axis=0, keepdims=True)
         norm_sums[...] = jnp.concatenate(total, axis=0)
-        outs.append(begin(dx1s, dx1, out_sems.at[4 * PIECES]))
-        outs.append(begin(das, da, out_sems.at[4 * PIECES + 1]))
+        outs.append(begin(dx1s, dx1, out_sems.at[2 * PIECES]))
+        outs.append(begin(das, da, out_sems.at[2 * PIECES + 1]))
     wait_proj.wait()
     dat[...] = dot_nt(das[...].reshape(tokens), wproj[...]).astype(BF16).reshape(2, TOK, cols_here)
 
-    def send(mat, made):
-        grads[mat] = made.astype(BF16)
-        is_own = core == mat // 2
+    def send(half):
+        is_own = core == half
         at = jnp.where(is_own, 32, 48)
         for piece in range(PIECES):
             place = pl.multiple_of(meta[at + piece] * rows, rows)
-            source = grads.at[mat, pl.ds(place, rows), :]
-            to = pl.ds(piece * rows, rows), pl.ds(mat % 2 * cols_here, cols_here)
-            sem = out_sems.at[mat * PIECES + piece]
-            copies = [pltpu.make_async_copy(source, ref.at[to], sem) for ref in (mine, theirs)]
+            source, to = grads.at[half, pl.ds(place, rows), :], pl.ds(piece * rows, rows)
+            sem = out_sems.at[half * PIECES + piece]
+            copies = [pltpu.make_async_copy(source, ref.at[to, :], sem) for ref in (mine, theirs)]
             pl.when(is_own)(copies[0].start)
             pl.when(~is_own)(copies[1].start)
             outs.append(copies[0])
 
     wait_att.wait()
-    turned_in[...] = atts[...].reshape(tokens).T
-    send(3, dot(turned_in[...], das[:, :, columns].reshape(2 * TOK, cols_here)))
+    made = dot_tn(atts[...].reshape(tokens), das[:, :, columns].reshape(2 * TOK, cols_here))
+    grads[1, :, cols_here:] = made.astype(BF16)
     finish(wait_qk + [wait_v])
     place = lanes(TOK)
     table_sum = jnp.zeros((LANES, LANES), F32)
@@ -516,12 +474,14 @@
         table_sum = table_sum + jnp.where(lanes(LANES) < 64, dts[0], dts[1])
     table_grad[...] = table_sum
     if not last:
-        outs.append(begin(dqkv, dqkv_out, out_sems.at[4 * PIECES + 2]))
+        outs.append(begin(dqkv, dqkv_out, out_sems.at[2 * PIECES + 2]))
     wait_n1.wait()
-    turned_in[...] = n1s[...].reshape(tokens).T
-    for mat in range(3):
+    for mat in (2, 0, 1):
         change = dqkv[mat].reshape(2 * TOK, cols_here)
-        send(mat, dot(turned_in[...], change))
+        made = dot_tn(n1s[...].reshape(tokens), change)
+        grads[mat // 2, :, pl.ds(mat % 2 * cols_here, cols_here)] = made.astype(BF16)
+        if mat != 0:
+            send(mat // 2)
         if mat != 1:
             bias_sums[mat // 2 : mat // 2 + 1] = jnp.sum(change.astype(F32), axis=0, keepdims=True)
     if last:
@@ -529,22 +489,25 @@
         total = [jnp.zeros((1, width), F32) for _ in range(2)]
         for window in range(2):
             grad = jnp.zeros((TOK, width), F32)
-            for part, change in enumerate([*changed, dqkv]):
-                here = pl.ds(part * cols_here, cols_here)
+            at = 0
+            for change in (*changed, dqkv):
+                here = pl.ds(at, change.shape[-1])
                 for mat in range(3):
                     grad = grad + dot_nt(change[mat, window], wqkv[mat, :, here])
+                at += change.shape[-1]
             xhat, inverse = moments(toks[window].astype(F32))
             results[window] = dx1s[window] + norm_back(grad, xhat, inverse, vecs[0:1])
-            outs.append(begin(results.at[window], result.at[window], out_sems.at[4 * PIECES + window]))
+            outs.append(begin(results.at[window], result.at[window], out_sems.at[2 * PIECES + window]))
             for slot, value in enumerate((grad * xhat, grad)):
                 total[slot] = total[slot] + jnp.sum(value, axis=0, keepdims=True)
         norm_sums[...] = jnp.concatenate(total, axis=0)
     finish(outs)
 
 
-def attend_back(start, count, meta, vecs, gather, table, q, k, v, p, weights, att, n1, ins):
+def attend_back(before, count, meta, vecs, gather, table, q, k, v, p, weights, att, n1, ins):
     width, cols_here = q.shape[-1], count * LANES
-    first, last, parts = start == 0, start + count == PAIRS, start // count
+    start, parts = sum(before), len(before)
+    first, last = start == 0, start + count == PAIRS
     rows, keys = (2, TOK, width), (2, KEYS, cols_here)
     part, flat = (2, TOK, cols_here), (2 * TOK, width)
     heads = (2, 2 * count, TOK, KEYS)
@@ -557,9 +520,9 @@
         small = [shape((4, width), F32)] + small
         large += [shape(rows, F32), shape(rows, BF16)]
     scratch = [rows, (cols_here, width), rows, rows, part, keys, keys, heads, part, (3,) + part]
-    scratch += [(4, width, cols_here), (width, 2 * TOK)]
+    scratch.append((2, width, 2 * cols_here))
     scratch = [pltpu.VMEM(dims, BF16) for dims in scratch]
-    scratch += [pltpu.SemaphoreType.DMA((15 + 2 * count + parts,)), pltpu.SemaphoreType.DMA((4 * PIECES + 3,))]
+    scratch += [pltpu.SemaphoreType.DMA((15 + 2 * count + parts,)), pltpu.SemaphoreType.DMA((2 * PIECES + 3,))]
     if first:
         scratch += [
             pltpu.VMEM(flat, F32),
@@ -574,17 +537,15 @@
             pltpu.VMEM(rows, BF16),
             pltpu.VMEM(rows, F32),
             pltpu.VMEM(rows, F32),
-        ] + [pltpu.VMEM((3,) + part, BF16)] * parts
+        ] + [pltpu.VMEM((3, 2, TOK, size * LANES), BF16) for size in before]
     return pl.pallas_call(
-        partial(attend_back_kernel, start, count),
+        partial(attend_back_kernel, before, count),
         out_shape=small + large,
         in_specs=[SMEM] + [WHOLE] * 3 + [HBM] * (7 + len(ins)),
         out_specs=[WHOLE] * len(small) + [HBM] * len(large),
         scratch_shapes=scratch,
         compiler_params=params(),
-        cost_estimate=pl.CostEstimate(
-            flops=8_000_000_000 * count, bytes_accessed=10_000_000 * count, transcendentals=0
-        ),
+        cost_estimate=COST,
         name="attend_back",
     )(meta, vecs, gather, table, q, k, v, p, weights, att, n1, *ins)
 
@@ -667,6 +628,7 @@
         half = self.keep.shape[0] // 2
         send = add(self.keep[half:], self.came[0][half:]).astype(BF16)
         self.near = add(self.keep[:half], self.came[0][:half])
+        self.sent = send
         self.came = [turn(send, self.dims, FIRST)]
 
     def third(self):
@@ -677,6 +639,22 @@
             turn(near[step * rows : (step + 1) * rows].astype(BF16), self.dims, ((0, self.dims[0] - step),) * 2)
             for step in range(1, self.dims[0])
         ]
+
+    def halve(self):
+        near = self.near + self.came[0].astype(F32)
+        rows = near.shape[0] // self.dims[0]
+        parts = [near[step * rows : (step + 1) * rows] for step in range(self.dims[0])]
+        even = lax.axis_index("dp") // (self.dims[1] * self.dims[2]) % 2 == 0
+        self.near = parts[0]
+        self.beside = jnp.where(even, parts[3], parts[1])
+        send = jnp.concatenate([parts[2], jnp.where(even, parts[1], parts[3])], axis=0).astype(BF16)
+        self.came = [swap_z(send, self.dims, 2)]
+
+    def quarter(self):
+        rows = self.near.shape[0]
+        came = self.came[0]
+        self.near = self.near + came[:rows].astype(F32)
+        self.came = [swap_z((self.beside + came[rows:].astype(F32)).astype(BF16), self.dims, 1)]
 
     def last(self):
         return sum((part.astype(F32) for part in self.came), self.near)
@@ -768,8 +746,6 @@
         jnp.arange(WIN)[None, None, :] < widths[:, None, None]
     )
     dm = padded(jnp.where(valid[..., None], out_grad, jnp.zeros_like(out_grad)))
-    dm_far = other_core(dm)
-
     vectors = (norm1_gain, norm1_bias, qv_bias[0], qv_bias[1], proj_bias, norm2_gain, norm2_bias, fc2_bias)
     small = jnp.pad(jnp.stack(vectors, axis=1), ((0, 0), (0, LANES - len(vectors))))
     qk = jnp.concatenate([qkv_weight[:, :width], small, qkv_weight[:, width : 2 * width]], axis=1)
@@ -779,70 +755,70 @@
         vp = lax.all_gather(vp, ("dp", "mp"), axis=0, tiled=True)
         attend_own = [jnp.where(is_first, qk, vp)]
         attend_far = [jnp.where(is_first, vp, qk)]
+        dm_far = other_core(dm)
         hidden_in = tuple(
             ((lax.all_gather(part, "dp", axis=0, tiled=True), 0),) for part in (fc1_weight, fc2_weight.T)
         )
     else:
         fc1, fc2 = fc1_weight, fc2_weight.T
         came = other_core(jnp.where(is_first, vp, qk))
+        own_h = jnp.concatenate([fc1, fc2], axis=1)
+        beside_h = turn(own_h, dims, FIRST)
         near = jnp.where(is_first, qk, vp)
         block = jnp.concatenate(
             [jnp.where(is_first, near, came), jnp.where(is_first, came, near)], axis=0
         )
-        attend_size, hidden_size = block.shape[1], fc1.shape[1]
-        own = jnp.concatenate([block, fc1, fc2], axis=1)
-        attend_z, beside = Flow(*along_z(block, dims)), Flow(turn(own, dims, FIRST))
-        dm_flow = Flow(dm_far)
-        fc1, fc2 = meet([attend_z, beside, dm_flow], fc1, fc2)
-        dm_far = dm_flow.came[0]
-
-        own = jnp.concatenate([own, *beside.came], axis=0)
-        over = Flow(turn(own, dims, SECOND))
-        attend_z = jnp.concatenate(attend_z.came, axis=0)
-        z_beside, fc1_z = Flow(turn(attend_z, dims, FIRST)), Flow(*along_z(fc1, dims))
-        (fc2,) = meet([over, z_beside, fc1_z], fc2)
-
-        over = over.came[0]
-        attend_z = jnp.concatenate([attend_z, *z_beside.came], axis=0)
-        fc1_z = jnp.concatenate(fc1_z.came, axis=0)
-        z_over, fc1_beside = Flow(turn(attend_z, dims, SECOND)), Flow(turn(fc1_z, dims, FIRST))
-        fc2_z = Flow(*along_z(fc2, dims))
-        own_attend = jnp.concatenate([own[:, :attend_size], over[:, :attend_size]], axis=0)
-        own_attend, attend_z = meet([z_over, fc1_beside, fc2_z], own_attend, attend_z)
-
-        z_over = z_over.came[0]
-        far = Flow(*(other_core(part) for part in (own_attend, attend_z, z_over)))
-        fc1_z = jnp.concatenate([fc1_z, *fc1_beside.came], axis=0)
-        fc1_over = Flow(turn(fc1_z, dims, SECOND))
-        fc2_z = jnp.concatenate(fc2_z.came, axis=0)
-        fc2_beside = Flow(turn(fc2_z, dims, FIRST))
-        tok, fc1_z, fc2_z = meet([far], tok, fc1_z, fc2_z)
-        attend_own, attend_far = [own, over, attend_z, z_over], far.came
+        attend_z = along_z(block, dims)
+        beside = turn(block, dims, FIRST)
+        own_h = jnp.concatenate([own_h, beside_h], axis=0)
+        over_h = turn(own_h, dims, SECOND)
+        own = jnp.concatenate([block, after(beside, own_h)], axis=0)
+        over = turn(own, dims, SECOND)
+        attend_z = jnp.concatenate([after(attend_z[0], own)] + attend_z[1:], axis=0)
+        z_beside = turn(attend_z, dims, FIRST)
+        fc1_z = along_z(after(fc1, attend_z), dims)
+        over, over_h, z_beside = meet([], over, over_h, z_beside)
+        own = jnp.concatenate([own, over], axis=0)
+        far = [other_core(own)]
+        attend_z = jnp.concatenate([attend_z, z_beside], axis=0)
+        z_over = turn(attend_z, dims, SECOND)
+        fc1_z = jnp.concatenate([after(fc1_z[0], attend_z)] + fc1_z[1:], axis=0)
+        fc1_beside = turn(fc1_z, dims, FIRST)
+        fc2_z = along_z(after(fc2, fc1_z), dims)
+        far.append(other_core(after(attend_z, fc1_z)))
+        z_over = after(z_over, fc1_z)
+        far.append(other_core(z_over))
+        fc1_z = jnp.concatenate([fc1_z, after(fc1_beside, z_over)], axis=0)
+        fc1_over = turn(fc1_z, dims, SECOND)
+        attend_own, attend_far = [own, attend_z, z_over], far
+        dm_far = other_core(after(dm, z_over))
+        tok = after(tok, fc1_z)
 
     dm_flat, dm_far = dm.reshape(-1, width), dm_far.reshape(-1, width)
-    dm_turned = jnp.concatenate([dm_flat, dm_far], axis=0).T
     spread, gather = constants()
     table, table_back = tables(rel_pos_h, rel_pos_w)
 
-    vecs, n1, q, k, v, p, att, weights = attend(
+    vecs, n1, q, k, v, p, att, weights, x1, n2 = attend(
         meta, tok, table, jnp.asarray(spread, BF16), attend_own, attend_far
     )
     if dims is not None:
-        (att,) = meet([fc1_over, fc2_beside], att)
-        fc2_z = jnp.concatenate([fc2_z, *fc2_beside.came], axis=0)
-        fc2_over = Flow(turn(fc2_z, dims, SECOND))
-        att = after(att, fc2_z)
-    x1, n2 = join(tok, att, weights, vecs)
+        fc2_z = jnp.concatenate([after(fc2_z[0], n2)] + fc2_z[1:], axis=0)
+        fc2_beside = turn(fc2_z, dims, FIRST)
     n2_far = other_core(n2).reshape(-1, width)
     n2 = n2.reshape(-1, width)
     bias = fc1_bias[None].astype(F32)
     if dims is not None:
-        places = (attend_size, attend_size), (attend_size + hidden_size,) * 2
-        hidden_in = [tuple(zip((own, over, fc1_z, *fc1_over.came), (*places[0], 0, 0)))]
-    fc2_part = hidden_fwd(meta, n2, n2_far, dm_turned, bias, hidden_in[0])
+        fc2_z = jnp.concatenate([fc2_z, after(fc2_beside, n2)], axis=0)
+        fc2_over = turn(fc2_z, dims, SECOND)
+        n2 = after(n2, fc2_z)
+        size = fc1.shape[1]
+        hidden_in = [
+            ((own_h, 0), (over_h, 0), (fc1_z, 0), (fc1_over, 0)),
+            ((own_h, size), (over_h, size), (fc2_z, 0), (fc2_over, 0)),
+        ]
+    fc2_part = hidden_fwd(meta, n2, n2_far, dm_flat, dm_far, bias, hidden_in[0])
     if dims is not None:
-        fc2_part = meet([fc2_over], *fc2_part)
-        hidden_in.append(tuple(zip((own, over, fc2_z, *fc2_over.came), (*places[1], 0, 0))))
+        fc2_part = meet([], *fc2_part, fc2_over)[:2]
         fc2_sum = Scatter(*fc2_part, dims)
     fc1_bias_part, *fc1_part, back_own, back_far, out_own, out_far = hidden_back(
         meta, n2, n2_far, dm_flat, dm_far, bias, *hidden_in
@@ -852,17 +828,18 @@
         fc1_part = meet([fc2_sum], *fc1_part)
         fc2_sum.second()
         fc1_sum = Scatter(*fc1_part, dims)
-    out_far = other_core(out_far)
+        back_own = after(back_own, fc2_sum.sent)
 
     shared = (meta, vecs, jnp.asarray(gather, BF16), table_back, q, k, v, p, weights, att, n1)
     bias_sums, table_grad, attend_sums, changes = [], 0.0, [], []
     ins = (back_own, back_far, x1, dm)
     half = width // 2
-    for start, count in BACK_PARTS:
-        made = attend_back(start, count, *shared, ins)
-        if start == 0:
+    for part, count in enumerate(BACK_PARTS):
+        last = part == len(BACK_PARTS) - 1
+        made = attend_back(BACK_PARTS[:part], count, *shared, ins)
+        if part == 0:
             sums2, *made, dx1, da = made
-        if start + count == PAIRS:
+        if last:
             sums1, *made = made
         bias_sums.append(made[0])
         table_grad = table_grad + made[1]
@@ -872,26 +849,16 @@
             attend_sums.append(
                 lax.psum_scatter(add(mine, other_core(theirs)), "dp", scatter_dimension=0, tiled=True)
             )
-        elif start + count < PAIRS:
+        elif not last:
             came = Flow(other_core(theirs))
-            if start == 0:
-                da, mine = meet([fc2_sum, fc1_sum], da, mine)
-                fc2_sum.third()
-                fc1_sum.second()
-            else:
-                da, mine = meet([fc2_sum, fc1_sum, *attend_sums], da, mine)
-                fc2_sum = fc2_sum.last()
-                fc1_sum.third()
-                attend_sums[0].second()
+            da, mine = meet([fc2_sum, fc1_sum], da, mine)
+            fc2_sum.third()
+            fc1_sum.second()
             both = add(mine, came.came[0]).astype(BF16)
-            attend_sums.append(Scatter(both[:half], both[half:], dims))
+            first = Scatter(both[:half], both[half:], dims)
             da = after(da, both)
-        ins = (da,) if start + 2 * count < PAIRS else (da, tok, dx1, *changes)
+        ins = (da, tok, dx1, *changes)
     result = change
-    branch = add(out_own, out_far).reshape(x1.shape) + vecs[7]
-    block_out = unpadded(x1 + branch)
-    block_out = jnp.where(valid[..., None], block_out, 0.0).astype(BF16)
-
     qv_sums = jnp.concatenate(bias_sums, axis=1)
     rel_sums = table_grad[:64, :HDIM] + table_grad[:64, HDIM:]
     fc1_sums = jnp.concatenate(
@@ -907,6 +874,7 @@
     )
     if dims is None:
         flat = lax.psum(flat + other_core(flat), "dp")
+        out_far = other_core(out_far)
         fc1_sum, fc2_sum = (
             lax.psum_scatter(
                 jnp.concatenate(parts, axis=0).astype(F32), "dp", scatter_dimension=0, tiled=True
@@ -914,48 +882,47 @@
             for parts in (fc1_part, fc2_part)
         )
     else:
-        mine, theirs, flat = meet([fc1_sum, *attend_sums], mine, theirs, flat)
+        mine, theirs, flat, out_far = meet([fc2_sum, fc1_sum, first], mine, theirs, flat, out_far)
         came, flat_came = Flow(other_core(theirs)), Flow(other_core(flat))
-        attend_sums[1].second()
-        fc1_sum = fc1_sum.last()
-        mine, flat = meet([came, flat_came, attend_sums[1]], mine, flat)
+        first.second()
+        fc1_sum.halve()
+        mine, flat, out_far = meet([came, flat_came, first], mine, flat, out_far)
         both = add(mine, came.came[0]).astype(BF16)
-        attend_sums.append(Scatter(both[:half], both[half:], dims))
+        second = Scatter(both[:half], both[half:], dims)
         flat = flat + flat_came.came[0]
         flat_came = Flow(turn(flat, dims, SECOND))
-        attend_sums[0].third()
-        (flat,) = meet([flat_came, attend_sums[0], attend_sums[2]], flat)
+        first.halve()
+        fc2_sum = fc2_sum.last()
+        out_far = other_core(out_far)
+        flat, result = meet([flat_came, second, fc1_sum], flat, result)
         flat = flat + flat_came.came[0]
         flat_came = Flow(turn(flat, dims, FIRST))
-        attend_sums[2].second()
-        attend_sums[1].third()
-        attend_sums[0] = attend_sums[0].last()
-        (flat,) = meet([flat_came, attend_sums[1], attend_sums[2]], flat)
+        second.second()
+        fc1_sum.quarter()
+        flat, out_far = meet([flat_came, first, second, fc1_sum], flat, out_far)
         flat = flat + flat_came.came[0]
         flat_came = Flow(swap_z(flat, dims, 2))
-        attend_sums[2].third()
-        attend_sums[1] = attend_sums[1].last()
-        (flat,) = meet([flat_came, attend_sums[2]], flat)
+        second.third()
+        first.quarter()
+        fc1_sum = fc1_sum.last()
+        flat, fc1_sum = meet([flat_came, second, first], flat, fc1_sum)
         flat = flat + flat_came.came[0]
         flat = flat + swap_z(flat, dims, 1)
-        attend_sums[2] = attend_sums[2].last()
-
-    whole = jnp.concatenate(attend_sums, axis=1)
-    rows = whole.shape[0] // 2
-    near = jnp.where(is_first, whole[:rows], whole[rows:])
-    came = other_core(jnp.where(is_first, whole[rows:], whole[:rows]))
-    halves = [[], []]
-    at = 0
-    for _, count in BACK_PARTS:
-        for half in range(2):
-            halves[half].append(slice(at, at + count * LANES))
-            at += count * LANES
-    qk, vp = jnp.where(is_first, near, came), jnp.where(is_first, came, near)
-    q_grad, k_grad, v_grad, proj_grad = (
-        jnp.concatenate([found[:, cols] for cols in half], axis=1)
-        for found in (qk, vp)
-        for half in halves
-    )
+        attend_sums = [first.last(), second.last()]
+    branch = add(out_own, out_far).reshape(x1.shape) + vecs[7]
+    block_out = unpadded(x1 + branch)
+    block_out = jnp.where(valid[..., None], block_out, 0.0).astype(BF16)
+
+    whole = jnp.stack(
+        [
+            jnp.concatenate([part[:, at * (part.shape[1] // 2) :][:, : part.shape[1] // 2] for part in attend_sums], axis=1)
+            for at in range(2)
+        ]
+    )
+    rows = whole.shape[1] // 2
+    near = jnp.where(is_first, whole[:, :rows], whole[:, rows:])
+    came = other_core(jnp.where(is_first, whole[:, rows:], whole[:, :rows]))
+    (q_grad, k_grad), (v_grad, proj_grad) = jnp.where(is_first, near, came), jnp.where(is_first, came, near)
     qkv_grad = jnp.concatenate([q_grad, k_grad, v_grad], axis=1)
     at = 8 * width // LANES
     vec_sums = flat[:at].reshape(8, width)

time: 264 us -> 232 us (0.88)
  Pallas kernels: 84 us -> 71.3 us
  starting transfers between devices: 69.2 us -> 61.5 us
  waiting for transfers between devices: 62.1 us -> 55.7 us
  local copies, waits for them, and re-layouts: 26.5 us -> 20.4 us
    ppermute x44 -> x35, waiting for transfers between devices: 54.2 us -> 40.5 us  [turn(): return lax.ppermute(values, ('dp', 'mp'), pairs)]
    ppermute x44 -> x35, starting transfers between devices: 64.5 us -> 52.5 us  [turn(): return lax.ppermute(values, ('dp', 'mp'), pairs)]
    pallas_call x4 -> x2, Pallas kernels: 39.9 us -> 30.2 us  [attend_back(): pl.pallas_call(partial(attend_back_kernel, before, count), out_shape=smal...]
    ppermute x2 -> x6, waiting for transfers between devices: 3.95 us -> 13 us  [swap_z(): return lax.ppermute(values, 'dp', pairs)]
    ppermute x2 -> x6, starting transfers between devices: 2.31 us -> 6.83 us  [swap_z(): return lax.ppermute(values, 'dp', pairs)]
    unnamed x110 -> x83, local copies, waits for them, and re-layouts: 14.6 us -> 11.1 us
    add x0 -> x2, other arithmetic: none -> 2.87 us  [halve(): near = self.near + self.came[0].astype(F32)]
    pallas_call x1, Pallas kernels: 20.4 us -> 17.6 us  [hidden_back(): pl.pallas_call(partial(hidden_back_kernel, bases0, bases1), out_shape=[sh...]
  transfers between devices with their start and end apart: 59 -> 53, of which waited for: 23 -> 18; matrix products, arithmetic and copies ran while one was open for 11% -> 11% of each run, Pallas kernels for 23% -> 31%
where the time goes in v4:
time: 232 us; the launch traced here: 228 us
  Pallas kernels  71.3 us (31%)
  starting transfers between devices  61.5 us (27%)
  waiting for transfers between devices  55.7 us (24%)
  local copies, waits for them, and re-layouts  20.4 us (9%)
  other arithmetic  17.5 us (8%)
    ppermute x35, starting transfers between devices, turn(): return lax.ppermute(values, ('dp', 'mp'), pairs)  52.5 us
    ppermute x35, waiting for transfers between devices, turn(): return lax.ppermute(values, ('dp', 'mp'), pairs)  40.5 us
    pallas_call x2, Pallas kernels, attend_back(): pl.pallas_call(partial(attend_back_kernel, before, count), out_shape=smal...  30.2 us
    pallas_call x1, Pallas kernels, hidden_back(): pl.pallas_call(partial(hidden_back_kernel, bases0, bases1), out_shape=[sh...  17.6 us
    pallas_call x1, Pallas kernels, attend(): pl.pallas_call(partial(attend_kernel, count, total), out_shape=[shape((8,...  14.1 us
    ppermute x6, waiting for transfers between devices, swap_z(): return lax.ppermute(values, 'dp', pairs)  13 us
    unnamed x83, local copies, waits for them, and re-layouts  11.1 us
    pallas_call x1, Pallas kernels, hidden_fwd(): pl.pallas_call(partial(hidden_fwd_kernel, bases), out_shape=[shape((width...  9.41 us
  transfers between devices with their start and end apart: 53, of which 18 were waited for; matrix products, arithmetic and copies ran while one was open for 11% of the time, Pallas kernels for 31%

profile of v4, /device:TPU:0, one launch (start us, length us, event | category | flops | bytes accessed | tf_op | source)
XLA Modules:
  0.0 228.2 jit_solution(1903749658773937711)
XLA Ops:
  5.4 2.6 %collective-permute-start.3 = (bf16[48,3072]{1,0:T(8,128)(2,1)S(1)}, bf16[48,3072]{1,0:T(8,128)(2,1)S(1)}, u32[]{:S(2)}, u32[]{:S(2)}) collective-permute-start(bf16[48,3072]{1,0:T(8,128)(2,1)S(1)} %pad_maximum_fusion.4), channel_id=1, source_target_pairs={{0,2},{1,5},{2,0},{3,7},{4,6},{5,1},{6,4},{7,3},{8,10},{9,13},{10,... | collective-permute-start | bytes 884744 | tf_op jit(solution)/shard_map/ppermute | solution.py:564
  9.1 1.9 collective-permute-start.1
  11.0 2.6 %collective-permute-start.4 = (bf16[48,1664]{1,0:T(8,128)(2,1)S(1)}, bf16[48,1664]{1,0:T(8,128)(2,1)S(1)}, u32[]{:S(2)}, u32[]{:S(2)}) collective-permute-start(bf16[48,1664]{1,0:T(8,128)(2,1)S(1)} %pad_maximum_fusion.8), channel_id=1, source_target_pairs={{0,16},{1,17},{2,18},{3,19},{4,20},{5,21},{6,22},{7,23},{8,24},{9,... | collective-permute-start | bytes 479240 | tf_op jit(solution)/shard_map/ppermute | solution.py:564
  18.8 5.4 %collective-permute-done.4 = bf16[48,1664]{1,0:T(8,128)(2,1)S(1)} collective-permute-done((bf16[48,1664]{1,0:T(8,128)(2,1)S(1)}, bf16[48,1664]{1,0:T(8,128)(2,1)S(1)}, u32[]{:S(2)}, u32[]{:S(2)}) %collective-permute-start.4) | collective-permute-done | bytes 159776 | tf_op jit(solution)/shard_map/ppermute | solution.py:564
  28.6 8.2 %collective-permute-done.7 = bf16[96,1664]{1,0:T(8,128)(2,1)} collective-permute-done((bf16[96,1664]{1,0:T(8,128)(2,1)S(1)}, bf16[96,1664]{1,0:T(8,128)(2,1)}, u32[]{:S(2)}, u32[]{:S(2)}) %collective-permute-start.7) | collective-permute-done | bytes 319520 | tf_op jit(solution)/shard_map/ppermute | solution.py:564
  39.2 3.3 %collective-permute-start.6 = (bf16[48,1536]{1,0:T(8,128)(2,1)S(1)}, bf16[48,1536]{1,0:T(8,128)(2,1)S(1)}, u32[]{:S(2)}, u32[]{:S(2)}) collective-permute-start(bf16[48,1536]{1,0:T(8,128)(2,1)S(1)} %copy-done.25), channel_id=1, source_target_pairs={{0,8},{1,9},{2,10},{3,11},{4,12},{5,13},{6,14},{7,15},{8,16},{9,17... | collective-permute-start | bytes 442376 | tf_op jit(solution)/shard_map/ppermute | solution.py:564
  45.5 1.9 collective-permute-done.6
  47.4 5.4 %collective-permute-done.10 = bf16[48,1536]{1,0:T(8,128)(2,1)S(1)} collective-permute-done((bf16[48,1536]{1,0:T(8,128)(2,1)S(1)}, bf16[48,1536]{1,0:T(8,128)(2,1)S(1)}, u32[]{:S(2)}, u32[]{:S(2)}) %collective-permute-start.10) | collective-permute-done | bytes 147488 | tf_op jit(solution)/shard_map/ppermute | solution.py:564
  59.2 3.6 %collective-permute-start.17 = (bf16[48,1536]{1,0:T(8,128)(2,1)S(1)}, bf16[48,1536]{1,0:T(8,128)(2,1)S(1)}, u32[]{:S(2)}, u32[]{:S(2)}) collective-permute-start(bf16[48,1536]{1,0:T(8,128)(2,1)S(1)} %bitcast.96), channel_id=1, source_target_pairs={{0,8},{1,9},{2,10},{3,11},{4,12},{5,13},{6,14},{7,15},{8,16},{9,17... | collective-permute-start | bytes 442376 | tf_op jit(solution)/shard_map/ppermute | solution.py:564
  62.9 2.2 collective-permute-done.12
  65.0 2.6 %collective-permute-start.18 = (bf16[48,1536]{1,0:T(8,128)(2,1)S(1)}, bf16[48,1536]{1,0:T(8,128)(2,1)S(1)}, u32[]{:S(2)}, u32[]{:S(2)}) collective-permute-start(bf16[48,1536]{1,0:T(8,128)(2,1)S(1)} %bitcast.97), channel_id=1, source_target_pairs={{0,16},{1,17},{2,18},{3,19},{4,20},{5,21},{6,22},{7,23},{8,24},{9,... | collective-permute-start | bytes 442376 | tf_op jit(solution)/shard_map/ppermute | solution.py:564
  67.7 3.6 %collective-permute-start.19 = (bf16[48,1536]{1,0:T(8,128)(2,1)S(1)}, bf16[48,1536]{1,0:T(8,128)(2,1)S(1)}, u32[]{:S(2)}, u32[]{:S(2)}) collective-permute-start(bf16[48,1536]{1,0:T(8,128)(2,1)S(1)} %bitcast.98), channel_id=1, source_target_pairs={{0,24},{1,25},{2,26},{3,27},{4,28},{5,29},{6,30},{7,31},{8,0},{9,1... | collective-permute-start | bytes 442376 | tf_op jit(solution)/shard_map/ppermute | solution.py:564
  72.8 14.1 %attend.1 = (f32[8,768]{1,0:T(8,128)S(1)}, bf16[2,224,768]{2,1,0:T(8,128)(2,1)}, bf16[2,224,768]{2,1,0:T(8,128)(2,1)}, bf16[2,256,768]{2,1,0:T(8,128)(2,1)}, bf1...) custom-call(s32[80]{0:T(128)S(1)} %concatenate.99.meta, ...), custom_call_target="tpu_custom_call" | custom-call | flops 1000 | bytes 1000 | tf_op jit(solution)/shard_map/attend/pallas_call | solution.py:194
  88.2 7.2 %collective-permute-done.20 = bf16[144,1536]{1,0:T(8,128)(2,1)S(1)} collective-permute-done((bf16[144,1536]{1,0:T(8,128)(2,1)S(1)}, bf16[144,1536]{1,0:T(8,128)(2,1)S(1)}, u32[]{:S(2)}, u32[]{:S(2)}) %collective-permute-start.20) | collective-permute-done | bytes 442400 | tf_op jit(solution)/shard_map/ppermute | solution.py:564
  101.0 9.4 %hidden_fwd.1 = (bf16[384,1536]{1,0:T(8,128)(2,1)}, bf16[384,1536]{1,0:T(8,128)(2,1)}) custom-call(s32[80]{0:T(128)S(1)} %concatenate.99.meta, bf16[448,768]{1,0:T(8,128)(2,1)S(1)} %bitcast.80, bf16[448,768]{1,0:T(8,128)(2,1)} %bitcast.90, bf16[448,768]{1,0:T(8,128)(2,1)} %bitcast.82, bf16[448,768]{1,0:T(8,128)(2,1)} %bitcast.88, ...), custom_call_target="tpu_custom_call" | custom-call | flops 1000 | bytes 1000 | tf_op jit(solution)/shard_map/hidden_fwd/pallas_call | solution.py:254
  113.0 17.6 %hidden_back.1 = (f32[1,1536]{1,0:T(1,128)S(1)}, bf16[384,1536]{1,0:T(8,128)(2,1)}, bf16[384,1536]{1,0:T(8,128)(2,1)}, f32[448,768]{1,0:T(8,128)}, bf16[448,768]...) custom-call(s32[80]{0:T(128)S(1)} %concatenate.99.meta, bf16[448,768]{1,0:T(8,128)(2,1)} %bitcast.79, ...), custom_call_target="tpu_custom_call" | custom-call | flops 1000 | bytes 1000 | tf_op jit(solution)/shard_map/hidden_back/pallas_call | solution.py:319
  134.6 17.4 %attend_back.2 = (f32[4,768]{1,0:T(4,128)S(1)}, f32[2,512]{1,0:T(2,128)S(1)}, f32[128,128]{1,0:T(8,128)S(1)}, bf16[768,1024]{1,0:T(8,128)(2,1)}, bf16[768,1024]{...) custom-call(s32[80]{0:T(128)S(1)} %concatenate.99.meta, ...), custom_call_target="tpu_custom_call" | custom-call | flops 1000 | bytes 1000 | tf_op jit(solution)/shard_map/attend_back/pallas_call | solution.py:541
  160.5 1.9 collective-permute-start.31
  162.4 12.8 %attend_back.3 = (f32[2,768]{1,0:T(2,128)S(1)}, f32[2,256]{1,0:T(2,128)S(1)}, f32[128,128]{1,0:T(8,128)S(1)}, bf16[768,512]{1,0:T(8,128)(2,1)}, bf16[768,512]{1,0:T(8,128)(2,1)}, /*index=5*/f32[2,224,768]{2,1,0:T(8,128)}) custom-call(s32[80]{0:T(128)S(1)} %concatenate.99.meta, f32[8,768]{1,0:T(8,128)S(1)} %get-tuple-element.136.vecs, ...), custom_call_target="tpu_custom_call" | custom-call | flops 1000 | bytes 1000 | tf_op jit(solution)/shard_map/attend_back/pallas_call | solution.py:541
  181.2 5.1 %collective-permute-done.37 = bf16[192,1024]{1,0:T(8,128)(2,1)S(1)} collective-permute-done((bf16[192,1024]{1,0:T(8,128)(2,1)S(1)}, bf16[192,1024]{1,0:T(8,128)(2,1)S(1)}, u32[]{:S(2)}, u32[]{:S(2)}) %collective-permute-start.37) | collective-permute-done | bytes 393248 | tf_op jit(solution)/shard_map/ppermute | solution.py:564
  191.3 8.9 %collective-permute-done.40 = bf16[96,1536]{1,0:T(8,128)(2,1)S(1)} collective-permute-done((bf16[96,1536]{1,0:T(8,128)(2,1)S(1)}, bf16[96,1536]{1,0:T(8,128)(2,1)S(1)}, u32[]{:S(2)}, u32[]{:S(2)}) %collective-permute-start.40) | collective-permute-done | bytes 294944 | tf_op jit(solution)/shard_map/ppermute | solution.py:578
  204.4 2.0 copy.68
  209.7 2.6 %collective-permute-start.47 = (bf16[48,512]{1,0:T(8,128)(2,1)S(1)}, bf16[48,512]{1,0:T(8,128)(2,1)S(1)}, u32[]{:S(2)}, u32[]{:S(2)}) collective-permute-start(bf16[48,512]{1,0:T(8,128)(2,1)S(1)} %get-tuple-element.221), channel_id=1, source_target_pairs={{0,24},{1,25},{2,26},{3,27},{4,28},{5,29},{6,30},{7,31},{8,0},{9,1... | collective-permute-start | bytes 147464 | tf_op jit(solution)/shard_map/ppermute | solution.py:564
  221.2 2.8 %collective-permute-done.51 = f32[104,128]{1,0:T(8,128)S(1)} collective-permute-done((f32[104,128]{1,0:T(8,128)S(1)}, f32[104,128]{1,0:T(8,128)S(1)}, u32[]{:S(2)}, u32[]{:S(2)}) %collective-permute-start.51) | collective-permute-done | bytes 53280 | tf_op jit(solution)/shard_map/ppermute | solution.py:578
  (266 shorter events, 81.3 us)
Async XLA Ops:
  11.0 13.2 %collective-permute-start.4 = (bf16[48,1664]{1,0:T(8,128)(2,1)S(1)}, bf16[48,1664]{1,0:T(8,128)(2,1)S(1)}, u32[]{:S(2)}, u32[]{:S(2)}) collective-permute-start(bf16[48,1664]{1,0:T(8,128)(2,1)S(1)} %pad_maximum_fusion.8), channel_id=1, source_target_pairs={{0,16},{1,17},{2,18},{3,19},{4,20},{5,21},{6,22},{7,23},{8,24},{9,... | collective-permute-start | bytes 479240 | tf_op jit(solution)/shard_map/ppermute | solution.py:564
  15.0 22.7 %collective-permute-start.8 = (bf16[96,3072]{1,0:T(8,128)(2,1)S(1)}, bf16[96,3072]{1,0:T(8,128)(2,1)S(1)}, u32[]{:S(2)}, u32[]{:S(2)}) collective-permute-start(bf16[96,3072]{1,0:T(8,128)(2,1)S(1)} %pad_maximum_fusion.1.refs_0_.refs_4_), channel_id=1, source_target_pairs={{0,4},{1,3},{2,6},{3,1},{4,0},{5,7},{6,2},{7,5},{8,12},{9,11},{10,... | collective-permute-start | bytes 1769480 | tf_op jit(solution)/shard_map/ppermute | solution.py:564
  25.6 12.1 %collective-permute-start.9 = (bf16[144,1664]{1,0:T(8,128)(2,1)S(1)}, bf16[144,1664]{1,0:T(8,128)(2,1)S(1)}, u32[]{:S(2)}, u32[]{:S(2)}) collective-permute-start(bf16[144,1664]{1,0:T(8,128)(2,1)S(1)} %get-tuple-element.223), channel_id=1, source_target_pairs={{0,2},{1,5},{2,0},{3,7},{4,6},{5,1},{6,4},{7,3},{8,10},{9,13},{10,... | collective-permute-start | bytes 1437704 | tf_op jit(solution)/shard_map/ppermute | solution.py:564
  38.5 15.2 %collective-permute-start.13 = (bf16[288,1664]{1,0:T(8,128)(2,1)}, bf16[288,1664]{1,0:T(8,128)(2,1)}, u32[]{:S(2)}, u32[]{:S(2)}) collective-permute-start(bf16[288,1664]{1,0:T(8,128)(2,1)} %constant_dynamic-update-slice_fusion.3.refs_1_), channel_id=1, source_target_pairs={{0,4},{1,3},{2,6},{3,1},{4,0},{5,7},{6,2},{7,5},{8,12},{9,11},{10,... | collective-permute-start | bytes 2875400 | tf_op jit(solution)/shard_map/ppermute | solution.py:564
  53.7 17.6 %collective-permute-start.15 = (bf16[288,1664]{1,0:T(8,128)(2,1)}, bf16[288,1664]{1,0:T(8,128)(2,1)}, u32[]{:S(2)}, u32[]{:S(2)}) collective-permute-start(bf16[288,1664]{1,0:T(8,128)(2,1)} %constant_dynamic-update-slice_fusion.3.refs_1_), channel_id=1, source_target_pairs={{0,1},{1,0},{2,3},{3,2},{4,5},{5,4},{6,7},{7,6},{8,9},{9,8},{10,11... | collective-permute-start | bytes 2875400 | tf_op jit(solution)/shard_map/ppermute | solution.py:582
  53.7 19.1 %collective-permute-start.16 = (bf16[288,1664]{1,0:T(8,128)(2,1)}, bf16[288,1664]{1,0:T(8,128)(2,1)}, u32[]{:S(2)}, u32[]{:S(2)}) collective-permute-start(bf16[288,1664]{1,0:T(8,128)(2,1)} %collective-permute-done.13.refs_2_), channel_id=1, source_target_pairs={{0,1},{1,0},{2,3},{3,2},{4,5},{5,4},{6,7},{7,6},{8,9},{9,8},{10,11... | collective-permute-start | bytes 2875400 | tf_op jit(solution)/shard_map/ppermute | solution.py:582
  59.2 27.7 %collective-permute-start.17 = (bf16[48,1536]{1,0:T(8,128)(2,1)S(1)}, bf16[48,1536]{1,0:T(8,128)(2,1)S(1)}, u32[]{:S(2)}, u32[]{:S(2)}) collective-permute-start(bf16[48,1536]{1,0:T(8,128)(2,1)S(1)} %bitcast.96), channel_id=1, source_target_pairs={{0,8},{1,9},{2,10},{3,11},{4,12},{5,13},{6,14},{7,15},{8,16},{9,17... | collective-permute-start | bytes 442376 | tf_op jit(solution)/shard_map/ppermute | solution.py:564
  65.0 22.0 %collective-permute-start.18 = (bf16[48,1536]{1,0:T(8,128)(2,1)S(1)}, bf16[48,1536]{1,0:T(8,128)(2,1)S(1)}, u32[]{:S(2)}, u32[]{:S(2)}) collective-permute-start(bf16[48,1536]{1,0:T(8,128)(2,1)S(1)} %bitcast.97), channel_id=1, source_target_pairs={{0,16},{1,17},{2,18},{3,19},{4,20},{5,21},{6,22},{7,23},{8,24},{9,... | collective-permute-start | bytes 442376 | tf_op jit(solution)/shard_map/ppermute | solution.py:564
  67.7 19.4 %collective-permute-start.19 = (bf16[48,1536]{1,0:T(8,128)(2,1)S(1)}, bf16[48,1536]{1,0:T(8,128)(2,1)S(1)}, u32[]{:S(2)}, u32[]{:S(2)}) collective-permute-start(bf16[48,1536]{1,0:T(8,128)(2,1)S(1)} %bitcast.98), channel_id=1, source_target_pairs={{0,24},{1,25},{2,26},{3,27},{4,28},{5,29},{6,30},{7,31},{8,0},{9,1... | collective-permute-start | bytes 442376 | tf_op jit(solution)/shard_map/ppermute | solution.py:564
  71.3 27.8 %collective-permute-start.23 = (bf16[288,1536]{1,0:T(8,128)(2,1)S(1)}, bf16[288,1536]{1,0:T(8,128)(2,1)S(1)}, u32[]{:S(2)}, u32[]{:S(2)}) collective-permute-start(bf16[288,1536]{1,0:T(8,128)(2,1)S(1)} %constant_dynamic-update-slice_fusion.10.refs_2_), channel_id=1, source_target_pairs={{0,4},{1,3},{2,6},{3,1},{4,0},{5,7},{6,2},{7,5},{8,12},{9,11},{10,... | collective-permute-start | bytes 2654216 | tf_op jit(solution)/shard_map/ppermute | solution.py:564
  95.5 14.9 %collective-permute-start.24 = (bf16[288,1536]{1,0:T(8,128)(2,1)S(1)}, bf16[288,1536]{1,0:T(8,128)(2,1)S(1)}, u32[]{:S(2)}, u32[]{:S(2)}) collective-permute-start(bf16[288,1536]{1,0:T(8,128)(2,1)S(1)} %constant_dynamic-update-slice_fusion.14.refs_6_), channel_id=1, source_target_pairs={{0,4},{1,3},{2,6},{3,1},{4,0},{5,7},{6,2},{7,5},{8,12},{9,11},{10,... | collective-permute-start | bytes 2654216 | tf_op jit(solution)/shard_map/ppermute | solution.py:564
  111.3 19.4 %collective-permute-start.25 = (bf16[384,1536]{1,0:T(8,128)(2,1)}, bf16[384,1536]{1,0:T(8,128)(2,1)S(1)}, u32[]{:S(2)}, u32[]{:S(2)}) collective-permute-start(bf16[384,1536]{1,0:T(8,128)(2,1)} %get-tuple-element.131), channel_id=1, source_target_pairs={{0,4},{1,3},{2,6},{3,1},{4,0},{5,7},{6,2},{7,5},{8,12},{9,11},{10,... | collective-permute-start | bytes 3538952 | tf_op jit(solution)/shard_map/ppermute | solution.py:564
  130.8 22.8 %collective-permute-start.27 = (bf16[384,1536]{1,0:T(8,128)(2,1)}, bf16[384,1536]{1,0:T(8,128)(2,1)S(1)}, u32[]{:S(2)}, u32[]{:S(2)}) collective-permute-start(bf16[384,1536]{1,0:T(8,128)(2,1)} %get-tuple-element.135), channel_id=1, source_target_pairs={{0,4},{1,3},{2,6},{3,1},{4,0},{5,7},{6,2},{7,5},{8,12},{9,11},{10,... | collective-permute-start | bytes 3538952 | tf_op jit(solution)/shard_map/ppermute | solution.py:564
  132.7 19.3 %collective-permute-start.26 = (bf16[192,1536]{1,0:T(8,128)(2,1)}, bf16[192,1536]{1,0:T(8,128)(2,1)S(1)}, u32[]{:S(2)}, u32[]{:S(2)}) collective-permute-start(bf16[192,1536]{1,0:T(8,128)(2,1)} %add_convert_fusion.3), channel_id=1, source_target_pairs={{0,2},{1,5},{2,0},{3,7},{4,6},{5,1},{6,4},{7,3},{8,10},{9,13},{10,... | collective-permute-start | bytes 1769480 | tf_op jit(solution)/shard_map/ppermute | solution.py:564
  154.6 20.9 %collective-permute-start.32 = (bf16[192,1536]{1,0:T(8,128)(2,1)}, bf16[192,1536]{1,0:T(8,128)(2,1)}, u32[]{:S(2)}, u32[]{:S(2)}) collective-permute-start(bf16[192,1536]{1,0:T(8,128)(2,1)} %add_convert_fusion.2), channel_id=1, source_target_pairs={{0,2},{1,5},{2,0},{3,7},{4,6},{5,1},{6,4},{7,3},{8,10},{9,13},{10,... | collective-permute-start | bytes 1769480 | tf_op jit(solution)/shard_map/ppermute | solution.py:564
  157.7 17.8 %collective-permute-start.34 = (bf16[384,1024]{1,0:T(8,128)(2,1)}, bf16[384,1024]{1,0:T(8,128)(2,1)}, u32[]{:S(2)}, u32[]{:S(2)}) collective-permute-start(bf16[384,1024]{1,0:T(8,128)(2,1)} %slice.283), channel_id=1, source_target_pairs={{0,4},{1,3},{2,6},{3,1},{4,0},{5,7},{6,2},{7,5},{8,12},{9,11},{10,... | collective-permute-start | bytes 2359304 | tf_op jit(solution)/shard_map/ppermute | solution.py:564
  158.7 16.8 %collective-permute-start.29 = (bf16[48,1536]{1,0:T(8,128)(2,1)S(1)}, bf16[48,1536]{1,0:T(8,128)(2,1)}, u32[]{:S(2)}, u32[]{:S(2)}) collective-permute-start(bf16[48,1536]{1,0:T(8,128)(2,1)S(1)} %get-tuple-element.212), channel_id=1, source_target_pairs={{0,24},{1,25},{2,26},{3,27},{4,28},{5,29},{6,30},{7,31},{8,0},{9,1... | collective-permute-start | bytes 442376 | tf_op jit(solution)/shard_map/ppermute | solution.py:564
  158.8 16.7 %collective-permute-start.30 = (bf16[48,1536]{1,0:T(8,128)(2,1)S(1)}, bf16[48,1536]{1,0:T(8,128)(2,1)}, u32[]{:S(2)}, u32[]{:S(2)}) collective-permute-start(bf16[48,1536]{1,0:T(8,128)(2,1)S(1)} %get-tuple-element.211), channel_id=1, source_target_pairs={{0,16},{1,17},{2,18},{3,19},{4,20},{5,21},{6,22},{7,23},{8,24},{9,... | collective-permute-start | bytes 442376 | tf_op jit(solution)/shard_map/ppermute | solution.py:564
  160.5 15.0 %collective-permute-start.31 = (bf16[48,1536]{1,0:T(8,128)(2,1)S(1)}, bf16[48,1536]{1,0:T(8,128)(2,1)}, u32[]{:S(2)}, u32[]{:S(2)}) collective-permute-start(bf16[48,1536]{1,0:T(8,128)(2,1)S(1)} %get-tuple-element.210), channel_id=1, source_target_pairs={{0,8},{1,9},{2,10},{3,11},{4,12},{5,13},{6,14},{7,15},{8,16},{9,17... | collective-permute-start | bytes 442376 | tf_op jit(solution)/shard_map/ppermute | solution.py:564
  180.1 20.1 %collective-permute-start.40 = (bf16[96,1536]{1,0:T(8,128)(2,1)S(1)}, bf16[96,1536]{1,0:T(8,128)(2,1)S(1)}, u32[]{:S(2)}, u32[]{:S(2)}) collective-permute-start(bf16[96,1536]{1,0:T(8,128)(2,1)S(1)} %pad_maximum_fusion.5), channel_id=1, source_target_pairs={{0,16},{2,18},{4,20},{6,22},{8,24},{10,26},{12,28},{14,30},{16,0},... | collective-permute-start | bytes 884744 | tf_op jit(solution)/shard_map/ppermute | solution.py:578
  186.6 13.6 %collective-permute-start.39 = (bf16[384,512]{1,0:T(8,128)(2,1)S(1)}, bf16[384,512]{1,0:T(8,128)(2,1)S(1)}, u32[]{:S(2)}, u32[]{:S(2)}) collective-permute-start(bf16[384,512]{1,0:T(8,128)(2,1)S(1)} %slice.287), channel_id=1, source_target_pairs={{0,4},{1,3},{2,6},{3,1},{4,0},{5,7},{6,2},{7,5},{8,12},{9,11},{10,... | collective-permute-start | bytes 1179656 | tf_op jit(solution)/shard_map/ppermute | solution.py:564
  188.0 12.2 %collective-permute-start.38 = (f32[104,128]{1,0:T(8,128)S(1)}, f32[104,128]{1,0:T(8,128)S(1)}, u32[]{:S(2)}, u32[]{:S(2)}) collective-permute-start(f32[104,128]{1,0:T(8,128)S(1)} %add.849), channel_id=1, source_target_pairs={{0,4},{1,3},{2,6},{3,1},{4,0},{5,7},{6,2},{7,5},{8,12},{9,11},{10,... | collective-permute-start | bytes 159752 | tf_op jit(solution)/shard_map/ppermute | solution.py:564
  190.0 16.3 %collective-permute-start.42 = (bf16[96,1024]{1,0:T(8,128)(2,1)S(1)}, bf16[96,1024]{1,0:T(8,128)(2,1)S(1)}, u32[]{:S(2)}, u32[]{:S(2)}) collective-permute-start(bf16[96,1024]{1,0:T(8,128)(2,1)S(1)} %pad_maximum_fusion.7), channel_id=1, source_target_pairs={{0,16},{2,18},{4,20},{6,22},{8,24},{10,26},{12,28},{14,30},{16,0},... | collective-permute-start | bytes 589832 | tf_op jit(solution)/shard_map/ppermute | solution.py:578
  191.3 16.2 %collective-permute-start.45 = (bf16[448,768]{1,0:T(8,128)(2,1)S(1)}, bf16[448,768]{1,0:T(8,128)(2,1)S(1)}, u32[]{:S(2)}, u32[]{:S(2)}) collective-permute-start(bf16[448,768]{1,0:T(8,128)(2,1)S(1)} %copy-done.34), channel_id=1, source_target_pairs={{0,1},{1,0},{2,3},{3,2},{4,5},{5,4},{6,7},{7,6},{8,9},{9,8},{10,11... | collective-permute-start | bytes 2064392 | tf_op jit(solution)/shard_map/ppermute | solution.py:582
  (64 other events, 455.4 us)

commit v5 on v4

--- a/solution.py
+++ b/solution.py
@@ -20,6 +20,7 @@
 EPSILON = 1e-06
 MASKED_SCORE = -1e30
 MASK_LANE = 60
+SMALL = 48
 CHUNK = 512
 BACK_PARTS = (4, 2)
 F32 = jnp.float32
@@ -364,11 +365,11 @@
     else:
         da, refs = refs[0], refs[1:]
         if last:
-            tok, dx1, *changes = refs[: 2 + parts]
-            norm_sums, bias_sums, table_grad, mine, theirs, result = refs[2 + parts : 8 + parts]
-            refs = refs[8 + parts :]
-            wqkv, toks, dx1s, results, *changed = refs[-4 - parts :]
-            refs = refs[: -4 - parts]
+            earlier, tok, dx1, *changes = refs[:4], *refs[4 : 6 + parts]
+            flat, mine, theirs, result = refs[6 + parts : 10 + parts]
+            refs = refs[10 + parts :]
+            bias_sums, wqkv, toks, dx1s, results, *changed = refs[-5 - parts :]
+            refs = refs[: -5 - parts]
         else:
             bias_sums, table_grad, mine, theirs, dqkv_out = refs[:5]
             refs = refs[5:]
@@ -445,7 +446,7 @@
     wait_att.wait()
     made = dot_tn(atts[...].reshape(tokens), das[:, :, columns].reshape(2 * TOK, cols_here))
     grads[1, :, cols_here:] = made.astype(BF16)
-    finish(wait_qk + [wait_v])
+    finish(wait_qk + [wait_v] + wait_p)
     place = lanes(TOK)
     table_sum = jnp.zeros((LANES, LANES), F32)
     for step in range(2 * count):
@@ -454,7 +455,6 @@
         q2, k2, v2, dat2 = (ref[window, :, cols] for ref in (qs, ks, vs, dat))
         q8 = (q2.astype(F32) * HDIM**-0.5).astype(BF16)
         k8 = (k2.astype(F32) * HDIM**-0.5).astype(BF16)
-        wait_p[step].wait()
         dqs, dks, dvs, dts = [], [], [], []
         for half in range(2):
             soft = ps[window, 2 * pair + half]
@@ -472,7 +472,8 @@
         dqkv[1, window, :, cols] = jnp.where(place < 64, dks[0][:TOK], dks[1][:TOK]).astype(BF16)
         dqkv[2, window, :, cols] = jnp.where(place < 64, dvs[0][:TOK], dvs[1][:TOK]).astype(BF16)
         table_sum = table_sum + jnp.where(lanes(LANES) < 64, dts[0], dts[1])
-    table_grad[...] = table_sum
+    if not last:
+        table_grad[...] = table_sum
     if not last:
         outs.append(begin(dqkv, dqkv_out, out_sems.at[2 * PIECES + 2]))
     wait_n1.wait()
@@ -500,8 +501,41 @@
             outs.append(begin(results.at[window], result.at[window], out_sems.at[2 * PIECES + window]))
             for slot, value in enumerate((grad * xhat, grad)):
                 total[slot] = total[slot] + jnp.sum(value, axis=0, keepdims=True)
-        norm_sums[...] = jnp.concatenate(total, axis=0)
+        norm2_sums, bias0, table0, hidden_sums = earlier
+        pack(meta, total, (bias0, bias_sums), norm2_sums, table0[...] + table_sum, hidden_sums, flat)
     finish(outs)
+
+
+def pack(meta, norm1, biases, norm2, table, hidden, flat):
+    flat[...] = jnp.zeros_like(flat)
+    parts = biases[0].shape[1] // LANES
+    for row in range(8):
+        for at in range(6):
+            cols = pl.ds(at * LANES, LANES)
+            if row < 2:
+                value = norm1[row][:, at * LANES : (at + 1) * LANES]
+            elif row < 4:
+                ref, place = (biases[0], at) if at < parts else (biases[1], at - parts)
+                value = ref[row - 2 : row - 1, pl.ds(place * LANES, LANES)]
+            else:
+                value = norm2[row - 4 : row - 3, cols]
+            block = 6 * row + at
+            flat[block // 4 : block // 4 + 1, pl.ds(block % 4 * LANES, LANES)] = value
+    for block in range(hidden.shape[1] // LANES):
+        value = hidden[:, pl.ds(block * LANES, LANES)]
+        for core in range(2):
+            at = 12 + 3 * core + block // 4
+            flat[at : at + 1, pl.ds(block % 4 * LANES, LANES)] = jnp.where(meta[64] == core, value, 0.0)
+    both = table[:64] + pltpu.roll(table[:64], HDIM, 1)
+    for group in range(4):
+        flat[24:40, pl.ds(group * LANES, LANES)] = both[16 * group : 16 * group + 16]
+
+
+def unpacked(flat, core):
+    vectors = flat[:12].reshape(8, -1)
+    hidden = lax.dynamic_slice_in_dim(flat, 12 + 3 * core, 3).reshape(-1)
+    table = flat[24:40].reshape(16, 4, LANES).transpose(1, 0, 2).reshape(64, LANES)[:, :HDIM]
+    return vectors, hidden, table
 
 
 def attend_back(before, count, meta, vecs, gather, table, q, k, v, p, weights, att, n1, ins):
@@ -515,7 +549,7 @@
     large = [shape((width, 2 * cols_here), BF16)] * 2
     large.append(shape(rows, F32) if last else shape((3,) + part, BF16))
     if last:
-        small = [shape((2, width), F32)] + small
+        small = [shape((SMALL, 2 * cols_here), F32)]
     if first:
         small = [shape((4, width), F32)] + small
         large += [shape(rows, F32), shape(rows, BF16)]
@@ -533,6 +567,7 @@
         ]
     if last:
         scratch += [
+            pltpu.VMEM((2, cols_here), F32),
             pltpu.VMEM((3, width, width), BF16),
             pltpu.VMEM(rows, BF16),
             pltpu.VMEM(rows, F32),
@@ -541,7 +576,7 @@
     return pl.pallas_call(
         partial(attend_back_kernel, before, count),
         out_shape=small + large,
-        in_specs=[SMEM] + [WHOLE] * 3 + [HBM] * (7 + len(ins)),
+        in_specs=[SMEM] + [WHOLE] * 3 + [HBM] * 8 + [WHOLE if last and at < 4 else HBM for at in range(len(ins) - 1)],
         out_specs=[WHOLE] * len(small) + [HBM] * len(large),
         scratch_shapes=scratch,
         compiler_params=params(),
@@ -586,6 +621,30 @@
     return lax.optimization_barrier((values, *others))[0]
 
 
+def stack_kernel(count, *refs):
+    ins, out, sems = refs[:count], refs[count], refs[count + 1]
+    copies, at = [], 0
+    for ref in ins:
+        rows = ref.shape[0]
+        copies.append(begin(ref, out.at[pl.ds(at, rows)], sems.at[len(copies)]))
+        at += rows
+    finish(copies)
+
+
+def stack(*parts):
+    rows = sum(part.shape[0] for part in parts)
+    return pl.pallas_call(
+        partial(stack_kernel, len(parts)),
+        out_shape=shape((rows, parts[0].shape[1]), BF16),
+        in_specs=[HBM] * len(parts),
+        out_specs=HBM,
+        scratch_shapes=[pltpu.SemaphoreType.DMA((len(parts),))],
+        compiler_params=params(),
+        cost_estimate=COST,
+        name="stack",
+    )(*parts)
+
+
 class Flow:
     def __init__(self, *came):
         self.came = list(came)
@@ -619,6 +678,68 @@
     return a.astype(F32) + b.astype(F32)
 
 
+def staged_kernel(kernel, starts, scalars, *refs):
+    count = len(starts)
+    meta, refs = refs[:scalars], refs[scalars:]
+    total = len(refs) // 2
+    held, sems = refs[total : 2 * total], refs[2 * total]
+    copies = []
+    for ref, start, dest in zip(refs, starts, held):
+        if start is not None:
+            ref = ref.at[pl.ds(start, dest.shape[0])]
+        copies.append(begin(ref, dest, sems.at[len(copies)]))
+    finish(copies)
+    kernel(*meta, *held)
+    finish([begin(held[at], refs[at], sems.at[at]) for at in range(count, total)])
+
+
+def staged(kernel, outs, *ins, meta=None):
+    ins = [part if isinstance(part, tuple) else (part, None, part.shape[0]) for part in ins]
+    arrays, starts, rows = zip(*ins)
+    scalars = () if meta is None else (meta,)
+    held = [pltpu.VMEM((count, *array.shape[1:]), array.dtype) for array, count in zip(arrays, rows)]
+    held += [pltpu.VMEM(out.shape, out.dtype) for out in outs]
+    return pl.pallas_call(
+        partial(staged_kernel, kernel, starts, len(scalars)),
+        out_shape=outs,
+        in_specs=[SMEM] * len(scalars) + [HBM] * len(arrays),
+        out_specs=[HBM] * len(outs),
+        scratch_shapes=held + [pltpu.SemaphoreType.DMA((len(held),))],
+        compiler_params=params(),
+        cost_estimate=COST,
+        name="staged",
+    )(*scalars, *arrays)
+
+
+def core_rows_kernel(count, meta, *refs):
+    *terms, own, far = refs
+    half, width = own.shape[1:]
+    one, two = (sum(ref[...].astype(F32) for ref in part) for part in (terms[:count], terms[count:]))
+    cut, last = one.shape[1] // 2, two.shape[1] // 2
+    for core in range(2):
+
+        def put(ref, at=slice(core * half, (core + 1) * half)):
+            for mat in range(2):
+                ref[mat, :, :cut] = one[at, mat * cut : (mat + 1) * cut]
+                ref[mat, :, cut:] = two[at, mat * last : (mat + 1) * last]
+
+        pl.when(meta[64] == core)(partial(put, own))
+        pl.when(meta[64] != core)(partial(put, far))
+
+
+def last_rows_kernel(meta, near, came, qkv, proj):
+    width = proj.shape[1]
+
+    def put(qk, vp):
+        qkv[:, :width] = qk[0]
+        qkv[:, width : 2 * width] = qk[1]
+        qkv[:, 2 * width :] = vp[0]
+        proj[...] = vp[1]
+
+    pl.when(meta[64] == 0)(partial(put, near, came))
+    pl.when(meta[64] != 0)(partial(put, came, near))
+
+
 class Scatter(Flow):
     def __init__(self, keep, far, dims):
         super().__init__(turn(far, dims, SECOND))
@@ -635,9 +756,10 @@
         near = self.near + self.came[0].astype(F32)
         rows = near.shape[0] // self.dims[0]
         self.near = near[:rows]
+        sends = [near[step * rows : (step + 1) * rows].astype(BF16) for step in range(1, self.dims[0])]
+        self.sent = sends[0]
         self.came = [
-            turn(near[step * rows : (step + 1) * rows].astype(BF16), self.dims, ((0, self.dims[0] - step),) * 2)
-            for step in range(1, self.dims[0])
+            turn(send, self.dims, ((0, self.dims[0] - step),) * 2) for step, send in enumerate(sends, 1)
         ]
 
     def halve(self):
@@ -654,7 +776,8 @@
         rows = self.near.shape[0]
         came = self.came[0]
         self.near = self.near + came[:rows].astype(F32)
-        self.came = [swap_z((self.beside + came[rows:].astype(F32)).astype(BF16), self.dims, 1)]
+        self.sent = (self.beside + came[rows:].astype(F32)).astype(BF16)
+        self.came = [swap_z(self.sent, self.dims, 1)]
 
     def last(self):
         return sum((part.astype(F32) for part in self.came), self.near)
@@ -731,21 +854,25 @@
     dims = grid_of(lax.axis_size("dp"))
     core = lax.axis_index("mp")
     is_first = core == 0
-    if dims is None:
-        orders = [jnp.tile(jnp.arange(PIECES, dtype=jnp.int32), 4)]
-    else:
-        own, far = place_orders(dims, core), place_orders(dims, 1 - core)
-        orders = [own[0], far[0], own[1], far[1]]
-    meta = jnp.concatenate(
-        orders + [core.astype(jnp.int32)[None], heights, widths, jnp.zeros((11,), jnp.int32)]
-    )
-
-    tok = padded(patches)
-    row_index = core * WIN + jnp.arange(WIN)
-    valid = (row_index[None, :, None] < heights[:, None, None]) & (
-        jnp.arange(WIN)[None, None, :] < widths[:, None, None]
-    )
-    dm = padded(jnp.where(valid[..., None], out_grad, jnp.zeros_like(out_grad)))
+    spread, gather = constants()
+
+    def prepare(patches, out_grad, heights, rel_pos_h, rel_pos_w):
+        if dims is None:
+            orders = [jnp.tile(jnp.arange(PIECES, dtype=jnp.int32), 4)]
+        else:
+            own, far = place_orders(dims, core), place_orders(dims, 1 - core)
+            orders = [own[0], far[0], own[1], far[1]]
+        meta = jnp.concatenate(
+            orders + [core.astype(jnp.int32)[None], heights, widths, jnp.zeros((11,), jnp.int32)]
+        )
+        row_index = core * WIN + jnp.arange(WIN)
+        valid = (row_index[None, :, None] < heights[:, None, None]) & (
+            jnp.arange(WIN)[None, None, :] < widths[:, None, None]
+        )
+        dm = padded(jnp.where(valid[..., None], out_grad, jnp.zeros_like(out_grad)))
+        return padded(patches), dm, meta, *tables(rel_pos_h, rel_pos_w)
+
+    wanted = (patches, out_grad, heights, rel_pos_h, rel_pos_w)
     vectors = (norm1_gain, norm1_bias, qv_bias[0], qv_bias[1], proj_bias, norm2_gain, norm2_bias, fc2_bias)
     small = jnp.pad(jnp.stack(vectors, axis=1), ((0, 0), (0, LANES - len(vectors))))
     qk = jnp.concatenate([qkv_weight[:, :width], small, qkv_weight[:, width : 2 * width]], axis=1)
@@ -755,66 +882,70 @@
         vp = lax.all_gather(vp, ("dp", "mp"), axis=0, tiled=True)
         attend_own = [jnp.where(is_first, qk, vp)]
         attend_far = [jnp.where(is_first, vp, qk)]
-        dm_far = other_core(dm)
+        tok, dm, meta, table, table_back = prepare(*wanted)
         hidden_in = tuple(
             ((lax.all_gather(part, "dp", axis=0, tiled=True), 0),) for part in (fc1_weight, fc2_weight.T)
         )
     else:
         fc1, fc2 = fc1_weight, fc2_weight.T
         came = other_core(jnp.where(is_first, vp, qk))
-        own_h = jnp.concatenate([fc1, fc2], axis=1)
-        beside_h = turn(own_h, dims, FIRST)
         near = jnp.where(is_first, qk, vp)
         block = jnp.concatenate(
             [jnp.where(is_first, near, came), jnp.where(is_first, came, near)], axis=0
         )
-        attend_z = along_z(block, dims)
-        beside = turn(block, dims, FIRST)
-        own_h = jnp.concatenate([own_h, beside_h], axis=0)
-        over_h = turn(own_h, dims, SECOND)
-        own = jnp.concatenate([block, after(beside, own_h)], axis=0)
-        over = turn(own, dims, SECOND)
-        attend_z = jnp.concatenate([after(attend_z[0], own)] + attend_z[1:], axis=0)
-        z_beside = turn(attend_z, dims, FIRST)
-        fc1_z = along_z(after(fc1, attend_z), dims)
-        over, over_h, z_beside = meet([], over, over_h, z_beside)
-        own = jnp.concatenate([own, over], axis=0)
-        far = [other_core(own)]
-        attend_z = jnp.concatenate([attend_z, z_beside], axis=0)
-        z_over = turn(attend_z, dims, SECOND)
-        fc1_z = jnp.concatenate([after(fc1_z[0], attend_z)] + fc1_z[1:], axis=0)
-        fc1_beside = turn(fc1_z, dims, FIRST)
-        fc2_z = along_z(after(fc2, fc1_z), dims)
-        far.append(other_core(after(attend_z, fc1_z)))
-        z_over = after(z_over, fc1_z)
-        far.append(other_core(z_over))
-        fc1_z = jnp.concatenate([fc1_z, after(fc1_beside, z_over)], axis=0)
-        fc1_over = turn(fc1_z, dims, SECOND)
-        attend_own, attend_far = [own, attend_z, z_over], far
-        dm_far = other_core(after(dm, z_over))
-        tok = after(tok, fc1_z)
-
-    dm_flat, dm_far = dm.reshape(-1, width), dm_far.reshape(-1, width)
-    spread, gather = constants()
-    table, table_back = tables(rel_pos_h, rel_pos_w)
+        attend_size, size = block.shape[1], fc1.shape[1]
+        tok, dm, meta, table, table_back = prepare(*meet([], *wanted, block)[:5])
+        own = jnp.concatenate([block, fc1, fc2], axis=1)
+        attend_z, beside = Flow(*along_z(block, dims)), Flow(turn(own, dims, FIRST))
+        fc1, fc2, tok, dm, table, table_back, meta = meet(
+            [attend_z, beside], fc1, fc2, tok, dm, table, table_back, meta
+        )
+
+        attend_z = stack(*attend_z.came)
+        z_beside = Flow(turn(attend_z, dims, FIRST))
+        own = stack(own, *beside.came)
+        over = Flow(turn(own, dims, SECOND))
+        fc1_z = Flow(*along_z(after(fc1, own), dims))
+        (fc2,) = meet([over, z_beside, fc1_z], fc2)
+
+        over = over.came[0]
+        attend_z = stack(attend_z, *z_beside.came)
+        z_over = Flow(turn(attend_z, dims, SECOND))
+        fc1_z = stack(after(fc1_z.came[0], attend_z), *fc1_z.came[1:])
+        fc1_beside = Flow(turn(fc1_z, dims, FIRST))
+        fc2_z = Flow(*along_z(after(fc2, fc1_z), dims))
+        own_attend = jnp.concatenate([own[:, :attend_size], over[:, :attend_size]], axis=0)
+        own_attend, attend_z = meet([z_over, fc1_beside, fc2_z], own_attend, attend_z)
+
+        z_over = z_over.came[0]
+        far = Flow(*(other_core(part) for part in (own_attend, attend_z, z_over)))
+        fc1_z = stack(fc1_z, *fc1_beside.came)
+        fc1_over = Flow(turn(fc1_z, dims, SECOND))
+        fc2_z = stack(*fc2_z.came)
+        fc2_beside = Flow(turn(fc2_z, dims, FIRST))
+        tok, fc1_z, fc2_z, dm = meet([far], tok, fc1_z, fc2_z, dm)
+        dm_far = Flow(other_core(dm))
+        attend_own, attend_far = [own, over, attend_z, z_over], far.came
 
     vecs, n1, q, k, v, p, att, weights, x1, n2 = attend(
         meta, tok, table, jnp.asarray(spread, BF16), attend_own, attend_far
     )
-    if dims is not None:
-        fc2_z = jnp.concatenate([after(fc2_z[0], n2)] + fc2_z[1:], axis=0)
-        fc2_beside = turn(fc2_z, dims, FIRST)
     n2_far = other_core(n2).reshape(-1, width)
+    if dims is None:
+        dm_far = other_core(dm)
+    else:
+        (n2,) = meet([fc1_over, fc2_beside, dm_far], n2)
+        (dm_far,) = dm_far.came
+        fc2_z = stack(fc2_z, *fc2_beside.came)
+        fc2_over = turn(fc2_z, dims, SECOND)
+    dm_flat, dm_far = dm.reshape(-1, width), dm_far.reshape(-1, width)
     n2 = n2.reshape(-1, width)
     bias = fc1_bias[None].astype(F32)
     if dims is not None:
-        fc2_z = jnp.concatenate([fc2_z, after(fc2_beside, n2)], axis=0)
-        fc2_over = turn(fc2_z, dims, SECOND)
         n2 = after(n2, fc2_z)
-        size = fc1.shape[1]
         hidden_in = [
-            ((own_h, 0), (over_h, 0), (fc1_z, 0), (fc1_over, 0)),
-            ((own_h, size), (over_h, size), (fc2_z, 0), (fc2_over, 0)),
+            ((own, attend_size), (over, attend_size), (fc1_z, 0), (*fc1_over.came, 0)),
+            ((own, attend_size + size), (over, attend_size + size), (fc2_z, 0), (fc2_over, 0)),
         ]
     fc2_part = hidden_fwd(meta, n2, n2_far, dm_flat, dm_far, bias, hidden_in[0])
     if dims is not None:
@@ -831,59 +962,59 @@
         back_own = after(back_own, fc2_sum.sent)
 
     shared = (meta, vecs, jnp.asarray(gather, BF16), table_back, q, k, v, p, weights, att, n1)
-    bias_sums, table_grad, attend_sums, changes = [], 0.0, [], []
-    ins = (back_own, back_far, x1, dm)
     half = width // 2
-    for part, count in enumerate(BACK_PARTS):
-        last = part == len(BACK_PARTS) - 1
-        made = attend_back(BACK_PARTS[:part], count, *shared, ins)
-        if part == 0:
-            sums2, *made, dx1, da = made
-        if last:
-            sums1, *made = made
-        bias_sums.append(made[0])
-        table_grad = table_grad + made[1]
-        mine, theirs, change = made[2:]
-        changes.append(change)
-        if dims is None:
-            attend_sums.append(
-                lax.psum_scatter(add(mine, other_core(theirs)), "dp", scatter_dimension=0, tiled=True)
-            )
-        elif not last:
-            came = Flow(other_core(theirs))
-            da, mine = meet([fc2_sum, fc1_sum], da, mine)
-            fc2_sum.third()
-            fc1_sum.second()
-            both = add(mine, came.came[0]).astype(BF16)
-            first = Scatter(both[:half], both[half:], dims)
-            da = after(da, both)
-        ins = (da, tok, dx1, *changes)
-    result = change
-    qv_sums = jnp.concatenate(bias_sums, axis=1)
-    rel_sums = table_grad[:64, :HDIM] + table_grad[:64, HDIM:]
-    fc1_sums = jnp.concatenate(
-        [jnp.where(is_first, fc1_bias_part, 0.0), jnp.where(is_first, 0.0, fc1_bias_part)], axis=1
+    def block_of(out_far):
+        branch = add(out_own, out_far).reshape(x1.shape) + vecs[7]
+        row_index = core * WIN + jnp.arange(WIN)
+        valid = (row_index[None, :, None] < heights[:, None, None]) & (
+            jnp.arange(WIN)[None, None, :] < widths[:, None, None]
+        )
+        return jnp.where(valid[..., None], unpadded(x1 + branch), 0.0).astype(BF16)
+
+    def core_rows(wholes):
+        whole = jnp.stack(
+            [
+                jnp.concatenate([part.reshape(part.shape[0], 2, -1)[:, at] for part in wholes], axis=1)
+                for at in range(2)
+            ]
+        )
+        rows = whole.shape[1] // 2
+        cuts = whole[:, :rows], whole[:, rows:]
+        return jnp.where(is_first, *cuts), jnp.where(is_first, *cuts[::-1])
+
+    count0, count1 = BACK_PARTS
+    sums2, bias0, table0, mine0, theirs0, change, dx1, da = attend_back(
+        (), count0, *shared, (back_own, back_far, x1, dm)
     )
-    flat = jnp.concatenate(
-        [
-            jnp.concatenate([sums1, qv_sums, sums2], axis=0).reshape(-1, LANES),
-            rel_sums.reshape(-1, LANES),
-            fc1_sums.reshape(-1, LANES),
-        ],
-        axis=0,
+    if dims is not None:
+        da, mine0, theirs0 = meet([fc2_sum, fc1_sum], da, mine0, theirs0)
+        came0 = other_core(theirs0)
+        fc2_sum.third()
+        fc1_sum.second()
+        both = add(mine0, came0).astype(BF16)
+        first = Scatter(both[:half], both[half:], dims)
+        da = after(da, both)
+    flat, mine, theirs, result = attend_back(
+        (count0,), count1, *shared, (da, sums2, bias0, table0, fc1_bias_part, tok, dx1, change)
     )
     if dims is None:
-        flat = lax.psum(flat + other_core(flat), "dp")
-        out_far = other_core(out_far)
+        result, block_out = unpadded(result), block_of(other_core(out_far))
         fc1_sum, fc2_sum = (
             lax.psum_scatter(
                 jnp.concatenate(parts, axis=0).astype(F32), "dp", scatter_dimension=0, tiled=True
             )
             for parts in (fc1_part, fc2_part)
         )
+        wholes = [
+            lax.psum_scatter(add(own, other_core(far)), "dp", scatter_dimension=0, tiled=True)
+            for own, far in ((mine0, theirs0), (mine, theirs))
+        ]
+        near, far = core_rows(wholes)
+        came = other_core(far)
+        flat = lax.psum(flat, ("dp", "mp"))
     else:
-        mine, theirs, flat, out_far = meet([fc2_sum, fc1_sum, first], mine, theirs, flat, out_far)
         came, flat_came = Flow(other_core(theirs)), Flow(other_core(flat))
+        mine, flat, out_far, result = meet([fc2_sum, fc1_sum, first], mine, flat, out_far, result)
         first.second()
         fc1_sum.halve()
         mine, flat, out_far = meet([came, flat_came, first], mine, flat, out_far)
@@ -892,49 +1023,43 @@
         flat = flat + flat_came.came[0]
         flat_came = Flow(turn(flat, dims, SECOND))
         first.halve()
-        fc2_sum = fc2_sum.last()
-        out_far = other_core(out_far)
+        late = Flow(other_core(out_far))
         flat, result = meet([flat_came, second, fc1_sum], flat, result)
         flat = flat + flat_came.came[0]
         flat_came = Flow(turn(flat, dims, FIRST))
         second.second()
         fc1_sum.quarter()
-        flat, out_far = meet([flat_came, first, second, fc1_sum], flat, out_far)
+        fc2_sum = fc2_sum.last()
+        result = unpadded(result)
+        flat, fc2_sum, result = meet([flat_came, first, second, fc1_sum, late], flat, fc2_sum, result)
         flat = flat + flat_came.came[0]
         flat_came = Flow(swap_z(flat, dims, 2))
         second.third()
         first.quarter()
+        fc1_sum.near, late.came[0] = meet([], fc1_sum.near, late.came[0], second.sent, first.sent)[:2]
         fc1_sum = fc1_sum.last()
-        flat, fc1_sum = meet([flat_came, second, first], flat, fc1_sum)
+        block_out = block_of(late.came[0])
+        flat, fc1_sum, block_out = meet([flat_came, second, first], flat, fc1_sum, block_out)
+
+        share = shape((2, width // len(FIRST) // dims[0] // dims[1] // dims[2], width), F32)
+        near, far = staged(
+            partial(core_rows_kernel, 2), [share, share], first.near, *first.came, second.near, *second.came, meta=meta
+        )
+        came = other_core(far)
         flat = flat + flat_came.came[0]
-        flat = flat + swap_z(flat, dims, 1)
-        attend_sums = [first.last(), second.last()]
-    branch = add(out_own, out_far).reshape(x1.shape) + vecs[7]
-    block_out = unpadded(x1 + branch)
-    block_out = jnp.where(valid[..., None], block_out, 0.0).astype(BF16)
-
-    whole = jnp.stack(
-        [
-            jnp.concatenate([part[:, at * (part.shape[1] // 2) :][:, : part.shape[1] // 2] for part in attend_sums], axis=1)
-            for at in range(2)
-        ]
-    )
-    rows = whole.shape[1] // 2
-    near = jnp.where(is_first, whole[:, :rows], whole[:, rows:])
-    came = other_core(jnp.where(is_first, whole[:, rows:], whole[:, :rows]))
-    (q_grad, k_grad), (v_grad, proj_grad) = jnp.where(is_first, near, came), jnp.where(is_first, came, near)
-    qkv_grad = jnp.concatenate([q_grad, k_grad, v_grad], axis=1)
-    at = 8 * width // LANES
-    vec_sums = flat[:at].reshape(8, width)
-    rel = flat[at : at + 32].reshape(64, HDIM)
-    fc1_bias_grad = lax.dynamic_index_in_dim(flat[at + 32 :].reshape(2, -1), core, 0, keepdims=False)
+        flat_came = swap_z(flat, dims, 1)
+        flat = flat + after(flat_came, far)
+    rows = near.shape[1]
+    outs = [shape((rows, 3 * width), F32), shape((rows, width), F32)]
+    qkv_grad, proj_grad = staged(last_rows_kernel, outs, near, came, meta=meta)
+    vec_sums, fc1_bias_grad, rel = unpacked(flat, core)
     share = norm1_gain.shape[0]
     device = lax.axis_index("dp") * 2 + core
     mine = lax.dynamic_slice_in_dim(vec_sums, device * share, share, axis=1)
     rels = rel_pos_h.shape[0]
     return (
         block_out,
-        unpadded(result),
+        result,
         mine[0],
         mine[1],
         qkv_grad,

time: 232 us -> 223 us (0.961)
  Pallas kernels: 71.3 us -> 77.1 us
  local copies, waits for them, and re-layouts: 20.4 us -> 15.1 us
  other arithmetic: 17.5 us -> 13.6 us
  waiting for transfers between devices: 55.7 us -> 52.3 us
    ppermute x35 -> x33, waiting for transfers between devices: 40.5 us -> 31.1 us  [turn(): return lax.ppermute(values, ('dp', 'mp'), pairs)]
    pallas_call x0 -> x9, Pallas kernels: none -> 7.4 us  [the longest x7 3.94 us: stack(): pl.pallas_call(partial(stack_kernel, len(parts)), out_shape=shape((rows,...]
    unnamed x83 -> x90, local copies, waits for them, and re-layouts: 11.1 us -> 4.4 us
    ppermute x12, waiting for transfers between devices: 2.27 us -> 7.04 us  [other_core(): return lax.ppermute(values, 'mp', [(0, 1), (1, 0)])]
    pallas_call x2, Pallas kernels: 30.2 us -> 27.4 us  [attend_back(): pl.pallas_call(partial(attend_back_kernel, before, count), out_shape=smal...]
    concatenate x9 -> x2, other arithmetic: 2.87 us -> 0.09 us  [the longest x1 0.05 us: local(): jnp.concatenate([own[:, :attend_size], over[:, :attend_size]], axis=0)]
    ppermute x35 -> x33, starting transfers between devices: 52.5 us -> 50.2 us  [turn(): return lax.ppermute(values, ('dp', 'mp'), pairs)]
  transfers between devices with their start and end apart: 53 -> 51, of which waited for: 18 -> 20; matrix products, arithmetic and copies ran while one was open for 11% -> 9% of each run, Pallas kernels for 31% -> 34%
where the time goes in v5:
time: 223 us; the launch traced here: 220 us
  Pallas kernels  77.1 us (35%)
  starting transfers between devices  59.7 us (27%)
  waiting for transfers between devices  52.3 us (23%)
  local copies, waits for them, and re-layouts  15.1 us (7%)
  other arithmetic  13.6 us (6%)
    ppermute x33, starting transfers between devices, turn(): return lax.ppermute(values, ('dp', 'mp'), pairs)  50.2 us
    ppermute x33, waiting for transfers between devices, turn(): return lax.ppermute(values, ('dp', 'mp'), pairs)  31.1 us
    pallas_call x2, Pallas kernels, attend_back(): pl.pallas_call(partial(attend_back_kernel, before, count), out_shape=smal...  27.4 us
    pallas_call x1, Pallas kernels, hidden_back(): pl.pallas_call(partial(hidden_back_kernel, bases0, bases1), out_shape=[sh...  18.5 us
    pallas_call x1, Pallas kernels, attend(): pl.pallas_call(partial(attend_kernel, count, total), out_shape=[shape((8,...  14.3 us
    ppermute x6, waiting for transfers between devices, swap_z(): return lax.ppermute(values, 'dp', pairs)  14.2 us
    pallas_call x1, Pallas kernels, hidden_fwd(): pl.pallas_call(partial(hidden_fwd_kernel, bases), out_shape=[shape((width...  9.49 us
    ppermute x6, starting transfers between devices, swap_z(): return lax.ppermute(values, 'dp', pairs)  8.03 us
  transfers between devices with their start and end apart: 51, of which 20 were waited for; matrix products, arithmetic and copies ran while one was open for 9% of the time, Pallas kernels for 34%

profile of v5, /device:TPU:0, one launch (start us, length us, event | category | flops | bytes accessed | tf_op | source)
XLA Modules:
  0.0 219.6 jit_solution(8940220323815708370)
XLA Ops:
  6.2 3.0 %collective-permute-start.1 = (bf16[48,1664]{1,0:T(8,128)(2,1)S(1)}, bf16[48,1664]{1,0:T(8,128)(2,1)S(1)}, u32[]{:S(2)}, u32[]{:S(2)}) collective-permute-start(bf16[48,1664]{1,0:T(8,128)(2,1)S(1)} %pad_maximum_fusion.4), channel_id=1, source_target_pairs={{0,8},{1,9},{2,10},{3,11},{4,12},{5,13},{6,14},{7,15},{8,16},{9,17... | collective-permute-start | bytes 479240 | tf_op jit(solution)/shard_map/ppermute | solution.py:599
  9.2 2.6 %collective-permute-start.2 = (bf16[48,1664]{1,0:T(8,128)(2,1)S(1)}, bf16[48,1664]{1,0:T(8,128)(2,1)S(1)}, u32[]{:S(2)}, u32[]{:S(2)}) collective-permute-start(bf16[48,1664]{1,0:T(8,128)(2,1)S(1)} %pad_maximum_fusion.4), channel_id=1, source_target_pairs={{0,16},{1,17},{2,18},{3,19},{4,20},{5,21},{6,22},{7,23},{8,24},{9,... | collective-permute-start | bytes 479240 | tf_op jit(solution)/shard_map/ppermute | solution.py:599
  18.6 4.0 %collective-permute-done.2.refs_1_ = bf16[48,1664]{1,0:T(8,128)(2,1)S(1)} collective-permute-done((bf16[48,1664]{1,0:T(8,128)(2,1)S(1)}, bf16[48,1664]{1,0:T(8,128)(2,1)S(1)}, u32[]{:S(2)}, u32[]{:S(2)}) %collective-permute-start.2) | collective-permute-done | bytes 159776 | tf_op jit(solution)/shard_map/ppermute | solution.py:599
  26.9 3.9 %collective-permute-start.7 = (bf16[48,1536]{1,0:T(8,128)(2,1)S(1)}, bf16[48,1536]{1,0:T(8,128)(2,1)S(1)}, u32[]{:S(2)}, u32[]{:S(2)}) collective-permute-start(bf16[48,1536]{1,0:T(8,128)(2,1)S(1)} %copy-done.37), channel_id=1, source_target_pairs={{0,8},{1,9},{2,10},{3,11},{4,12},{5,13},{6,14},{7,15},{8,16},{9,17... | collective-permute-start | bytes 442376 | tf_op jit(solution)/shard_map/ppermute | solution.py:599
  33.2 3.5 %collective-permute-done.7.refs_0_ = bf16[48,1536]{1,0:T(8,128)(2,1)S(1)} collective-permute-done((bf16[48,1536]{1,0:T(8,128)(2,1)S(1)}, bf16[48,1536]{1,0:T(8,128)(2,1)S(1)}, u32[]{:S(2)}, u32[]{:S(2)}) %collective-permute-start.7) | collective-permute-done | bytes 147488 | tf_op jit(solution)/shard_map/ppermute | solution.py:599
  36.7 4.5 %collective-permute-done.8.refs_1_ = bf16[48,1536]{1,0:T(8,128)(2,1)S(1)} collective-permute-done((bf16[48,1536]{1,0:T(8,128)(2,1)S(1)}, bf16[48,1536]{1,0:T(8,128)(2,1)S(1)}, u32[]{:S(2)}, u32[]{:S(2)}) %collective-permute-start.8) | collective-permute-done | bytes 147488 | tf_op jit(solution)/shard_map/ppermute | solution.py:599
  45.9 4.0 %collective-permute-start.12 = (bf16[48,1536]{1,0:T(8,128)(2,1)S(1)}, bf16[48,1536]{1,0:T(8,128)(2,1)S(1)}, u32[]{:S(2)}, u32[]{:S(2)}) collective-permute-start(bf16[48,1536]{1,0:T(8,128)(2,1)S(1)} %bitcast.84), channel_id=1, source_target_pairs={{0,8},{1,9},{2,10},{3,11},{4,12},{5,13},{6,14},{7,15},{8,16},{9,17... | collective-permute-start | bytes 442376 | tf_op jit(solution)/shard_map/ppermute | solution.py:599
  53.0 2.2 collective-permute-done.12.refs_0_
  55.2 4.4 %collective-permute-done.13.refs_1_ = bf16[48,1536]{1,0:T(8,128)(2,1)S(1)} collective-permute-done((bf16[48,1536]{1,0:T(8,128)(2,1)S(1)}, bf16[48,1536]{1,0:T(8,128)(2,1)S(1)}, u32[]{:S(2)}, u32[]{:S(2)}) %collective-permute-start.13) | collective-permute-done | bytes 147488 | tf_op jit(solution)/shard_map/ppermute | solution.py:599
  67.0 14.3 %attend.1 = (f32[8,768]{1,0:T(8,128)S(1)}, bf16[2,224,768]{2,1,0:T(8,128)(2,1)S(1)}, bf16[2,224,768]{2,1,0:T(8,128)(2,1)}, bf16[2,256,768]{2,1,0:T(8,128)(2,1)},...) custom-call(s32[80]{0:T(128)S(1)} %concatenate.60.meta.refs_0_, ...), custom_call_target="tpu_custom_call" | custom-call | flops 1000 | bytes 1000 | tf_op jit(solution)/shard_map/attend/pallas_call | solution.py:195
  84.4 2.1 collective-permute-done.21
  86.6 9.5 %hidden_fwd.1 = (bf16[384,1536]{1,0:T(8,128)(2,1)}, bf16[384,1536]{1,0:T(8,128)(2,1)}) custom-call(s32[80]{0:T(128)S(1)} %concatenate.60.meta.refs_0_, bf16[448,768]{1,0:T(8,128)(2,1)S(1)} %bitcast.68, bf16[448,768]{1,0:T(8,128)(2,1)S(1)} %bitcast.69, bf16[448,768]{1,0:T(8,128)(2,1)} %bitcast.72, bf16[448,768]{1,0:T(8,128)(2,1)} %bitcast.79, ...), custom_call_target="tpu_custom_call" | custom-call | flops 1000 | bytes 1000 | tf_op jit(solution)/shard_map/hidden_fwd/pallas_call | solution.py:255
  97.5 18.5 %hidden_back.1 = (f32[1,1536]{1,0:T(1,128)S(1)}, bf16[384,1536]{1,0:T(8,128)(2,1)}, bf16[384,1536]{1,0:T(8,128)(2,1)}, f32[448,768]{1,0:T(8,128)}, bf16[448,768]...) custom-call(s32[80]{0:T(128)S(1)} %concatenate.60.meta.refs_0_, bf16[448,768]{1,0:T(8,128)(2,1)} %bitcast.67, ...), custom_call_target="tpu_custom_call" | custom-call | flops 1000 | bytes 1000 | tf_op jit(solution)/shard_map/hidden_back/pallas_call | solution.py:320
  120.1 15.0 %attend_back.2 = (f32[4,768]{1,0:T(4,128)S(1)}, f32[2,512]{1,0:T(2,128)S(1)}, f32[128,128]{1,0:T(8,128)S(1)}, bf16[768,1024]{1,0:T(8,128)(2,1)}, bf16[768,1024]{...) custom-call(s32[80]{0:T(128)S(1)} %concatenate.60.meta.refs_0_, ...), custom_call_target="tpu_custom_call" | custom-call | flops 1000 | bytes 1000 | tf_op jit(solution)/shard_map/attend_back/pallas_call | solution.py:576
  135.1 3.8 %collective-permute-done.25 = bf16[384,1536]{1,0:T(8,128)(2,1)S(1)} collective-permute-done((bf16[384,1536]{1,0:T(8,128)(2,1)}, bf16[384,1536]{1,0:T(8,128)(2,1)S(1)}, u32[]{:S(2)}, u32[]{:S(2)}) %collective-permute-start.25) | collective-permute-done | bytes 1179680 | tf_op jit(solution)/shard_map/ppermute | solution.py:599
  146.2 4.4 %collective-permute-start.30 = (bf16[48,1536]{1,0:T(8,128)(2,1)}, bf16[48,1536]{1,0:T(8,128)(2,1)}, u32[]{:S(2)}, u32[]{:S(2)}) collective-permute-start(bf16[48,1536]{1,0:T(8,128)(2,1)} %get-tuple-element.290), channel_id=1, source_target_pairs={{0,24},{1,25},{2,26},{3,27},{4,28},{5,29},{6,30},{7,31},{8,0},{9,1... | collective-permute-start | bytes 442376 | tf_op jit(solution)/shard_map/ppermute | solution.py:599
  151.7 12.4 %attend_back.3 = (f32[48,512]{1,0:T(8,128)S(1)}, bf16[768,512]{1,0:T(8,128)(2,1)}, bf16[768,512]{1,0:T(8,128)(2,1)}, f32[2,224,768]{2,1,0:T(8,128)}) custom-call(s32[80]{0:T(128)S(1)} %concatenate.60.meta.refs_0_, f32[8,768]{1,0:T(8,128)S(1)} %get-tuple-element.181.vecs, bf16[256,128]{1,0:T(8,128)(2,1)S(1)} %copy-done.10, ...), custom_call_target="tpu_custom_call" | custom-call | flops 1000 | bytes 1000 | tf_op jit(solution)/shard_map/attend_back/pallas_call | solution.py:576
  170.5 5.2 %collective-permute-done.35 = bf16[192,1024]{1,0:T(8,128)(2,1)S(1)} collective-permute-done((bf16[192,1024]{1,0:T(8,128)(2,1)S(1)}, bf16[192,1024]{1,0:T(8,128)(2,1)S(1)}, u32[]{:S(2)}, u32[]{:S(2)}) %collective-permute-start.35) | collective-permute-done | bytes 393248 | tf_op jit(solution)/shard_map/ppermute | solution.py:599
  181.0 9.5 %collective-permute-done.38 = bf16[96,1536]{1,0:T(8,128)(2,1)S(1)} collective-permute-done((bf16[96,1536]{1,0:T(8,128)(2,1)S(1)}, bf16[96,1536]{1,0:T(8,128)(2,1)S(1)}, u32[]{:S(2)}, u32[]{:S(2)}) %collective-permute-start.38) | collective-permute-done | bytes 294944 | tf_op jit(solution)/shard_map/ppermute | solution.py:613
  194.7 2.0 copy.67
  197.6 2.1 collective-permute-start.48
  201.9 2.8 %collective-permute-start.44 = (f32[48,512]{1,0:T(8,128)S(1)}, f32[48,512]{1,0:T(8,128)S(1)}, u32[]{:S(2)}, u32[]{:S(2)}) collective-permute-start(f32[48,512]{1,0:T(8,128)S(1)} %add.845), channel_id=1, source_target_pairs={{0,16},{2,18},{4,20},{6,22},{8,24},{10,26},{12,28},{14,30},{16,0},... | collective-permute-start | bytes 294920 | tf_op jit(solution)/shard_map/ppermute | solution.py:613
  208.5 2.0 collective-permute-done.44
  212.5 2.7 %collective-permute-done.49 = f32[48,512]{1,0:T(8,128)S(1)} collective-permute-done((f32[48,512]{1,0:T(8,128)S(1)}, f32[48,512]{1,0:T(8,128)S(1)}, u32[]{:S(2)}, u32[]{:S(2)}) %collective-permute-start.49) | collective-permute-done | bytes 98336 | tf_op jit(solution)/shard_map/ppermute | solution.py:613
  (258 shorter events, 79.5 us)
Async XLA Ops:
  6.2 12.4 %collective-permute-start.1 = (bf16[48,1664]{1,0:T(8,128)(2,1)S(1)}, bf16[48,1664]{1,0:T(8,128)(2,1)S(1)}, u32[]{:S(2)}, u32[]{:S(2)}) collective-permute-start(bf16[48,1664]{1,0:T(8,128)(2,1)S(1)} %pad_maximum_fusion.4), channel_id=1, source_target_pairs={{0,8},{1,9},{2,10},{3,11},{4,12},{5,13},{6,14},{7,15},{8,16},{9,17... | collective-permute-start | bytes 479240 | tf_op jit(solution)/shard_map/ppermute | solution.py:599
  9.2 13.4 %collective-permute-start.2 = (bf16[48,1664]{1,0:T(8,128)(2,1)S(1)}, bf16[48,1664]{1,0:T(8,128)(2,1)S(1)}, u32[]{:S(2)}, u32[]{:S(2)}) collective-permute-start(bf16[48,1664]{1,0:T(8,128)(2,1)S(1)} %pad_maximum_fusion.4), channel_id=1, source_target_pairs={{0,16},{1,17},{2,18},{3,19},{4,20},{5,21},{6,22},{7,23},{8,24},{9,... | collective-permute-start | bytes 479240 | tf_op jit(solution)/shard_map/ppermute | solution.py:599
  23.2 18.5 %collective-permute-start.5 = (bf16[96,4736]{1,0:T(8,128)(2,1)S(1)}, bf16[96,4736]{1,0:T(8,128)(2,1)S(1)}, u32[]{:S(2)}, u32[]{:S(2)}) collective-permute-start(bf16[96,4736]{1,0:T(8,128)(2,1)S(1)} %stack.184.refs_0_.refs_4_), channel_id=1, source_target_pairs={{0,4},{1,3},{2,6},{3,1},{4,0},{5,7},{6,2},{7,5},{8,12},{9,11},{10,... | collective-permute-start | bytes 2727944 | tf_op jit(solution)/shard_map/ppermute | solution.py:599
  25.4 15.8 %collective-permute-start.6 = (bf16[144,1664]{1,0:T(8,128)(2,1)S(1)}, bf16[144,1664]{1,0:T(8,128)(2,1)S(1)}, u32[]{:S(2)}, u32[]{:S(2)}) collective-permute-start(bf16[144,1664]{1,0:T(8,128)(2,1)S(1)} %stack.183.refs_0_), channel_id=1, source_target_pairs={{0,2},{1,5},{2,0},{3,7},{4,6},{5,1},{6,4},{7,3},{8,10},{9,13},{10,... | collective-permute-start | bytes 1437704 | tf_op jit(solution)/shard_map/ppermute | solution.py:599
  42.3 18.6 %collective-permute-start.10 = (bf16[288,1664]{1,0:T(8,128)(2,1)S(1)}, bf16[288,1664]{1,0:T(8,128)(2,1)S(1)}, u32[]{:S(2)}, u32[]{:S(2)}) collective-permute-start(bf16[288,1664]{1,0:T(8,128)(2,1)S(1)} %stack.185.refs_2_), channel_id=1, source_target_pairs={{0,4},{1,3},{2,6},{3,1},{4,0},{5,7},{6,2},{7,5},{8,12},{9,11},{10,... | collective-permute-start | bytes 2875400 | tf_op jit(solution)/shard_map/ppermute | solution.py:599
  44.5 15.4 %collective-permute-start.11 = (bf16[144,1536]{1,0:T(8,128)(2,1)S(1)}, bf16[144,1536]{1,0:T(8,128)(2,1)S(1)}, u32[]{:S(2)}, u32[]{:S(2)}) collective-permute-start(bf16[144,1536]{1,0:T(8,128)(2,1)S(1)} %stack.186.refs_0_), channel_id=1, source_target_pairs={{0,2},{1,5},{2,0},{3,7},{4,6},{5,1},{6,4},{7,3},{8,10},{9,13},{10,... | collective-permute-start | bytes 1327112 | tf_op jit(solution)/shard_map/ppermute | solution.py:599
  62.0 20.2 %collective-permute-start.18 = (bf16[288,1536]{1,0:T(8,128)(2,1)S(1)}, bf16[288,1536]{1,0:T(8,128)(2,1)S(1)}, u32[]{:S(2)}, u32[]{:S(2)}) collective-permute-start(bf16[288,1536]{1,0:T(8,128)(2,1)S(1)} %stack.187.refs_2_), channel_id=1, source_target_pairs={{0,4},{1,3},{2,6},{3,1},{4,0},{5,7},{6,2},{7,5},{8,12},{9,11},{10,... | collective-permute-start | bytes 2654216 | tf_op jit(solution)/shard_map/ppermute | solution.py:599
  65.7 16.5 %collective-permute-start.20 = (bf16[2,224,768]{2,1,0:T(8,128)(2,1)S(1)}, bf16[2,224,768]{2,1,0:T(8,128)(2,1)S(1)}, u32[]{:S(2)}, u32[]{:S(2)}) collective-permute-start(bf16[2,224,768]{2,1,0:T(8,128)(2,1)S(1)} %bitcast.71), channel_id=1, source_target_pairs={{0,1},{1,0},{2,3},{3,2},{4,5},{5,4},{6,7},{7,6},{8,9},{9,8},{10,11... | collective-permute-start | bytes 2064392 | tf_op jit(solution)/shard_map/ppermute | solution.py:617
  65.9 16.3 %collective-permute-start.19 = (bf16[144,1536]{1,0:T(8,128)(2,1)S(1)}, bf16[144,1536]{1,0:T(8,128)(2,1)S(1)}, u32[]{:S(2)}, u32[]{:S(2)}) collective-permute-start(bf16[144,1536]{1,0:T(8,128)(2,1)S(1)} %stack.188.refs_0_), channel_id=1, source_target_pairs={{0,2},{1,5},{2,0},{3,7},{4,6},{5,1},{6,4},{7,3},{8,10},{9,13},{10,... | collective-permute-start | bytes 1327112 | tf_op jit(solution)/shard_map/ppermute | solution.py:599
  82.8 13.3 %collective-permute-start.22 = (bf16[288,1536]{1,0:T(8,128)(2,1)S(1)}, bf16[288,1536]{1,0:T(8,128)(2,1)S(1)}, u32[]{:S(2)}, u32[]{:S(2)}) collective-permute-start(bf16[288,1536]{1,0:T(8,128)(2,1)S(1)} %stack.189.refs_6_), channel_id=1, source_target_pairs={{0,4},{1,3},{2,6},{3,1},{4,0},{5,7},{6,2},{7,5},{8,12},{9,11},{10,... | collective-permute-start | bytes 2654216 | tf_op jit(solution)/shard_map/ppermute | solution.py:599
  96.1 19.9 %collective-permute-start.23 = (bf16[384,1536]{1,0:T(8,128)(2,1)}, bf16[384,1536]{1,0:T(8,128)(2,1)S(1)}, u32[]{:S(2)}, u32[]{:S(2)}) collective-permute-start(bf16[384,1536]{1,0:T(8,128)(2,1)} %get-tuple-element.202), channel_id=1, source_target_pairs={{0,4},{1,3},{2,6},{3,1},{4,0},{5,7},{6,2},{7,5},{8,12},{9,11},{10,... | collective-permute-start | bytes 3538952 | tf_op jit(solution)/shard_map/ppermute | solution.py:599
  116.0 22.8 %collective-permute-start.25 = (bf16[384,1536]{1,0:T(8,128)(2,1)}, bf16[384,1536]{1,0:T(8,128)(2,1)S(1)}, u32[]{:S(2)}, u32[]{:S(2)}) collective-permute-start(bf16[384,1536]{1,0:T(8,128)(2,1)} %get-tuple-element.206), channel_id=1, source_target_pairs={{0,4},{1,3},{2,6},{3,1},{4,0},{5,7},{6,2},{7,5},{8,12},{9,11},{10,... | collective-permute-start | bytes 3538952 | tf_op jit(solution)/shard_map/ppermute | solution.py:599
  117.2 17.9 %collective-permute-start.24 = (bf16[192,1536]{1,0:T(8,128)(2,1)S(1)}, bf16[192,1536]{1,0:T(8,128)(2,1)S(1)}, u32[]{:S(2)}, u32[]{:S(2)}) collective-permute-start(bf16[192,1536]{1,0:T(8,128)(2,1)S(1)} %add_convert_fusion.3), channel_id=1, source_target_pairs={{0,2},{1,5},{2,0},{3,7},{4,6},{5,1},{6,4},{7,3},{8,10},{9,13},{10,... | collective-permute-start | bytes 1769480 | tf_op jit(solution)/shard_map/ppermute | solution.py:599
  140.0 25.0 %collective-permute-start.33 = (bf16[192,1536]{1,0:T(8,128)(2,1)}, bf16[192,1536]{1,0:T(8,128)(2,1)}, u32[]{:S(2)}, u32[]{:S(2)}) collective-permute-start(bf16[192,1536]{1,0:T(8,128)(2,1)} %add_convert_fusion.2), channel_id=1, source_target_pairs={{0,2},{1,5},{2,0},{3,7},{4,6},{5,1},{6,4},{7,3},{8,10},{9,13},{10,... | collective-permute-start | bytes 1769480 | tf_op jit(solution)/shard_map/ppermute | solution.py:599
  144.2 20.8 %collective-permute-start.34 = (bf16[384,1024]{1,0:T(8,128)(2,1)}, bf16[384,1024]{1,0:T(8,128)(2,1)}, u32[]{:S(2)}, u32[]{:S(2)}) collective-permute-start(bf16[384,1024]{1,0:T(8,128)(2,1)} %slice.258), channel_id=1, source_target_pairs={{0,4},{1,3},{2,6},{3,1},{4,0},{5,7},{6,2},{7,5},{8,12},{9,11},{10,... | collective-permute-start | bytes 2359304 | tf_op jit(solution)/shard_map/ppermute | solution.py:599
  146.2 17.8 %collective-permute-start.30 = (bf16[48,1536]{1,0:T(8,128)(2,1)}, bf16[48,1536]{1,0:T(8,128)(2,1)}, u32[]{:S(2)}, u32[]{:S(2)}) collective-permute-start(bf16[48,1536]{1,0:T(8,128)(2,1)} %get-tuple-element.290), channel_id=1, source_target_pairs={{0,24},{1,25},{2,26},{3,27},{4,28},{5,29},{6,30},{7,31},{8,0},{9,1... | collective-permute-start | bytes 442376 | tf_op jit(solution)/shard_map/ppermute | solution.py:599
  150.6 14.5 %collective-permute-start.31 = (bf16[48,1536]{1,0:T(8,128)(2,1)}, bf16[48,1536]{1,0:T(8,128)(2,1)}, u32[]{:S(2)}, u32[]{:S(2)}) collective-permute-start(bf16[48,1536]{1,0:T(8,128)(2,1)} %get-tuple-element.289), channel_id=1, source_target_pairs={{0,16},{1,17},{2,18},{3,19},{4,20},{5,21},{6,22},{7,23},{8,24},{9,... | collective-permute-start | bytes 442376 | tf_op jit(solution)/shard_map/ppermute | solution.py:599
  151.6 13.4 %collective-permute-start.32 = (bf16[48,1536]{1,0:T(8,128)(2,1)}, bf16[48,1536]{1,0:T(8,128)(2,1)}, u32[]{:S(2)}, u32[]{:S(2)}) collective-permute-start(bf16[48,1536]{1,0:T(8,128)(2,1)} %get-tuple-element.288), channel_id=1, source_target_pairs={{0,8},{1,9},{2,10},{3,11},{4,12},{5,13},{6,14},{7,15},{8,16},{9,17... | collective-permute-start | bytes 442376 | tf_op jit(solution)/shard_map/ppermute | solution.py:599
  169.1 21.4 %collective-permute-start.38 = (bf16[96,1536]{1,0:T(8,128)(2,1)S(1)}, bf16[96,1536]{1,0:T(8,128)(2,1)S(1)}, u32[]{:S(2)}, u32[]{:S(2)}) collective-permute-start(bf16[96,1536]{1,0:T(8,128)(2,1)S(1)} %pad_maximum_fusion.2), channel_id=1, source_target_pairs={{0,16},{2,18},{4,20},{6,22},{8,24},{10,26},{12,28},{14,30},{16,0},... | collective-permute-start | bytes 884744 | tf_op jit(solution)/shard_map/ppermute | solution.py:613
  176.0 14.4 %collective-permute-start.37 = (bf16[384,512]{1,0:T(8,128)(2,1)S(1)}, bf16[384,512]{1,0:T(8,128)(2,1)S(1)}, u32[]{:S(2)}, u32[]{:S(2)}) collective-permute-start(bf16[384,512]{1,0:T(8,128)(2,1)S(1)} %slice.259), channel_id=1, source_target_pairs={{0,4},{1,3},{2,6},{3,1},{4,0},{5,7},{6,2},{7,5},{8,12},{9,11},{10,... | collective-permute-start | bytes 1179656 | tf_op jit(solution)/shard_map/ppermute | solution.py:599
  177.0 13.4 %collective-permute-start.36 = (f32[48,512]{1,0:T(8,128)S(1)}, f32[48,512]{1,0:T(8,128)S(1)}, u32[]{:S(2)}, u32[]{:S(2)}) collective-permute-start(f32[48,512]{1,0:T(8,128)S(1)} %add.832), channel_id=1, source_target_pairs={{0,4},{1,3},{2,6},{3,1},{4,0},{5,7},{6,2},{7,5},{8,12},{9,11},{10,... | collective-permute-start | bytes 294920 | tf_op jit(solution)/shard_map/ppermute | solution.py:599
  179.4 17.2 %collective-permute-start.40 = (bf16[96,1024]{1,0:T(8,128)(2,1)S(1)}, bf16[96,1024]{1,0:T(8,128)(2,1)S(1)}, u32[]{:S(2)}, u32[]{:S(2)}) collective-permute-start(bf16[96,1024]{1,0:T(8,128)(2,1)S(1)} %pad_maximum_fusion.3), channel_id=1, source_target_pairs={{0,16},{2,18},{4,20},{6,22},{8,24},{10,26},{12,28},{14,30},{16,0},... | collective-permute-start | bytes 589832 | tf_op jit(solution)/shard_map/ppermute | solution.py:613
  181.0 16.5 %collective-permute-start.43 = (bf16[448,768]{1,0:T(8,128)(2,1)S(1)}, bf16[448,768]{1,0:T(8,128)(2,1)S(1)}, u32[]{:S(2)}, u32[]{:S(2)}) collective-permute-start(bf16[448,768]{1,0:T(8,128)(2,1)S(1)} %get-tuple-element.247), channel_id=1, source_target_pairs={{0,1},{1,0},{2,3},{3,2},{4,5},{5,4},{6,7},{7,6},{8,9},{9,8},{10,11... | collective-permute-start | bytes 2064392 | tf_op jit(solution)/shard_map/ppermute | solution.py:617
  197.6 10.8 %collective-permute-start.48 = (bf16[48,1024]{1,0:T(8,128)(2,1)S(1)}, bf16[48,1024]{1,0:T(8,128)(2,1)S(1)}, u32[]{:S(2)}, u32[]{:S(2)}) collective-permute-start(bf16[48,1024]{1,0:T(8,128)(2,1)S(1)} %get-tuple-element.285), channel_id=1, source_target_pairs={{0,8},{2,10},{4,12},{6,14},{8,0},{10,2},{12,4},{14,6},{16,24},{18,... | collective-permute-start | bytes 294920 | tf_op jit(solution)/shard_map/ppermute | solution.py:613
  (71 other events, 577.8 us)

commit v6 on v5

--- a/solution.py
+++ b/solution.py
@@ -275,8 +275,8 @@
     count = len(bases0)
     ins0, ins1 = list(zip(refs[:count], bases0)), list(zip(refs[count : 2 * count], bases1))
     refs = refs[2 * count :]
-    bias_grad, keep, send, back_own, back_far, out_own, out_far = refs[:7]
-    w0, w1, n2s, dms, acts, backs, grad, big, small, sems, out_sems = refs[7:]
+    bias_grad, keep, send, back_own, back_far, acts_out = refs[:6]
+    w0, w1, n2s, dms, acts, backs, grad, big, small, sems, out_sems = refs[6:]
     width, hidden = w0.shape
     halves = (pl.ds(0, 2 * TOK), pl.ds(2 * TOK, 2 * TOK))
     at = 2 * PIECES
@@ -301,13 +301,11 @@
         bias_grad[:, cols] = jnp.sum(back_pre.astype(F32), axis=0, keepdims=True)
         grad[:, cols] = dot_tn(n2s[...], back_pre).astype(BF16)
     outs = pieces_out(meta, grad, pl.ds(0, hidden), keep, send, out_sems, 0)
-    for which, (left, right, own, far) in enumerate(
-        ((backs, w0, back_own, back_far), (acts, w1, out_own, out_far))
-    ):
-        small[which] = dot_nt(left[halves[1]], right[...]).astype(BF16)
-        outs.append(begin(small.at[which], far, out_sems.at[len(outs)]))
-        big[which] = dot_nt(left[halves[0]], right[...])
-        outs.append(begin(big.at[which], own, out_sems.at[len(outs)]))
+    outs.append(begin(acts, acts_out, out_sems.at[len(outs)]))
+    small[...] = dot_nt(backs[halves[1]], w0[...]).astype(BF16)
+    outs.append(begin(small, back_far, out_sems.at[len(outs)]))
+    big[...] = dot_nt(backs[halves[0]], w0[...])
+    outs.append(begin(big, back_own, out_sems.at[len(outs)]))
     finish(outs)
 
 
@@ -321,9 +319,9 @@
         partial(hidden_back_kernel, bases0, bases1),
         out_shape=[shape((1, hidden), F32)]
         + [shape((width // 2, hidden), BF16)] * 2
-        + [shape(one, F32), shape(one, BF16)] * 2,
+        + [shape(one, F32), shape(one, BF16), shape((4 * TOK, hidden), BF16)],
         in_specs=[SMEM] + [HBM] * 4 + [WHOLE] + [HBM] * (2 * len(refs0)),
-        out_specs=[WHOLE] + [HBM] * 6,
+        out_specs=[WHOLE] + [HBM] * 5,
         scratch_shapes=[
             wide,
             wide,
@@ -332,15 +330,52 @@
             pltpu.VMEM((4 * TOK, hidden), BF16),
             pltpu.VMEM((4 * TOK, hidden), BF16),
             wide,
-            pltpu.VMEM((2,) + one, F32),
-            pltpu.VMEM((2,) + one, BF16),
+            pltpu.VMEM(one, F32),
+            pltpu.VMEM(one, BF16),
             pltpu.SemaphoreType.DMA((2 * PIECES + 4,)),
-            pltpu.SemaphoreType.DMA((PIECES + 4,)),
+            pltpu.SemaphoreType.DMA((PIECES + 3,)),
         ],
         compiler_params=params(),
         cost_estimate=COST,
         name="hidden_back",
     )(meta, n2a, n2b, dma, dmb, bias, *refs0, *refs1)
+
+
+def hidden_out_kernel(bases, meta, acts_in, *refs):
+    count = len(bases)
+    ins, (own, far) = list(zip(refs[:count], bases)), refs[count : count + 2]
+    w1, acts, big, small, sems, out_sems = refs[count + 2 :]
+    copies = [begin(acts_in, acts, sems.at[PIECES])]
+    copies += pieces_in(meta, 0, ins, 0, w1, sems, 0)
+    finish(copies)
+    big[...] = dot_nt(acts[: 2 * TOK], w1[...])
+    outs = [begin(big, own, out_sems.at[0])]
+    small[...] = dot_nt(acts[2 * TOK :], w1[...]).astype(BF16)
+    outs.append(begin(small, far, out_sems.at[1]))
+    finish(outs)
+
+
+def hidden_out(meta, acts, width, ins):
+    refs, bases = zip(*ins)
+    hidden = acts.shape[1]
+    one = (2 * TOK, width)
+    return pl.pallas_call(
+        partial(hidden_out_kernel, bases),
+        out_shape=[shape(one, F32), shape(one, BF16)],
+        in_specs=[SMEM] + [HBM] * (1 + len(refs)),
+        out_specs=[HBM] * 2,
+        scratch_shapes=[
+            pltpu.VMEM((width, hidden), BF16),
+            pltpu.VMEM(acts.shape, BF16),
+            pltpu.VMEM(one, F32),
+            pltpu.VMEM(one, BF16),
+            pltpu.SemaphoreType.DMA((PIECES + 1,)),
+            pltpu.SemaphoreType.DMA((2,)),
+        ],
+        compiler_params=params(),
+        cost_estimate=COST,
+        name="hidden_out",
+    )(meta, acts, *refs)
 
 
 def unrelative(grads):
@@ -743,7 +778,7 @@
 class Scatter(Flow):
     def __init__(self, keep, far, dims):
         super().__init__(turn(far, dims, SECOND))
-        self.keep, self.dims = keep, dims
+        self.keep, self.dims, self.sent = keep, dims, far
 
     def second(self):
         half = self.keep.shape[0] // 2
@@ -769,8 +804,8 @@
         even = lax.axis_index("dp") // (self.dims[1] * self.dims[2]) % 2 == 0
         self.near = parts[0]
         self.beside = jnp.where(even, parts[3], parts[1])
-        send = jnp.concatenate([parts[2], jnp.where(even, parts[1], parts[3])], axis=0).astype(BF16)
-        self.came = [swap_z(send, self.dims, 2)]
+        self.sent = jnp.concatenate([parts[2], jnp.where(even, parts[1], parts[3])], axis=0).astype(BF16)
+        self.came = [swap_z(self.sent, self.dims, 2)]
 
     def quarter(self):
         rows = self.near.shape[0]
@@ -951,7 +986,7 @@
     if dims is not None:
         fc2_part = meet([], *fc2_part, fc2_over)[:2]
         fc2_sum = Scatter(*fc2_part, dims)
-    fc1_bias_part, *fc1_part, back_own, back_far, out_own, out_far = hidden_back(
+    fc1_bias_part, *fc1_part, back_own, back_far, acts = hidden_back(
         meta, n2, n2_far, dm_flat, dm_far, bias, *hidden_in
     )
     back_far = other_core(back_far)
@@ -963,7 +998,7 @@
 
     shared = (meta, vecs, jnp.asarray(gather, BF16), table_back, q, k, v, p, weights, att, n1)
     half = width // 2
-    def block_of(out_far):
+    def block_of(out_own, out_far):
         branch = add(out_own, out_far).reshape(x1.shape) + vecs[7]
         row_index = core * WIN + jnp.arange(WIN)
         valid = (row_index[None, :, None] < heights[:, None, None]) & (
@@ -987,8 +1022,9 @@
         (), count0, *shared, (back_own, back_far, x1, dm)
     )
     if dims is not None:
-        da, mine0, theirs0 = meet([fc2_sum, fc1_sum], da, mine0, theirs0)
+        da, mine0, theirs0 = meet([fc2_sum], da, mine0, theirs0)
         came0 = other_core(theirs0)
+        da, mine0 = meet([fc1_sum, fc2_sum], da, mine0)
         fc2_sum.third()
         fc1_sum.second()
         both = add(mine0, came0).astype(BF16)
@@ -998,7 +1034,8 @@
         (count0,), count1, *shared, (da, sums2, bias0, table0, fc1_bias_part, tok, dx1, change)
     )
     if dims is None:
-        result, block_out = unpadded(result), block_of(other_core(out_far))
+        out_own, out_far = hidden_out(meta, acts, width, hidden_in[1])
+        result, block_out = unpadded(result), block_of(out_own, other_core(out_far))
         fc1_sum, fc2_sum = (
             lax.psum_scatter(
                 jnp.concatenate(parts, axis=0).astype(F32), "dp", scatter_dimension=0, tiled=True
@@ -1014,17 +1051,19 @@
         flat = lax.psum(flat, ("dp", "mp"))
     else:
         came, flat_came = Flow(other_core(theirs)), Flow(other_core(flat))
-        mine, flat, out_far, result = meet([fc2_sum, fc1_sum, first], mine, flat, out_far, result)
+        mine, flat, acts, result = meet([fc2_sum, fc1_sum, first], mine, flat, acts, result)
         first.second()
         fc1_sum.halve()
-        mine, flat, out_far = meet([came, flat_came, first], mine, flat, out_far)
+        mine, flat, acts = meet([came, flat_came, first], mine, flat, acts)
         both = add(mine, came.came[0]).astype(BF16)
         second = Scatter(both[:half], both[half:], dims)
         flat = flat + flat_came.came[0]
         flat_came = Flow(turn(flat, dims, SECOND))
         first.halve()
+        acts = after(acts, first.sent, second.sent)
+        out_own, out_far = hidden_out(meta, acts, width, hidden_in[1])
+        flat, result, out_far = meet([flat_came, second, fc1_sum], flat, result, out_far)
         late = Flow(other_core(out_far))
-        flat, result = meet([flat_came, second, fc1_sum], flat, result)
         flat = flat + flat_came.came[0]
         flat_came = Flow(turn(flat, dims, FIRST))
         second.second()
@@ -1038,7 +1077,7 @@
         first.quarter()
         fc1_sum.near, late.came[0] = meet([], fc1_sum.near, late.came[0], second.sent, first.sent)[:2]
         fc1_sum = fc1_sum.last()
-        block_out = block_of(late.came[0])
+        block_out = block_of(out_own, late.came[0])
         flat, fc1_sum, block_out = meet([flat_came, second, first], flat, fc1_sum, block_out)
 
         share = shape((2, width // len(FIRST) // dims[0] // dims[1] // dims[2], width), F32)

time: 223 us -> 220 us (0.987)
  waiting for transfers between devices: 52.3 us -> 44.3 us
  Pallas kernels: 77.1 us -> 80.5 us
    pallas_call x0 -> x1, Pallas kernels: none -> 5.97 us  [hidden_out(): pl.pallas_call(partial(hidden_out_kernel, bases), out_shape=[shape(one, F...]
    ppermute x6, waiting for transfers between devices: 14.2 us -> 8.49 us  [swap_z(): return lax.ppermute(values, 'dp', pairs)]
    pallas_call x1, Pallas kernels: 18.5 us -> 16.1 us  [hidden_back(): pl.pallas_call(partial(hidden_back_kernel, bases0, bases1), out_shape=[sh...]
    ppermute x12, waiting for transfers between devices: 7.04 us -> 4.6 us  [other_core(): return lax.ppermute(values, 'mp', [(0, 1), (1, 0)])]
  transfers between devices with their start and end apart: 51 -> 51, of which waited for: 20 -> 19; matrix products, arithmetic and copies ran while one was open for 9% -> 10% of each run, Pallas kernels for 34% -> 36%
where the time goes in v6:
time: 220 us; the launch traced here: 216 us
  Pallas kernels  80.5 us (37%)
  starting transfers between devices  60.5 us (28%)
  waiting for transfers between devices  44.3 us (20%)
  other arithmetic  15.5 us (7%)
  local copies, waits for them, and re-layouts  13.1 us (6%)
    ppermute x33, starting transfers between devices, turn(): return lax.ppermute(values, ('dp', 'mp'), pairs)  50.5 us
    ppermute x33, waiting for transfers between devices, turn(): return lax.ppermute(values, ('dp', 'mp'), pairs)  31.2 us
    pallas_call x2, Pallas kernels, attend_back(): pl.pallas_call(partial(attend_back_kernel, before, count), out_shape=smal...  27.2 us
    pallas_call x1, Pallas kernels, hidden_back(): pl.pallas_call(partial(hidden_back_kernel, bases0, bases1), out_shape=[sh...  16.1 us
    pallas_call x1, Pallas kernels, attend(): pl.pallas_call(partial(attend_kernel, count, total), out_shape=[shape((8,...  14.3 us
    pallas_call x1, Pallas kernels, hidden_fwd(): pl.pallas_call(partial(hidden_fwd_kernel, bases), out_shape=[shape((width...  9.5 us
    ppermute x6, waiting for transfers between devices, swap_z(): return lax.ppermute(values, 'dp', pairs)  8.49 us
    ppermute x6, starting transfers between devices, swap_z(): return lax.ppermute(values, 'dp', pairs)  8.26 us
  transfers between devices with their start and end apart: 51, of which 19 were waited for; matrix products, arithmetic and copies ran while one was open for 10% of the time, Pallas kernels for 36%

profile of v6, /device:TPU:0, one launch (start us, length us, event | category | flops | bytes accessed | tf_op | source)
XLA Modules:
  0.0 215.8 jit_solution(9579691045435107551)
XLA Ops:
  6.2 3.0 %collective-permute-start.1 = (bf16[48,1664]{1,0:T(8,128)(2,1)S(1)}, bf16[48,1664]{1,0:T(8,128)(2,1)S(1)}, u32[]{:S(2)}, u32[]{:S(2)}) collective-permute-start(bf16[48,1664]{1,0:T(8,128)(2,1)S(1)} %pad_maximum_fusion.4), channel_id=1, source_target_pairs={{0,8},{1,9},{2,10},{3,11},{4,12},{5,13},{6,14},{7,15},{8,16},{9,17... | collective-permute-start | bytes 479240 | tf_op jit(solution)/shard_map/ppermute | solution.py:634
  9.2 2.6 %collective-permute-start.2 = (bf16[48,1664]{1,0:T(8,128)(2,1)S(1)}, bf16[48,1664]{1,0:T(8,128)(2,1)S(1)}, u32[]{:S(2)}, u32[]{:S(2)}) collective-permute-start(bf16[48,1664]{1,0:T(8,128)(2,1)S(1)} %pad_maximum_fusion.4), channel_id=1, source_target_pairs={{0,16},{1,17},{2,18},{3,19},{4,20},{5,21},{6,22},{7,23},{8,24},{9,... | collective-permute-start | bytes 479240 | tf_op jit(solution)/shard_map/ppermute | solution.py:634
  18.5 4.0 %collective-permute-done.2.refs_1_ = bf16[48,1664]{1,0:T(8,128)(2,1)S(1)} collective-permute-done((bf16[48,1664]{1,0:T(8,128)(2,1)S(1)}, bf16[48,1664]{1,0:T(8,128)(2,1)S(1)}, u32[]{:S(2)}, u32[]{:S(2)}) %collective-permute-start.2) | collective-permute-done | bytes 159776 | tf_op jit(solution)/shard_map/ppermute | solution.py:634
  26.9 3.9 %collective-permute-start.7 = (bf16[48,1536]{1,0:T(8,128)(2,1)S(1)}, bf16[48,1536]{1,0:T(8,128)(2,1)S(1)}, u32[]{:S(2)}, u32[]{:S(2)}) collective-permute-start(bf16[48,1536]{1,0:T(8,128)(2,1)S(1)} %copy-done.34), channel_id=1, source_target_pairs={{0,8},{1,9},{2,10},{3,11},{4,12},{5,13},{6,14},{7,15},{8,16},{9,17... | collective-permute-start | bytes 442376 | tf_op jit(solution)/shard_map/ppermute | solution.py:634
  33.2 3.5 %collective-permute-done.7.refs_0_ = bf16[48,1536]{1,0:T(8,128)(2,1)S(1)} collective-permute-done((bf16[48,1536]{1,0:T(8,128)(2,1)S(1)}, bf16[48,1536]{1,0:T(8,128)(2,1)S(1)}, u32[]{:S(2)}, u32[]{:S(2)}) %collective-permute-start.7) | collective-permute-done | bytes 147488 | tf_op jit(solution)/shard_map/ppermute | solution.py:634
  36.7 4.5 %collective-permute-done.8.refs_1_ = bf16[48,1536]{1,0:T(8,128)(2,1)S(1)} collective-permute-done((bf16[48,1536]{1,0:T(8,128)(2,1)S(1)}, bf16[48,1536]{1,0:T(8,128)(2,1)S(1)}, u32[]{:S(2)}, u32[]{:S(2)}) %collective-permute-start.8) | collective-permute-done | bytes 147488 | tf_op jit(solution)/shard_map/ppermute | solution.py:634
  46.0 4.0 %collective-permute-start.12 = (bf16[48,1536]{1,0:T(8,128)(2,1)S(1)}, bf16[48,1536]{1,0:T(8,128)(2,1)S(1)}, u32[]{:S(2)}, u32[]{:S(2)}) collective-permute-start(bf16[48,1536]{1,0:T(8,128)(2,1)S(1)} %bitcast.84), channel_id=1, source_target_pairs={{0,8},{1,9},{2,10},{3,11},{4,12},{5,13},{6,14},{7,15},{8,16},{9,17... | collective-permute-start | bytes 442376 | tf_op jit(solution)/shard_map/ppermute | solution.py:634
  53.0 2.2 %collective-permute-done.12.refs_0_ = bf16[48,1536]{1,0:T(8,128)(2,1)S(1)} collective-permute-done((bf16[48,1536]{1,0:T(8,128)(2,1)S(1)}, bf16[48,1536]{1,0:T(8,128)(2,1)S(1)}, u32[]{:S(2)}, u32[]{:S(2)}) %collective-permute-start.12) | collective-permute-done | bytes 147488 | tf_op jit(solution)/shard_map/ppermute | solution.py:634
  55.2 4.4 %collective-permute-done.13.refs_1_ = bf16[48,1536]{1,0:T(8,128)(2,1)S(1)} collective-permute-done((bf16[48,1536]{1,0:T(8,128)(2,1)S(1)}, bf16[48,1536]{1,0:T(8,128)(2,1)S(1)}, u32[]{:S(2)}, u32[]{:S(2)}) %collective-permute-start.13) | collective-permute-done | bytes 147488 | tf_op jit(solution)/shard_map/ppermute | solution.py:634
  67.0 14.3 %attend.1 = (f32[8,768]{1,0:T(8,128)S(1)}, bf16[2,224,768]{2,1,0:T(8,128)(2,1)S(1)}, bf16[2,224,768]{2,1,0:T(8,128)(2,1)}, bf16[2,256,768]{2,1,0:T(8,128)(2,1)},...) custom-call(s32[80]{0:T(128)S(1)} %concatenate.60.meta.refs_0_, ...), custom_call_target="tpu_custom_call" | custom-call | flops 1000 | bytes 1000 | tf_op jit(solution)/shard_map/attend/pallas_call | solution.py:195
  84.4 2.1 collective-permute-done.21
  86.5 9.5 %hidden_fwd.1 = (bf16[384,1536]{1,0:T(8,128)(2,1)}, bf16[384,1536]{1,0:T(8,128)(2,1)}) custom-call(s32[80]{0:T(128)S(1)} %concatenate.60.meta.refs_0_, bf16[448,768]{1,0:T(8,128)(2,1)S(1)} %bitcast.67, bf16[448,768]{1,0:T(8,128)(2,1)S(1)} %bitcast.69, bf16[448,768]{1,0:T(8,128)(2,1)} %bitcast.71, bf16[448,768]{1,0:T(8,128)(2,1)} %bitcast.79, ...), custom_call_target="tpu_custom_call" | custom-call | flops 1000 | bytes 1000 | tf_op jit(solution)/shard_map/hidden_fwd/pallas_call | solution.py:255
  97.4 16.1 %hidden_back.1 = (f32[1,1536]{1,0:T(1,128)S(1)}, bf16[384,1536]{1,0:T(8,128)(2,1)}, bf16[384,1536]{1,0:T(8,128)(2,1)}, f32[448,768]{1,0:T(8,128)}, bf16[448,768]...) custom-call(s32[80]{0:T(128)S(1)} %concatenate.60.meta.refs_0_, bf16[448,768]{1,0:T(8,128)(2,1)S(1)} %bitcast.68, ...), custom_call_target="tpu_custom_call" | custom-call | flops 1000 | bytes 1000 | tf_op jit(solution)/shard_map/hidden_back/pallas_call | solution.py:318
  116.6 15.0 %attend_back.2 = (f32[4,768]{1,0:T(4,128)S(1)}, f32[2,512]{1,0:T(2,128)S(1)}, f32[128,128]{1,0:T(8,128)S(1)}, bf16[768,1024]{1,0:T(8,128)(2,1)}, bf16[768,1024]{...) custom-call(s32[80]{0:T(128)S(1)} %concatenate.60.meta.refs_0_, ...), custom_call_target="tpu_custom_call" | custom-call | flops 1000 | bytes 1000 | tf_op jit(solution)/shard_map/attend_back/pallas_call | solution.py:611
  131.8 4.2 %collective-permute-done.24 = bf16[384,1536]{1,0:T(8,128)(2,1)} collective-permute-done((bf16[384,1536]{1,0:T(8,128)(2,1)}, bf16[384,1536]{1,0:T(8,128)(2,1)}, u32[]{:S(2)}, u32[]{:S(2)}) %collective-permute-start.24) | collective-permute-done | bytes 1179680 | tf_op jit(solution)/shard_map/ppermute | solution.py:634
  136.0 2.0 add_convert_fusion.2
  142.1 4.4 %collective-permute-start.30 = (bf16[48,1536]{1,0:T(8,128)(2,1)S(1)}, bf16[48,1536]{1,0:T(8,128)(2,1)S(1)}, u32[]{:S(2)}, u32[]{:S(2)}) collective-permute-start(bf16[48,1536]{1,0:T(8,128)(2,1)S(1)} %get-tuple-element.302), channel_id=1, source_target_pairs={{0,24},{1,25},{2,26},{3,27},{4,28},{5,29},{6,30},{7,31},{8,0},{9,1... | collective-permute-start | bytes 442376 | tf_op jit(solution)/shard_map/ppermute | solution.py:634
  147.6 12.2 %attend_back.3 = (f32[48,512]{1,0:T(8,128)S(1)}, bf16[768,512]{1,0:T(8,128)(2,1)}, bf16[768,512]{1,0:T(8,128)(2,1)}, f32[2,224,768]{2,1,0:T(8,128)}) custom-call(s32[80]{0:T(128)S(1)} %concatenate.60.meta.refs_0_, f32[8,768]{1,0:T(8,128)S(1)} %get-tuple-element.187.vecs, bf16[256,128]{1,0:T(8,128)(2,1)S(1)} %copy-done.11, ...), custom_call_target="tpu_custom_call" | custom-call | flops 1000 | bytes 1000 | tf_op jit(solution)/shard_map/attend_back/pallas_call | solution.py:611
  166.3 3.3 %collective-permute-done.35 = bf16[192,1024]{1,0:T(8,128)(2,1)S(1)} collective-permute-done((bf16[192,1024]{1,0:T(8,128)(2,1)S(1)}, bf16[192,1024]{1,0:T(8,128)(2,1)S(1)}, u32[]{:S(2)}, u32[]{:S(2)}) %collective-permute-start.35) | collective-permute-done | bytes 393248 | tf_op jit(solution)/shard_map/ppermute | solution.py:634
  175.1 6.0 %hidden_out.1 = (f32[448,768]{1,0:T(8,128)}, bf16[448,768]{1,0:T(8,128)(2,1)S(1)}) custom-call(s32[80]{0:T(128)S(1)} %concatenate.60.meta.refs_0_, bf16[896,1536]{1,0:T(8,128)(2,1)} %get-tuple-element.253.acts_in, bf16[96,4736]{1,0:T(8,128)(2,1)} %copy-done, bf16[96,4736]{1,0:T(8,128)(2,1)} %copy-done.13, bf16[288,1536]{1,0:T(8,128)(2,1)S(1)} %copy-done.2, ...), custom_call_target="tpu_custom_call" | custom-call | flops 1000 | bytes 1000 | tf_op jit(solution)/shard_map/hidden_out/pallas_call | solution.py:362
  181.1 4.7 %collective-permute-done.38 = bf16[96,1536]{1,0:T(8,128)(2,1)S(1)} collective-permute-done((bf16[96,1536]{1,0:T(8,128)(2,1)S(1)}, bf16[96,1536]{1,0:T(8,128)(2,1)S(1)}, u32[]{:S(2)}, u32[]{:S(2)}) %collective-permute-start.38) | collective-permute-done | bytes 294944 | tf_op jit(solution)/shard_map/ppermute | solution.py:648
  193.1 2.0 collective-permute-start.48
  197.7 2.5 %collective-permute-start.44 = (f32[48,512]{1,0:T(8,128)S(1)}, f32[48,512]{1,0:T(8,128)S(1)}, u32[]{:S(2)}, u32[]{:S(2)}) collective-permute-start(f32[48,512]{1,0:T(8,128)S(1)} %add.845), channel_id=1, source_target_pairs={{0,16},{2,18},{4,20},{6,22},{8,24},{10,26},{12,28},{14,30},{16,0},... | collective-permute-start | bytes 294920 | tf_op jit(solution)/shard_map/ppermute | solution.py:648
  208.6 2.7 %collective-permute-done.49 = f32[48,512]{1,0:T(8,128)S(1)} collective-permute-done((f32[48,512]{1,0:T(8,128)S(1)}, f32[48,512]{1,0:T(8,128)S(1)}, u32[]{:S(2)}, u32[]{:S(2)}) %collective-permute-start.49) | collective-permute-done | bytes 98336 | tf_op jit(solution)/shard_map/ppermute | solution.py:648
  (267 shorter events, 80.7 us)
Async XLA Ops:
  6.2 12.3 %collective-permute-start.1 = (bf16[48,1664]{1,0:T(8,128)(2,1)S(1)}, bf16[48,1664]{1,0:T(8,128)(2,1)S(1)}, u32[]{:S(2)}, u32[]{:S(2)}) collective-permute-start(bf16[48,1664]{1,0:T(8,128)(2,1)S(1)} %pad_maximum_fusion.4), channel_id=1, source_target_pairs={{0,8},{1,9},{2,10},{3,11},{4,12},{5,13},{6,14},{7,15},{8,16},{9,17... | collective-permute-start | bytes 479240 | tf_op jit(solution)/shard_map/ppermute | solution.py:634
  9.2 13.4 %collective-permute-start.2 = (bf16[48,1664]{1,0:T(8,128)(2,1)S(1)}, bf16[48,1664]{1,0:T(8,128)(2,1)S(1)}, u32[]{:S(2)}, u32[]{:S(2)}) collective-permute-start(bf16[48,1664]{1,0:T(8,128)(2,1)S(1)} %pad_maximum_fusion.4), channel_id=1, source_target_pairs={{0,16},{1,17},{2,18},{3,19},{4,20},{5,21},{6,22},{7,23},{8,24},{9,... | collective-permute-start | bytes 479240 | tf_op jit(solution)/shard_map/ppermute | solution.py:634
  11.8 10.8 %collective-permute-start.3 = (bf16[48,1664]{1,0:T(8,128)(2,1)S(1)}, bf16[48,1664]{1,0:T(8,128)(2,1)S(1)}, u32[]{:S(2)}, u32[]{:S(2)}) collective-permute-start(bf16[48,1664]{1,0:T(8,128)(2,1)S(1)} %pad_maximum_fusion.4), channel_id=1, source_target_pairs={{0,24},{1,25},{2,26},{3,27},{4,28},{5,29},{6,30},{7,31},{8,0},{9,1... | collective-permute-start | bytes 479240 | tf_op jit(solution)/shard_map/ppermute | solution.py:634
  23.2 18.5 %collective-permute-start.5 = (bf16[96,4736]{1,0:T(8,128)(2,1)S(1)}, bf16[96,4736]{1,0:T(8,128)(2,1)S(1)}, u32[]{:S(2)}, u32[]{:S(2)}) collective-permute-start(bf16[96,4736]{1,0:T(8,128)(2,1)S(1)} %stack.184.refs_0_.refs_4_), channel_id=1, source_target_pairs={{0,4},{1,3},{2,6},{3,1},{4,0},{5,7},{6,2},{7,5},{8,12},{9,11},{10,... | collective-permute-start | bytes 2727944 | tf_op jit(solution)/shard_map/ppermute | solution.py:634
  25.4 15.8 %collective-permute-start.6 = (bf16[144,1664]{1,0:T(8,128)(2,1)S(1)}, bf16[144,1664]{1,0:T(8,128)(2,1)S(1)}, u32[]{:S(2)}, u32[]{:S(2)}) collective-permute-start(bf16[144,1664]{1,0:T(8,128)(2,1)S(1)} %stack.183.refs_0_), channel_id=1, source_target_pairs={{0,2},{1,5},{2,0},{3,7},{4,6},{5,1},{6,4},{7,3},{8,10},{9,13},{10,... | collective-permute-start | bytes 1437704 | tf_op jit(solution)/shard_map/ppermute | solution.py:634
  42.3 18.6 %collective-permute-start.10 = (bf16[288,1664]{1,0:T(8,128)(2,1)S(1)}, bf16[288,1664]{1,0:T(8,128)(2,1)S(1)}, u32[]{:S(2)}, u32[]{:S(2)}) collective-permute-start(bf16[288,1664]{1,0:T(8,128)(2,1)S(1)} %stack.185.refs_2_), channel_id=1, source_target_pairs={{0,4},{1,3},{2,6},{3,1},{4,0},{5,7},{6,2},{7,5},{8,12},{9,11},{10,... | collective-permute-start | bytes 2875400 | tf_op jit(solution)/shard_map/ppermute | solution.py:634
  44.5 15.4 %collective-permute-start.11 = (bf16[144,1536]{1,0:T(8,128)(2,1)S(1)}, bf16[144,1536]{1,0:T(8,128)(2,1)S(1)}, u32[]{:S(2)}, u32[]{:S(2)}) collective-permute-start(bf16[144,1536]{1,0:T(8,128)(2,1)S(1)} %stack.186.refs_0_), channel_id=1, source_target_pairs={{0,2},{1,5},{2,0},{3,7},{4,6},{5,1},{6,4},{7,3},{8,10},{9,13},{10,... | collective-permute-start | bytes 1327112 | tf_op jit(solution)/shard_map/ppermute | solution.py:634
  62.0 20.2 %collective-permute-start.18 = (bf16[288,1536]{1,0:T(8,128)(2,1)S(1)}, bf16[288,1536]{1,0:T(8,128)(2,1)S(1)}, u32[]{:S(2)}, u32[]{:S(2)}) collective-permute-start(bf16[288,1536]{1,0:T(8,128)(2,1)S(1)} %stack.187.refs_2_), channel_id=1, source_target_pairs={{0,4},{1,3},{2,6},{3,1},{4,0},{5,7},{6,2},{7,5},{8,12},{9,11},{10,... | collective-permute-start | bytes 2654216 | tf_op jit(solution)/shard_map/ppermute | solution.py:634
  65.8 16.5 %collective-permute-start.20 = (bf16[2,224,768]{2,1,0:T(8,128)(2,1)S(1)}, bf16[2,224,768]{2,1,0:T(8,128)(2,1)S(1)}, u32[]{:S(2)}, u32[]{:S(2)}) collective-permute-start(bf16[2,224,768]{2,1,0:T(8,128)(2,1)S(1)} %bitcast.74), channel_id=1, source_target_pairs={{0,1},{1,0},{2,3},{3,2},{4,5},{5,4},{6,7},{7,6},{8,9},{9,8},{10,11... | collective-permute-start | bytes 2064392 | tf_op jit(solution)/shard_map/ppermute | solution.py:652
  66.0 16.3 %collective-permute-start.19 = (bf16[144,1536]{1,0:T(8,128)(2,1)S(1)}, bf16[144,1536]{1,0:T(8,128)(2,1)S(1)}, u32[]{:S(2)}, u32[]{:S(2)}) collective-permute-start(bf16[144,1536]{1,0:T(8,128)(2,1)S(1)} %stack.188.refs_0_), channel_id=1, source_target_pairs={{0,2},{1,5},{2,0},{3,7},{4,6},{5,1},{6,4},{7,3},{8,10},{9,13},{10,... | collective-permute-start | bytes 1327112 | tf_op jit(solution)/shard_map/ppermute | solution.py:634
  82.8 13.3 %collective-permute-start.22 = (bf16[288,1536]{1,0:T(8,128)(2,1)S(1)}, bf16[288,1536]{1,0:T(8,128)(2,1)S(1)}, u32[]{:S(2)}, u32[]{:S(2)}) collective-permute-start(bf16[288,1536]{1,0:T(8,128)(2,1)S(1)} %stack.189.refs_6_.refs_2_), channel_id=1, source_target_pairs={{0,4},{1,3},{2,6},{3,1},{4,0},{5,7},{6,2},{7,5},{8,12},{9,11},{10,... | collective-permute-start | bytes 2654216 | tf_op jit(solution)/shard_map/ppermute | solution.py:634
  96.1 17.5 %collective-permute-start.23 = (bf16[384,1536]{1,0:T(8,128)(2,1)}, bf16[384,1536]{1,0:T(8,128)(2,1)S(1)}, u32[]{:S(2)}, u32[]{:S(2)}) collective-permute-start(bf16[384,1536]{1,0:T(8,128)(2,1)} %get-tuple-element.207), channel_id=1, source_target_pairs={{0,4},{1,3},{2,6},{3,1},{4,0},{5,7},{6,2},{7,5},{8,12},{9,11},{10,... | collective-permute-start | bytes 3538952 | tf_op jit(solution)/shard_map/ppermute | solution.py:634
  113.8 17.9 %collective-permute-start.25 = (bf16[192,1536]{1,0:T(8,128)(2,1)S(1)}, bf16[192,1536]{1,0:T(8,128)(2,1)S(1)}, u32[]{:S(2)}, u32[]{:S(2)}) collective-permute-start(bf16[192,1536]{1,0:T(8,128)(2,1)S(1)} %add_convert_fusion.3), channel_id=1, source_target_pairs={{0,2},{1,5},{2,0},{3,7},{4,6},{5,1},{6,4},{7,3},{8,10},{9,13},{10,... | collective-permute-start | bytes 1769480 | tf_op jit(solution)/shard_map/ppermute | solution.py:634
  114.8 21.2 %collective-permute-start.24 = (bf16[384,1536]{1,0:T(8,128)(2,1)}, bf16[384,1536]{1,0:T(8,128)(2,1)}, u32[]{:S(2)}, u32[]{:S(2)}) collective-permute-start(bf16[384,1536]{1,0:T(8,128)(2,1)} %get-tuple-element.210), channel_id=1, source_target_pairs={{0,4},{1,3},{2,6},{3,1},{4,0},{5,7},{6,2},{7,5},{8,12},{9,11},{10,... | collective-permute-start | bytes 3538952 | tf_op jit(solution)/shard_map/ppermute | solution.py:634
  138.0 22.5 %collective-permute-start.33 = (bf16[192,1536]{1,0:T(8,128)(2,1)}, bf16[192,1536]{1,0:T(8,128)(2,1)}, u32[]{:S(2)}, u32[]{:S(2)}) collective-permute-start(bf16[192,1536]{1,0:T(8,128)(2,1)} %add_convert_fusion.2), channel_id=1, source_target_pairs={{0,2},{1,5},{2,0},{3,7},{4,6},{5,1},{6,4},{7,3},{8,10},{9,13},{10,... | collective-permute-start | bytes 1769480 | tf_op jit(solution)/shard_map/ppermute | solution.py:634
  139.8 20.7 %collective-permute-start.34 = (bf16[384,1024]{1,0:T(8,128)(2,1)S(1)}, bf16[384,1024]{1,0:T(8,128)(2,1)}, u32[]{:S(2)}, u32[]{:S(2)}) collective-permute-start(bf16[384,1024]{1,0:T(8,128)(2,1)S(1)} %slice.258), channel_id=1, source_target_pairs={{0,4},{1,3},{2,6},{3,1},{4,0},{5,7},{6,2},{7,5},{8,12},{9,11},{10,... | collective-permute-start | bytes 2359304 | tf_op jit(solution)/shard_map/ppermute | solution.py:634
  142.1 17.7 %collective-permute-start.30 = (bf16[48,1536]{1,0:T(8,128)(2,1)S(1)}, bf16[48,1536]{1,0:T(8,128)(2,1)S(1)}, u32[]{:S(2)}, u32[]{:S(2)}) collective-permute-start(bf16[48,1536]{1,0:T(8,128)(2,1)S(1)} %get-tuple-element.302), channel_id=1, source_target_pairs={{0,24},{1,25},{2,26},{3,27},{4,28},{5,29},{6,30},{7,31},{8,0},{9,1... | collective-permute-start | bytes 442376 | tf_op jit(solution)/shard_map/ppermute | solution.py:634
  146.5 14.0 %collective-permute-start.31 = (bf16[48,1536]{1,0:T(8,128)(2,1)S(1)}, bf16[48,1536]{1,0:T(8,128)(2,1)S(1)}, u32[]{:S(2)}, u32[]{:S(2)}) collective-permute-start(bf16[48,1536]{1,0:T(8,128)(2,1)S(1)} %get-tuple-element.301), channel_id=1, source_target_pairs={{0,16},{1,17},{2,18},{3,19},{4,20},{5,21},{6,22},{7,23},{8,24},{9,... | collective-permute-start | bytes 442376 | tf_op jit(solution)/shard_map/ppermute | solution.py:634
  147.5 13.0 %collective-permute-start.32 = (bf16[48,1536]{1,0:T(8,128)(2,1)S(1)}, bf16[48,1536]{1,0:T(8,128)(2,1)S(1)}, u32[]{:S(2)}, u32[]{:S(2)}) collective-permute-start(bf16[48,1536]{1,0:T(8,128)(2,1)S(1)} %get-tuple-element.300), channel_id=1, source_target_pairs={{0,8},{1,9},{2,10},{3,11},{4,12},{5,13},{6,14},{7,15},{8,16},{9,17... | collective-permute-start | bytes 442376 | tf_op jit(solution)/shard_map/ppermute | solution.py:634
  164.5 21.3 %collective-permute-start.38 = (bf16[96,1536]{1,0:T(8,128)(2,1)S(1)}, bf16[96,1536]{1,0:T(8,128)(2,1)S(1)}, u32[]{:S(2)}, u32[]{:S(2)}) collective-permute-start(bf16[96,1536]{1,0:T(8,128)(2,1)S(1)} %pad_maximum_fusion.2), channel_id=1, source_target_pairs={{0,16},{2,18},{4,20},{6,22},{8,24},{10,26},{12,28},{14,30},{16,0},... | collective-permute-start | bytes 884744 | tf_op jit(solution)/shard_map/ppermute | solution.py:648
  169.9 15.9 %collective-permute-start.37 = (bf16[384,512]{1,0:T(8,128)(2,1)S(1)}, bf16[384,512]{1,0:T(8,128)(2,1)S(1)}, u32[]{:S(2)}, u32[]{:S(2)}) collective-permute-start(bf16[384,512]{1,0:T(8,128)(2,1)S(1)} %slice.259), channel_id=1, source_target_pairs={{0,4},{1,3},{2,6},{3,1},{4,0},{5,7},{6,2},{7,5},{8,12},{9,11},{10,... | collective-permute-start | bytes 1179656 | tf_op jit(solution)/shard_map/ppermute | solution.py:634
  172.3 13.5 %collective-permute-start.36 = (f32[48,512]{1,0:T(8,128)S(1)}, f32[48,512]{1,0:T(8,128)S(1)}, u32[]{:S(2)}, u32[]{:S(2)}) collective-permute-start(f32[48,512]{1,0:T(8,128)S(1)} %add.832), channel_id=1, source_target_pairs={{0,4},{1,3},{2,6},{3,1},{4,0},{5,7},{6,2},{7,5},{8,12},{9,11},{10,... | collective-permute-start | bytes 294920 | tf_op jit(solution)/shard_map/ppermute | solution.py:634
  173.3 18.7 %collective-permute-start.40 = (bf16[96,1024]{1,0:T(8,128)(2,1)S(1)}, bf16[96,1024]{1,0:T(8,128)(2,1)S(1)}, u32[]{:S(2)}, u32[]{:S(2)}) collective-permute-start(bf16[96,1024]{1,0:T(8,128)(2,1)S(1)} %pad_maximum_fusion.3), channel_id=1, source_target_pairs={{0,16},{2,18},{4,20},{6,22},{8,24},{10,26},{12,28},{14,30},{16,0},... | collective-permute-start | bytes 589832 | tf_op jit(solution)/shard_map/ppermute | solution.py:648
  193.1 12.5 %collective-permute-start.48 = (bf16[48,1024]{1,0:T(8,128)(2,1)S(1)}, bf16[48,1024]{1,0:T(8,128)(2,1)S(1)}, u32[]{:S(2)}, u32[]{:S(2)}) collective-permute-start(bf16[48,1024]{1,0:T(8,128)(2,1)S(1)} %get-tuple-element.297), channel_id=1, source_target_pairs={{0,8},{2,10},{4,12},{6,14},{8,0},{10,2},{12,4},{14,6},{16,24},{18,... | collective-permute-start | bytes 294920 | tf_op jit(solution)/shard_map/ppermute | solution.py:648
  (75 other events, 542.8 us)

commit v7 on v6

--- a/solution.py
+++ b/solution.py
@@ -1025,7 +1025,7 @@
         da, mine0, theirs0 = meet([fc2_sum], da, mine0, theirs0)
         came0 = other_core(theirs0)
         da, mine0 = meet([fc1_sum, fc2_sum], da, mine0)
-        fc2_sum.third()
+        fc2_sum.halve()
         fc1_sum.second()
         both = add(mine0, came0).astype(BF16)
         first = Scatter(both[:half], both[half:], dims)
@@ -1060,9 +1060,11 @@
         flat = flat + flat_came.came[0]
         flat_came = Flow(turn(flat, dims, SECOND))
         first.halve()
-        acts = after(acts, first.sent, second.sent)
+        fc2_sum.came[0] = after(fc2_sum.came[0], first.sent)
+        fc2_sum.quarter()
+        acts = after(acts, first.sent, second.sent, fc2_sum.sent)
         out_own, out_far = hidden_out(meta, acts, width, hidden_in[1])
-        flat, result, out_far = meet([flat_came, second, fc1_sum], flat, result, out_far)
+        flat, result, out_far = meet([flat_came, second, fc1_sum, fc2_sum], flat, result, out_far)
         late = Flow(other_core(out_far))
         flat = flat + flat_came.came[0]
         flat_came = Flow(turn(flat, dims, FIRST))

time: 220 us -> 214 us (0.973)
  other arithmetic: 15.5 us -> 10.7 us
    ppermute x33 -> x30, starting transfers between devices: 50.5 us -> 44.8 us  [turn(): return lax.ppermute(values, ('dp', 'mp'), pairs)]
    ppermute x6 -> x8, starting transfers between devices: 8.26 us -> 12.3 us  [swap_z(): return lax.ppermute(values, 'dp', pairs)]
    convert_element_type x4, other arithmetic: 3.44 us -> 0.51 us  [second(): send = add(self.keep[half:], self.came[0][half:]).astype(BF16)]
    ppermute x6 -> x8, waiting for transfers between devices: 8.49 us -> 6.43 us  [swap_z(): return lax.ppermute(values, 'dp', pairs)]
    unnamed x98 -> x90, local copies, waits for them, and re-layouts: 3.39 us -> 5.13 us
    ppermute x33 -> x30, waiting for transfers between devices: 31.2 us -> 31.8 us  [turn(): return lax.ppermute(values, ('dp', 'mp'), pairs)]
  transfers between devices with their start and end apart: 51 -> 50, of which waited for: 19 -> 20; matrix products, arithmetic and copies ran while one was open for 10% -> 8% of each run, Pallas kernels for 36% -> 37%
where the time goes in v7:
time: 214 us; the launch traced here: 210 us
  Pallas kernels  80.5 us (38%)
  starting transfers between devices  59.2 us (28%)
  waiting for transfers between devices  43.3 us (20%)
  local copies, waits for them, and re-layouts  14.8 us (7%)
  other arithmetic  10.7 us (5%)
    ppermute x30, starting transfers between devices, turn(): return lax.ppermute(values, ('dp', 'mp'), pairs)  44.8 us
    ppermute x30, waiting for transfers between devices, turn(): return lax.ppermute(values, ('dp', 'mp'), pairs)  31.8 us
    pallas_call x2, Pallas kernels, attend_back(): pl.pallas_call(partial(attend_back_kernel, before, count), out_shape=smal...  27.3 us
    pallas_call x1, Pallas kernels, hidden_back(): pl.pallas_call(partial(hidden_back_kernel, bases0, bases1), out_shape=[sh...  16 us
    pallas_call x1, Pallas kernels, attend(): pl.pallas_call(partial(attend_kernel, count, total), out_shape=[shape((8,...  14.4 us
    ppermute x8, starting transfers between devices, swap_z(): return lax.ppermute(values, 'dp', pairs)  12.3 us
    pallas_call x1, Pallas kernels, hidden_fwd(): pl.pallas_call(partial(hidden_fwd_kernel, bases), out_shape=[shape((width...  9.48 us
    ppermute x8, waiting for transfers between devices, swap_z(): return lax.ppermute(values, 'dp', pairs)  6.43 us
  transfers between devices with their start and end apart: 50, of which 20 were waited for; matrix products, arithmetic and copies ran while one was open for 8% of the time, Pallas kernels for 37%

profile of v7, /device:TPU:0, one launch (start us, length us, event | category | flops | bytes accessed | tf_op | source)
XLA Modules:
  0.0 210.3 jit_solution(16829259522144781904)
XLA Ops:
  6.2 3.0 %collective-permute-start.1 = (bf16[48,1664]{1,0:T(8,128)(2,1)S(1)}, bf16[48,1664]{1,0:T(8,128)(2,1)S(1)}, u32[]{:S(2)}, u32[]{:S(2)}) collective-permute-start(bf16[48,1664]{1,0:T(8,128)(2,1)S(1)} %pad_maximum_fusion.5), channel_id=1, source_target_pairs={{0,8},{1,9},{2,10},{3,11},{4,12},{5,13},{6,14},{7,15},{8,16},{9,17... | collective-permute-start | bytes 479240 | tf_op jit(solution)/shard_map/ppermute | solution.py:634
  9.2 2.6 %collective-permute-start.2 = (bf16[48,1664]{1,0:T(8,128)(2,1)S(1)}, bf16[48,1664]{1,0:T(8,128)(2,1)S(1)}, u32[]{:S(2)}, u32[]{:S(2)}) collective-permute-start(bf16[48,1664]{1,0:T(8,128)(2,1)S(1)} %pad_maximum_fusion.5), channel_id=1, source_target_pairs={{0,16},{1,17},{2,18},{3,19},{4,20},{5,21},{6,22},{7,23},{8,24},{9,... | collective-permute-start | bytes 479240 | tf_op jit(solution)/shard_map/ppermute | solution.py:634
  18.6 4.0 %collective-permute-done.2.refs_1_ = bf16[48,1664]{1,0:T(8,128)(2,1)S(1)} collective-permute-done((bf16[48,1664]{1,0:T(8,128)(2,1)S(1)}, bf16[48,1664]{1,0:T(8,128)(2,1)S(1)}, u32[]{:S(2)}, u32[]{:S(2)}) %collective-permute-start.2) | collective-permute-done | bytes 159776 | tf_op jit(solution)/shard_map/ppermute | solution.py:634
  26.9 3.9 %collective-permute-start.7 = (bf16[48,1536]{1,0:T(8,128)(2,1)S(1)}, bf16[48,1536]{1,0:T(8,128)(2,1)S(1)}, u32[]{:S(2)}, u32[]{:S(2)}) collective-permute-start(bf16[48,1536]{1,0:T(8,128)(2,1)S(1)} %copy-done.37), channel_id=1, source_target_pairs={{0,8},{1,9},{2,10},{3,11},{4,12},{5,13},{6,14},{7,15},{8,16},{9,17... | collective-permute-start | bytes 442376 | tf_op jit(solution)/shard_map/ppermute | solution.py:634
  33.2 3.5 %collective-permute-done.7.refs_0_ = bf16[48,1536]{1,0:T(8,128)(2,1)S(1)} collective-permute-done((bf16[48,1536]{1,0:T(8,128)(2,1)S(1)}, bf16[48,1536]{1,0:T(8,128)(2,1)S(1)}, u32[]{:S(2)}, u32[]{:S(2)}) %collective-permute-start.7) | collective-permute-done | bytes 147488 | tf_op jit(solution)/shard_map/ppermute | solution.py:634
  36.7 4.5 %collective-permute-done.8.refs_1_ = bf16[48,1536]{1,0:T(8,128)(2,1)S(1)} collective-permute-done((bf16[48,1536]{1,0:T(8,128)(2,1)S(1)}, bf16[48,1536]{1,0:T(8,128)(2,1)S(1)}, u32[]{:S(2)}, u32[]{:S(2)}) %collective-permute-start.8) | collective-permute-done | bytes 147488 | tf_op jit(solution)/shard_map/ppermute | solution.py:634
  45.9 4.0 %collective-permute-start.12 = (bf16[48,1536]{1,0:T(8,128)(2,1)S(1)}, bf16[48,1536]{1,0:T(8,128)(2,1)S(1)}, u32[]{:S(2)}, u32[]{:S(2)}) collective-permute-start(bf16[48,1536]{1,0:T(8,128)(2,1)S(1)} %bitcast.84), channel_id=1, source_target_pairs={{0,8},{1,9},{2,10},{3,11},{4,12},{5,13},{6,14},{7,15},{8,16},{9,17... | collective-permute-start | bytes 442376 | tf_op jit(solution)/shard_map/ppermute | solution.py:634
  53.0 2.2 %collective-permute-done.12.refs_0_ = bf16[48,1536]{1,0:T(8,128)(2,1)S(1)} collective-permute-done((bf16[48,1536]{1,0:T(8,128)(2,1)S(1)}, bf16[48,1536]{1,0:T(8,128)(2,1)S(1)}, u32[]{:S(2)}, u32[]{:S(2)}) %collective-permute-start.12) | collective-permute-done | bytes 147488 | tf_op jit(solution)/shard_map/ppermute | solution.py:634
  55.2 4.4 %collective-permute-done.13.refs_1_ = bf16[48,1536]{1,0:T(8,128)(2,1)S(1)} collective-permute-done((bf16[48,1536]{1,0:T(8,128)(2,1)S(1)}, bf16[48,1536]{1,0:T(8,128)(2,1)S(1)}, u32[]{:S(2)}, u32[]{:S(2)}) %collective-permute-start.13) | collective-permute-done | bytes 147488 | tf_op jit(solution)/shard_map/ppermute | solution.py:634
  67.0 14.4 %attend.1 = (f32[8,768]{1,0:T(8,128)S(1)}, bf16[2,224,768]{2,1,0:T(8,128)(2,1)S(1)}, bf16[2,224,768]{2,1,0:T(8,128)(2,1)}, bf16[2,256,768]{2,1,0:T(8,128)(2,1)},...) custom-call(s32[80]{0:T(128)S(1)} %concatenate.64.meta.refs_0_, ...), custom_call_target="tpu_custom_call" | custom-call | flops 1000 | bytes 1000 | tf_op jit(solution)/shard_map/attend/pallas_call | solution.py:195
  84.4 2.1 %collective-permute-done.21 = bf16[2,224,768]{2,1,0:T(8,128)(2,1)S(1)} collective-permute-done((bf16[2,224,768]{2,1,0:T(8,128)(2,1)S(1)}, bf16[2,224,768]{2,1,0:T(8,128)(2,1)S(1)}, u32[]{:S(2)}, u32[]{:S(2)}) %collective-permute-start.21) | collective-permute-done | bytes 688160 | tf_op jit(solution)/shard_map/ppermute | solution.py:652
  86.6 9.5 %hidden_fwd.1 = (bf16[384,1536]{1,0:T(8,128)(2,1)}, bf16[384,1536]{1,0:T(8,128)(2,1)}) custom-call(s32[80]{0:T(128)S(1)} %concatenate.64.meta.refs_0_, bf16[448,768]{1,0:T(8,128)(2,1)S(1)} %bitcast.67, bf16[448,768]{1,0:T(8,128)(2,1)S(1)} %bitcast.69, bf16[448,768]{1,0:T(8,128)(2,1)} %bitcast.71, bf16[448,768]{1,0:T(8,128)(2,1)} %bitcast.79, ...), custom_call_target="tpu_custom_call" | custom-call | flops 1000 | bytes 1000 | tf_op jit(solution)/shard_map/hidden_fwd/pallas_call | solution.py:255
  97.5 16.0 %hidden_back.1 = (f32[1,1536]{1,0:T(1,128)S(1)}, bf16[384,1536]{1,0:T(8,128)(2,1)}, bf16[384,1536]{1,0:T(8,128)(2,1)}, f32[448,768]{1,0:T(8,128)}, bf16[448,768]...) custom-call(s32[80]{0:T(128)S(1)} %concatenate.64.meta.refs_0_, bf16[448,768]{1,0:T(8,128)(2,1)S(1)} %bitcast.68, ...), custom_call_target="tpu_custom_call" | custom-call | flops 1000 | bytes 1000 | tf_op jit(solution)/shard_map/hidden_back/pallas_call | solution.py:318
  116.7 15.1 %attend_back.2 = (f32[4,768]{1,0:T(4,128)S(1)}, f32[2,512]{1,0:T(2,128)S(1)}, f32[128,128]{1,0:T(8,128)S(1)}, bf16[768,1024]{1,0:T(8,128)(2,1)}, bf16[768,1024]{...) custom-call(s32[80]{0:T(128)S(1)} %concatenate.64.meta.refs_0_, ...), custom_call_target="tpu_custom_call" | custom-call | flops 1000 | bytes 1000 | tf_op jit(solution)/shard_map/attend_back/pallas_call | solution.py:611
  133.5 2.9 %collective-permute-done.24 = bf16[384,1536]{1,0:T(8,128)(2,1)S(1)} collective-permute-done((bf16[384,1536]{1,0:T(8,128)(2,1)}, bf16[384,1536]{1,0:T(8,128)(2,1)S(1)}, u32[]{:S(2)}, u32[]{:S(2)}) %collective-permute-start.24) | collective-permute-done | bytes 1179680 | tf_op jit(solution)/shard_map/ppermute | solution.py:634
  139.0 2.1 add_convert_fusion
  142.2 3.0 %collective-permute-start.30 = (bf16[96,1536]{1,0:T(8,128)(2,1)S(1)}, bf16[96,1536]{1,0:T(8,128)(2,1)S(1)}, u32[]{:S(2)}, u32[]{:S(2)}) collective-permute-start(bf16[96,1536]{1,0:T(8,128)(2,1)S(1)} %pad_maximum_fusion.2), channel_id=1, source_target_pairs={{0,16},{2,18},{4,20},{6,22},{8,24},{10,26},{12,28},{14,30},{16,0},... | collective-permute-start | bytes 884744 | tf_op jit(solution)/shard_map/ppermute | solution.py:648
  145.2 12.3 %attend_back.3 = (f32[48,512]{1,0:T(8,128)S(1)}, bf16[768,512]{1,0:T(8,128)(2,1)}, bf16[768,512]{1,0:T(8,128)(2,1)}, f32[2,224,768]{2,1,0:T(8,128)}) custom-call(s32[80]{0:T(128)S(1)} %concatenate.64.meta.refs_0_, f32[8,768]{1,0:T(8,128)S(1)} %get-tuple-element.187.vecs, bf16[256,128]{1,0:T(8,128)(2,1)S(1)} %copy-done.11, ...), custom_call_target="tpu_custom_call" | custom-call | flops 1000 | bytes 1000 | tf_op jit(solution)/shard_map/attend_back/pallas_call | solution.py:611
  160.2 5.9 %collective-permute-done.33 = bf16[192,1024]{1,0:T(8,128)(2,1)S(1)} collective-permute-done((bf16[192,1024]{1,0:T(8,128)(2,1)S(1)}, bf16[192,1024]{1,0:T(8,128)(2,1)S(1)}, u32[]{:S(2)}, u32[]{:S(2)}) %collective-permute-start.33) | collective-permute-done | bytes 393248 | tf_op jit(solution)/shard_map/ppermute | solution.py:634
  167.8 2.1 collective-permute-start.37
  172.9 5.9 %hidden_out.1 = (f32[448,768]{1,0:T(8,128)}, bf16[448,768]{1,0:T(8,128)(2,1)S(1)}) custom-call(s32[80]{0:T(128)S(1)} %concatenate.64.meta.refs_0_, bf16[896,1536]{1,0:T(8,128)(2,1)} %get-tuple-element.255.acts_in, bf16[96,4736]{1,0:T(8,128)(2,1)} %copy-done, bf16[96,4736]{1,0:T(8,128)(2,1)} %copy-done.13, bf16[288,1536]{1,0:T(8,128)(2,1)S(1)} %copy-done.2, ...), custom_call_target="tpu_custom_call" | custom-call | flops 1000 | bytes 1000 | tf_op jit(solution)/shard_map/hidden_out/pallas_call | solution.py:362
  178.8 2.2 %collective-permute-done.36 = bf16[96,1536]{1,0:T(8,128)(2,1)S(1)} collective-permute-done((bf16[96,1536]{1,0:T(8,128)(2,1)S(1)}, bf16[96,1536]{1,0:T(8,128)(2,1)S(1)}, u32[]{:S(2)}, u32[]{:S(2)}) %collective-permute-start.36) | collective-permute-done | bytes 294944 | tf_op jit(solution)/shard_map/ppermute | solution.py:648
  192.4 3.0 %collective-permute-start.43 = (f32[48,512]{1,0:T(8,128)S(1)}, f32[48,512]{1,0:T(8,128)S(1)}, u32[]{:S(2)}, u32[]{:S(2)}) collective-permute-start(f32[48,512]{1,0:T(8,128)S(1)} %add.846), channel_id=1, source_target_pairs={{0,16},{2,18},{4,20},{6,22},{8,24},{10,26},{12,28},{14,30},{16,0},... | collective-permute-start | bytes 294920 | tf_op jit(solution)/shard_map/ppermute | solution.py:648
  203.2 2.7 %collective-permute-done.48 = f32[48,512]{1,0:T(8,128)S(1)} collective-permute-done((f32[48,512]{1,0:T(8,128)S(1)}, f32[48,512]{1,0:T(8,128)S(1)}, u32[]{:S(2)}, u32[]{:S(2)}) %collective-permute-start.48) | collective-permute-done | bytes 98336 | tf_op jit(solution)/shard_map/ppermute | solution.py:648
  (259 shorter events, 77.3 us)
Async XLA Ops:
  6.2 12.3 %collective-permute-start.1 = (bf16[48,1664]{1,0:T(8,128)(2,1)S(1)}, bf16[48,1664]{1,0:T(8,128)(2,1)S(1)}, u32[]{:S(2)}, u32[]{:S(2)}) collective-permute-start(bf16[48,1664]{1,0:T(8,128)(2,1)S(1)} %pad_maximum_fusion.5), channel_id=1, source_target_pairs={{0,8},{1,9},{2,10},{3,11},{4,12},{5,13},{6,14},{7,15},{8,16},{9,17... | collective-permute-start | bytes 479240 | tf_op jit(solution)/shard_map/ppermute | solution.py:634
  9.2 13.4 %collective-permute-start.2 = (bf16[48,1664]{1,0:T(8,128)(2,1)S(1)}, bf16[48,1664]{1,0:T(8,128)(2,1)S(1)}, u32[]{:S(2)}, u32[]{:S(2)}) collective-permute-start(bf16[48,1664]{1,0:T(8,128)(2,1)S(1)} %pad_maximum_fusion.5), channel_id=1, source_target_pairs={{0,16},{1,17},{2,18},{3,19},{4,20},{5,21},{6,22},{7,23},{8,24},{9,... | collective-permute-start | bytes 479240 | tf_op jit(solution)/shard_map/ppermute | solution.py:634
  11.8 10.8 %collective-permute-start.3 = (bf16[48,1664]{1,0:T(8,128)(2,1)S(1)}, bf16[48,1664]{1,0:T(8,128)(2,1)S(1)}, u32[]{:S(2)}, u32[]{:S(2)}) collective-permute-start(bf16[48,1664]{1,0:T(8,128)(2,1)S(1)} %pad_maximum_fusion.5), channel_id=1, source_target_pairs={{0,24},{1,25},{2,26},{3,27},{4,28},{5,29},{6,30},{7,31},{8,0},{9,1... | collective-permute-start | bytes 479240 | tf_op jit(solution)/shard_map/ppermute | solution.py:634
  23.2 18.5 %collective-permute-start.5 = (bf16[96,4736]{1,0:T(8,128)(2,1)S(1)}, bf16[96,4736]{1,0:T(8,128)(2,1)S(1)}, u32[]{:S(2)}, u32[]{:S(2)}) collective-permute-start(bf16[96,4736]{1,0:T(8,128)(2,1)S(1)} %stack.184.refs_0_.refs_4_), channel_id=1, source_target_pairs={{0,4},{1,3},{2,6},{3,1},{4,0},{5,7},{6,2},{7,5},{8,12},{9,11},{10,... | collective-permute-start | bytes 2727944 | tf_op jit(solution)/shard_map/ppermute | solution.py:634
  25.4 15.8 %collective-permute-start.6 = (bf16[144,1664]{1,0:T(8,128)(2,1)S(1)}, bf16[144,1664]{1,0:T(8,128)(2,1)S(1)}, u32[]{:S(2)}, u32[]{:S(2)}) collective-permute-start(bf16[144,1664]{1,0:T(8,128)(2,1)S(1)} %stack.183.refs_0_), channel_id=1, source_target_pairs={{0,2},{1,5},{2,0},{3,7},{4,6},{5,1},{6,4},{7,3},{8,10},{9,13},{10,... | collective-permute-start | bytes 1437704 | tf_op jit(solution)/shard_map/ppermute | solution.py:634
  30.8 10.4 %collective-permute-start.8 = (bf16[48,1536]{1,0:T(8,128)(2,1)S(1)}, bf16[48,1536]{1,0:T(8,128)(2,1)S(1)}, u32[]{:S(2)}, u32[]{:S(2)}) collective-permute-start(bf16[48,1536]{1,0:T(8,128)(2,1)S(1)} %copy-done.37), channel_id=1, source_target_pairs={{0,16},{1,17},{2,18},{3,19},{4,20},{5,21},{6,22},{7,23},{8,24},{9,... | collective-permute-start | bytes 442376 | tf_op jit(solution)/shard_map/ppermute | solution.py:634
  42.3 18.6 %collective-permute-start.10 = (bf16[288,1664]{1,0:T(8,128)(2,1)S(1)}, bf16[288,1664]{1,0:T(8,128)(2,1)S(1)}, u32[]{:S(2)}, u32[]{:S(2)}) collective-permute-start(bf16[288,1664]{1,0:T(8,128)(2,1)S(1)} %stack.185.refs_2_), channel_id=1, source_target_pairs={{0,4},{1,3},{2,6},{3,1},{4,0},{5,7},{6,2},{7,5},{8,12},{9,11},{10,... | collective-permute-start | bytes 2875400 | tf_op jit(solution)/shard_map/ppermute | solution.py:634
  44.5 15.4 %collective-permute-start.11 = (bf16[144,1536]{1,0:T(8,128)(2,1)S(1)}, bf16[144,1536]{1,0:T(8,128)(2,1)S(1)}, u32[]{:S(2)}, u32[]{:S(2)}) collective-permute-start(bf16[144,1536]{1,0:T(8,128)(2,1)S(1)} %stack.186.refs_0_), channel_id=1, source_target_pairs={{0,2},{1,5},{2,0},{3,7},{4,6},{5,1},{6,4},{7,3},{8,10},{9,13},{10,... | collective-permute-start | bytes 1327112 | tf_op jit(solution)/shard_map/ppermute | solution.py:634
  62.0 20.2 %collective-permute-start.18 = (bf16[288,1536]{1,0:T(8,128)(2,1)S(1)}, bf16[288,1536]{1,0:T(8,128)(2,1)S(1)}, u32[]{:S(2)}, u32[]{:S(2)}) collective-permute-start(bf16[288,1536]{1,0:T(8,128)(2,1)S(1)} %stack.187.refs_2_), channel_id=1, source_target_pairs={{0,4},{1,3},{2,6},{3,1},{4,0},{5,7},{6,2},{7,5},{8,12},{9,11},{10,... | collective-permute-start | bytes 2654216 | tf_op jit(solution)/shard_map/ppermute | solution.py:634
  65.7 16.5 %collective-permute-start.20 = (bf16[2,224,768]{2,1,0:T(8,128)(2,1)S(1)}, bf16[2,224,768]{2,1,0:T(8,128)(2,1)S(1)}, u32[]{:S(2)}, u32[]{:S(2)}) collective-permute-start(bf16[2,224,768]{2,1,0:T(8,128)(2,1)S(1)} %bitcast.74), channel_id=1, source_target_pairs={{0,1},{1,0},{2,3},{3,2},{4,5},{5,4},{6,7},{7,6},{8,9},{9,8},{10,11... | collective-permute-start | bytes 2064392 | tf_op jit(solution)/shard_map/ppermute | solution.py:652
  65.9 16.3 %collective-permute-start.19 = (bf16[144,1536]{1,0:T(8,128)(2,1)S(1)}, bf16[144,1536]{1,0:T(8,128)(2,1)S(1)}, u32[]{:S(2)}, u32[]{:S(2)}) collective-permute-start(bf16[144,1536]{1,0:T(8,128)(2,1)S(1)} %stack.188.refs_0_), channel_id=1, source_target_pairs={{0,2},{1,5},{2,0},{3,7},{4,6},{5,1},{6,4},{7,3},{8,10},{9,13},{10,... | collective-permute-start | bytes 1327112 | tf_op jit(solution)/shard_map/ppermute | solution.py:634
  82.8 13.3 %collective-permute-start.22 = (bf16[288,1536]{1,0:T(8,128)(2,1)S(1)}, bf16[288,1536]{1,0:T(8,128)(2,1)S(1)}, u32[]{:S(2)}, u32[]{:S(2)}) collective-permute-start(bf16[288,1536]{1,0:T(8,128)(2,1)S(1)} %stack.189.refs_6_.refs_2_), channel_id=1, source_target_pairs={{0,4},{1,3},{2,6},{3,1},{4,0},{5,7},{6,2},{7,5},{8,12},{9,11},{10,... | collective-permute-start | bytes 2654216 | tf_op jit(solution)/shard_map/ppermute | solution.py:634
  96.1 17.5 %collective-permute-start.23 = (bf16[384,1536]{1,0:T(8,128)(2,1)}, bf16[384,1536]{1,0:T(8,128)(2,1)S(1)}, u32[]{:S(2)}, u32[]{:S(2)}) collective-permute-start(bf16[384,1536]{1,0:T(8,128)(2,1)} %get-tuple-element.207), channel_id=1, source_target_pairs={{0,4},{1,3},{2,6},{3,1},{4,0},{5,7},{6,2},{7,5},{8,12},{9,11},{10,... | collective-permute-start | bytes 3538952 | tf_op jit(solution)/shard_map/ppermute | solution.py:634
  113.6 22.8 %collective-permute-start.24 = (bf16[384,1536]{1,0:T(8,128)(2,1)}, bf16[384,1536]{1,0:T(8,128)(2,1)S(1)}, u32[]{:S(2)}, u32[]{:S(2)}) collective-permute-start(bf16[384,1536]{1,0:T(8,128)(2,1)} %get-tuple-element.210), channel_id=1, source_target_pairs={{0,4},{1,3},{2,6},{3,1},{4,0},{5,7},{6,2},{7,5},{8,12},{9,11},{10,... | collective-permute-start | bytes 3538952 | tf_op jit(solution)/shard_map/ppermute | solution.py:634
  114.7 17.9 %collective-permute-start.25 = (bf16[192,1536]{1,0:T(8,128)(2,1)S(1)}, bf16[192,1536]{1,0:T(8,128)(2,1)S(1)}, u32[]{:S(2)}, u32[]{:S(2)}) collective-permute-start(bf16[192,1536]{1,0:T(8,128)(2,1)S(1)} %add_convert_fusion.3), channel_id=1, source_target_pairs={{0,2},{1,5},{2,0},{3,7},{4,6},{5,1},{6,4},{7,3},{8,10},{9,13},{10,... | collective-permute-start | bytes 1769480 | tf_op jit(solution)/shard_map/ppermute | solution.py:634
  136.6 21.4 %collective-permute-start.31 = (bf16[192,1536]{1,0:T(8,128)(2,1)S(1)}, bf16[192,1536]{1,0:T(8,128)(2,1)S(1)}, u32[]{:S(2)}, u32[]{:S(2)}) collective-permute-start(bf16[192,1536]{1,0:T(8,128)(2,1)S(1)} %add_convert_fusion.2), channel_id=1, source_target_pairs={{0,2},{1,5},{2,0},{3,7},{4,6},{5,1},{6,4},{7,3},{8,10},{9,13},{10,... | collective-permute-start | bytes 1769480 | tf_op jit(solution)/shard_map/ppermute | solution.py:634
  141.2 16.9 %collective-permute-start.32 = (bf16[384,1024]{1,0:T(8,128)(2,1)S(1)}, bf16[384,1024]{1,0:T(8,128)(2,1)S(1)}, u32[]{:S(2)}, u32[]{:S(2)}) collective-permute-start(bf16[384,1024]{1,0:T(8,128)(2,1)S(1)} %slice.264), channel_id=1, source_target_pairs={{0,4},{1,3},{2,6},{3,1},{4,0},{5,7},{6,2},{7,5},{8,12},{9,11},{10,... | collective-permute-start | bytes 2359304 | tf_op jit(solution)/shard_map/ppermute | solution.py:634
  142.2 15.8 %collective-permute-start.30 = (bf16[96,1536]{1,0:T(8,128)(2,1)S(1)}, bf16[96,1536]{1,0:T(8,128)(2,1)S(1)}, u32[]{:S(2)}, u32[]{:S(2)}) collective-permute-start(bf16[96,1536]{1,0:T(8,128)(2,1)S(1)} %pad_maximum_fusion.2), channel_id=1, source_target_pairs={{0,16},{2,18},{4,20},{6,22},{8,24},{10,26},{12,28},{14,30},{16,0},... | collective-permute-start | bytes 884744 | tf_op jit(solution)/shard_map/ppermute | solution.py:648
  159.6 21.4 %collective-permute-start.36 = (bf16[96,1536]{1,0:T(8,128)(2,1)S(1)}, bf16[96,1536]{1,0:T(8,128)(2,1)S(1)}, u32[]{:S(2)}, u32[]{:S(2)}) collective-permute-start(bf16[96,1536]{1,0:T(8,128)(2,1)S(1)} %pad_maximum_fusion.3), channel_id=1, source_target_pairs={{0,16},{2,18},{4,20},{6,22},{8,24},{10,26},{12,28},{14,30},{16,0},... | collective-permute-start | bytes 884744 | tf_op jit(solution)/shard_map/ppermute | solution.py:648
  166.6 14.5 %collective-permute-start.35 = (bf16[384,512]{1,0:T(8,128)(2,1)S(1)}, bf16[384,512]{1,0:T(8,128)(2,1)S(1)}, u32[]{:S(2)}, u32[]{:S(2)}) collective-permute-start(bf16[384,512]{1,0:T(8,128)(2,1)S(1)} %slice.265), channel_id=1, source_target_pairs={{0,4},{1,3},{2,6},{3,1},{4,0},{5,7},{6,2},{7,5},{8,12},{9,11},{10,... | collective-permute-start | bytes 1179656 | tf_op jit(solution)/shard_map/ppermute | solution.py:634
  167.8 13.2 %collective-permute-start.37 = (bf16[48,1536]{1,0:T(8,128)(2,1)S(1)}, bf16[48,1536]{1,0:T(8,128)(2,1)S(1)}, u32[]{:S(2)}, u32[]{:S(2)}) collective-permute-start(bf16[48,1536]{1,0:T(8,128)(2,1)S(1)} %add_convert_fusion.7), channel_id=1, source_target_pairs={{0,8},{2,10},{4,12},{6,14},{8,0},{10,2},{12,4},{14,6},{16,24},{18,... | collective-permute-start | bytes 442376 | tf_op jit(solution)/shard_map/ppermute | solution.py:648
  169.9 11.1 %collective-permute-start.34 = (f32[48,512]{1,0:T(8,128)S(1)}, f32[48,512]{1,0:T(8,128)S(1)}, u32[]{:S(2)}, u32[]{:S(2)}) collective-permute-start(f32[48,512]{1,0:T(8,128)S(1)} %add.834), channel_id=1, source_target_pairs={{0,4},{1,3},{2,6},{3,1},{4,0},{5,7},{6,2},{7,5},{8,12},{9,11},{10,... | collective-permute-start | bytes 294920 | tf_op jit(solution)/shard_map/ppermute | solution.py:634
  170.9 15.4 %collective-permute-start.39 = (bf16[96,1024]{1,0:T(8,128)(2,1)S(1)}, bf16[96,1024]{1,0:T(8,128)(2,1)S(1)}, u32[]{:S(2)}, u32[]{:S(2)}) collective-permute-start(bf16[96,1024]{1,0:T(8,128)(2,1)S(1)} %pad_maximum_fusion.4), channel_id=1, source_target_pairs={{0,16},{2,18},{4,20},{6,22},{8,24},{10,26},{12,28},{14,30},{16,0},... | collective-permute-start | bytes 589832 | tf_op jit(solution)/shard_map/ppermute | solution.py:648
  188.3 11.4 %collective-permute-start.47 = (bf16[48,1024]{1,0:T(8,128)(2,1)S(1)}, bf16[48,1024]{1,0:T(8,128)(2,1)S(1)}, u32[]{:S(2)}, u32[]{:S(2)}) collective-permute-start(bf16[48,1024]{1,0:T(8,128)(2,1)S(1)} %get-tuple-element.297), channel_id=1, source_target_pairs={{0,8},{2,10},{4,12},{6,14},{8,0},{10,2},{12,4},{14,6},{16,24},{18,... | collective-permute-start | bytes 294920 | tf_op jit(solution)/shard_map/ppermute | solution.py:648
  (70 other events, 510.9 us)

commit v8 on v7

--- a/solution.py
+++ b/solution.py
@@ -167,9 +167,8 @@
             scores = dot_nt(jnp.concatenate([mine, rel], axis=1), keys_aug)
             terms = jnp.exp(scores - jnp.max(scores, axis=-1, keepdims=True))
             soft = terms * (1.0 / jnp.sum(terms, axis=-1, keepdims=True))
-            soft = soft.astype(BF16)
             ps[window, 2 * pair + half] = soft
-            parts.append(dot(soft, v2))
+            parts.append(dot(soft.astype(BF16), v2))
         atts[window, :, cols] = jnp.where(place < 64, parts[0], parts[1]).astype(BF16)
         heads = pl.ds(2 * pair, 2)
         outs.append(begin(ps.at[window, heads], p.at[window, heads], out_sems.at[len(outs)]))
@@ -189,7 +188,7 @@
     count, total, width = len(own), len(own) + len(other), tok.shape[-1]
     rows, keys, heads = (2, TOK, width), (2, KEYS, width), (2, HEADS, TOK, KEYS)
     halves = (2, width, 2 * width + LANES)
-    outs = [shape(dims, BF16) for dims in (rows, rows, keys, keys, heads, rows, halves)]
+    outs = [shape(dims, F32 if dims == heads else BF16) for dims in (rows, rows, keys, keys, heads, rows, halves)]
     outs += [shape(rows, F32), shape(rows, BF16)]
     scratch = (rows, halves, (2, KEYS, LANES), rows, rows, keys, keys, heads, rows)
     return pl.pallas_call(
@@ -197,7 +196,7 @@
         out_shape=[shape((8, width), F32)] + outs,
         in_specs=[SMEM, HBM, WHOLE, WHOLE] + [HBM] * total,
         out_specs=[WHOLE] + [HBM] * len(outs),
-        scratch_shapes=[pltpu.VMEM(dims, BF16) for dims in scratch]
+        scratch_shapes=[pltpu.VMEM(dims, F32 if dims == heads else BF16) for dims in scratch]
         + [
             pltpu.VMEM(rows, F32),
             pltpu.VMEM(rows, BF16),
@@ -492,8 +491,8 @@
         k8 = (k2.astype(F32) * HDIM**-0.5).astype(BF16)
         dqs, dks, dvs, dts = [], [], [], []
         for half in range(2):
-            soft = ps[window, 2 * pair + half]
-            soft32 = soft.astype(F32)
+            soft32 = ps[window, 2 * pair + half]
+            soft = soft32.astype(BF16)
             own_lanes = jnp.where(place // 64 == half, dat2.astype(F32), 0.0).astype(BF16)
             weighted = soft32 * dot_nt(own_lanes, v2)
             ds = (weighted - soft32 * jnp.sum(weighted, axis=-1, keepdims=True)).astype(BF16)
@@ -590,7 +589,7 @@
         large += [shape(rows, F32), shape(rows, BF16)]
     scratch = [rows, (cols_here, width), rows, rows, part, keys, keys, heads, part, (3,) + part]
     scratch.append((2, width, 2 * cols_here))
-    scratch = [pltpu.VMEM(dims, BF16) for dims in scratch]
+    scratch = [pltpu.VMEM(dims, F32 if dims == heads else BF16) for dims in scratch]
     scratch += [pltpu.SemaphoreType.DMA((15 + 2 * count + parts,)), pltpu.SemaphoreType.DMA((2 * PIECES + 3,))]
     if first:
         scratch += [

time: 214 us -> 214 us (level)
  no operation moved by 1% of the time
where the time goes in v8:
time: 214 us; the launch traced here: 210 us
  Pallas kernels  80.4 us (38%)
  starting transfers between devices  59.2 us (28%)
  waiting for transfers between devices  43.3 us (20%)
  local copies, waits for them, and re-layouts  14.9 us (7%)
  other arithmetic  10.7 us (5%)
    ppermute x30, starting transfers between devices, turn(): return lax.ppermute(values, ('dp', 'mp'), pairs)  44.8 us
    ppermute x30, waiting for transfers between devices, turn(): return lax.ppermute(values, ('dp', 'mp'), pairs)  31.8 us
    pallas_call x2, Pallas kernels, attend_back(): pl.pallas_call(partial(attend_back_kernel, before, count), out_shape=smal...  27.2 us
    pallas_call x1, Pallas kernels, hidden_back(): pl.pallas_call(partial(hidden_back_kernel, bases0, bases1), out_shape=[sh...  16 us
    pallas_call x1, Pallas kernels, attend(): pl.pallas_call(partial(attend_kernel, count, total), out_shape=[shape((8,...  14.3 us
    ppermute x8, starting transfers between devices, swap_z(): return lax.ppermute(values, 'dp', pairs)  12.3 us
    pallas_call x1, Pallas kernels, hidden_fwd(): pl.pallas_call(partial(hidden_fwd_kernel, bases), out_shape=[shape((width...  9.51 us
    ppermute x8, waiting for transfers between devices, swap_z(): return lax.ppermute(values, 'dp', pairs)  6.45 us
  transfers between devices with their start and end apart: 50, of which 20 were waited for; matrix products, arithmetic and copies ran while one was open for 8% of the time, Pallas kernels for 37%

profile of v8, /device:TPU:0, one launch (start us, length us, event | category | flops | bytes accessed | tf_op | source)
XLA Modules:
  0.0 210.2 jit_solution(11932152678408945029)
XLA Ops:
  6.2 3.0 %collective-permute-start.1 = (bf16[48,1664]{1,0:T(8,128)(2,1)S(1)}, bf16[48,1664]{1,0:T(8,128)(2,1)S(1)}, u32[]{:S(2)}, u32[]{:S(2)}) collective-permute-start(bf16[48,1664]{1,0:T(8,128)(2,1)S(1)} %pad_maximum_fusion.5), channel_id=1, source_target_pairs={{0,8},{1,9},{2,10},{3,11},{4,12},{5,13},{6,14},{7,15},{8,16},{9,17... | collective-permute-start | bytes 479240 | tf_op jit(solution)/shard_map/ppermute | solution.py:633
  9.2 2.6 %collective-permute-start.2 = (bf16[48,1664]{1,0:T(8,128)(2,1)S(1)}, bf16[48,1664]{1,0:T(8,128)(2,1)S(1)}, u32[]{:S(2)}, u32[]{:S(2)}) collective-permute-start(bf16[48,1664]{1,0:T(8,128)(2,1)S(1)} %pad_maximum_fusion.5), channel_id=1, source_target_pairs={{0,16},{1,17},{2,18},{3,19},{4,20},{5,21},{6,22},{7,23},{8,24},{9,... | collective-permute-start | bytes 479240 | tf_op jit(solution)/shard_map/ppermute | solution.py:633
  18.6 4.0 %collective-permute-done.2.refs_1_ = bf16[48,1664]{1,0:T(8,128)(2,1)S(1)} collective-permute-done((bf16[48,1664]{1,0:T(8,128)(2,1)S(1)}, bf16[48,1664]{1,0:T(8,128)(2,1)S(1)}, u32[]{:S(2)}, u32[]{:S(2)}) %collective-permute-start.2) | collective-permute-done | bytes 159776 | tf_op jit(solution)/shard_map/ppermute | solution.py:633
  26.9 3.9 %collective-permute-start.7 = (bf16[48,1536]{1,0:T(8,128)(2,1)S(1)}, bf16[48,1536]{1,0:T(8,128)(2,1)S(1)}, u32[]{:S(2)}, u32[]{:S(2)}) collective-permute-start(bf16[48,1536]{1,0:T(8,128)(2,1)S(1)} %copy-done.37), channel_id=1, source_target_pairs={{0,8},{1,9},{2,10},{3,11},{4,12},{5,13},{6,14},{7,15},{8,16},{9,17... | collective-permute-start | bytes 442376 | tf_op jit(solution)/shard_map/ppermute | solution.py:633
  33.2 3.5 %collective-permute-done.7.refs_0_ = bf16[48,1536]{1,0:T(8,128)(2,1)S(1)} collective-permute-done((bf16[48,1536]{1,0:T(8,128)(2,1)S(1)}, bf16[48,1536]{1,0:T(8,128)(2,1)S(1)}, u32[]{:S(2)}, u32[]{:S(2)}) %collective-permute-start.7) | collective-permute-done | bytes 147488 | tf_op jit(solution)/shard_map/ppermute | solution.py:633
  36.7 4.5 %collective-permute-done.8.refs_1_ = bf16[48,1536]{1,0:T(8,128)(2,1)S(1)} collective-permute-done((bf16[48,1536]{1,0:T(8,128)(2,1)S(1)}, bf16[48,1536]{1,0:T(8,128)(2,1)S(1)}, u32[]{:S(2)}, u32[]{:S(2)}) %collective-permute-start.8) | collective-permute-done | bytes 147488 | tf_op jit(solution)/shard_map/ppermute | solution.py:633
  45.9 4.0 %collective-permute-start.12 = (bf16[48,1536]{1,0:T(8,128)(2,1)S(1)}, bf16[48,1536]{1,0:T(8,128)(2,1)S(1)}, u32[]{:S(2)}, u32[]{:S(2)}) collective-permute-start(bf16[48,1536]{1,0:T(8,128)(2,1)S(1)} %bitcast.84), channel_id=1, source_target_pairs={{0,8},{1,9},{2,10},{3,11},{4,12},{5,13},{6,14},{7,15},{8,16},{9,17... | collective-permute-start | bytes 442376 | tf_op jit(solution)/shard_map/ppermute | solution.py:633
  53.0 2.2 %collective-permute-done.12.refs_0_ = bf16[48,1536]{1,0:T(8,128)(2,1)S(1)} collective-permute-done((bf16[48,1536]{1,0:T(8,128)(2,1)S(1)}, bf16[48,1536]{1,0:T(8,128)(2,1)S(1)}, u32[]{:S(2)}, u32[]{:S(2)}) %collective-permute-start.12) | collective-permute-done | bytes 147488 | tf_op jit(solution)/shard_map/ppermute | solution.py:633
  55.2 4.4 %collective-permute-done.13.refs_1_ = bf16[48,1536]{1,0:T(8,128)(2,1)S(1)} collective-permute-done((bf16[48,1536]{1,0:T(8,128)(2,1)S(1)}, bf16[48,1536]{1,0:T(8,128)(2,1)S(1)}, u32[]{:S(2)}, u32[]{:S(2)}) %collective-permute-start.13) | collective-permute-done | bytes 147488 | tf_op jit(solution)/shard_map/ppermute | solution.py:633
  67.0 14.3 %attend.1 = (f32[8,768]{1,0:T(8,128)S(1)}, bf16[2,224,768]{2,1,0:T(8,128)(2,1)S(1)}, bf16[2,224,768]{2,1,0:T(8,128)(2,1)}, bf16[2,256,768]{2,1,0:T(8,128)(2,1)},...) custom-call(s32[80]{0:T(128)S(1)} %concatenate.64.meta.refs_0_, ...), custom_call_target="tpu_custom_call" | custom-call | flops 1000 | bytes 1000 | tf_op jit(solution)/shard_map/attend/pallas_call | solution.py:194
  84.4 2.1 %collective-permute-done.21 = bf16[2,224,768]{2,1,0:T(8,128)(2,1)S(1)} collective-permute-done((bf16[2,224,768]{2,1,0:T(8,128)(2,1)S(1)}, bf16[2,224,768]{2,1,0:T(8,128)(2,1)S(1)}, u32[]{:S(2)}, u32[]{:S(2)}) %collective-permute-start.21) | collective-permute-done | bytes 688160 | tf_op jit(solution)/shard_map/ppermute | solution.py:651
  86.5 9.5 %hidden_fwd.1 = (bf16[384,1536]{1,0:T(8,128)(2,1)}, bf16[384,1536]{1,0:T(8,128)(2,1)}) custom-call(s32[80]{0:T(128)S(1)} %concatenate.64.meta.refs_0_, bf16[448,768]{1,0:T(8,128)(2,1)S(1)} %bitcast.67, bf16[448,768]{1,0:T(8,128)(2,1)S(1)} %bitcast.69, bf16[448,768]{1,0:T(8,128)(2,1)} %bitcast.71, bf16[448,768]{1,0:T(8,128)(2,1)} %bitcast.79, ...), custom_call_target="tpu_custom_call" | custom-call | flops 1000 | bytes 1000 | tf_op jit(solution)/shard_map/hidden_fwd/pallas_call | solution.py:254
  97.4 16.0 %hidden_back.1 = (f32[1,1536]{1,0:T(1,128)S(1)}, bf16[384,1536]{1,0:T(8,128)(2,1)}, bf16[384,1536]{1,0:T(8,128)(2,1)}, f32[448,768]{1,0:T(8,128)}, bf16[448,768]...) custom-call(s32[80]{0:T(128)S(1)} %concatenate.64.meta.refs_0_, bf16[448,768]{1,0:T(8,128)(2,1)S(1)} %bitcast.68, ...), custom_call_target="tpu_custom_call" | custom-call | flops 1000 | bytes 1000 | tf_op jit(solution)/shard_map/hidden_back/pallas_call | solution.py:317
  116.7 15.0 %attend_back.2 = (f32[4,768]{1,0:T(4,128)S(1)}, f32[2,512]{1,0:T(2,128)S(1)}, f32[128,128]{1,0:T(8,128)S(1)}, bf16[768,1024]{1,0:T(8,128)(2,1)}, bf16[768,1024]{...) custom-call(s32[80]{0:T(128)S(1)} %concatenate.64.meta.refs_0_, ...), custom_call_target="tpu_custom_call" | custom-call | flops 1000 | bytes 1000 | tf_op jit(solution)/shard_map/attend_back/pallas_call | solution.py:610
  133.4 2.9 %collective-permute-done.24 = bf16[384,1536]{1,0:T(8,128)(2,1)S(1)} collective-permute-done((bf16[384,1536]{1,0:T(8,128)(2,1)}, bf16[384,1536]{1,0:T(8,128)(2,1)S(1)}, u32[]{:S(2)}, u32[]{:S(2)}) %collective-permute-start.24) | collective-permute-done | bytes 1179680 | tf_op jit(solution)/shard_map/ppermute | solution.py:633
  139.0 2.1 add_convert_fusion
  142.2 3.0 %collective-permute-start.30 = (bf16[96,1536]{1,0:T(8,128)(2,1)S(1)}, bf16[96,1536]{1,0:T(8,128)(2,1)S(1)}, u32[]{:S(2)}, u32[]{:S(2)}) collective-permute-start(bf16[96,1536]{1,0:T(8,128)(2,1)S(1)} %pad_maximum_fusion.2), channel_id=1, source_target_pairs={{0,16},{2,18},{4,20},{6,22},{8,24},{10,26},{12,28},{14,30},{16,0},... | collective-permute-start | bytes 884744 | tf_op jit(solution)/shard_map/ppermute | solution.py:647
  145.2 12.2 %attend_back.3 = (f32[48,512]{1,0:T(8,128)S(1)}, bf16[768,512]{1,0:T(8,128)(2,1)}, bf16[768,512]{1,0:T(8,128)(2,1)}, f32[2,224,768]{2,1,0:T(8,128)}) custom-call(s32[80]{0:T(128)S(1)} %concatenate.64.meta.refs_0_, f32[8,768]{1,0:T(8,128)S(1)} %get-tuple-element.187.vecs, bf16[256,128]{1,0:T(8,128)(2,1)S(1)} %copy-done.11, ...), custom_call_target="tpu_custom_call" | custom-call | flops 1000 | bytes 1000 | tf_op jit(solution)/shard_map/attend_back/pallas_call | solution.py:610
  160.1 5.9 %collective-permute-done.33 = bf16[192,1024]{1,0:T(8,128)(2,1)S(1)} collective-permute-done((bf16[192,1024]{1,0:T(8,128)(2,1)S(1)}, bf16[192,1024]{1,0:T(8,128)(2,1)S(1)}, u32[]{:S(2)}, u32[]{:S(2)}) %collective-permute-start.33) | collective-permute-done | bytes 393248 | tf_op jit(solution)/shard_map/ppermute | solution.py:633
  167.7 2.1 collective-permute-start.37
  172.8 5.9 %hidden_out.1 = (f32[448,768]{1,0:T(8,128)}, bf16[448,768]{1,0:T(8,128)(2,1)S(1)}) custom-call(s32[80]{0:T(128)S(1)} %concatenate.64.meta.refs_0_, bf16[896,1536]{1,0:T(8,128)(2,1)} %get-tuple-element.255.acts_in, bf16[96,4736]{1,0:T(8,128)(2,1)} %copy-done, bf16[96,4736]{1,0:T(8,128)(2,1)} %copy-done.13, bf16[288,1536]{1,0:T(8,128)(2,1)S(1)} %copy-done.2, ...), custom_call_target="tpu_custom_call" | custom-call | flops 1000 | bytes 1000 | tf_op jit(solution)/shard_map/hidden_out/pallas_call | solution.py:361
  178.7 2.2 %collective-permute-done.36 = bf16[96,1536]{1,0:T(8,128)(2,1)S(1)} collective-permute-done((bf16[96,1536]{1,0:T(8,128)(2,1)S(1)}, bf16[96,1536]{1,0:T(8,128)(2,1)S(1)}, u32[]{:S(2)}, u32[]{:S(2)}) %collective-permute-start.36) | collective-permute-done | bytes 294944 | tf_op jit(solution)/shard_map/ppermute | solution.py:647
  192.3 3.0 %collective-permute-start.43 = (f32[48,512]{1,0:T(8,128)S(1)}, f32[48,512]{1,0:T(8,128)S(1)}, u32[]{:S(2)}, u32[]{:S(2)}) collective-permute-start(f32[48,512]{1,0:T(8,128)S(1)} %add.846), channel_id=1, source_target_pairs={{0,16},{2,18},{4,20},{6,22},{8,24},{10,26},{12,28},{14,30},{16,0},... | collective-permute-start | bytes 294920 | tf_op jit(solution)/shard_map/ppermute | solution.py:647
  203.1 2.7 %collective-permute-done.48 = f32[48,512]{1,0:T(8,128)S(1)} collective-permute-done((f32[48,512]{1,0:T(8,128)S(1)}, f32[48,512]{1,0:T(8,128)S(1)}, u32[]{:S(2)}, u32[]{:S(2)}) %collective-permute-start.48) | collective-permute-done | bytes 98336 | tf_op jit(solution)/shard_map/ppermute | solution.py:647
  (259 shorter events, 77.3 us)
Async XLA Ops:
  6.2 12.4 %collective-permute-start.1 = (bf16[48,1664]{1,0:T(8,128)(2,1)S(1)}, bf16[48,1664]{1,0:T(8,128)(2,1)S(1)}, u32[]{:S(2)}, u32[]{:S(2)}) collective-permute-start(bf16[48,1664]{1,0:T(8,128)(2,1)S(1)} %pad_maximum_fusion.5), channel_id=1, source_target_pairs={{0,8},{1,9},{2,10},{3,11},{4,12},{5,13},{6,14},{7,15},{8,16},{9,17... | collective-permute-start | bytes 479240 | tf_op jit(solution)/shard_map/ppermute | solution.py:633
  9.2 13.4 %collective-permute-start.2 = (bf16[48,1664]{1,0:T(8,128)(2,1)S(1)}, bf16[48,1664]{1,0:T(8,128)(2,1)S(1)}, u32[]{:S(2)}, u32[]{:S(2)}) collective-permute-start(bf16[48,1664]{1,0:T(8,128)(2,1)S(1)} %pad_maximum_fusion.5), channel_id=1, source_target_pairs={{0,16},{1,17},{2,18},{3,19},{4,20},{5,21},{6,22},{7,23},{8,24},{9,... | collective-permute-start | bytes 479240 | tf_op jit(solution)/shard_map/ppermute | solution.py:633
  11.8 10.8 %collective-permute-start.3 = (bf16[48,1664]{1,0:T(8,128)(2,1)S(1)}, bf16[48,1664]{1,0:T(8,128)(2,1)S(1)}, u32[]{:S(2)}, u32[]{:S(2)}) collective-permute-start(bf16[48,1664]{1,0:T(8,128)(2,1)S(1)} %pad_maximum_fusion.5), channel_id=1, source_target_pairs={{0,24},{1,25},{2,26},{3,27},{4,28},{5,29},{6,30},{7,31},{8,0},{9,1... | collective-permute-start | bytes 479240 | tf_op jit(solution)/shard_map/ppermute | solution.py:633
  23.2 18.5 %collective-permute-start.5 = (bf16[96,4736]{1,0:T(8,128)(2,1)S(1)}, bf16[96,4736]{1,0:T(8,128)(2,1)S(1)}, u32[]{:S(2)}, u32[]{:S(2)}) collective-permute-start(bf16[96,4736]{1,0:T(8,128)(2,1)S(1)} %stack.184.refs_0_.refs_4_), channel_id=1, source_target_pairs={{0,4},{1,3},{2,6},{3,1},{4,0},{5,7},{6,2},{7,5},{8,12},{9,11},{10,... | collective-permute-start | bytes 2727944 | tf_op jit(solution)/shard_map/ppermute | solution.py:633
  25.4 15.8 %collective-permute-start.6 = (bf16[144,1664]{1,0:T(8,128)(2,1)S(1)}, bf16[144,1664]{1,0:T(8,128)(2,1)S(1)}, u32[]{:S(2)}, u32[]{:S(2)}) collective-permute-start(bf16[144,1664]{1,0:T(8,128)(2,1)S(1)} %stack.183.refs_0_), channel_id=1, source_target_pairs={{0,2},{1,5},{2,0},{3,7},{4,6},{5,1},{6,4},{7,3},{8,10},{9,13},{10,... | collective-permute-start | bytes 1437704 | tf_op jit(solution)/shard_map/ppermute | solution.py:633
  30.8 10.4 %collective-permute-start.8 = (bf16[48,1536]{1,0:T(8,128)(2,1)S(1)}, bf16[48,1536]{1,0:T(8,128)(2,1)S(1)}, u32[]{:S(2)}, u32[]{:S(2)}) collective-permute-start(bf16[48,1536]{1,0:T(8,128)(2,1)S(1)} %copy-done.37), channel_id=1, source_target_pairs={{0,16},{1,17},{2,18},{3,19},{4,20},{5,21},{6,22},{7,23},{8,24},{9,... | collective-permute-start | bytes 442376 | tf_op jit(solution)/shard_map/ppermute | solution.py:633
  42.3 18.6 %collective-permute-start.10 = (bf16[288,1664]{1,0:T(8,128)(2,1)S(1)}, bf16[288,1664]{1,0:T(8,128)(2,1)S(1)}, u32[]{:S(2)}, u32[]{:S(2)}) collective-permute-start(bf16[288,1664]{1,0:T(8,128)(2,1)S(1)} %stack.185.refs_2_), channel_id=1, source_target_pairs={{0,4},{1,3},{2,6},{3,1},{4,0},{5,7},{6,2},{7,5},{8,12},{9,11},{10,... | collective-permute-start | bytes 2875400 | tf_op jit(solution)/shard_map/ppermute | solution.py:633
  44.5 15.4 %collective-permute-start.11 = (bf16[144,1536]{1,0:T(8,128)(2,1)S(1)}, bf16[144,1536]{1,0:T(8,128)(2,1)S(1)}, u32[]{:S(2)}, u32[]{:S(2)}) collective-permute-start(bf16[144,1536]{1,0:T(8,128)(2,1)S(1)} %stack.186.refs_0_), channel_id=1, source_target_pairs={{0,2},{1,5},{2,0},{3,7},{4,6},{5,1},{6,4},{7,3},{8,10},{9,13},{10,... | collective-permute-start | bytes 1327112 | tf_op jit(solution)/shard_map/ppermute | solution.py:633
  62.0 20.2 %collective-permute-start.18 = (bf16[288,1536]{1,0:T(8,128)(2,1)S(1)}, bf16[288,1536]{1,0:T(8,128)(2,1)S(1)}, u32[]{:S(2)}, u32[]{:S(2)}) collective-permute-start(bf16[288,1536]{1,0:T(8,128)(2,1)S(1)} %stack.187.refs_2_), channel_id=1, source_target_pairs={{0,4},{1,3},{2,6},{3,1},{4,0},{5,7},{6,2},{7,5},{8,12},{9,11},{10,... | collective-permute-start | bytes 2654216 | tf_op jit(solution)/shard_map/ppermute | solution.py:633
  65.7 16.5 %collective-permute-start.20 = (bf16[2,224,768]{2,1,0:T(8,128)(2,1)S(1)}, bf16[2,224,768]{2,1,0:T(8,128)(2,1)S(1)}, u32[]{:S(2)}, u32[]{:S(2)}) collective-permute-start(bf16[2,224,768]{2,1,0:T(8,128)(2,1)S(1)} %bitcast.74), channel_id=1, source_target_pairs={{0,1},{1,0},{2,3},{3,2},{4,5},{5,4},{6,7},{7,6},{8,9},{9,8},{10,11... | collective-permute-start | bytes 2064392 | tf_op jit(solution)/shard_map/ppermute | solution.py:651
  65.9 16.3 %collective-permute-start.19 = (bf16[144,1536]{1,0:T(8,128)(2,1)S(1)}, bf16[144,1536]{1,0:T(8,128)(2,1)S(1)}, u32[]{:S(2)}, u32[]{:S(2)}) collective-permute-start(bf16[144,1536]{1,0:T(8,128)(2,1)S(1)} %stack.188.refs_0_), channel_id=1, source_target_pairs={{0,2},{1,5},{2,0},{3,7},{4,6},{5,1},{6,4},{7,3},{8,10},{9,13},{10,... | collective-permute-start | bytes 1327112 | tf_op jit(solution)/shard_map/ppermute | solution.py:633
  82.8 13.3 %collective-permute-start.22 = (bf16[288,1536]{1,0:T(8,128)(2,1)S(1)}, bf16[288,1536]{1,0:T(8,128)(2,1)S(1)}, u32[]{:S(2)}, u32[]{:S(2)}) collective-permute-start(bf16[288,1536]{1,0:T(8,128)(2,1)S(1)} %stack.189.refs_6_.refs_2_), channel_id=1, source_target_pairs={{0,4},{1,3},{2,6},{3,1},{4,0},{5,7},{6,2},{7,5},{8,12},{9,11},{10,... | collective-permute-start | bytes 2654216 | tf_op jit(solution)/shard_map/ppermute | solution.py:633
  96.1 17.5 %collective-permute-start.23 = (bf16[384,1536]{1,0:T(8,128)(2,1)}, bf16[384,1536]{1,0:T(8,128)(2,1)S(1)}, u32[]{:S(2)}, u32[]{:S(2)}) collective-permute-start(bf16[384,1536]{1,0:T(8,128)(2,1)} %get-tuple-element.207), channel_id=1, source_target_pairs={{0,4},{1,3},{2,6},{3,1},{4,0},{5,7},{6,2},{7,5},{8,12},{9,11},{10,... | collective-permute-start | bytes 3538952 | tf_op jit(solution)/shard_map/ppermute | solution.py:633
  113.6 22.8 %collective-permute-start.24 = (bf16[384,1536]{1,0:T(8,128)(2,1)}, bf16[384,1536]{1,0:T(8,128)(2,1)S(1)}, u32[]{:S(2)}, u32[]{:S(2)}) collective-permute-start(bf16[384,1536]{1,0:T(8,128)(2,1)} %get-tuple-element.210), channel_id=1, source_target_pairs={{0,4},{1,3},{2,6},{3,1},{4,0},{5,7},{6,2},{7,5},{8,12},{9,11},{10,... | collective-permute-start | bytes 3538952 | tf_op jit(solution)/shard_map/ppermute | solution.py:633
  114.7 17.9 %collective-permute-start.25 = (bf16[192,1536]{1,0:T(8,128)(2,1)S(1)}, bf16[192,1536]{1,0:T(8,128)(2,1)S(1)}, u32[]{:S(2)}, u32[]{:S(2)}) collective-permute-start(bf16[192,1536]{1,0:T(8,128)(2,1)S(1)} %add_convert_fusion.3), channel_id=1, source_target_pairs={{0,2},{1,5},{2,0},{3,7},{4,6},{5,1},{6,4},{7,3},{8,10},{9,13},{10,... | collective-permute-start | bytes 1769480 | tf_op jit(solution)/shard_map/ppermute | solution.py:633
  136.6 21.4 %collective-permute-start.31 = (bf16[192,1536]{1,0:T(8,128)(2,1)S(1)}, bf16[192,1536]{1,0:T(8,128)(2,1)S(1)}, u32[]{:S(2)}, u32[]{:S(2)}) collective-permute-start(bf16[192,1536]{1,0:T(8,128)(2,1)S(1)} %add_convert_fusion.2), channel_id=1, source_target_pairs={{0,2},{1,5},{2,0},{3,7},{4,6},{5,1},{6,4},{7,3},{8,10},{9,13},{10,... | collective-permute-start | bytes 1769480 | tf_op jit(solution)/shard_map/ppermute | solution.py:633
  141.1 16.8 %collective-permute-start.32 = (bf16[384,1024]{1,0:T(8,128)(2,1)S(1)}, bf16[384,1024]{1,0:T(8,128)(2,1)S(1)}, u32[]{:S(2)}, u32[]{:S(2)}) collective-permute-start(bf16[384,1024]{1,0:T(8,128)(2,1)S(1)} %slice.264), channel_id=1, source_target_pairs={{0,4},{1,3},{2,6},{3,1},{4,0},{5,7},{6,2},{7,5},{8,12},{9,11},{10,... | collective-permute-start | bytes 2359304 | tf_op jit(solution)/shard_map/ppermute | solution.py:633
  142.2 15.8 %collective-permute-start.30 = (bf16[96,1536]{1,0:T(8,128)(2,1)S(1)}, bf16[96,1536]{1,0:T(8,128)(2,1)S(1)}, u32[]{:S(2)}, u32[]{:S(2)}) collective-permute-start(bf16[96,1536]{1,0:T(8,128)(2,1)S(1)} %pad_maximum_fusion.2), channel_id=1, source_target_pairs={{0,16},{2,18},{4,20},{6,22},{8,24},{10,26},{12,28},{14,30},{16,0},... | collective-permute-start | bytes 884744 | tf_op jit(solution)/shard_map/ppermute | solution.py:647
  159.5 21.4 %collective-permute-start.36 = (bf16[96,1536]{1,0:T(8,128)(2,1)S(1)}, bf16[96,1536]{1,0:T(8,128)(2,1)S(1)}, u32[]{:S(2)}, u32[]{:S(2)}) collective-permute-start(bf16[96,1536]{1,0:T(8,128)(2,1)S(1)} %pad_maximum_fusion.3), channel_id=1, source_target_pairs={{0,16},{2,18},{4,20},{6,22},{8,24},{10,26},{12,28},{14,30},{16,0},... | collective-permute-start | bytes 884744 | tf_op jit(solution)/shard_map/ppermute | solution.py:647
  166.5 14.5 %collective-permute-start.35 = (bf16[384,512]{1,0:T(8,128)(2,1)S(1)}, bf16[384,512]{1,0:T(8,128)(2,1)S(1)}, u32[]{:S(2)}, u32[]{:S(2)}) collective-permute-start(bf16[384,512]{1,0:T(8,128)(2,1)S(1)} %slice.265), channel_id=1, source_target_pairs={{0,4},{1,3},{2,6},{3,1},{4,0},{5,7},{6,2},{7,5},{8,12},{9,11},{10,... | collective-permute-start | bytes 1179656 | tf_op jit(solution)/shard_map/ppermute | solution.py:633
  167.7 13.2 %collective-permute-start.37 = (bf16[48,1536]{1,0:T(8,128)(2,1)S(1)}, bf16[48,1536]{1,0:T(8,128)(2,1)S(1)}, u32[]{:S(2)}, u32[]{:S(2)}) collective-permute-start(bf16[48,1536]{1,0:T(8,128)(2,1)S(1)} %add_convert_fusion.7), channel_id=1, source_target_pairs={{0,8},{2,10},{4,12},{6,14},{8,0},{10,2},{12,4},{14,6},{16,24},{18,... | collective-permute-start | bytes 442376 | tf_op jit(solution)/shard_map/ppermute | solution.py:647
  169.8 11.2 %collective-permute-start.34 = (f32[48,512]{1,0:T(8,128)S(1)}, f32[48,512]{1,0:T(8,128)S(1)}, u32[]{:S(2)}, u32[]{:S(2)}) collective-permute-start(f32[48,512]{1,0:T(8,128)S(1)} %add.834), channel_id=1, source_target_pairs={{0,4},{1,3},{2,6},{3,1},{4,0},{5,7},{6,2},{7,5},{8,12},{9,11},{10,... | collective-permute-start | bytes 294920 | tf_op jit(solution)/shard_map/ppermute | solution.py:633
  170.8 15.4 %collective-permute-start.39 = (bf16[96,1024]{1,0:T(8,128)(2,1)S(1)}, bf16[96,1024]{1,0:T(8,128)(2,1)S(1)}, u32[]{:S(2)}, u32[]{:S(2)}) collective-permute-start(bf16[96,1024]{1,0:T(8,128)(2,1)S(1)} %pad_maximum_fusion.4), channel_id=1, source_target_pairs={{0,16},{2,18},{4,20},{6,22},{8,24},{10,26},{12,28},{14,30},{16,0},... | collective-permute-start | bytes 589832 | tf_op jit(solution)/shard_map/ppermute | solution.py:647
  188.2 11.4 %collective-permute-start.47 = (bf16[48,1024]{1,0:T(8,128)(2,1)S(1)}, bf16[48,1024]{1,0:T(8,128)(2,1)S(1)}, u32[]{:S(2)}, u32[]{:S(2)}) collective-permute-start(bf16[48,1024]{1,0:T(8,128)(2,1)S(1)} %get-tuple-element.297), channel_id=1, source_target_pairs={{0,8},{2,10},{4,12},{6,14},{8,0},{10,2},{12,4},{14,6},{16,24},{18,... | collective-permute-start | bytes 294920 | tf_op jit(solution)/shard_map/ppermute | solution.py:647
  (70 other events, 510.9 us)

commit v9 on v8

--- a/solution.py
+++ b/solution.py
@@ -214,7 +214,7 @@
     copies = []
     for piece in range(PIECES):
         dest = keep if piece < PIECES // 2 else send
-        place = pl.multiple_of(meta[32 + piece] * rows, rows)
+        place = pl.multiple_of(meta[80 + piece] * rows, rows)
         at = pl.ds(piece % (PIECES // 2) * rows, rows)
         source = made.at[pl.ds(place, rows), cols]
         copies.append(begin(source, dest.at[at, cols], sems.at[first + len(copies)]))
@@ -467,7 +467,7 @@
 
     def send(half):
         is_own = core == half
-        at = jnp.where(is_own, 32, 48)
+        at = jnp.where(is_own, 32, 48) if last else jnp.where(is_own, 80, 96)
         for piece in range(PIECES):
             place = pl.multiple_of(meta[at + piece] * rows, rows)
             source, to = grads.at[half, pl.ds(place, rows), :], pl.ds(piece * rows, rows)
@@ -696,16 +696,20 @@
     here = lax.axis_index("dp")
     z, y, x = here // (dims[1] * dims[2]), here // dims[2] % dims[1], here % dims[2]
 
-    def chip(step, inner, outer):
+    def chip(at_z, inner, outer):
         by_x = jnp.where(core == 0, inner, outer)
         by_y = jnp.where(core == 0, outer, inner)
-        return ((z - step) % dims[0] * dims[1] + (y + by_y) % 2) * dims[2] + (x + by_x) % 2
+        return (at_z * dims[1] + (y + by_y) % 2) * dims[2] + (x + by_x) % 2
+
+    back = [(z - step) % dims[0] for step in range(dims[0])]
+    pairs = [z ^ step for step in range(dims[0])]
 
     square = [(inner, outer) for outer in range(2) for inner in range(2)]
-    gather = [chip(0, *at) for at in square]
-    gather += [chip(step, *at) for at in square for step in range(1, dims[0])]
-    scatter = [chip(step, *at) for at in square for step in range(dims[0])]
-    return [jnp.stack(found).astype(jnp.int32) for found in (gather, scatter)]
+    gather = [chip(z, *at) for at in square]
+    gather += [chip(place, *at) for at in square for place in back[1:]]
+    scatter = [chip(place, *at) for at in square for place in back]
+    halving = [chip(place, *at) for at in square for place in pairs]
+    return [jnp.stack(found).astype(jnp.int32) for found in (gather, scatter, halving)]
 
 
 def add(a, b):
@@ -799,11 +803,8 @@
     def halve(self):
         near = self.near + self.came[0].astype(F32)
         rows = near.shape[0] // self.dims[0]
-        parts = [near[step * rows : (step + 1) * rows] for step in range(self.dims[0])]
-        even = lax.axis_index("dp") // (self.dims[1] * self.dims[2]) % 2 == 0
-        self.near = parts[0]
-        self.beside = jnp.where(even, parts[3], parts[1])
-        self.sent = jnp.concatenate([parts[2], jnp.where(even, parts[1], parts[3])], axis=0).astype(BF16)
+        self.near, self.beside = near[:rows], near[rows : 2 * rows]
+        self.sent = near[2 * rows :].astype(BF16)
         self.came = [swap_z(self.sent, self.dims, 2)]
 
     def quarter(self):
@@ -893,11 +894,13 @@
     def prepare(patches, out_grad, heights, rel_pos_h, rel_pos_w):
         if dims is None:
             orders = [jnp.tile(jnp.arange(PIECES, dtype=jnp.int32), 4)]
+            halving = [orders[0][: 2 * PIECES]]
         else:
             own, far = place_orders(dims, core), place_orders(dims, 1 - core)
             orders = [own[0], far[0], own[1], far[1]]
+            halving = [own[2], far[2]]
         meta = jnp.concatenate(
-            orders + [core.astype(jnp.int32)[None], heights, widths, jnp.zeros((11,), jnp.int32)]
+            orders + [core.astype(jnp.int32)[None], heights, widths, jnp.zeros((11,), jnp.int32)] + halving
         )
         row_index = core * WIN + jnp.arange(WIN)
         valid = (row_index[None, :, None] < heights[:, None, None]) & (

time: 214 us -> 212 us (level)
  other arithmetic: 10.7 us -> 7.23 us
    unnamed x90 -> x86, local copies, waits for them, and re-layouts: 5.09 us -> 5.39 us
  transfers between devices with their start and end apart: 50 -> 50, of which waited for: 20 -> 20; matrix products, arithmetic and copies ran while one was open for 8% -> 6% of each run, Pallas kernels for 37% -> 37%
where the time goes in v9:
time: 212 us; the launch traced here: 208 us
  Pallas kernels  80.4 us (38%)
  starting transfers between devices  61.3 us (29%)
  waiting for transfers between devices  43.2 us (20%)
  local copies, waits for them, and re-layouts  14.5 us (7%)
  other arithmetic  7.23 us (3%)
    ppermute x30, starting transfers between devices, turn(): return lax.ppermute(values, ('dp', 'mp'), pairs)  45.7 us
    ppermute x30, waiting for transfers between devices, turn(): return lax.ppermute(values, ('dp', 'mp'), pairs)  32 us
    pallas_call x2, Pallas kernels, attend_back(): pl.pallas_call(partial(attend_back_kernel, before, count), out_shape=smal...  27.2 us
    pallas_call x1, Pallas kernels, hidden_back(): pl.pallas_call(partial(hidden_back_kernel, bases0, bases1), out_shape=[sh...  16 us
    pallas_call x1, Pallas kernels, attend(): pl.pallas_call(partial(attend_kernel, count, total), out_shape=[shape((8,...  14.4 us
    ppermute x8, starting transfers between devices, swap_z(): return lax.ppermute(values, 'dp', pairs)  13 us
    pallas_call x1, Pallas kernels, hidden_fwd(): pl.pallas_call(partial(hidden_fwd_kernel, bases), out_shape=[shape((width...  9.48 us
    ppermute x8, waiting for transfers between devices, swap_z(): return lax.ppermute(values, 'dp', pairs)  6.93 us
  transfers between devices with their start and end apart: 50, of which 20 were waited for; matrix products, arithmetic and copies ran while one was open for 6% of the time, Pallas kernels for 37%

profile of v9, /device:TPU:0, one launch (start us, length us, event | category | flops | bytes accessed | tf_op | source)
XLA Modules:
  0.0 208.3 jit_solution(912737576774512362)
XLA Ops:
  5.5 3.0 %collective-permute-start.1 = (bf16[48,1664]{1,0:T(8,128)(2,1)S(1)}, bf16[48,1664]{1,0:T(8,128)(2,1)S(1)}, u32[]{:S(2)}, u32[]{:S(2)}) collective-permute-start(bf16[48,1664]{1,0:T(8,128)(2,1)S(1)} %pad_maximum_fusion.2), channel_id=1, source_target_pairs={{0,8},{1,9},{2,10},{3,11},{4,12},{5,13},{6,14},{7,15},{8,16},{9,17... | collective-permute-start | bytes 479240 | tf_op jit(solution)/shard_map/ppermute | solution.py:633
  8.4 2.6 %collective-permute-start.2 = (bf16[48,1664]{1,0:T(8,128)(2,1)S(1)}, bf16[48,1664]{1,0:T(8,128)(2,1)S(1)}, u32[]{:S(2)}, u32[]{:S(2)}) collective-permute-start(bf16[48,1664]{1,0:T(8,128)(2,1)S(1)} %pad_maximum_fusion.2), channel_id=1, source_target_pairs={{0,16},{1,17},{2,18},{3,19},{4,20},{5,21},{6,22},{7,23},{8,24},{9,... | collective-permute-start | bytes 479240 | tf_op jit(solution)/shard_map/ppermute | solution.py:633
  17.9 3.9 %collective-permute-done.2.refs_1_ = bf16[48,1664]{1,0:T(8,128)(2,1)S(1)} collective-permute-done((bf16[48,1664]{1,0:T(8,128)(2,1)S(1)}, bf16[48,1664]{1,0:T(8,128)(2,1)S(1)}, u32[]{:S(2)}, u32[]{:S(2)}) %collective-permute-start.2) | collective-permute-done | bytes 159776 | tf_op jit(solution)/shard_map/ppermute | solution.py:633
  26.2 3.9 %collective-permute-start.7 = (bf16[48,1536]{1,0:T(8,128)(2,1)S(1)}, bf16[48,1536]{1,0:T(8,128)(2,1)S(1)}, u32[]{:S(2)}, u32[]{:S(2)}) collective-permute-start(bf16[48,1536]{1,0:T(8,128)(2,1)S(1)} %copy-done.35), channel_id=1, source_target_pairs={{0,8},{1,9},{2,10},{3,11},{4,12},{5,13},{6,14},{7,15},{8,16},{9,17... | collective-permute-start | bytes 442376 | tf_op jit(solution)/shard_map/ppermute | solution.py:633
  32.4 3.5 %collective-permute-done.7.refs_0_ = bf16[48,1536]{1,0:T(8,128)(2,1)S(1)} collective-permute-done((bf16[48,1536]{1,0:T(8,128)(2,1)S(1)}, bf16[48,1536]{1,0:T(8,128)(2,1)S(1)}, u32[]{:S(2)}, u32[]{:S(2)}) %collective-permute-start.7) | collective-permute-done | bytes 147488 | tf_op jit(solution)/shard_map/ppermute | solution.py:633
  35.9 4.5 %collective-permute-done.8.refs_1_ = bf16[48,1536]{1,0:T(8,128)(2,1)S(1)} collective-permute-done((bf16[48,1536]{1,0:T(8,128)(2,1)S(1)}, bf16[48,1536]{1,0:T(8,128)(2,1)S(1)}, u32[]{:S(2)}, u32[]{:S(2)}) %collective-permute-start.8) | collective-permute-done | bytes 147488 | tf_op jit(solution)/shard_map/ppermute | solution.py:633
  45.2 4.0 %collective-permute-start.12 = (bf16[48,1536]{1,0:T(8,128)(2,1)S(1)}, bf16[48,1536]{1,0:T(8,128)(2,1)S(1)}, u32[]{:S(2)}, u32[]{:S(2)}) collective-permute-start(bf16[48,1536]{1,0:T(8,128)(2,1)S(1)} %bitcast.108), channel_id=1, source_target_pairs={{0,8},{1,9},{2,10},{3,11},{4,12},{5,13},{6,14},{7,15},{8,16},{9,17... | collective-permute-start | bytes 442376 | tf_op jit(solution)/shard_map/ppermute | solution.py:633
  52.2 2.2 %collective-permute-done.12.refs_0_ = bf16[48,1536]{1,0:T(8,128)(2,1)S(1)} collective-permute-done((bf16[48,1536]{1,0:T(8,128)(2,1)S(1)}, bf16[48,1536]{1,0:T(8,128)(2,1)S(1)}, u32[]{:S(2)}, u32[]{:S(2)}) %collective-permute-start.12) | collective-permute-done | bytes 147488 | tf_op jit(solution)/shard_map/ppermute | solution.py:633
  54.4 4.4 %collective-permute-done.13.refs_1_ = bf16[48,1536]{1,0:T(8,128)(2,1)S(1)} collective-permute-done((bf16[48,1536]{1,0:T(8,128)(2,1)S(1)}, bf16[48,1536]{1,0:T(8,128)(2,1)S(1)}, u32[]{:S(2)}, u32[]{:S(2)}) %collective-permute-start.13) | collective-permute-done | bytes 147488 | tf_op jit(solution)/shard_map/ppermute | solution.py:633
  67.1 14.4 %attend.1 = (f32[8,768]{1,0:T(8,128)S(1)}, bf16[2,224,768]{2,1,0:T(8,128)(2,1)S(1)}, bf16[2,224,768]{2,1,0:T(8,128)(2,1)}, bf16[2,256,768]{2,1,0:T(8,128)(2,1)},...) custom-call(s32[112]{0:T(128)S(1)} %concatenate.52.meta.refs_0_, ...), custom_call_target="tpu_custom_call" | custom-call | flops 1000 | bytes 1000 | tf_op jit(solution)/shard_map/attend/pallas_call | solution.py:194
  86.3 9.5 %hidden_fwd.1 = (bf16[384,1536]{1,0:T(8,128)(2,1)}, bf16[384,1536]{1,0:T(8,128)(2,1)}) custom-call(s32[112]{0:T(128)S(1)} %concatenate.52.meta.refs_0_, bf16[448,768]{1,0:T(8,128)(2,1)S(1)} %bitcast.91, bf16[448,768]{1,0:T(8,128)(2,1)S(1)} %bitcast.93, bf16[448,768]{1,0:T(8,128)(2,1)} %bitcast.96, bf16[448,768]{1,0:T(8,128)(2,1)} %bitcast.103, ...), custom_call_target="tpu_custom_call" | custom-call | flops 1000 | bytes 1000 | tf_op jit(solution)/shard_map/hidden_fwd/pallas_call | solution.py:254
  97.1 16.0 %hidden_back.1 = (f32[1,1536]{1,0:T(1,128)S(1)}, bf16[384,1536]{1,0:T(8,128)(2,1)}, bf16[384,1536]{1,0:T(8,128)(2,1)}, f32[448,768]{1,0:T(8,128)}, bf16[448,768]...) custom-call(s32[112]{0:T(128)S(1)} %concatenate.52.meta.refs_0_, bf16[448,768]{1,0:T(8,128)(2,1)S(1)} %bitcast.92, ...), custom_call_target="tpu_custom_call" | custom-call | flops 1000 | bytes 1000 | tf_op jit(solution)/shard_map/hidden_back/pallas_call | solution.py:317
  116.8 15.0 %attend_back.2 = (f32[4,768]{1,0:T(4,128)S(1)}, f32[2,512]{1,0:T(2,128)S(1)}, f32[128,128]{1,0:T(8,128)S(1)}, bf16[768,1024]{1,0:T(8,128)(2,1)}, bf16[768,1024]{...) custom-call(s32[112]{0:T(128)S(1)} %concatenate.52.meta.refs_0_, ...), custom_call_target="tpu_custom_call" | custom-call | flops 1000 | bytes 1000 | tf_op jit(solution)/shard_map/attend_back/pallas_call | solution.py:610
  131.9 3.6 %collective-permute-done.24 = bf16[384,1536]{1,0:T(8,128)(2,1)S(1)} collective-permute-done((bf16[384,1536]{1,0:T(8,128)(2,1)}, bf16[384,1536]{1,0:T(8,128)(2,1)S(1)}, u32[]{:S(2)}, u32[]{:S(2)}) %collective-permute-start.24) | collective-permute-done | bytes 1179680 | tf_op jit(solution)/shard_map/ppermute | solution.py:633
  139.6 3.0 %collective-permute-start.30 = (bf16[96,1536]{1,0:T(8,128)(2,1)S(1)}, bf16[96,1536]{1,0:T(8,128)(2,1)S(1)}, u32[]{:S(2)}, u32[]{:S(2)}) collective-permute-start(bf16[96,1536]{1,0:T(8,128)(2,1)S(1)} %slice.322), channel_id=1, source_target_pairs={{0,16},{2,18},{4,20},{6,22},{8,24},{10,26},{12,28},{14,30},{16,0},... | collective-permute-start | bytes 884744 | tf_op jit(solution)/shard_map/ppermute | solution.py:647
  142.6 12.2 %attend_back.3 = (f32[48,512]{1,0:T(8,128)S(1)}, bf16[768,512]{1,0:T(8,128)(2,1)}, bf16[768,512]{1,0:T(8,128)(2,1)}, f32[2,224,768]{2,1,0:T(8,128)}) custom-call(s32[112]{0:T(128)S(1)} %concatenate.52.meta.refs_0_, f32[8,768]{1,0:T(8,128)S(1)} %get-tuple-element.187.vecs, bf16[256,128]{1,0:T(8,128)(2,1)S(1)} %copy-done.11, ...), custom_call_target="tpu_custom_call" | custom-call | flops 1000 | bytes 1000 | tf_op jit(solution)/shard_map/attend_back/pallas_call | solution.py:610
  158.3 5.2 %collective-permute-done.33 = bf16[192,1024]{1,0:T(8,128)(2,1)S(1)} collective-permute-done((bf16[192,1024]{1,0:T(8,128)(2,1)S(1)}, bf16[192,1024]{1,0:T(8,128)(2,1)S(1)}, u32[]{:S(2)}, u32[]{:S(2)}) %collective-permute-start.33) | collective-permute-done | bytes 393248 | tf_op jit(solution)/shard_map/ppermute | solution.py:633
  168.2 2.4 %collective-permute-start.39 = (bf16[96,1024]{1,0:T(8,128)(2,1)S(1)}, bf16[96,1024]{1,0:T(8,128)(2,1)S(1)}, u32[]{:S(2)}, u32[]{:S(2)}) collective-permute-start(bf16[96,1024]{1,0:T(8,128)(2,1)S(1)} %slice.323), channel_id=1, source_target_pairs={{0,16},{2,18},{4,20},{6,22},{8,24},{10,26},{12,28},{14,30},{16,0},... | collective-permute-start | bytes 589832 | tf_op jit(solution)/shard_map/ppermute | solution.py:647
  170.5 5.9 %hidden_out.1 = (f32[448,768]{1,0:T(8,128)}, bf16[448,768]{1,0:T(8,128)(2,1)S(1)}) custom-call(s32[112]{0:T(128)S(1)} %concatenate.52.meta.refs_0_, bf16[896,1536]{1,0:T(8,128)(2,1)} %get-tuple-element.255.acts_in, bf16[96,4736]{1,0:T(8,128)(2,1)} %copy-done, bf16[96,4736]{1,0:T(8,128)(2,1)} %copy-done.13, bf16[288,1536]{1,0:T(8,128)(2,1)S(1)} %copy-done.2, ...), custom_call_target="tpu_custom_call" | custom-call | flops 1000 | bytes 1000 | tf_op jit(solution)/shard_map/hidden_out/pallas_call | solution.py:361
  176.5 2.6 %collective-permute-done.36 = bf16[96,1536]{1,0:T(8,128)(2,1)S(1)} collective-permute-done((bf16[96,1536]{1,0:T(8,128)(2,1)S(1)}, bf16[96,1536]{1,0:T(8,128)(2,1)S(1)}, u32[]{:S(2)}, u32[]{:S(2)}) %collective-permute-start.36) | collective-permute-done | bytes 294944 | tf_op jit(solution)/shard_map/ppermute | solution.py:647
  182.3 2.0 copy.67
  186.3 2.0 collective-permute-start.47
  190.4 3.0 %collective-permute-start.43 = (f32[48,512]{1,0:T(8,128)S(1)}, f32[48,512]{1,0:T(8,128)S(1)}, u32[]{:S(2)}, u32[]{:S(2)}) collective-permute-start(f32[48,512]{1,0:T(8,128)S(1)} %add.1120), channel_id=1, source_target_pairs={{0,16},{2,18},{4,20},{6,22},{8,24},{10,26},{12,28},{14,30},{16,0},... | collective-permute-start | bytes 294920 | tf_op jit(solution)/shard_map/ppermute | solution.py:647
  201.2 2.7 %collective-permute-done.48 = f32[48,512]{1,0:T(8,128)S(1)} collective-permute-done((f32[48,512]{1,0:T(8,128)S(1)}, f32[48,512]{1,0:T(8,128)S(1)}, u32[]{:S(2)}, u32[]{:S(2)}) %collective-permute-start.48) | collective-permute-done | bytes 98336 | tf_op jit(solution)/shard_map/ppermute | solution.py:647
  (252 shorter events, 75.1 us)
Async XLA Ops:
  5.5 12.5 %collective-permute-start.1 = (bf16[48,1664]{1,0:T(8,128)(2,1)S(1)}, bf16[48,1664]{1,0:T(8,128)(2,1)S(1)}, u32[]{:S(2)}, u32[]{:S(2)}) collective-permute-start(bf16[48,1664]{1,0:T(8,128)(2,1)S(1)} %pad_maximum_fusion.2), channel_id=1, source_target_pairs={{0,8},{1,9},{2,10},{3,11},{4,12},{5,13},{6,14},{7,15},{8,16},{9,17... | collective-permute-start | bytes 479240 | tf_op jit(solution)/shard_map/ppermute | solution.py:633
  8.4 13.4 %collective-permute-start.2 = (bf16[48,1664]{1,0:T(8,128)(2,1)S(1)}, bf16[48,1664]{1,0:T(8,128)(2,1)S(1)}, u32[]{:S(2)}, u32[]{:S(2)}) collective-permute-start(bf16[48,1664]{1,0:T(8,128)(2,1)S(1)} %pad_maximum_fusion.2), channel_id=1, source_target_pairs={{0,16},{1,17},{2,18},{3,19},{4,20},{5,21},{6,22},{7,23},{8,24},{9,... | collective-permute-start | bytes 479240 | tf_op jit(solution)/shard_map/ppermute | solution.py:633
  11.0 10.8 %collective-permute-start.3 = (bf16[48,1664]{1,0:T(8,128)(2,1)S(1)}, bf16[48,1664]{1,0:T(8,128)(2,1)S(1)}, u32[]{:S(2)}, u32[]{:S(2)}) collective-permute-start(bf16[48,1664]{1,0:T(8,128)(2,1)S(1)} %pad_maximum_fusion.2), channel_id=1, source_target_pairs={{0,24},{1,25},{2,26},{3,27},{4,28},{5,29},{6,30},{7,31},{8,0},{9,1... | collective-permute-start | bytes 479240 | tf_op jit(solution)/shard_map/ppermute | solution.py:633
  22.4 18.5 %collective-permute-start.5 = (bf16[96,4736]{1,0:T(8,128)(2,1)S(1)}, bf16[96,4736]{1,0:T(8,128)(2,1)S(1)}, u32[]{:S(2)}, u32[]{:S(2)}) collective-permute-start(bf16[96,4736]{1,0:T(8,128)(2,1)S(1)} %stack.288.refs_0_.refs_4_), channel_id=1, source_target_pairs={{0,4},{1,3},{2,6},{3,1},{4,0},{5,7},{6,2},{7,5},{8,12},{9,11},{10,... | collective-permute-start | bytes 2727944 | tf_op jit(solution)/shard_map/ppermute | solution.py:633
  24.6 15.8 %collective-permute-start.6 = (bf16[144,1664]{1,0:T(8,128)(2,1)S(1)}, bf16[144,1664]{1,0:T(8,128)(2,1)S(1)}, u32[]{:S(2)}, u32[]{:S(2)}) collective-permute-start(bf16[144,1664]{1,0:T(8,128)(2,1)S(1)} %stack.287.refs_0_), channel_id=1, source_target_pairs={{0,2},{1,5},{2,0},{3,7},{4,6},{5,1},{6,4},{7,3},{8,10},{9,13},{10,... | collective-permute-start | bytes 1437704 | tf_op jit(solution)/shard_map/ppermute | solution.py:633
  30.1 10.4 %collective-permute-start.8 = (bf16[48,1536]{1,0:T(8,128)(2,1)S(1)}, bf16[48,1536]{1,0:T(8,128)(2,1)S(1)}, u32[]{:S(2)}, u32[]{:S(2)}) collective-permute-start(bf16[48,1536]{1,0:T(8,128)(2,1)S(1)} %copy-done.35), channel_id=1, source_target_pairs={{0,16},{1,17},{2,18},{3,19},{4,20},{5,21},{6,22},{7,23},{8,24},{9,... | collective-permute-start | bytes 442376 | tf_op jit(solution)/shard_map/ppermute | solution.py:633
  41.6 18.6 %collective-permute-start.10 = (bf16[288,1664]{1,0:T(8,128)(2,1)S(1)}, bf16[288,1664]{1,0:T(8,128)(2,1)S(1)}, u32[]{:S(2)}, u32[]{:S(2)}) collective-permute-start(bf16[288,1664]{1,0:T(8,128)(2,1)S(1)} %stack.289.refs_2_), channel_id=1, source_target_pairs={{0,4},{1,3},{2,6},{3,1},{4,0},{5,7},{6,2},{7,5},{8,12},{9,11},{10,... | collective-permute-start | bytes 2875400 | tf_op jit(solution)/shard_map/ppermute | solution.py:633
  43.7 15.4 %collective-permute-start.11 = (bf16[144,1536]{1,0:T(8,128)(2,1)S(1)}, bf16[144,1536]{1,0:T(8,128)(2,1)S(1)}, u32[]{:S(2)}, u32[]{:S(2)}) collective-permute-start(bf16[144,1536]{1,0:T(8,128)(2,1)S(1)} %stack.290.refs_0_), channel_id=1, source_target_pairs={{0,2},{1,5},{2,0},{3,7},{4,6},{5,1},{6,4},{7,3},{8,10},{9,13},{10,... | collective-permute-start | bytes 1327112 | tf_op jit(solution)/shard_map/ppermute | solution.py:633
  61.3 21.1 %collective-permute-start.18 = (bf16[288,1536]{1,0:T(8,128)(2,1)S(1)}, bf16[288,1536]{1,0:T(8,128)(2,1)S(1)}, u32[]{:S(2)}, u32[]{:S(2)}) collective-permute-start(bf16[288,1536]{1,0:T(8,128)(2,1)S(1)} %stack.291.refs_2_), channel_id=1, source_target_pairs={{0,4},{1,3},{2,6},{3,1},{4,0},{5,7},{6,2},{7,5},{8,12},{9,11},{10,... | collective-permute-start | bytes 2654216 | tf_op jit(solution)/shard_map/ppermute | solution.py:633
  66.0 16.4 %collective-permute-start.20 = (bf16[2,224,768]{2,1,0:T(8,128)(2,1)S(1)}, bf16[2,224,768]{2,1,0:T(8,128)(2,1)S(1)}, u32[]{:S(2)}, u32[]{:S(2)}) collective-permute-start(bf16[2,224,768]{2,1,0:T(8,128)(2,1)S(1)} %bitcast.95), channel_id=1, source_target_pairs={{0,1},{1,0},{2,3},{3,2},{4,5},{5,4},{6,7},{7,6},{8,9},{9,8},{10,11... | collective-permute-start | bytes 2064392 | tf_op jit(solution)/shard_map/ppermute | solution.py:651
  66.1 16.2 %collective-permute-start.19 = (bf16[144,1536]{1,0:T(8,128)(2,1)S(1)}, bf16[144,1536]{1,0:T(8,128)(2,1)S(1)}, u32[]{:S(2)}, u32[]{:S(2)}) collective-permute-start(bf16[144,1536]{1,0:T(8,128)(2,1)S(1)} %stack.292.refs_0_), channel_id=1, source_target_pairs={{0,2},{1,5},{2,0},{3,7},{4,6},{5,1},{6,4},{7,3},{8,10},{9,13},{10,... | collective-permute-start | bytes 1327112 | tf_op jit(solution)/shard_map/ppermute | solution.py:633
  82.9 13.1 %collective-permute-start.22 = (bf16[288,1536]{1,0:T(8,128)(2,1)S(1)}, bf16[288,1536]{1,0:T(8,128)(2,1)S(1)}, u32[]{:S(2)}, u32[]{:S(2)}) collective-permute-start(bf16[288,1536]{1,0:T(8,128)(2,1)S(1)} %stack.293.refs_6_.refs_2_), channel_id=1, source_target_pairs={{0,4},{1,3},{2,6},{3,1},{4,0},{5,7},{6,2},{7,5},{8,12},{9,11},{10,... | collective-permute-start | bytes 2654216 | tf_op jit(solution)/shard_map/ppermute | solution.py:633
  96.0 17.3 %collective-permute-start.23 = (bf16[384,1536]{1,0:T(8,128)(2,1)}, bf16[384,1536]{1,0:T(8,128)(2,1)S(1)}, u32[]{:S(2)}, u32[]{:S(2)}) collective-permute-start(bf16[384,1536]{1,0:T(8,128)(2,1)} %get-tuple-element.207), channel_id=1, source_target_pairs={{0,4},{1,3},{2,6},{3,1},{4,0},{5,7},{6,2},{7,5},{8,12},{9,11},{10,... | collective-permute-start | bytes 3538952 | tf_op jit(solution)/shard_map/ppermute | solution.py:633
  113.5 18.4 %collective-permute-start.25 = (bf16[192,1536]{1,0:T(8,128)(2,1)S(1)}, bf16[192,1536]{1,0:T(8,128)(2,1)S(1)}, u32[]{:S(2)}, u32[]{:S(2)}) collective-permute-start(bf16[192,1536]{1,0:T(8,128)(2,1)S(1)} %add_convert_fusion.3), channel_id=1, source_target_pairs={{0,2},{1,5},{2,0},{3,7},{4,6},{5,1},{6,4},{7,3},{8,10},{9,13},{10,... | collective-permute-start | bytes 1769480 | tf_op jit(solution)/shard_map/ppermute | solution.py:633
  115.0 20.5 %collective-permute-start.24 = (bf16[384,1536]{1,0:T(8,128)(2,1)}, bf16[384,1536]{1,0:T(8,128)(2,1)S(1)}, u32[]{:S(2)}, u32[]{:S(2)}) collective-permute-start(bf16[384,1536]{1,0:T(8,128)(2,1)} %get-tuple-element.210), channel_id=1, source_target_pairs={{0,4},{1,3},{2,6},{3,1},{4,0},{5,7},{6,2},{7,5},{8,12},{9,11},{10,... | collective-permute-start | bytes 3538952 | tf_op jit(solution)/shard_map/ppermute | solution.py:633
  135.7 19.9 %collective-permute-start.31 = (bf16[192,1536]{1,0:T(8,128)(2,1)S(1)}, bf16[192,1536]{1,0:T(8,128)(2,1)S(1)}, u32[]{:S(2)}, u32[]{:S(2)}) collective-permute-start(bf16[192,1536]{1,0:T(8,128)(2,1)S(1)} %add_convert_fusion.2), channel_id=1, source_target_pairs={{0,2},{1,5},{2,0},{3,7},{4,6},{5,1},{6,4},{7,3},{8,10},{9,13},{10,... | collective-permute-start | bytes 1769480 | tf_op jit(solution)/shard_map/ppermute | solution.py:633
  138.0 17.5 %collective-permute-start.32 = (bf16[384,1024]{1,0:T(8,128)(2,1)S(1)}, bf16[384,1024]{1,0:T(8,128)(2,1)S(1)}, u32[]{:S(2)}, u32[]{:S(2)}) collective-permute-start(bf16[384,1024]{1,0:T(8,128)(2,1)S(1)} %slice.250), channel_id=1, source_target_pairs={{0,4},{1,3},{2,6},{3,1},{4,0},{5,7},{6,2},{7,5},{8,12},{9,11},{10,... | collective-permute-start | bytes 2359304 | tf_op jit(solution)/shard_map/ppermute | solution.py:633
  139.6 16.0 %collective-permute-start.30 = (bf16[96,1536]{1,0:T(8,128)(2,1)S(1)}, bf16[96,1536]{1,0:T(8,128)(2,1)S(1)}, u32[]{:S(2)}, u32[]{:S(2)}) collective-permute-start(bf16[96,1536]{1,0:T(8,128)(2,1)S(1)} %slice.322), channel_id=1, source_target_pairs={{0,16},{2,18},{4,20},{6,22},{8,24},{10,26},{12,28},{14,30},{16,0},... | collective-permute-start | bytes 884744 | tf_op jit(solution)/shard_map/ppermute | solution.py:647
  157.5 21.6 %collective-permute-start.36 = (bf16[96,1536]{1,0:T(8,128)(2,1)S(1)}, bf16[96,1536]{1,0:T(8,128)(2,1)S(1)}, u32[]{:S(2)}, u32[]{:S(2)}) collective-permute-start(bf16[96,1536]{1,0:T(8,128)(2,1)S(1)} %slice.321), channel_id=1, source_target_pairs={{0,16},{2,18},{4,20},{6,22},{8,24},{10,26},{12,28},{14,30},{16,0},... | collective-permute-start | bytes 884744 | tf_op jit(solution)/shard_map/ppermute | solution.py:647
  164.1 15.0 %collective-permute-start.35 = (bf16[384,512]{1,0:T(8,128)(2,1)S(1)}, bf16[384,512]{1,0:T(8,128)(2,1)S(1)}, u32[]{:S(2)}, u32[]{:S(2)}) collective-permute-start(bf16[384,512]{1,0:T(8,128)(2,1)S(1)} %slice.251), channel_id=1, source_target_pairs={{0,4},{1,3},{2,6},{3,1},{4,0},{5,7},{6,2},{7,5},{8,12},{9,11},{10,... | collective-permute-start | bytes 1179656 | tf_op jit(solution)/shard_map/ppermute | solution.py:633
  165.3 13.8 %collective-permute-start.37 = (bf16[48,1536]{1,0:T(8,128)(2,1)S(1)}, bf16[48,1536]{1,0:T(8,128)(2,1)S(1)}, u32[]{:S(2)}, u32[]{:S(2)}) collective-permute-start(bf16[48,1536]{1,0:T(8,128)(2,1)S(1)} %fusion.3), channel_id=1, source_target_pairs={{0,8},{2,10},{4,12},{6,14},{8,0},{10,2},{12,4},{14,6},{16,24},{18,... | collective-permute-start | bytes 442376 | tf_op jit(solution)/shard_map/ppermute | solution.py:647
  167.0 12.1 %collective-permute-start.34 = (f32[48,512]{1,0:T(8,128)S(1)}, f32[48,512]{1,0:T(8,128)S(1)}, u32[]{:S(2)}, u32[]{:S(2)}) collective-permute-start(f32[48,512]{1,0:T(8,128)S(1)} %add.1108), channel_id=1, source_target_pairs={{0,4},{1,3},{2,6},{3,1},{4,0},{5,7},{6,2},{7,5},{8,12},{9,11},{10,... | collective-permute-start | bytes 294920 | tf_op jit(solution)/shard_map/ppermute | solution.py:633
  168.2 16.1 %collective-permute-start.39 = (bf16[96,1024]{1,0:T(8,128)(2,1)S(1)}, bf16[96,1024]{1,0:T(8,128)(2,1)S(1)}, u32[]{:S(2)}, u32[]{:S(2)}) collective-permute-start(bf16[96,1024]{1,0:T(8,128)(2,1)S(1)} %slice.323), channel_id=1, source_target_pairs={{0,16},{2,18},{4,20},{6,22},{8,24},{10,26},{12,28},{14,30},{16,0},... | collective-permute-start | bytes 589832 | tf_op jit(solution)/shard_map/ppermute | solution.py:647
  186.3 11.5 %collective-permute-start.47 = (bf16[48,1024]{1,0:T(8,128)(2,1)S(1)}, bf16[48,1024]{1,0:T(8,128)(2,1)S(1)}, u32[]{:S(2)}, u32[]{:S(2)}) collective-permute-start(bf16[48,1024]{1,0:T(8,128)(2,1)S(1)} %get-tuple-element.293), channel_id=1, source_target_pairs={{0,8},{2,10},{4,12},{6,14},{8,0},{10,2},{12,4},{14,6},{16,24},{18,... | collective-permute-start | bytes 294920 | tf_op jit(solution)/shard_map/ppermute | solution.py:647
  (68 other events, 523.2 us)

commit v10 on v9

--- a/solution.py
+++ b/solution.py
@@ -1071,6 +1071,7 @@
         flat = flat + flat_came.came[0]
         flat_came = Flow(turn(flat, dims, FIRST))
         second.second()
+        fc1_sum.came[0] = after(fc1_sum.came[0], second.sent)
         fc1_sum.quarter()
         fc2_sum = fc2_sum.last()
         result = unpadded(result)
@@ -1078,6 +1079,7 @@
         flat = flat + flat_came.came[0]
         flat_came = Flow(swap_z(flat, dims, 2))
         second.third()
+        first.came[0] = after(first.came[0], second.sent, flat)
         first.quarter()
         fc1_sum.near, late.came[0] = meet([], fc1_sum.near, late.came[0], second.sent, first.sent)[:2]
         fc1_sum = fc1_sum.last()

time: 212 us -> 211 us (level)
    ppermute x8, starting transfers between devices: 13 us -> 9.13 us  [swap_z(): return lax.ppermute(values, 'dp', pairs)]
    ppermute x30, starting transfers between devices: 45.7 us -> 48.9 us  [turn(): return lax.ppermute(values, ('dp', 'mp'), pairs)]
    unnamed x86 -> x94, local copies, waits for them, and re-layouts: 5.39 us -> 6.16 us
where the time goes in v10:
time: 211 us; the launch traced here: 207 us
  Pallas kernels  80.4 us (38%)
  starting transfers between devices  60.6 us (29%)
  waiting for transfers between devices  41.8 us (20%)
  local copies, waits for them, and re-layouts  15.2 us (7%)
  other arithmetic  7.3 us (3%)
    ppermute x30, starting transfers between devices, turn(): return lax.ppermute(values, ('dp', 'mp'), pairs)  48.9 us
    ppermute x30, waiting for transfers between devices, turn(): return lax.ppermute(values, ('dp', 'mp'), pairs)  32 us
    pallas_call x2, Pallas kernels, attend_back(): pl.pallas_call(partial(attend_back_kernel, before, count), out_shape=smal...  27.2 us
    pallas_call x1, Pallas kernels, hidden_back(): pl.pallas_call(partial(hidden_back_kernel, bases0, bases1), out_shape=[sh...  16 us
    pallas_call x1, Pallas kernels, attend(): pl.pallas_call(partial(attend_kernel, count, total), out_shape=[shape((8,...  14.4 us
    pallas_call x1, Pallas kernels, hidden_fwd(): pl.pallas_call(partial(hidden_fwd_kernel, bases), out_shape=[shape((width...  9.48 us
    ppermute x8, starting transfers between devices, swap_z(): return lax.ppermute(values, 'dp', pairs)  9.13 us
    unnamed x94, local copies, waits for them, and re-layouts  6.16 us
  transfers between devices with their start and end apart: 50, of which 20 were waited for; matrix products, arithmetic and copies ran while one was open for 6% of the time, Pallas kernels for 37%

profile of v10, /device:TPU:0, one launch (start us, length us, event | category | flops | bytes accessed | tf_op | source)
XLA Modules:
  0.0 207.0 jit_solution(13331344906517609720)
XLA Ops:
  5.5 3.0 %collective-permute-start.1 = (bf16[48,1664]{1,0:T(8,128)(2,1)S(1)}, bf16[48,1664]{1,0:T(8,128)(2,1)S(1)}, u32[]{:S(2)}, u32[]{:S(2)}) collective-permute-start(bf16[48,1664]{1,0:T(8,128)(2,1)S(1)} %pad_maximum_fusion.2), channel_id=1, source_target_pairs={{0,8},{1,9},{2,10},{3,11},{4,12},{5,13},{6,14},{7,15},{8,16},{9,17... | collective-permute-start | bytes 479240 | tf_op jit(solution)/shard_map/ppermute | solution.py:633
  8.4 2.6 %collective-permute-start.2 = (bf16[48,1664]{1,0:T(8,128)(2,1)S(1)}, bf16[48,1664]{1,0:T(8,128)(2,1)S(1)}, u32[]{:S(2)}, u32[]{:S(2)}) collective-permute-start(bf16[48,1664]{1,0:T(8,128)(2,1)S(1)} %pad_maximum_fusion.2), channel_id=1, source_target_pairs={{0,16},{1,17},{2,18},{3,19},{4,20},{5,21},{6,22},{7,23},{8,24},{9,... | collective-permute-start | bytes 479240 | tf_op jit(solution)/shard_map/ppermute | solution.py:633
  17.9 3.9 %collective-permute-done.2.refs_1_ = bf16[48,1664]{1,0:T(8,128)(2,1)S(1)} collective-permute-done((bf16[48,1664]{1,0:T(8,128)(2,1)S(1)}, bf16[48,1664]{1,0:T(8,128)(2,1)S(1)}, u32[]{:S(2)}, u32[]{:S(2)}) %collective-permute-start.2) | collective-permute-done | bytes 159776 | tf_op jit(solution)/shard_map/ppermute | solution.py:633
  26.2 3.9 %collective-permute-start.7 = (bf16[48,1536]{1,0:T(8,128)(2,1)S(1)}, bf16[48,1536]{1,0:T(8,128)(2,1)S(1)}, u32[]{:S(2)}, u32[]{:S(2)}) collective-permute-start(bf16[48,1536]{1,0:T(8,128)(2,1)S(1)} %copy-done.39), channel_id=1, source_target_pairs={{0,8},{1,9},{2,10},{3,11},{4,12},{5,13},{6,14},{7,15},{8,16},{9,17... | collective-permute-start | bytes 442376 | tf_op jit(solution)/shard_map/ppermute | solution.py:633
  32.4 3.5 %collective-permute-done.7.refs_0_ = bf16[48,1536]{1,0:T(8,128)(2,1)S(1)} collective-permute-done((bf16[48,1536]{1,0:T(8,128)(2,1)S(1)}, bf16[48,1536]{1,0:T(8,128)(2,1)S(1)}, u32[]{:S(2)}, u32[]{:S(2)}) %collective-permute-start.7) | collective-permute-done | bytes 147488 | tf_op jit(solution)/shard_map/ppermute | solution.py:633
  35.9 4.5 %collective-permute-done.8.refs_1_ = bf16[48,1536]{1,0:T(8,128)(2,1)S(1)} collective-permute-done((bf16[48,1536]{1,0:T(8,128)(2,1)S(1)}, bf16[48,1536]{1,0:T(8,128)(2,1)S(1)}, u32[]{:S(2)}, u32[]{:S(2)}) %collective-permute-start.8) | collective-permute-done | bytes 147488 | tf_op jit(solution)/shard_map/ppermute | solution.py:633
  45.2 4.0 %collective-permute-start.12 = (bf16[48,1536]{1,0:T(8,128)(2,1)S(1)}, bf16[48,1536]{1,0:T(8,128)(2,1)S(1)}, u32[]{:S(2)}, u32[]{:S(2)}) collective-permute-start(bf16[48,1536]{1,0:T(8,128)(2,1)S(1)} %bitcast.108), channel_id=1, source_target_pairs={{0,8},{1,9},{2,10},{3,11},{4,12},{5,13},{6,14},{7,15},{8,16},{9,17... | collective-permute-start | bytes 442376 | tf_op jit(solution)/shard_map/ppermute | solution.py:633
  50.2 1.9 collective-permute-start.14
  52.2 2.2 %collective-permute-done.12.refs_0_ = bf16[48,1536]{1,0:T(8,128)(2,1)S(1)} collective-permute-done((bf16[48,1536]{1,0:T(8,128)(2,1)S(1)}, bf16[48,1536]{1,0:T(8,128)(2,1)S(1)}, u32[]{:S(2)}, u32[]{:S(2)}) %collective-permute-start.12) | collective-permute-done | bytes 147488 | tf_op jit(solution)/shard_map/ppermute | solution.py:633
  54.4 4.4 %collective-permute-done.13.refs_1_ = bf16[48,1536]{1,0:T(8,128)(2,1)S(1)} collective-permute-done((bf16[48,1536]{1,0:T(8,128)(2,1)S(1)}, bf16[48,1536]{1,0:T(8,128)(2,1)S(1)}, u32[]{:S(2)}, u32[]{:S(2)}) %collective-permute-start.13) | collective-permute-done | bytes 147488 | tf_op jit(solution)/shard_map/ppermute | solution.py:633
  67.0 14.4 %attend.1 = (f32[8,768]{1,0:T(8,128)S(1)}, bf16[2,224,768]{2,1,0:T(8,128)(2,1)S(1)}, bf16[2,224,768]{2,1,0:T(8,128)(2,1)}, bf16[2,256,768]{2,1,0:T(8,128)(2,1)},...) custom-call(s32[112]{0:T(128)S(1)} %concatenate.52.meta.refs_0_, ...), custom_call_target="tpu_custom_call" | custom-call | flops 1000 | bytes 1000 | tf_op jit(solution)/shard_map/attend/pallas_call | solution.py:194
  86.3 9.5 %hidden_fwd.1 = (bf16[384,1536]{1,0:T(8,128)(2,1)}, bf16[384,1536]{1,0:T(8,128)(2,1)}) custom-call(s32[112]{0:T(128)S(1)} %concatenate.52.meta.refs_0_, bf16[448,768]{1,0:T(8,128)(2,1)S(1)} %bitcast.91, bf16[448,768]{1,0:T(8,128)(2,1)S(1)} %bitcast.93, bf16[448,768]{1,0:T(8,128)(2,1)} %bitcast.96, bf16[448,768]{1,0:T(8,128)(2,1)} %bitcast.103, ...), custom_call_target="tpu_custom_call" | custom-call | flops 1000 | bytes 1000 | tf_op jit(solution)/shard_map/hidden_fwd/pallas_call | solution.py:254
  97.1 16.0 %hidden_back.1 = (f32[1,1536]{1,0:T(1,128)S(1)}, bf16[384,1536]{1,0:T(8,128)(2,1)}, bf16[384,1536]{1,0:T(8,128)(2,1)}, f32[448,768]{1,0:T(8,128)}, bf16[448,768]...) custom-call(s32[112]{0:T(128)S(1)} %concatenate.52.meta.refs_0_, bf16[448,768]{1,0:T(8,128)(2,1)S(1)} %bitcast.92, ...), custom_call_target="tpu_custom_call" | custom-call | flops 1000 | bytes 1000 | tf_op jit(solution)/shard_map/hidden_back/pallas_call | solution.py:317
  116.7 15.0 %attend_back.2 = (f32[4,768]{1,0:T(4,128)S(1)}, f32[2,512]{1,0:T(2,128)S(1)}, f32[128,128]{1,0:T(8,128)S(1)}, bf16[768,1024]{1,0:T(8,128)(2,1)}, bf16[768,1024]{...) custom-call(s32[112]{0:T(128)S(1)} %concatenate.52.meta.refs_0_, ...), custom_call_target="tpu_custom_call" | custom-call | flops 1000 | bytes 1000 | tf_op jit(solution)/shard_map/attend_back/pallas_call | solution.py:610
  132.6 2.9 %collective-permute-done.24 = bf16[384,1536]{1,0:T(8,128)(2,1)S(1)} collective-permute-done((bf16[384,1536]{1,0:T(8,128)(2,1)}, bf16[384,1536]{1,0:T(8,128)(2,1)S(1)}, u32[]{:S(2)}, u32[]{:S(2)}) %collective-permute-start.24) | collective-permute-done | bytes 1179680 | tf_op jit(solution)/shard_map/ppermute | solution.py:633
  139.6 3.0 %collective-permute-start.30 = (bf16[96,1536]{1,0:T(8,128)(2,1)S(1)}, bf16[96,1536]{1,0:T(8,128)(2,1)S(1)}, u32[]{:S(2)}, u32[]{:S(2)}) collective-permute-start(bf16[96,1536]{1,0:T(8,128)(2,1)S(1)} %slice.322), channel_id=1, source_target_pairs={{0,16},{2,18},{4,20},{6,22},{8,24},{10,26},{12,28},{14,30},{16,0},... | collective-permute-start | bytes 884744 | tf_op jit(solution)/shard_map/ppermute | solution.py:647
  142.6 12.2 %attend_back.3 = (f32[48,512]{1,0:T(8,128)S(1)}, bf16[768,512]{1,0:T(8,128)(2,1)}, bf16[768,512]{1,0:T(8,128)(2,1)}, f32[2,224,768]{2,1,0:T(8,128)}) custom-call(s32[112]{0:T(128)S(1)} %concatenate.52.meta.refs_0_, f32[8,768]{1,0:T(8,128)S(1)} %get-tuple-element.189.vecs, bf16[256,128]{1,0:T(8,128)(2,1)S(1)} %copy-done.11, ...), custom_call_target="tpu_custom_call" | custom-call | flops 1000 | bytes 1000 | tf_op jit(solution)/shard_map/attend_back/pallas_call | solution.py:610
  158.3 5.2 %collective-permute-done.33 = bf16[192,1024]{1,0:T(8,128)(2,1)S(1)} collective-permute-done((bf16[192,1024]{1,0:T(8,128)(2,1)S(1)}, bf16[192,1024]{1,0:T(8,128)(2,1)S(1)}, u32[]{:S(2)}, u32[]{:S(2)}) %collective-permute-start.33) | collective-permute-done | bytes 393248 | tf_op jit(solution)/shard_map/ppermute | solution.py:633
  168.2 2.4 %collective-permute-start.39 = (bf16[96,1024]{1,0:T(8,128)(2,1)S(1)}, bf16[96,1024]{1,0:T(8,128)(2,1)S(1)}, u32[]{:S(2)}, u32[]{:S(2)}) collective-permute-start(bf16[96,1024]{1,0:T(8,128)(2,1)S(1)} %slice.323), channel_id=1, source_target_pairs={{0,16},{2,18},{4,20},{6,22},{8,24},{10,26},{12,28},{14,30},{16,0},... | collective-permute-start | bytes 589832 | tf_op jit(solution)/shard_map/ppermute | solution.py:647
  170.5 5.9 %hidden_out.1 = (f32[448,768]{1,0:T(8,128)}, bf16[448,768]{1,0:T(8,128)(2,1)S(1)}) custom-call(s32[112]{0:T(128)S(1)} %concatenate.52.meta.refs_0_, bf16[896,1536]{1,0:T(8,128)(2,1)} %get-tuple-element.257.acts_in, bf16[96,4736]{1,0:T(8,128)(2,1)} %copy-done, bf16[96,4736]{1,0:T(8,128)(2,1)} %copy-done.13, bf16[288,1536]{1,0:T(8,128)(2,1)S(1)} %copy-done.2, ...), custom_call_target="tpu_custom_call" | custom-call | flops 1000 | bytes 1000 | tf_op jit(solution)/shard_map/hidden_out/pallas_call | solution.py:361
  176.4 2.5 %collective-permute-done.36 = bf16[96,1536]{1,0:T(8,128)(2,1)S(1)} collective-permute-done((bf16[96,1536]{1,0:T(8,128)(2,1)S(1)}, bf16[96,1536]{1,0:T(8,128)(2,1)S(1)}, u32[]{:S(2)}, u32[]{:S(2)}) %collective-permute-start.36) | collective-permute-done | bytes 294944 | tf_op jit(solution)/shard_map/ppermute | solution.py:647
  182.1 2.0 copy.67
  188.7 2.6 %collective-permute-start.45 = (bf16[48,512]{1,0:T(8,128)(2,1)S(1)}, bf16[48,512]{1,0:T(8,128)(2,1)S(1)}, u32[]{:S(2)}, u32[]{:S(2)}) collective-permute-start(bf16[48,512]{1,0:T(8,128)(2,1)S(1)} %get-tuple-element.301), channel_id=1, source_target_pairs={{0,16},{1,17},{2,18},{3,19},{4,20},{5,21},{6,22},{7,23},{8,24},{9,... | collective-permute-start | bytes 147464 | tf_op jit(solution)/shard_map/ppermute | solution.py:633
  199.8 2.7 %collective-permute-done.48 = f32[48,512]{1,0:T(8,128)S(1)} collective-permute-done((f32[48,512]{1,0:T(8,128)S(1)}, f32[48,512]{1,0:T(8,128)S(1)}, u32[]{:S(2)}, u32[]{:S(2)}) %collective-permute-start.48) | collective-permute-done | bytes 98336 | tf_op jit(solution)/shard_map/ppermute | solution.py:647
  (260 shorter events, 75.0 us)
Async XLA Ops:
  5.5 12.4 %collective-permute-start.1 = (bf16[48,1664]{1,0:T(8,128)(2,1)S(1)}, bf16[48,1664]{1,0:T(8,128)(2,1)S(1)}, u32[]{:S(2)}, u32[]{:S(2)}) collective-permute-start(bf16[48,1664]{1,0:T(8,128)(2,1)S(1)} %pad_maximum_fusion.2), channel_id=1, source_target_pairs={{0,8},{1,9},{2,10},{3,11},{4,12},{5,13},{6,14},{7,15},{8,16},{9,17... | collective-permute-start | bytes 479240 | tf_op jit(solution)/shard_map/ppermute | solution.py:633
  8.4 13.4 %collective-permute-start.2 = (bf16[48,1664]{1,0:T(8,128)(2,1)S(1)}, bf16[48,1664]{1,0:T(8,128)(2,1)S(1)}, u32[]{:S(2)}, u32[]{:S(2)}) collective-permute-start(bf16[48,1664]{1,0:T(8,128)(2,1)S(1)} %pad_maximum_fusion.2), channel_id=1, source_target_pairs={{0,16},{1,17},{2,18},{3,19},{4,20},{5,21},{6,22},{7,23},{8,24},{9,... | collective-permute-start | bytes 479240 | tf_op jit(solution)/shard_map/ppermute | solution.py:633
  11.0 10.8 %collective-permute-start.3 = (bf16[48,1664]{1,0:T(8,128)(2,1)S(1)}, bf16[48,1664]{1,0:T(8,128)(2,1)S(1)}, u32[]{:S(2)}, u32[]{:S(2)}) collective-permute-start(bf16[48,1664]{1,0:T(8,128)(2,1)S(1)} %pad_maximum_fusion.2), channel_id=1, source_target_pairs={{0,24},{1,25},{2,26},{3,27},{4,28},{5,29},{6,30},{7,31},{8,0},{9,1... | collective-permute-start | bytes 479240 | tf_op jit(solution)/shard_map/ppermute | solution.py:633
  22.4 18.5 %collective-permute-start.5 = (bf16[96,4736]{1,0:T(8,128)(2,1)S(1)}, bf16[96,4736]{1,0:T(8,128)(2,1)S(1)}, u32[]{:S(2)}, u32[]{:S(2)}) collective-permute-start(bf16[96,4736]{1,0:T(8,128)(2,1)S(1)} %stack.288.refs_0_.refs_4_), channel_id=1, source_target_pairs={{0,4},{1,3},{2,6},{3,1},{4,0},{5,7},{6,2},{7,5},{8,12},{9,11},{10,... | collective-permute-start | bytes 2727944 | tf_op jit(solution)/shard_map/ppermute | solution.py:633
  24.6 15.8 %collective-permute-start.6 = (bf16[144,1664]{1,0:T(8,128)(2,1)S(1)}, bf16[144,1664]{1,0:T(8,128)(2,1)S(1)}, u32[]{:S(2)}, u32[]{:S(2)}) collective-permute-start(bf16[144,1664]{1,0:T(8,128)(2,1)S(1)} %stack.287.refs_0_), channel_id=1, source_target_pairs={{0,2},{1,5},{2,0},{3,7},{4,6},{5,1},{6,4},{7,3},{8,10},{9,13},{10,... | collective-permute-start | bytes 1437704 | tf_op jit(solution)/shard_map/ppermute | solution.py:633
  30.1 10.4 %collective-permute-start.8 = (bf16[48,1536]{1,0:T(8,128)(2,1)S(1)}, bf16[48,1536]{1,0:T(8,128)(2,1)S(1)}, u32[]{:S(2)}, u32[]{:S(2)}) collective-permute-start(bf16[48,1536]{1,0:T(8,128)(2,1)S(1)} %copy-done.39), channel_id=1, source_target_pairs={{0,16},{1,17},{2,18},{3,19},{4,20},{5,21},{6,22},{7,23},{8,24},{9,... | collective-permute-start | bytes 442376 | tf_op jit(solution)/shard_map/ppermute | solution.py:633
  41.6 18.6 %collective-permute-start.10 = (bf16[288,1664]{1,0:T(8,128)(2,1)S(1)}, bf16[288,1664]{1,0:T(8,128)(2,1)S(1)}, u32[]{:S(2)}, u32[]{:S(2)}) collective-permute-start(bf16[288,1664]{1,0:T(8,128)(2,1)S(1)} %stack.289.refs_2_), channel_id=1, source_target_pairs={{0,4},{1,3},{2,6},{3,1},{4,0},{5,7},{6,2},{7,5},{8,12},{9,11},{10,... | collective-permute-start | bytes 2875400 | tf_op jit(solution)/shard_map/ppermute | solution.py:633
  43.7 15.4 %collective-permute-start.11 = (bf16[144,1536]{1,0:T(8,128)(2,1)S(1)}, bf16[144,1536]{1,0:T(8,128)(2,1)S(1)}, u32[]{:S(2)}, u32[]{:S(2)}) collective-permute-start(bf16[144,1536]{1,0:T(8,128)(2,1)S(1)} %stack.290.refs_0_), channel_id=1, source_target_pairs={{0,2},{1,5},{2,0},{3,7},{4,6},{5,1},{6,4},{7,3},{8,10},{9,13},{10,... | collective-permute-start | bytes 1327112 | tf_op jit(solution)/shard_map/ppermute | solution.py:633
  61.3 21.0 %collective-permute-start.18 = (bf16[288,1536]{1,0:T(8,128)(2,1)S(1)}, bf16[288,1536]{1,0:T(8,128)(2,1)S(1)}, u32[]{:S(2)}, u32[]{:S(2)}) collective-permute-start(bf16[288,1536]{1,0:T(8,128)(2,1)S(1)} %stack.291.refs_2_), channel_id=1, source_target_pairs={{0,4},{1,3},{2,6},{3,1},{4,0},{5,7},{6,2},{7,5},{8,12},{9,11},{10,... | collective-permute-start | bytes 2654216 | tf_op jit(solution)/shard_map/ppermute | solution.py:633
  66.0 16.3 %collective-permute-start.20 = (bf16[2,224,768]{2,1,0:T(8,128)(2,1)S(1)}, bf16[2,224,768]{2,1,0:T(8,128)(2,1)S(1)}, u32[]{:S(2)}, u32[]{:S(2)}) collective-permute-start(bf16[2,224,768]{2,1,0:T(8,128)(2,1)S(1)} %bitcast.95), channel_id=1, source_target_pairs={{0,1},{1,0},{2,3},{3,2},{4,5},{5,4},{6,7},{7,6},{8,9},{9,8},{10,11... | collective-permute-start | bytes 2064392 | tf_op jit(solution)/shard_map/ppermute | solution.py:651
  66.1 16.2 %collective-permute-start.19 = (bf16[144,1536]{1,0:T(8,128)(2,1)S(1)}, bf16[144,1536]{1,0:T(8,128)(2,1)S(1)}, u32[]{:S(2)}, u32[]{:S(2)}) collective-permute-start(bf16[144,1536]{1,0:T(8,128)(2,1)S(1)} %stack.292.refs_0_), channel_id=1, source_target_pairs={{0,2},{1,5},{2,0},{3,7},{4,6},{5,1},{6,4},{7,3},{8,10},{9,13},{10,... | collective-permute-start | bytes 1327112 | tf_op jit(solution)/shard_map/ppermute | solution.py:633
  82.9 13.1 %collective-permute-start.22 = (bf16[288,1536]{1,0:T(8,128)(2,1)S(1)}, bf16[288,1536]{1,0:T(8,128)(2,1)S(1)}, u32[]{:S(2)}, u32[]{:S(2)}) collective-permute-start(bf16[288,1536]{1,0:T(8,128)(2,1)S(1)} %stack.293.refs_6_.refs_2_), channel_id=1, source_target_pairs={{0,4},{1,3},{2,6},{3,1},{4,0},{5,7},{6,2},{7,5},{8,12},{9,11},{10,... | collective-permute-start | bytes 2654216 | tf_op jit(solution)/shard_map/ppermute | solution.py:633
  96.0 17.3 %collective-permute-start.23 = (bf16[384,1536]{1,0:T(8,128)(2,1)}, bf16[384,1536]{1,0:T(8,128)(2,1)S(1)}, u32[]{:S(2)}, u32[]{:S(2)}) collective-permute-start(bf16[384,1536]{1,0:T(8,128)(2,1)} %get-tuple-element.209), channel_id=1, source_target_pairs={{0,4},{1,3},{2,6},{3,1},{4,0},{5,7},{6,2},{7,5},{8,12},{9,11},{10,... | collective-permute-start | bytes 3538952 | tf_op jit(solution)/shard_map/ppermute | solution.py:633
  113.4 18.3 %collective-permute-start.25 = (bf16[192,1536]{1,0:T(8,128)(2,1)S(1)}, bf16[192,1536]{1,0:T(8,128)(2,1)S(1)}, u32[]{:S(2)}, u32[]{:S(2)}) collective-permute-start(bf16[192,1536]{1,0:T(8,128)(2,1)S(1)} %add_convert_fusion.3), channel_id=1, source_target_pairs={{0,2},{1,5},{2,0},{3,7},{4,6},{5,1},{6,4},{7,3},{8,10},{9,13},{10,... | collective-permute-start | bytes 1769480 | tf_op jit(solution)/shard_map/ppermute | solution.py:633
  115.0 20.5 %collective-permute-start.24 = (bf16[384,1536]{1,0:T(8,128)(2,1)}, bf16[384,1536]{1,0:T(8,128)(2,1)S(1)}, u32[]{:S(2)}, u32[]{:S(2)}) collective-permute-start(bf16[384,1536]{1,0:T(8,128)(2,1)} %get-tuple-element.212), channel_id=1, source_target_pairs={{0,4},{1,3},{2,6},{3,1},{4,0},{5,7},{6,2},{7,5},{8,12},{9,11},{10,... | collective-permute-start | bytes 3538952 | tf_op jit(solution)/shard_map/ppermute | solution.py:633
  135.7 19.9 %collective-permute-start.31 = (bf16[192,1536]{1,0:T(8,128)(2,1)S(1)}, bf16[192,1536]{1,0:T(8,128)(2,1)S(1)}, u32[]{:S(2)}, u32[]{:S(2)}) collective-permute-start(bf16[192,1536]{1,0:T(8,128)(2,1)S(1)} %add_convert_fusion.2), channel_id=1, source_target_pairs={{0,2},{1,5},{2,0},{3,7},{4,6},{5,1},{6,4},{7,3},{8,10},{9,13},{10,... | collective-permute-start | bytes 1769480 | tf_op jit(solution)/shard_map/ppermute | solution.py:633
  138.0 17.5 %collective-permute-start.32 = (bf16[384,1024]{1,0:T(8,128)(2,1)S(1)}, bf16[384,1024]{1,0:T(8,128)(2,1)S(1)}, u32[]{:S(2)}, u32[]{:S(2)}) collective-permute-start(bf16[384,1024]{1,0:T(8,128)(2,1)S(1)} %slice.250), channel_id=1, source_target_pairs={{0,4},{1,3},{2,6},{3,1},{4,0},{5,7},{6,2},{7,5},{8,12},{9,11},{10,... | collective-permute-start | bytes 2359304 | tf_op jit(solution)/shard_map/ppermute | solution.py:633
  139.6 15.9 %collective-permute-start.30 = (bf16[96,1536]{1,0:T(8,128)(2,1)S(1)}, bf16[96,1536]{1,0:T(8,128)(2,1)S(1)}, u32[]{:S(2)}, u32[]{:S(2)}) collective-permute-start(bf16[96,1536]{1,0:T(8,128)(2,1)S(1)} %slice.322), channel_id=1, source_target_pairs={{0,16},{2,18},{4,20},{6,22},{8,24},{10,26},{12,28},{14,30},{16,0},... | collective-permute-start | bytes 884744 | tf_op jit(solution)/shard_map/ppermute | solution.py:647
  157.5 21.5 %collective-permute-start.36 = (bf16[96,1536]{1,0:T(8,128)(2,1)S(1)}, bf16[96,1536]{1,0:T(8,128)(2,1)S(1)}, u32[]{:S(2)}, u32[]{:S(2)}) collective-permute-start(bf16[96,1536]{1,0:T(8,128)(2,1)S(1)} %slice.321), channel_id=1, source_target_pairs={{0,16},{2,18},{4,20},{6,22},{8,24},{10,26},{12,28},{14,30},{16,0},... | collective-permute-start | bytes 884744 | tf_op jit(solution)/shard_map/ppermute | solution.py:647
  164.0 14.9 %collective-permute-start.35 = (bf16[384,512]{1,0:T(8,128)(2,1)S(1)}, bf16[384,512]{1,0:T(8,128)(2,1)S(1)}, u32[]{:S(2)}, u32[]{:S(2)}) collective-permute-start(bf16[384,512]{1,0:T(8,128)(2,1)S(1)} %slice.251), channel_id=1, source_target_pairs={{0,4},{1,3},{2,6},{3,1},{4,0},{5,7},{6,2},{7,5},{8,12},{9,11},{10,... | collective-permute-start | bytes 1179656 | tf_op jit(solution)/shard_map/ppermute | solution.py:633
  165.3 13.6 %collective-permute-start.37 = (bf16[48,1536]{1,0:T(8,128)(2,1)S(1)}, bf16[48,1536]{1,0:T(8,128)(2,1)S(1)}, u32[]{:S(2)}, u32[]{:S(2)}) collective-permute-start(bf16[48,1536]{1,0:T(8,128)(2,1)S(1)} %fusion.3), channel_id=1, source_target_pairs={{0,8},{2,10},{4,12},{6,14},{8,0},{10,2},{12,4},{14,6},{16,24},{18,... | collective-permute-start | bytes 442376 | tf_op jit(solution)/shard_map/ppermute | solution.py:647
  166.9 12.0 %collective-permute-start.34 = (f32[48,512]{1,0:T(8,128)S(1)}, f32[48,512]{1,0:T(8,128)S(1)}, u32[]{:S(2)}, u32[]{:S(2)}) collective-permute-start(f32[48,512]{1,0:T(8,128)S(1)} %add.1108), channel_id=1, source_target_pairs={{0,4},{1,3},{2,6},{3,1},{4,0},{5,7},{6,2},{7,5},{8,12},{9,11},{10,... | collective-permute-start | bytes 294920 | tf_op jit(solution)/shard_map/ppermute | solution.py:633
  168.2 15.9 %collective-permute-start.39 = (bf16[96,1024]{1,0:T(8,128)(2,1)S(1)}, bf16[96,1024]{1,0:T(8,128)(2,1)S(1)}, u32[]{:S(2)}, u32[]{:S(2)}) collective-permute-start(bf16[96,1024]{1,0:T(8,128)(2,1)S(1)} %slice.323), channel_id=1, source_target_pairs={{0,16},{2,18},{4,20},{6,22},{8,24},{10,26},{12,28},{14,30},{16,0},... | collective-permute-start | bytes 589832 | tf_op jit(solution)/shard_map/ppermute | solution.py:647
  187.4 10.4 %collective-permute-start.43 = (f32[48,512]{1,0:T(8,128)S(1)}, f32[48,512]{1,0:T(8,128)S(1)}, u32[]{:S(2)}, u32[]{:S(2)}) collective-permute-start(f32[48,512]{1,0:T(8,128)S(1)} %add.1120), channel_id=1, source_target_pairs={{0,16},{2,18},{4,20},{6,22},{8,24},{10,26},{12,28},{14,30},{16,0},... | collective-permute-start | bytes 294920 | tf_op jit(solution)/shard_map/ppermute | solution.py:647
  (72 other events, 528.0 us)

commit v11 on v10

--- a/solution.py
+++ b/solution.py
@@ -960,8 +960,7 @@
         fc1_over = Flow(turn(fc1_z, dims, SECOND))
         fc2_z = stack(*fc2_z.came)
         fc2_beside = Flow(turn(fc2_z, dims, FIRST))
-        tok, fc1_z, fc2_z, dm = meet([far], tok, fc1_z, fc2_z, dm)
-        dm_far = Flow(other_core(dm))
+        tok, fc1_z, fc2_z = meet([far], tok, fc1_z, fc2_z)
         attend_own, attend_far = [own, over, attend_z, z_over], far.came
 
     vecs, n1, q, k, v, p, att, weights, x1, n2 = attend(
@@ -971,8 +970,8 @@
     if dims is None:
         dm_far = other_core(dm)
     else:
-        (n2,) = meet([fc1_over, fc2_beside, dm_far], n2)
-        (dm_far,) = dm_far.came
+        n2, dm = meet([fc1_over, fc2_beside], n2, dm)
+        dm_far = other_core(dm)
         fc2_z = stack(fc2_z, *fc2_beside.came)
         fc2_over = turn(fc2_z, dims, SECOND)
     dm_flat, dm_far = dm.reshape(-1, width), dm_far.reshape(-1, width)

time: 211 us -> 210 us (level)
  starting transfers between devices: 60.6 us -> 57.4 us
  waiting for transfers between devices: 41.8 us -> 44.8 us
    ppermute x30, starting transfers between devices: 48.9 us -> 44.8 us  [turn(): return lax.ppermute(values, ('dp', 'mp'), pairs)]
    unnamed x94 -> x92, local copies, waits for them, and re-layouts: 6.16 us -> 6.13 us
  transfers between devices with their start and end apart: 50 -> 50, of which waited for: 20 -> 21; matrix products, arithmetic and copies ran while one was open for 6% -> 6% of each run, Pallas kernels for 37% -> 37%
where the time goes in v11:
time: 210 us; the launch traced here: 207 us
  Pallas kernels  80.4 us (38%)
  starting transfers between devices  57.4 us (27%)
  waiting for transfers between devices  44.8 us (21%)
  local copies, waits for them, and re-layouts  15.2 us (7%)
  other arithmetic  7.3 us (3%)
    ppermute x30, starting transfers between devices, turn(): return lax.ppermute(values, ('dp', 'mp'), pairs)  44.8 us
    ppermute x30, waiting for transfers between devices, turn(): return lax.ppermute(values, ('dp', 'mp'), pairs)  33.4 us
    pallas_call x2, Pallas kernels, attend_back(): pl.pallas_call(partial(attend_back_kernel, before, count), out_shape=smal...  27.2 us
    pallas_call x1, Pallas kernels, hidden_back(): pl.pallas_call(partial(hidden_back_kernel, bases0, bases1), out_shape=[sh...  16 us
    pallas_call x1, Pallas kernels, attend(): pl.pallas_call(partial(attend_kernel, count, total), out_shape=[shape((8,...  14.4 us
    ppermute x8, starting transfers between devices, swap_z(): return lax.ppermute(values, 'dp', pairs)  10.1 us
    pallas_call x1, Pallas kernels, hidden_fwd(): pl.pallas_call(partial(hidden_fwd_kernel, bases), out_shape=[shape((width...  9.47 us
    ppermute x8, waiting for transfers between devices, swap_z(): return lax.ppermute(values, 'dp', pairs)  6.77 us
  transfers between devices with their start and end apart: 50, of which 21 were waited for; matrix products, arithmetic and copies ran while one was open for 6% of the time, Pallas kernels for 37%

profile of v11, /device:TPU:0, one launch (start us, length us, event | category | flops | bytes accessed | tf_op | source)
XLA Modules:
  0.0 206.8 jit_solution(1509249123148234163)
XLA Ops:
  5.5 3.0 %collective-permute-start.1 = (bf16[48,1664]{1,0:T(8,128)(2,1)S(1)}, bf16[48,1664]{1,0:T(8,128)(2,1)S(1)}, u32[]{:S(2)}, u32[]{:S(2)}) collective-permute-start(bf16[48,1664]{1,0:T(8,128)(2,1)S(1)} %pad_maximum_fusion.2), channel_id=1, source_target_pairs={{0,8},{1,9},{2,10},{3,11},{4,12},{5,13},{6,14},{7,15},{8,16},{9,17... | collective-permute-start | bytes 479240 | tf_op jit(solution)/shard_map/ppermute | solution.py:633
  8.4 2.6 %collective-permute-start.2 = (bf16[48,1664]{1,0:T(8,128)(2,1)S(1)}, bf16[48,1664]{1,0:T(8,128)(2,1)S(1)}, u32[]{:S(2)}, u32[]{:S(2)}) collective-permute-start(bf16[48,1664]{1,0:T(8,128)(2,1)S(1)} %pad_maximum_fusion.2), channel_id=1, source_target_pairs={{0,16},{1,17},{2,18},{3,19},{4,20},{5,21},{6,22},{7,23},{8,24},{9,... | collective-permute-start | bytes 479240 | tf_op jit(solution)/shard_map/ppermute | solution.py:633
  17.9 3.9 %collective-permute-done.2.refs_1_ = bf16[48,1664]{1,0:T(8,128)(2,1)S(1)} collective-permute-done((bf16[48,1664]{1,0:T(8,128)(2,1)S(1)}, bf16[48,1664]{1,0:T(8,128)(2,1)S(1)}, u32[]{:S(2)}, u32[]{:S(2)}) %collective-permute-start.2) | collective-permute-done | bytes 159776 | tf_op jit(solution)/shard_map/ppermute | solution.py:633
  26.2 3.9 %collective-permute-start.7 = (bf16[48,1536]{1,0:T(8,128)(2,1)S(1)}, bf16[48,1536]{1,0:T(8,128)(2,1)S(1)}, u32[]{:S(2)}, u32[]{:S(2)}) collective-permute-start(bf16[48,1536]{1,0:T(8,128)(2,1)S(1)} %copy-done.38), channel_id=1, source_target_pairs={{0,8},{1,9},{2,10},{3,11},{4,12},{5,13},{6,14},{7,15},{8,16},{9,17... | collective-permute-start | bytes 442376 | tf_op jit(solution)/shard_map/ppermute | solution.py:633
  32.4 3.5 %collective-permute-done.7.refs_0_ = bf16[48,1536]{1,0:T(8,128)(2,1)S(1)} collective-permute-done((bf16[48,1536]{1,0:T(8,128)(2,1)S(1)}, bf16[48,1536]{1,0:T(8,128)(2,1)S(1)}, u32[]{:S(2)}, u32[]{:S(2)}) %collective-permute-start.7) | collective-permute-done | bytes 147488 | tf_op jit(solution)/shard_map/ppermute | solution.py:633
  35.9 4.5 %collective-permute-done.8.refs_1_ = bf16[48,1536]{1,0:T(8,128)(2,1)S(1)} collective-permute-done((bf16[48,1536]{1,0:T(8,128)(2,1)S(1)}, bf16[48,1536]{1,0:T(8,128)(2,1)S(1)}, u32[]{:S(2)}, u32[]{:S(2)}) %collective-permute-start.8) | collective-permute-done | bytes 147488 | tf_op jit(solution)/shard_map/ppermute | solution.py:633
  45.2 4.0 %collective-permute-start.12 = (bf16[48,1536]{1,0:T(8,128)(2,1)S(1)}, bf16[48,1536]{1,0:T(8,128)(2,1)S(1)}, u32[]{:S(2)}, u32[]{:S(2)}) collective-permute-start(bf16[48,1536]{1,0:T(8,128)(2,1)S(1)} %bitcast.108), channel_id=1, source_target_pairs={{0,8},{1,9},{2,10},{3,11},{4,12},{5,13},{6,14},{7,15},{8,16},{9,17... | collective-permute-start | bytes 442376 | tf_op jit(solution)/shard_map/ppermute | solution.py:633
  50.2 1.9 collective-permute-start.14
  52.2 2.2 %collective-permute-done.12.refs_0_ = bf16[48,1536]{1,0:T(8,128)(2,1)S(1)} collective-permute-done((bf16[48,1536]{1,0:T(8,128)(2,1)S(1)}, bf16[48,1536]{1,0:T(8,128)(2,1)S(1)}, u32[]{:S(2)}, u32[]{:S(2)}) %collective-permute-start.12) | collective-permute-done | bytes 147488 | tf_op jit(solution)/shard_map/ppermute | solution.py:633
  54.4 4.4 %collective-permute-done.13.refs_1_ = bf16[48,1536]{1,0:T(8,128)(2,1)S(1)} collective-permute-done((bf16[48,1536]{1,0:T(8,128)(2,1)S(1)}, bf16[48,1536]{1,0:T(8,128)(2,1)S(1)}, u32[]{:S(2)}, u32[]{:S(2)}) %collective-permute-start.13) | collective-permute-done | bytes 147488 | tf_op jit(solution)/shard_map/ppermute | solution.py:633
  65.9 14.4 %attend.1 = (f32[8,768]{1,0:T(8,128)S(1)}, bf16[2,224,768]{2,1,0:T(8,128)(2,1)S(1)}, bf16[2,224,768]{2,1,0:T(8,128)(2,1)}, bf16[2,256,768]{2,1,0:T(8,128)(2,1)},...) custom-call(s32[112]{0:T(128)S(1)} %concatenate.52.meta.refs_0_, ...), custom_call_target="tpu_custom_call" | custom-call | flops 1000 | bytes 1000 | tf_op jit(solution)/shard_map/attend/pallas_call | solution.py:194
  86.5 9.5 %hidden_fwd.1 = (bf16[384,1536]{1,0:T(8,128)(2,1)}, bf16[384,1536]{1,0:T(8,128)(2,1)}) custom-call(s32[112]{0:T(128)S(1)} %concatenate.52.meta.refs_0_, bf16[448,768]{1,0:T(8,128)(2,1)S(1)} %bitcast.91, bf16[448,768]{1,0:T(8,128)(2,1)S(1)} %bitcast.93, bf16[448,768]{1,0:T(8,128)(2,1)} %bitcast.96, bf16[448,768]{1,0:T(8,128)(2,1)} %bitcast.103, ...), custom_call_target="tpu_custom_call" | custom-call | flops 1000 | bytes 1000 | tf_op jit(solution)/shard_map/hidden_fwd/pallas_call | solution.py:254
  96.9 16.0 %hidden_back.1 = (f32[1,1536]{1,0:T(1,128)S(1)}, bf16[384,1536]{1,0:T(8,128)(2,1)}, bf16[384,1536]{1,0:T(8,128)(2,1)}, f32[448,768]{1,0:T(8,128)}, bf16[448,768]...) custom-call(s32[112]{0:T(128)S(1)} %concatenate.52.meta.refs_0_, bf16[448,768]{1,0:T(8,128)(2,1)S(1)} %bitcast.92, ...), custom_call_target="tpu_custom_call" | custom-call | flops 1000 | bytes 1000 | tf_op jit(solution)/shard_map/hidden_back/pallas_call | solution.py:317
  116.0 15.0 %attend_back.2 = (f32[4,768]{1,0:T(4,128)S(1)}, f32[2,512]{1,0:T(2,128)S(1)}, f32[128,128]{1,0:T(8,128)S(1)}, bf16[768,1024]{1,0:T(8,128)(2,1)}, bf16[768,1024]{...) custom-call(s32[112]{0:T(128)S(1)} %concatenate.52.meta.refs_0_, ...), custom_call_target="tpu_custom_call" | custom-call | flops 1000 | bytes 1000 | tf_op jit(solution)/shard_map/attend_back/pallas_call | solution.py:610
  131.9 3.4 %collective-permute-done.24 = bf16[384,1536]{1,0:T(8,128)(2,1)S(1)} collective-permute-done((bf16[384,1536]{1,0:T(8,128)(2,1)}, bf16[384,1536]{1,0:T(8,128)(2,1)S(1)}, u32[]{:S(2)}, u32[]{:S(2)}) %collective-permute-start.24) | collective-permute-done | bytes 1179680 | tf_op jit(solution)/shard_map/ppermute | solution.py:633
  138.6 3.0 %collective-permute-start.30 = (bf16[96,1536]{1,0:T(8,128)(2,1)S(1)}, bf16[96,1536]{1,0:T(8,128)(2,1)S(1)}, u32[]{:S(2)}, u32[]{:S(2)}) collective-permute-start(bf16[96,1536]{1,0:T(8,128)(2,1)S(1)} %slice.322), channel_id=1, source_target_pairs={{0,16},{2,18},{4,20},{6,22},{8,24},{10,26},{12,28},{14,30},{16,0},... | collective-permute-start | bytes 884744 | tf_op jit(solution)/shard_map/ppermute | solution.py:647
  141.6 12.2 %attend_back.3 = (f32[48,512]{1,0:T(8,128)S(1)}, bf16[768,512]{1,0:T(8,128)(2,1)}, bf16[768,512]{1,0:T(8,128)(2,1)}, f32[2,224,768]{2,1,0:T(8,128)}) custom-call(s32[112]{0:T(128)S(1)} %concatenate.52.meta.refs_0_, f32[8,768]{1,0:T(8,128)S(1)} %get-tuple-element.187.vecs, bf16[256,128]{1,0:T(8,128)(2,1)S(1)} %copy-done.11, ...), custom_call_target="tpu_custom_call" | custom-call | flops 1000 | bytes 1000 | tf_op jit(solution)/shard_map/attend_back/pallas_call | solution.py:610
  157.6 6.0 %collective-permute-done.33 = bf16[192,1024]{1,0:T(8,128)(2,1)S(1)} collective-permute-done((bf16[192,1024]{1,0:T(8,128)(2,1)S(1)}, bf16[192,1024]{1,0:T(8,128)(2,1)S(1)}, u32[]{:S(2)}, u32[]{:S(2)}) %collective-permute-start.33) | collective-permute-done | bytes 393248 | tf_op jit(solution)/shard_map/ppermute | solution.py:633
  168.0 2.6 %collective-permute-start.39 = (bf16[96,1024]{1,0:T(8,128)(2,1)S(1)}, bf16[96,1024]{1,0:T(8,128)(2,1)S(1)}, u32[]{:S(2)}, u32[]{:S(2)}) collective-permute-start(bf16[96,1024]{1,0:T(8,128)(2,1)S(1)} %slice.323), channel_id=1, source_target_pairs={{0,16},{2,18},{4,20},{6,22},{8,24},{10,26},{12,28},{14,30},{16,0},... | collective-permute-start | bytes 589832 | tf_op jit(solution)/shard_map/ppermute | solution.py:647
  170.6 5.9 %hidden_out.1 = (f32[448,768]{1,0:T(8,128)}, bf16[448,768]{1,0:T(8,128)(2,1)S(1)}) custom-call(s32[112]{0:T(128)S(1)} %concatenate.52.meta.refs_0_, bf16[896,1536]{1,0:T(8,128)(2,1)} %get-tuple-element.255.acts_in, bf16[96,4736]{1,0:T(8,128)(2,1)} %copy-done, bf16[96,4736]{1,0:T(8,128)(2,1)} %copy-done.13, bf16[288,1536]{1,0:T(8,128)(2,1)S(1)} %copy-done.2, ...), custom_call_target="tpu_custom_call" | custom-call | flops 1000 | bytes 1000 | tf_op jit(solution)/shard_map/hidden_out/pallas_call | solution.py:361
  181.3 2.0 copy.67
  188.5 2.9 %collective-permute-start.45 = (bf16[48,512]{1,0:T(8,128)(2,1)S(1)}, bf16[48,512]{1,0:T(8,128)(2,1)S(1)}, u32[]{:S(2)}, u32[]{:S(2)}) collective-permute-start(bf16[48,512]{1,0:T(8,128)(2,1)S(1)} %get-tuple-element.299), channel_id=1, source_target_pairs={{0,16},{1,17},{2,18},{3,19},{4,20},{5,21},{6,22},{7,23},{8,24},{9,... | collective-permute-start | bytes 147464 | tf_op jit(solution)/shard_map/ppermute | solution.py:633
  195.7 1.9 collective-permute-done.45.refs_5_
  199.7 2.7 %collective-permute-done.48 = f32[48,512]{1,0:T(8,128)S(1)} collective-permute-done((f32[48,512]{1,0:T(8,128)S(1)}, f32[48,512]{1,0:T(8,128)S(1)}, u32[]{:S(2)}, u32[]{:S(2)}) %collective-permute-start.48) | collective-permute-done | bytes 98336 | tf_op jit(solution)/shard_map/ppermute | solution.py:647
  (258 shorter events, 73.6 us)
Async XLA Ops:
  5.5 12.5 %collective-permute-start.1 = (bf16[48,1664]{1,0:T(8,128)(2,1)S(1)}, bf16[48,1664]{1,0:T(8,128)(2,1)S(1)}, u32[]{:S(2)}, u32[]{:S(2)}) collective-permute-start(bf16[48,1664]{1,0:T(8,128)(2,1)S(1)} %pad_maximum_fusion.2), channel_id=1, source_target_pairs={{0,8},{1,9},{2,10},{3,11},{4,12},{5,13},{6,14},{7,15},{8,16},{9,17... | collective-permute-start | bytes 479240 | tf_op jit(solution)/shard_map/ppermute | solution.py:633
  8.4 13.4 %collective-permute-start.2 = (bf16[48,1664]{1,0:T(8,128)(2,1)S(1)}, bf16[48,1664]{1,0:T(8,128)(2,1)S(1)}, u32[]{:S(2)}, u32[]{:S(2)}) collective-permute-start(bf16[48,1664]{1,0:T(8,128)(2,1)S(1)} %pad_maximum_fusion.2), channel_id=1, source_target_pairs={{0,16},{1,17},{2,18},{3,19},{4,20},{5,21},{6,22},{7,23},{8,24},{9,... | collective-permute-start | bytes 479240 | tf_op jit(solution)/shard_map/ppermute | solution.py:633
  11.0 10.8 %collective-permute-start.3 = (bf16[48,1664]{1,0:T(8,128)(2,1)S(1)}, bf16[48,1664]{1,0:T(8,128)(2,1)S(1)}, u32[]{:S(2)}, u32[]{:S(2)}) collective-permute-start(bf16[48,1664]{1,0:T(8,128)(2,1)S(1)} %pad_maximum_fusion.2), channel_id=1, source_target_pairs={{0,24},{1,25},{2,26},{3,27},{4,28},{5,29},{6,30},{7,31},{8,0},{9,1... | collective-permute-start | bytes 479240 | tf_op jit(solution)/shard_map/ppermute | solution.py:633
  22.4 18.5 %collective-permute-start.5 = (bf16[96,4736]{1,0:T(8,128)(2,1)S(1)}, bf16[96,4736]{1,0:T(8,128)(2,1)S(1)}, u32[]{:S(2)}, u32[]{:S(2)}) collective-permute-start(bf16[96,4736]{1,0:T(8,128)(2,1)S(1)} %stack.288.refs_0_.refs_4_), channel_id=1, source_target_pairs={{0,4},{1,3},{2,6},{3,1},{4,0},{5,7},{6,2},{7,5},{8,12},{9,11},{10,... | collective-permute-start | bytes 2727944 | tf_op jit(solution)/shard_map/ppermute | solution.py:633
  24.6 15.8 %collective-permute-start.6 = (bf16[144,1664]{1,0:T(8,128)(2,1)S(1)}, bf16[144,1664]{1,0:T(8,128)(2,1)S(1)}, u32[]{:S(2)}, u32[]{:S(2)}) collective-permute-start(bf16[144,1664]{1,0:T(8,128)(2,1)S(1)} %stack.287.refs_0_), channel_id=1, source_target_pairs={{0,2},{1,5},{2,0},{3,7},{4,6},{5,1},{6,4},{7,3},{8,10},{9,13},{10,... | collective-permute-start | bytes 1437704 | tf_op jit(solution)/shard_map/ppermute | solution.py:633
  26.2 9.7 %collective-permute-start.7 = (bf16[48,1536]{1,0:T(8,128)(2,1)S(1)}, bf16[48,1536]{1,0:T(8,128)(2,1)S(1)}, u32[]{:S(2)}, u32[]{:S(2)}) collective-permute-start(bf16[48,1536]{1,0:T(8,128)(2,1)S(1)} %copy-done.38), channel_id=1, source_target_pairs={{0,8},{1,9},{2,10},{3,11},{4,12},{5,13},{6,14},{7,15},{8,16},{9,17... | collective-permute-start | bytes 442376 | tf_op jit(solution)/shard_map/ppermute | solution.py:633
  30.1 10.4 %collective-permute-start.8 = (bf16[48,1536]{1,0:T(8,128)(2,1)S(1)}, bf16[48,1536]{1,0:T(8,128)(2,1)S(1)}, u32[]{:S(2)}, u32[]{:S(2)}) collective-permute-start(bf16[48,1536]{1,0:T(8,128)(2,1)S(1)} %copy-done.38), channel_id=1, source_target_pairs={{0,16},{1,17},{2,18},{3,19},{4,20},{5,21},{6,22},{7,23},{8,24},{9,... | collective-permute-start | bytes 442376 | tf_op jit(solution)/shard_map/ppermute | solution.py:633
  41.6 18.6 %collective-permute-start.10 = (bf16[288,1664]{1,0:T(8,128)(2,1)S(1)}, bf16[288,1664]{1,0:T(8,128)(2,1)S(1)}, u32[]{:S(2)}, u32[]{:S(2)}) collective-permute-start(bf16[288,1664]{1,0:T(8,128)(2,1)S(1)} %stack.289.refs_2_), channel_id=1, source_target_pairs={{0,4},{1,3},{2,6},{3,1},{4,0},{5,7},{6,2},{7,5},{8,12},{9,11},{10,... | collective-permute-start | bytes 2875400 | tf_op jit(solution)/shard_map/ppermute | solution.py:633
  43.7 15.4 %collective-permute-start.11 = (bf16[144,1536]{1,0:T(8,128)(2,1)S(1)}, bf16[144,1536]{1,0:T(8,128)(2,1)S(1)}, u32[]{:S(2)}, u32[]{:S(2)}) collective-permute-start(bf16[144,1536]{1,0:T(8,128)(2,1)S(1)} %stack.290.refs_0_), channel_id=1, source_target_pairs={{0,2},{1,5},{2,0},{3,7},{4,6},{5,1},{6,4},{7,3},{8,10},{9,13},{10,... | collective-permute-start | bytes 1327112 | tf_op jit(solution)/shard_map/ppermute | solution.py:633
  61.2 20.0 %collective-permute-start.18 = (bf16[288,1536]{1,0:T(8,128)(2,1)S(1)}, bf16[288,1536]{1,0:T(8,128)(2,1)S(1)}, u32[]{:S(2)}, u32[]{:S(2)}) collective-permute-start(bf16[288,1536]{1,0:T(8,128)(2,1)S(1)} %stack.291.refs_2_), channel_id=1, source_target_pairs={{0,4},{1,3},{2,6},{3,1},{4,0},{5,7},{6,2},{7,5},{8,12},{9,11},{10,... | collective-permute-start | bytes 2654216 | tf_op jit(solution)/shard_map/ppermute | solution.py:633
  63.4 17.8 %collective-permute-start.19 = (bf16[144,1536]{1,0:T(8,128)(2,1)S(1)}, bf16[144,1536]{1,0:T(8,128)(2,1)S(1)}, u32[]{:S(2)}, u32[]{:S(2)}) collective-permute-start(bf16[144,1536]{1,0:T(8,128)(2,1)S(1)} %stack.292.refs_0_), channel_id=1, source_target_pairs={{0,2},{1,5},{2,0},{3,7},{4,6},{5,1},{6,4},{7,3},{8,10},{9,13},{10,... | collective-permute-start | bytes 1327112 | tf_op jit(solution)/shard_map/ppermute | solution.py:633
  81.7 14.2 %collective-permute-start.22 = (bf16[288,1536]{1,0:T(8,128)(2,1)S(1)}, bf16[288,1536]{1,0:T(8,128)(2,1)S(1)}, u32[]{:S(2)}, u32[]{:S(2)}) collective-permute-start(bf16[288,1536]{1,0:T(8,128)(2,1)S(1)} %stack.293.refs_6_.refs_2_), channel_id=1, source_target_pairs={{0,4},{1,3},{2,6},{3,1},{4,0},{5,7},{6,2},{7,5},{8,12},{9,11},{10,... | collective-permute-start | bytes 2654216 | tf_op jit(solution)/shard_map/ppermute | solution.py:633
  96.0 17.1 %collective-permute-start.23 = (bf16[384,1536]{1,0:T(8,128)(2,1)}, bf16[384,1536]{1,0:T(8,128)(2,1)S(1)}, u32[]{:S(2)}, u32[]{:S(2)}) collective-permute-start(bf16[384,1536]{1,0:T(8,128)(2,1)} %get-tuple-element.207), channel_id=1, source_target_pairs={{0,4},{1,3},{2,6},{3,1},{4,0},{5,7},{6,2},{7,5},{8,12},{9,11},{10,... | collective-permute-start | bytes 3538952 | tf_op jit(solution)/shard_map/ppermute | solution.py:633
  113.3 17.8 %collective-permute-start.25 = (bf16[192,1536]{1,0:T(8,128)(2,1)S(1)}, bf16[192,1536]{1,0:T(8,128)(2,1)S(1)}, u32[]{:S(2)}, u32[]{:S(2)}) collective-permute-start(bf16[192,1536]{1,0:T(8,128)(2,1)S(1)} %add_convert_fusion.3), channel_id=1, source_target_pairs={{0,2},{1,5},{2,0},{3,7},{4,6},{5,1},{6,4},{7,3},{8,10},{9,13},{10,... | collective-permute-start | bytes 1769480 | tf_op jit(solution)/shard_map/ppermute | solution.py:633
  114.3 21.0 %collective-permute-start.24 = (bf16[384,1536]{1,0:T(8,128)(2,1)}, bf16[384,1536]{1,0:T(8,128)(2,1)S(1)}, u32[]{:S(2)}, u32[]{:S(2)}) collective-permute-start(bf16[384,1536]{1,0:T(8,128)(2,1)} %get-tuple-element.210), channel_id=1, source_target_pairs={{0,4},{1,3},{2,6},{3,1},{4,0},{5,7},{6,2},{7,5},{8,12},{9,11},{10,... | collective-permute-start | bytes 3538952 | tf_op jit(solution)/shard_map/ppermute | solution.py:633
  135.5 20.2 %collective-permute-start.31 = (bf16[192,1536]{1,0:T(8,128)(2,1)S(1)}, bf16[192,1536]{1,0:T(8,128)(2,1)S(1)}, u32[]{:S(2)}, u32[]{:S(2)}) collective-permute-start(bf16[192,1536]{1,0:T(8,128)(2,1)S(1)} %add_convert_fusion.2), channel_id=1, source_target_pairs={{0,2},{1,5},{2,0},{3,7},{4,6},{5,1},{6,4},{7,3},{8,10},{9,13},{10,... | collective-permute-start | bytes 1769480 | tf_op jit(solution)/shard_map/ppermute | solution.py:633
  137.0 18.6 %collective-permute-start.32 = (bf16[384,1024]{1,0:T(8,128)(2,1)S(1)}, bf16[384,1024]{1,0:T(8,128)(2,1)S(1)}, u32[]{:S(2)}, u32[]{:S(2)}) collective-permute-start(bf16[384,1024]{1,0:T(8,128)(2,1)S(1)} %slice.250), channel_id=1, source_target_pairs={{0,4},{1,3},{2,6},{3,1},{4,0},{5,7},{6,2},{7,5},{8,12},{9,11},{10,... | collective-permute-start | bytes 2359304 | tf_op jit(solution)/shard_map/ppermute | solution.py:633
  138.6 17.1 %collective-permute-start.30 = (bf16[96,1536]{1,0:T(8,128)(2,1)S(1)}, bf16[96,1536]{1,0:T(8,128)(2,1)S(1)}, u32[]{:S(2)}, u32[]{:S(2)}) collective-permute-start(bf16[96,1536]{1,0:T(8,128)(2,1)S(1)} %slice.322), channel_id=1, source_target_pairs={{0,16},{2,18},{4,20},{6,22},{8,24},{10,26},{12,28},{14,30},{16,0},... | collective-permute-start | bytes 884744 | tf_op jit(solution)/shard_map/ppermute | solution.py:647
  156.7 21.4 %collective-permute-start.36 = (bf16[96,1536]{1,0:T(8,128)(2,1)S(1)}, bf16[96,1536]{1,0:T(8,128)(2,1)S(1)}, u32[]{:S(2)}, u32[]{:S(2)}) collective-permute-start(bf16[96,1536]{1,0:T(8,128)(2,1)S(1)} %slice.321), channel_id=1, source_target_pairs={{0,16},{2,18},{4,20},{6,22},{8,24},{10,26},{12,28},{14,30},{16,0},... | collective-permute-start | bytes 884744 | tf_op jit(solution)/shard_map/ppermute | solution.py:647
  164.1 14.0 %collective-permute-start.35 = (bf16[384,512]{1,0:T(8,128)(2,1)S(1)}, bf16[384,512]{1,0:T(8,128)(2,1)S(1)}, u32[]{:S(2)}, u32[]{:S(2)}) collective-permute-start(bf16[384,512]{1,0:T(8,128)(2,1)S(1)} %slice.251), channel_id=1, source_target_pairs={{0,4},{1,3},{2,6},{3,1},{4,0},{5,7},{6,2},{7,5},{8,12},{9,11},{10,... | collective-permute-start | bytes 1179656 | tf_op jit(solution)/shard_map/ppermute | solution.py:633
  165.1 13.0 %collective-permute-start.37 = (bf16[48,1536]{1,0:T(8,128)(2,1)S(1)}, bf16[48,1536]{1,0:T(8,128)(2,1)S(1)}, u32[]{:S(2)}, u32[]{:S(2)}) collective-permute-start(bf16[48,1536]{1,0:T(8,128)(2,1)S(1)} %fusion.3), channel_id=1, source_target_pairs={{0,8},{2,10},{4,12},{6,14},{8,0},{10,2},{12,4},{14,6},{16,24},{18,... | collective-permute-start | bytes 442376 | tf_op jit(solution)/shard_map/ppermute | solution.py:647
  167.0 11.1 %collective-permute-start.34 = (f32[48,512]{1,0:T(8,128)S(1)}, f32[48,512]{1,0:T(8,128)S(1)}, u32[]{:S(2)}, u32[]{:S(2)}) collective-permute-start(f32[48,512]{1,0:T(8,128)S(1)} %add.1108), channel_id=1, source_target_pairs={{0,4},{1,3},{2,6},{3,1},{4,0},{5,7},{6,2},{7,5},{8,12},{9,11},{10,... | collective-permute-start | bytes 294920 | tf_op jit(solution)/shard_map/ppermute | solution.py:633
  168.0 15.3 %collective-permute-start.39 = (bf16[96,1024]{1,0:T(8,128)(2,1)S(1)}, bf16[96,1024]{1,0:T(8,128)(2,1)S(1)}, u32[]{:S(2)}, u32[]{:S(2)}) collective-permute-start(bf16[96,1024]{1,0:T(8,128)(2,1)S(1)} %slice.323), channel_id=1, source_target_pairs={{0,16},{2,18},{4,20},{6,22},{8,24},{10,26},{12,28},{14,30},{16,0},... | collective-permute-start | bytes 589832 | tf_op jit(solution)/shard_map/ppermute | solution.py:647
  186.9 10.8 %collective-permute-start.43 = (f32[48,512]{1,0:T(8,128)S(1)}, f32[48,512]{1,0:T(8,128)S(1)}, u32[]{:S(2)}, u32[]{:S(2)}) collective-permute-start(f32[48,512]{1,0:T(8,128)S(1)} %add.1120), channel_id=1, source_target_pairs={{0,16},{2,18},{4,20},{6,22},{8,24},{10,26},{12,28},{14,30},{16,0},... | collective-permute-start | bytes 294920 | tf_op jit(solution)/shard_map/ppermute | solution.py:647
  (71 other events, 530.1 us)
